TPU v7x, 32 devices: a whole 2x2x4 slice. The times are simulated.
32 devices in a mesh: grp: 1, ep: 16 (over z, y, x), pd: 2 (over core).
Axes of the slice: x: 2, y: 2, z: 4, core: 2. Of those that a mesh axis runs over, the one named last changes fastest.
Arguments:
- prompt_kv: bfloat16 [256, 2, 16, 4, 128], P(('grp', 'ep'), None, None, 'pd'), may hold values from -6 to 6
- page_owner: int32 [256, 1], P('grp'), may hold values from 0 to 15; in each aligned block of 16 rows (0 to 15, 16 to 31, ...) at most 2 rows name the same one
- page_slot: int32 [256], P('grp'), may hold values from 0 to 7
- page_fill: int32 [256], P('grp'), may hold values from 1 to 16
- queries: bfloat16 [128, 3, 64, 128], P(('grp', 'ep'), None, 'pd'), may hold values from -400 to 400
- new_kv: bfloat16 [128, 3, 2, 4, 128], P(('grp', 'ep'), None, None, 'pd'), may hold values from -8 to 8
- moe_input: bfloat16 [128, 3, 4096], P(('grp', 'ep')), may hold values from -6 to 6
- expert_routes: int32 [3, 128, 8], P(None, ('grp', 'ep')), may hold values from 0 to 15, all different within a row; in each aligned block of 8 rows (0 to 7, 8 to 15, ..., all dimensions but the last counted through in order) at most 8 rows name the same one
- route_probs: float32 [128, 3, 8], P(('grp', 'ep')), may hold values from 0.02 to 0.5
- w_gate: bfloat16 [16, 4096, 768], P('ep', None, 'pd'), may hold values from -0.09375 to 0.09375
- w_up: bfloat16 [16, 4096, 768], P('ep', None, 'pd'), may hold values from -0.09375 to 0.09375
- w_down: bfloat16 [16, 768, 4096], P('ep', None, 'pd'), may hold values from -0.21875 to 0.21875
Outputs:
- attn_out: bfloat16 [128, 3, 64, 128], P(('grp', 'ep'), None, 'pd')
- moe_out: bfloat16 [128, 3, 4096], P(('grp', 'ep'), None, 'pd')
Inputs may be any that keep to these rules, and one draw needn't show every extreme that they name: `page_owner`: the 16 pages of one index of ep name any decode owner at most 2 times, a bound that some block reaches. `expert_routes`: each token's 8 experts differ; in one decode step the 8 tokens of one index of ep name any expert at most 8 times, and this bound is reached.
All inputs are finite; a program needn't handle non-finite values.
Results may differ from a plain program's by a relative error of at most 0.0057.
Values may be sent and summed in bfloat16 or wider, within the bound.
No kernel may reach another device: no remote copies, remote signals or barrier semaphores. Data moves between devices by JAX's collectives and lax.ppermute only.
A program may use at most 64 MiB of HBM per device.

v0:
```python
import math

import jax
import jax.numpy as jnp
from jax import lax
from jax.sharding import PartitionSpec as P

CAP = 2


LIMIT = 448.0


def quantize(blocks):
    values = blocks.astype(jnp.float32)
    largest = jnp.max(jnp.abs(values), axis=(2, 4), keepdims=True)
    block_scale = jnp.full(largest.shape, 2.0 ** (-16), jnp.float32)
    inverse = jnp.full(largest.shape, 2.0**16, jnp.float32)
    for exponent in range(-16, 4):
        exceeds = largest > LIMIT * 2.0**exponent
        block_scale = jnp.where(exceeds, block_scale * 2.0, block_scale)
        inverse = jnp.where(exceeds, inverse * 0.5, inverse)
    scaled = values * inverse
    magnitude = jnp.abs(scaled)
    grid_step = jnp.full(scaled.shape, 2.0 ** (-9), jnp.float32)
    grid_inverse = jnp.full(scaled.shape, 2.0**9, jnp.float32)
    for exponent in range(-5, 9):
        exceeds = magnitude >= 2.0**exponent
        grid_step = jnp.where(exceeds, grid_step * 2.0, grid_step)
        grid_inverse = jnp.where(exceeds, grid_inverse * 0.5, grid_inverse)
    levels = jnp.minimum(jnp.floor(magnitude * grid_inverse + 0.5) * grid_step, LIMIT)
    page_quant = (jnp.sign(scaled) * levels).astype(jnp.bfloat16)
    page_scale = block_scale.astype(jnp.bfloat16)
    return (page_quant, page_scale)


def dequantize(page_quant, page_scale):
    return (page_quant.astype(jnp.float32) * page_scale.astype(jnp.float32)).astype(jnp.bfloat16)


def attend(queries, cache_keys, cache_values, visible, fresh_keys, fresh_values):
    requests, steps, heads, width = queries.shape
    groups = cache_keys.shape[1]
    grouped = queries.reshape(requests, steps, groups, heads // groups, width)
    factor = 1.0 / math.sqrt(width)
    cache_scores = (
        jnp.einsum("rskgd,jkd->rskgj", grouped, cache_keys, preferred_element_type=jnp.float32)
        * factor
    )
    fresh_scores = (
        jnp.einsum("rskgd,rtkd->rskgt", grouped, fresh_keys, preferred_element_type=jnp.float32)
        * factor
    )
    cache_mask = visible[:, None, None, None, :]
    fresh_mask = (jnp.arange(steps)[None, :] <= jnp.arange(steps)[:, None])[None, :, None, None, :]
    cache_scores = jnp.where(cache_mask, cache_scores, -jnp.inf)
    fresh_scores = jnp.where(fresh_mask, fresh_scores, -jnp.inf)
    peak = jnp.maximum(
        jnp.max(cache_scores, axis=-1, keepdims=True), jnp.max(fresh_scores, axis=-1, keepdims=True)
    )
    cache_weight = jnp.where(cache_mask, jnp.exp(cache_scores - peak), 0.0)
    fresh_weight = jnp.where(fresh_mask, jnp.exp(fresh_scores - peak), 0.0)
    total_weight = jnp.sum(cache_weight, axis=-1, keepdims=True) + jnp.sum(
        fresh_weight, axis=-1, keepdims=True
    )
    mixed = jnp.einsum(
        "rskgj,jkd->rskgd",
        cache_weight.astype(jnp.bfloat16),
        cache_values,
        preferred_element_type=jnp.float32,
    )
    mixed = mixed + jnp.einsum(
        "rskgt,rtkd->rskgd",
        fresh_weight.astype(jnp.bfloat16),
        fresh_values,
        preferred_element_type=jnp.float32,
    )
    return (mixed / total_weight).reshape(requests, steps, heads, width).astype(jnp.bfloat16)


def pack(rows, routes, capacity, experts):
    count, top = routes.shape
    flat = routes.reshape(-1)
    onehot = (flat[:, None] == jnp.arange(experts)[None, :]).astype(jnp.int32)
    earlier = jnp.sum(onehot * (jnp.cumsum(onehot, axis=0) - 1), axis=1)
    target = flat * capacity + earlier
    source = jnp.arange(count * top) // top
    send = jnp.zeros((experts * capacity, rows.shape[1]), rows.dtype).at[target].set(rows[source])
    return (send.reshape(experts, capacity, rows.shape[1]), target)


def expert_front(received, w_gate, w_up):
    gate = jnp.einsum("nid,df->nif", received, w_gate[0], preferred_element_type=jnp.float32)
    up = jnp.einsum("nid,df->nif", received, w_up[0], preferred_element_type=jnp.float32)
    return (jax.nn.silu(gate) * up).astype(jnp.bfloat16)


def add_down(w_down, piece):
    down_rows = w_down[0]
    return jnp.einsum("nif,fd->nid", piece, down_rows, preferred_element_type=jnp.float32)


def experts_step(received, w_gate, w_up, w_down):
    hidden = expert_front(received, w_gate, w_up)
    total = add_down(w_down, lax.all_gather(hidden, "pd", axis=2, tiled=True))
    return lax.all_to_all(total.astype(jnp.bfloat16), "ep", split_axis=0, concat_axis=0, tiled=True)


def combine(returned, target, probs):
    chosen = returned[target].reshape(probs.shape + (returned.shape[1],))
    return jnp.sum(probs[..., None] * chosen.astype(jnp.float32), axis=1).astype(jnp.bfloat16)


def body(
    prompt_kv,
    page_owner,
    page_slot,
    page_fill,
    queries,
    new_kv,
    moe_input,
    expert_routes,
    route_probs,
    w_gate,
    w_up,
    w_down,
):
    owners_count = lax.axis_size("ep")
    own_index = lax.axis_index("ep")
    pages_local = prompt_kv.shape[0]
    page_len = prompt_kv.shape[2]
    heads_local = prompt_kv.shape[3]
    width = prompt_kv.shape[4]
    requests_own = queries.shape[0]
    steps = queries.shape[1]
    slots_total = owners_count * CAP
    owner_table = page_owner[:, 0].reshape(owners_count, pages_local)
    page_quant, page_scale = quantize(prompt_kv)
    own_row = lax.dynamic_index_in_dim(owner_table, own_index, 0, keepdims=False)
    choose_owner = (own_row[:, None] == jnp.arange(owners_count)[None, :]).astype(jnp.int32)
    earlier = jnp.sum(choose_owner * (jnp.cumsum(choose_owner, axis=0) - 1), axis=1)
    target = own_row * CAP + earlier
    send_quant = (
        jnp.zeros((slots_total,) + page_quant.shape[1:], jnp.bfloat16).at[target].set(page_quant)
    )
    send_scale = (
        jnp.zeros((slots_total,) + page_scale.shape[1:], jnp.bfloat16).at[target].set(page_scale)
    )
    recv_quant, recv_scale = (
        lax.all_to_all(send_quant, "ep", split_axis=0, concat_axis=0, tiled=True),
        lax.all_to_all(send_scale, "ep", split_axis=0, concat_axis=0, tiled=True),
    )
    cache = dequantize(recv_quant, recv_scale)
    mine = (owner_table == own_index).astype(jnp.int32)
    mine_rank = jnp.cumsum(mine, axis=1) - 1
    picked = mine[:, None, :] * (mine_rank[:, None, :] == jnp.arange(CAP)[None, :, None]).astype(
        jnp.int32
    )
    local_page = jnp.sum(picked * jnp.arange(pages_local)[None, None, :], axis=2)
    occupied = (jnp.sum(picked, axis=2) > 0).reshape(-1)
    global_page = (jnp.arange(owners_count)[:, None] * pages_local + local_page).reshape(-1)
    slot_of = page_slot[global_page]
    fill_of = page_fill[global_page]
    visible = occupied[None, :, None] & (
        slot_of[None, :, None] == jnp.arange(requests_own)[:, None, None]
    )
    visible = visible & (jnp.arange(page_len)[None, None, :] < fill_of[None, :, None])
    visible = visible.reshape(requests_own, slots_total * page_len)
    cache_keys = cache[:, 0].reshape(slots_total * page_len, heads_local, width)
    cache_values = cache[:, 1].reshape(slots_total * page_len, heads_local, width)
    attn_out = attend(queries, cache_keys, cache_values, visible, new_kv[:, :, 0], new_kv[:, :, 1])
    top = expert_routes.shape[-1]
    step_cap = min(requests_own, max(2, 2 * requests_own * top // owners_count))
    half_width = w_down.shape[2]
    mixed_steps = []
    for step in range(steps):
        send, target_rows = pack(moe_input[:, step], expert_routes[step], step_cap, owners_count)
        back = experts_step(
            lax.all_to_all(send, "ep", split_axis=0, concat_axis=0, tiled=True),
            w_gate=w_gate,
            w_up=w_up,
            w_down=w_down,
        )
        mixed_steps.append(combine(back.reshape(-1, half_width), target_rows, route_probs[:, step]))
    moe_out = jnp.stack(mixed_steps, axis=1)
    return (attn_out, moe_out)


def solution(mesh):
    return jax.shard_map(
        body,
        mesh=mesh,
        in_specs=(
            P(("grp", "ep"), None, None, "pd", None),
            P("grp", None),
            P("grp"),
            P("grp"),
            P(("grp", "ep"), None, "pd", None),
            P(("grp", "ep"), None, None, "pd", None),
            P(("grp", "ep"), None, None),
            P(None, ("grp", "ep"), None),
            P(("grp", "ep"), None, None),
            P("ep", None, "pd"),
            P("ep", None, "pd"),
            P("ep", None, "pd"),
        ),
        out_specs=(P(("grp", "ep"), None, "pd", None), P(("grp", "ep"), None, "pd")),
        check_vma=False,
    )
```

profile of v0, /device:TPU:0, one launch (start us, length us, event | category | flops | bytes accessed | tf_op | source)
XLA Modules:
  0.0 202.7 jit_solution(13676067973437071252)
XLA Ops:
  7.6 2.3 %scatter_fusion.1 = bf16[32,2,2]{2,1,0:T(2,128)(2,1)} fusion(bf16[32,2,2]{2,1,0:T(2,128)(2,1)} %broadcast.870, s32[16]{0:T(128)S(1)} %fusion.91, bf16[16,2,2]{2,1,0:T(2,128)(2,1)S(1)} %copy.172), kind=kCustom, calls=%fused_computation.9 | custom fusion | bytes 448 | tf_op jit(solution)/shard_map/scatter | solution.py:147
  9.9 8.3 %all-to-all-start.1 = ((bf16[32,2,1,2,1]{3,1,4,2,0:T(2,128)(2,1)}), bf16[32,2,1,2,1]{3,1,4,2,0:T(2,128)(2,1)S(1)}, u32[]{:S(2)}, u32[]{:S(2)}) async-start(bf16[32,2,1,2,1]{3,1,4,2,0:T(2,128)(2,1)} %bitcast.77), calls=%async_computation.1 | async-start | bytes 32768 | tf_op jit(solution)/shard_map/all_to_all | solution.py:151
  20.3 6.9 %fusion.57 = bf16[16,2,16,2,128]{4,3,2,1,0:T(2,128)(2,1)S(1)} fusion(bf16[16,2,16,2,128]{4,3,2,1,0:T(2,128)(2,1)} %param.12, f32[16,2,2]{2,1,0:T(2,128)S(1)} %get-tuple-element.33), kind=kLoop, calls=%fused_computation.84 | loop fusion | flops 10354688 | bytes 524544 | tf_op jit(solution)/shard_map/convert_element_type | solution.py:32
  30.9 2.7 %scatter_fusion = bf16[32,2,16,2,128]{4,2,3,1,0:T(8,128)(2,1)} fusion(bf16[32,2,16,2,128]{4,2,3,1,0:T(8,128)(2,1)} %broadcast_in_dim.50, s32[16]{0:T(128)S(1)} %fusion.91, bf16[16,2,16,2,128]{4,2,3,1,0:T(8,128)(2,1)} %copy.151), kind=kCustom, calls=%fused_computation.8 | custom fusion | bytes 786496 | tf_op jit(solution)/shard_map/scatter | solution.py:144
  33.6 7.0 %all-to-all-start = ((bf16[32,2,16,2,128]{4,2,3,1,0:T(8,128)(2,1)}), bf16[32,2,16,2,128]{4,2,3,1,0:T(8,128)(2,1)}, u32[]{:S(2)}, u32[]{:S(2)}) async-start(bf16[32,2,16,2,128]{4,2,3,1,0:T(8,128)(2,1)} %scatter_fusion), calls=%async_computation | async-start | bytes 1048576 | tf_op jit(solution)/shard_map/all_to_all | solution.py:150
  42.8 3.9 %scatter_custom_fusion.3 = bf16[128,4096]{1,0:T(8,128)(2,1)} fusion(s32[64]{0:T(128)S(1)} %fusion.94, bf16[8,4096]{1,0:T(8,128)(2,1)S(1)} %get-tuple-element.8, s32[1024]{0:T(1024)S(1)} %pad_clamp_fusion.3, bf16[]{:T(256)} %constant.58.clone.1), kind=kCustom, calls=%fused_computation.98 | custom fusion | bytes 1048578 | tf_op jit(solution)/shard_map/scatter | solution.py:88
  46.8 8.5 %all-to-all-done = bf16[32,2,16,2,128]{4,2,3,1,0:T(8,128)(2,1)} async-done(((bf16[32,2,16,2,128]{4,2,3,1,0:T(8,128)(2,1)}), bf16[32,2,16,2,128]{4,2,3,1,0:T(8,128)(2,1)}, u32[]{:S(2)}, u32[]{:S(2)}) %all-to-all-start) | async-done | bytes 524320 | tf_op jit(solution)/shard_map/all_to_all | solution.py:150
  55.2 4.3 %all-to-all-start.4 = ((bf16[16,8,4096]{2,1,0:T(8,128)(2,1)}), bf16[16,8,4096]{2,1,0:T(8,128)(2,1)}, u32[]{:S(2)}, u32[]{:S(2)}) async-start(bf16[16,8,4096]{2,1,0:T(8,128)(2,1)} %bitcast.296), calls=%async_computation.4 | async-start | bytes 2097152 | tf_op jit(solution)/shard_map/all_to_all | solution.py:179
  60.5 5.1 %scatter_custom_fusion.4 = bf16[128,4096]{1,0:T(8,128)(2,1)} fusion(s32[64]{0:T(128)S(1)} %fusion.95, bf16[8,4096]{1,0:T(8,128)(2,1)} %get-tuple-element.7, s32[1024]{0:T(1024)S(1)} %pad_clamp_fusion.3, bf16[]{:T(256)} %constant.58.clone.1), kind=kCustom, calls=%fused_computation.96 | custom fusion | bytes 1049088 | tf_op jit(solution)/shard_map/scatter | solution.py:88
  66.4 16.5 %all-to-all-done.4 = bf16[16,8,4096]{2,1,0:T(8,128)(2,1)} async-done(((bf16[16,8,4096]{2,1,0:T(8,128)(2,1)}), bf16[16,8,4096]{2,1,0:T(8,128)(2,1)}, u32[]{:S(2)}, u32[]{:S(2)}) %all-to-all-start.4) | async-done | bytes 1048608 | tf_op jit(solution)/shard_map/all_to_all | solution.py:179
  82.9 5.9 %all-to-all-start.6 = ((bf16[16,8,4096]{2,1,0:T(8,128)(2,1)}), bf16[16,8,4096]{2,1,0:T(8,128)(2,1)}, u32[]{:S(2)}, u32[]{:S(2)}) async-start(bf16[16,8,4096]{2,1,0:T(8,128)(2,1)} %bitcast.294), calls=%async_computation.6 | async-start | bytes 2097152 | tf_op jit(solution)/shard_map/all_to_all | solution.py:179
  90.2 5.1 %scatter_custom_fusion.2 = bf16[128,4096]{1,0:T(8,128)(2,1)} fusion(s32[64]{0:T(128)S(1)} %fusion.93, bf16[8,4096]{1,0:T(8,128)(2,1)} %get-tuple-element.6, s32[1024]{0:T(1024)S(1)} %pad_clamp_fusion.3, bf16[]{:T(256)} %constant.58.clone.1), kind=kCustom, calls=%fused_computation.100 | custom fusion | bytes 1049088 | tf_op jit(solution)/shard_map/scatter | solution.py:88
  99.9 12.0 %all-to-all-done.6 = bf16[16,8,4096]{2,1,0:T(8,128)(2,1)} async-done(((bf16[16,8,4096]{2,1,0:T(8,128)(2,1)}), bf16[16,8,4096]{2,1,0:T(8,128)(2,1)}, u32[]{:S(2)}, u32[]{:S(2)}) %all-to-all-start.6) | async-done | bytes 1048608 | tf_op jit(solution)/shard_map/all_to_all | solution.py:179
  111.8 6.1 %all-to-all-start.2 = ((bf16[16,8,4096]{2,1,0:T(8,128)(2,1)}), bf16[16,8,4096]{2,1,0:T(8,128)(2,1)}, u32[]{:S(2)}, u32[]{:S(2)}) async-start(bf16[16,8,4096]{2,1,0:T(8,128)(2,1)} %bitcast.295), calls=%async_computation.2 | async-start | bytes 2097152 | tf_op jit(solution)/shard_map/all_to_all | solution.py:179
  119.4 2.5 %fusion.101 = (f32[8,3,2,16]{3,1,0,2:T(4,128)S(1)}, f32[8,3,2,16,512]{4,3,1,0,2:T(8,128)}) fusion(bf16[512,2,128,1,1]{2,0,4,3,1:T(8,128)(2,1)S(1)} %bitcast.297, bf16[8,3,2,16,128]{4,3,2,1,0:T(8,128)(2,1)} %bitcast.298, pred[8,512]{1,0:T(8,128)(4,1)S(1)} %broadcast_and_fusion), kind=kOutput, calls=%fused_computation.250 | convolution fusion | flops 101842176 | bytes 2038784 | tf_op jit(solution)/shard_map/rskgd,jkd->rskgj/dot_general | solution.py:47
  122.5 2.1 %fusion.14 = f32[16,8,384]{2,1,0:T(8,128)S(1)} fusion(bf16[16,8,4096]{2,1,0:T(8,128)(2,1)} %all-to-all-done.4, bf16[1,4096,384]{2,1,0:T(8,128)(2,1)S(1)} %copy-done.3), kind=kOutput, calls=%fused_computation.27 | convolution fusion | flops 402653184 | bytes 4390912 | tf_op jit(solution)/shard_map/nid,df->nif/dot_general | solution.py:93
  124.7 2.0 fusion.44
  130.0 11.4 %all-to-all-done.2 = bf16[16,8,4096]{2,1,0:T(8,128)(2,1)} async-done(((bf16[16,8,4096]{2,1,0:T(8,128)(2,1)}), bf16[16,8,4096]{2,1,0:T(8,128)(2,1)}, u32[]{:S(2)}, u32[]{:S(2)}) %all-to-all-start.2) | async-done | bytes 1048608 | tf_op jit(solution)/shard_map/all_to_all | solution.py:179
  141.4 5.9 %all-to-all-start.5 = ((bf16[16,8,2048]{2,1,0:T(8,128)(2,1)}), bf16[16,8,2048]{2,1,0:T(8,128)(2,1)}, u32[]{:S(2)}, u32[]{:S(2)}) async-start(bf16[16,8,2048]{2,1,0:T(8,128)(2,1)} %fusion.21), calls=%async_computation.5 | async-start | bytes 1048576 | tf_op jit(solution)/shard_map/all_to_all | solution.py:106
  147.3 3.1 %fusion.12 = f32[16,8,384]{2,1,0:T(8,128)S(1)} fusion(bf16[16,8,4096]{2,1,0:T(8,128)(2,1)} %all-to-all-done.6, bf16[1,4096,384]{2,1,0:T(8,128)(2,1)} %param.21), kind=kOutput, calls=%fused_computation.25 | convolution fusion | flops 402653184 | bytes 4390912 | tf_op jit(solution)/shard_map/nid,df->nif/dot_general | solution.py:93
  150.4 2.0 fusion.41
  152.4 1.9 all_gather.11
  155.7 5.3 %all-to-all-done.5 = bf16[16,8,2048]{2,1,0:T(8,128)(2,1)} async-done(((bf16[16,8,2048]{2,1,0:T(8,128)(2,1)}), bf16[16,8,2048]{2,1,0:T(8,128)(2,1)}, u32[]{:S(2)}, u32[]{:S(2)}) %all-to-all-start.5) | async-done | bytes 524320 | tf_op jit(solution)/shard_map/all_to_all | solution.py:106
  161.1 4.2 %all-to-all-start.7 = ((bf16[16,8,2048]{2,1,0:T(8,128)(2,1)}), bf16[16,8,2048]{2,1,0:T(8,128)(2,1)}, u32[]{:S(2)}, u32[]{:S(2)}) async-start(bf16[16,8,2048]{2,1,0:T(8,128)(2,1)} %fusion.24), calls=%async_computation.7 | async-start | bytes 1048576 | tf_op jit(solution)/shard_map/all_to_all | solution.py:106
  165.3 3.1 %fusion.16 = f32[16,8,384]{2,1,0:T(8,128)S(1)} fusion(bf16[16,8,4096]{2,1,0:T(8,128)(2,1)} %all-to-all-done.2, bf16[1,4096,384]{2,1,0:T(8,128)(2,1)} %param.21), kind=kOutput, calls=%fused_computation.29 | convolution fusion | flops 402653184 | bytes 4390912 | tf_op jit(solution)/shard_map/nid,df->nif/dot_general | solution.py:93
  168.5 2.0 fusion.47
  173.8 5.0 %all-to-all-done.7 = bf16[16,8,2048]{2,1,0:T(8,128)(2,1)} async-done(((bf16[16,8,2048]{2,1,0:T(8,128)(2,1)}), bf16[16,8,2048]{2,1,0:T(8,128)(2,1)}, u32[]{:S(2)}, u32[]{:S(2)}) %all-to-all-start.7) | async-done | bytes 524320 | tf_op jit(solution)/shard_map/all_to_all | solution.py:106
  178.7 4.5 %all-to-all-start.3 = ((bf16[16,8,2048]{2,1,0:T(8,128)(2,1)}), bf16[16,8,2048]{2,1,0:T(8,128)(2,1)}, u32[]{:S(2)}, u32[]{:S(2)}) async-start(bf16[16,8,2048]{2,1,0:T(8,128)(2,1)} %fusion.18), calls=%async_computation.3 | async-start | bytes 1048576 | tf_op jit(solution)/shard_map/all_to_all | solution.py:106
  188.1 2.2 %gather_fusion.3 = bf16[64,2048]{1,0:T(8,128)(2,1)S(1)} fusion(bf16[128,2048]{1,0:T(8,128)(2,1)} %bitcast.66, s32[1024]{0:T(1024)} %pad_clamp_fusion.1), kind=kCustom, calls=%fused_computation.5 | custom fusion | bytes 524544 | tf_op jit(solution)/shard_map/gather | solution.py:110
  190.3 2.9 %gather_fusion.4 = bf16[64,2048]{1,0:T(8,128)(2,1)} fusion(bf16[128,2048]{1,0:T(8,128)(2,1)} %bitcast.74, s32[1024]{0:T(1024)} %pad_clamp_fusion), kind=kCustom, calls=%fused_computation.7 | custom fusion | bytes 524544 | tf_op jit(solution)/shard_map/gather | solution.py:110
  193.2 3.3 %all-to-all-done.3 = bf16[16,8,2048]{2,1,0:T(8,128)(2,1)} async-done(((bf16[16,8,2048]{2,1,0:T(8,128)(2,1)}), bf16[16,8,2048]{2,1,0:T(8,128)(2,1)}, u32[]{:S(2)}, u32[]{:S(2)}) %all-to-all-start.3) | async-done | bytes 524320 | tf_op jit(solution)/shard_map/all_to_all | solution.py:106
  196.5 2.9 %gather_fusion.2 = bf16[64,2048]{1,0:T(8,128)(2,1)} fusion(bf16[128,2048]{1,0:T(8,128)(2,1)} %bitcast.58, s32[1024]{0:T(1024)} %pad_clamp_fusion.2), kind=kCustom, calls=%fused_computation.3 | custom fusion | bytes 524544 | tf_op jit(solution)/shard_map/gather | solution.py:110
  (150 shorter events, 41.0 us)
Async XLA Ops:
  0.6 128.0 %copy-start = (bf16[1,768,2048]{2,1,0:T(8,128)(2,1)S(1)}, bf16[1,768,2048]{2,1,0:T(8,128)(2,1)}, u32[]{:S(2)}) copy-start(bf16[1,768,2048]{2,1,0:T(8,128)(2,1)} %param.23) | copy-start | bytes 9437188
  9.9 23.7 %all-to-all-start.1 = ((bf16[32,2,1,2,1]{3,1,4,2,0:T(2,128)(2,1)}), bf16[32,2,1,2,1]{3,1,4,2,0:T(2,128)(2,1)S(1)}, u32[]{:S(2)}, u32[]{:S(2)}) async-start(bf16[32,2,1,2,1]{3,1,4,2,0:T(2,128)(2,1)} %bitcast.77), calls=%async_computation.1 | async-start | bytes 32768 | tf_op jit(solution)/shard_map/all_to_all | solution.py:151
  30.0 30.5 %copy-start.17 = (s32[64,1]{0,1:T(1,128)S(1)}, s32[64,1]{0,1:T(1,128)}, u32[]{:S(2)}) copy-start(s32[64,1]{0,1:T(1,128)} %mul.742) | copy-start | bytes 772
  30.9 34.7 %copy-start.1 = (s32[256]{0:T(256)S(1)}, s32[256]{0:T(256)}, u32[]{:S(2)}) copy-start(s32[256]{0:T(256)} %param.14) | copy-start | bytes 3076
  33.6 21.6 %all-to-all-start = ((bf16[32,2,16,2,128]{4,2,3,1,0:T(8,128)(2,1)}), bf16[32,2,16,2,128]{4,2,3,1,0:T(8,128)(2,1)}, u32[]{:S(2)}, u32[]{:S(2)}) async-start(bf16[32,2,16,2,128]{4,2,3,1,0:T(8,128)(2,1)} %scatter_fusion), calls=%async_computation | async-start | bytes 1048576 | tf_op jit(solution)/shard_map/all_to_all | solution.py:150
  46.7 42.5 %copy-start.2 = (s32[256]{0:T(256)S(1)}, s32[256]{0:T(256)}, u32[]{:S(2)}) copy-start(s32[256]{0:T(256)} %param.15) | copy-start | bytes 3076
  55.2 27.7 %all-to-all-start.4 = ((bf16[16,8,4096]{2,1,0:T(8,128)(2,1)}), bf16[16,8,4096]{2,1,0:T(8,128)(2,1)}, u32[]{:S(2)}, u32[]{:S(2)}) async-start(bf16[16,8,4096]{2,1,0:T(8,128)(2,1)} %bitcast.296), calls=%async_computation.4 | async-start | bytes 2097152 | tf_op jit(solution)/shard_map/all_to_all | solution.py:179
  59.6 37.6 %copy-start.10 = (bf16[8,3,2,2,128]{4,3,2,1,0:T(2,128)(2,1)S(1)}, bf16[8,3,2,2,128]{4,3,2,1,0:T(2,128)(2,1)}, u32[]{:S(2)}) copy-start(bf16[8,3,2,2,128]{4,3,2,1,0:T(2,128)(2,1)} %param.17) | copy-start | bytes 73732
  59.6 38.2 %copy-start.7 = (bf16[8,3,32,128]{3,2,1,0:T(8,128)(2,1)S(1)}, bf16[8,3,32,128]{3,2,1,0:T(8,128)(2,1)}, u32[]{:S(2)}) copy-start(bf16[8,3,32,128]{3,2,1,0:T(8,128)(2,1)} %param.16) | copy-start | bytes 589828
  82.9 28.9 %all-to-all-start.6 = ((bf16[16,8,4096]{2,1,0:T(8,128)(2,1)}), bf16[16,8,4096]{2,1,0:T(8,128)(2,1)}, u32[]{:S(2)}, u32[]{:S(2)}) async-start(bf16[16,8,4096]{2,1,0:T(8,128)(2,1)} %bitcast.294), calls=%async_computation.6 | async-start | bytes 2097152 | tf_op jit(solution)/shard_map/all_to_all | solution.py:179
  95.3 2.9 %copy-start.15 = (pred[3,3]{1,0:T(4,128)(4,1)}, pred[3,3]{1,0:T(4,128)(4,1)S(1)}, u32[]{:S(2)}) copy-start(pred[3,3]{1,0:T(4,128)(4,1)S(1)} %iota_compare_fusion.6) | copy-start | bytes 31
  98.3 23.5 %copy-start.8 = (pred[8,512]{1,0:T(8,128)(4,1)}, pred[8,512]{1,0:T(8,128)(4,1)S(1)}, u32[]{:S(2)}) copy-start(pred[8,512]{1,0:T(8,128)(4,1)S(1)} %broadcast_and_fusion) | copy-start | bytes 12292
  111.8 29.6 %all-to-all-start.2 = ((bf16[16,8,4096]{2,1,0:T(8,128)(2,1)}), bf16[16,8,4096]{2,1,0:T(8,128)(2,1)}, u32[]{:S(2)}, u32[]{:S(2)}) async-start(bf16[16,8,4096]{2,1,0:T(8,128)(2,1)} %bitcast.295), calls=%async_computation.2 | async-start | bytes 2097152 | tf_op jit(solution)/shard_map/all_to_all | solution.py:179
  117.9 4.6 %copy-start.3 = (bf16[1,4096,384]{2,1,0:T(8,128)(2,1)S(1)}, bf16[1,4096,384]{2,1,0:T(8,128)(2,1)}, u32[]{:S(2)}) copy-start(bf16[1,4096,384]{2,1,0:T(8,128)(2,1)} %param.21) | copy-start | bytes 9437188
  122.5 2.2 %copy-start.4 = (bf16[1,4096,384]{2,1,0:T(8,128)(2,1)S(1)}, bf16[1,4096,384]{2,1,0:T(8,128)(2,1)}, u32[]{:S(2)}) copy-start(bf16[1,4096,384]{2,1,0:T(8,128)(2,1)} %param.22) | copy-start | bytes 9437188
  141.4 19.6 %all-to-all-start.5 = ((bf16[16,8,2048]{2,1,0:T(8,128)(2,1)}), bf16[16,8,2048]{2,1,0:T(8,128)(2,1)}, u32[]{:S(2)}, u32[]{:S(2)}) async-start(bf16[16,8,2048]{2,1,0:T(8,128)(2,1)} %fusion.21), calls=%async_computation.5 | async-start | bytes 1048576 | tf_op jit(solution)/shard_map/all_to_all | solution.py:106
  147.3 3.2 %copy-start.5 = (bf16[1,4096,384]{2,1,0:T(8,128)(2,1)S(1)}, bf16[1,4096,384]{2,1,0:T(8,128)(2,1)}, u32[]{:S(2)}) copy-start(bf16[1,4096,384]{2,1,0:T(8,128)(2,1)} %param.22) | copy-start | bytes 9437188
  161.1 17.7 %all-to-all-start.7 = ((bf16[16,8,2048]{2,1,0:T(8,128)(2,1)}), bf16[16,8,2048]{2,1,0:T(8,128)(2,1)}, u32[]{:S(2)}, u32[]{:S(2)}) async-start(bf16[16,8,2048]{2,1,0:T(8,128)(2,1)} %fusion.24), calls=%async_computation.7 | async-start | bytes 1048576 | tf_op jit(solution)/shard_map/all_to_all | solution.py:106
  165.3 3.2 %copy-start.6 = (bf16[1,4096,384]{2,1,0:T(8,128)(2,1)S(1)}, bf16[1,4096,384]{2,1,0:T(8,128)(2,1)}, u32[]{:S(2)}) copy-start(bf16[1,4096,384]{2,1,0:T(8,128)(2,1)} %param.22) | copy-start | bytes 9437188
  170.4 12.8 %copy-start.9 = (pred[8,512]{1,0:T(8,128)(4,1)S(1)}, pred[8,512]{1,0:T(8,128)(4,1)}, u32[]{:S(2)}) copy-start(pred[8,512]{1,0:T(8,128)(4,1)} %copy-done.8) | copy-start | bytes 12292
  172.4 12.7 %copy-start.16 = (pred[3,3]{1,0:T(4,128)(4,1)S(1)}, pred[3,3]{1,0:T(4,128)(4,1)}, u32[]{:S(2)}) copy-start(pred[3,3]{1,0:T(4,128)(4,1)} %copy-done.15) | copy-start | bytes 31
  173.8 13.3 %copy-start.14 = (bf16[8,3,1,2,128]{4,3,2,1,0:T(2,128)(2,1)S(1)}, bf16[8,3,1,2,128]{4,3,2,1,0:T(2,128)(2,1)}, u32[]{:S(2)}) copy-start(bf16[8,3,1,2,128]{4,3,2,1,0:T(2,128)(2,1)} %get-tuple-element.11) | copy-start | bytes 36868
  178.7 17.8 %all-to-all-start.3 = ((bf16[16,8,2048]{2,1,0:T(8,128)(2,1)}), bf16[16,8,2048]{2,1,0:T(8,128)(2,1)}, u32[]{:S(2)}, u32[]{:S(2)}) async-start(bf16[16,8,2048]{2,1,0:T(8,128)(2,1)} %fusion.18), calls=%async_computation.3 | async-start | bytes 1048576 | tf_op jit(solution)/shard_map/all_to_all | solution.py:106
  188.1 11.3 %copy-start.13 = (f32[8,8]{1,0:T(8,128)S(1)}, f32[8,8]{1,0:T(8,128)}, u32[]{:S(2)}) copy-start(f32[8,8]{1,0:T(8,128)} %get-tuple-element.34) | copy-start | bytes 772
  188.1 12.5 %copy-start.11 = (f32[8,8]{1,0:T(8,128)S(1)}, f32[8,8]{1,0:T(8,128)}, u32[]{:S(2)}) copy-start(f32[8,8]{1,0:T(8,128)} %get-tuple-element.35) | copy-start | bytes 772
  188.1 12.5 %copy-start.12 = (f32[8,8]{1,0:T(8,128)S(1)}, f32[8,8]{1,0:T(8,128)}, u32[]{:S(2)}) copy-start(f32[8,8]{1,0:T(8,128)} %get-tuple-element.36) | copy-start | bytes 772
where the time goes:
time: 205 us; the launch traced here: 203 us
  waiting for transfers between devices  61.9 us (30%)
  starting transfers between devices  46.1 us (22%)
  local copies, waits for them, and re-layouts  41.5 us (20%)
  matrix products  23.2 us (11%)
  other arithmetic  23 us (11%)
  blocking collectives  5.84 us (3%)
    all_to_all x3, waiting for transfers between devices, body(): lax.all_to_all(send, 'ep', split_axis=0, concat_axis=0, tiled=True)  39.9 us
    all_to_all x3, starting transfers between devices, body(): lax.all_to_all(send, 'ep', split_axis=0, concat_axis=0, tiled=True)  16.3 us
    all_to_all x3, starting transfers between devices, experts_step(): lax.all_to_all(total.astype(jnp.bfloat16), 'ep', split_axis=0, concat_axi...  14.5 us
    scatter x3, local copies, waits for them, and re-layouts, pack(): jnp.zeros((experts * capacity, rows.shape[1]), rows.dtype).at[target]  14.1 us
    all_to_all x3, waiting for transfers between devices, experts_step(): lax.all_to_all(total.astype(jnp.bfloat16), 'ep', split_axis=0, concat_axi...  13.6 us
    all_to_all x1, waiting for transfers between devices, body(): lax.all_to_all(send_quant, 'ep', split_axis=0, concat_axis=0, tiled=True)  8.46 us
    all_to_all x1, starting transfers between devices, body(): lax.all_to_all(send_scale, 'ep', split_axis=0, concat_axis=0, tiled=True)  8.31 us
    dot_general x3, matrix products, expert_front(): jnp.einsum('nid,df->nif', received, w_gate[0], preferred_element_type=jnp...  8.21 us
  transfers between devices with their start and end apart: 8, of which 7 were waited for; matrix products, arithmetic and copies ran while one was open for 36% of the time, Pallas kernels for 0%

commit v1 on v0

v1 whole, which is shorter than its diff:
```python
import functools
import math

import jax
import jax.numpy as jnp
from jax import lax
from jax.experimental import pallas as pl
from jax.experimental.pallas import tpu as pltpu
from jax.sharding import PartitionSpec as P

CAP = 2
LIMIT = 448.0
MIB = 1024 * 1024


def vmem():
    return pl.BlockSpec(memory_space=pltpu.VMEM)


def smem():
    return pl.BlockSpec(memory_space=pltpu.SMEM)


def page_kernel(pages, me_ref, owner_ref, kv_ref, send_ref, count_ref):
    values = kv_ref[...].astype(jnp.float32)
    largest = jnp.max(jnp.abs(values), axis=(3, 4), keepdims=True)
    scale = jnp.full(largest.shape, 2.0 ** (-16), jnp.float32)
    inverse = jnp.full(largest.shape, 2.0**16, jnp.float32)
    for exponent in range(-16, 4):
        exceeds = largest > LIMIT * 2.0**exponent
        scale = jnp.where(exceeds, scale * 2.0, scale)
        inverse = jnp.where(exceeds, inverse * 0.5, inverse)
    scaled = values * inverse
    magnitude = jnp.abs(scaled)
    step = jnp.full(scaled.shape, 2.0 ** (-9), jnp.float32)
    back = jnp.full(scaled.shape, 2.0**9, jnp.float32)
    for exponent in range(-5, 9):
        exceeds = magnitude >= 2.0**exponent
        step = jnp.where(exceeds, step * 2.0, step)
        back = jnp.where(exceeds, back * 0.5, back)
    levels = jnp.minimum(jnp.floor(magnitude * back + 0.5) * step, LIMIT)
    cache = (jnp.where(scaled < 0.0, -levels, levels) * scale).astype(jnp.bfloat16)

    send_ref[...] = jnp.zeros(send_ref.shape, send_ref.dtype)

    def clear(o, carry):
        count_ref[o] = 0
        return carry

    lax.fori_loop(0, count_ref.shape[0], clear, 0)
    first = me_ref[0] * pages
    for page in range(pages):
        owner = owner_ref[first + page]
        rank = count_ref[owner]
        count_ref[owner] = rank + 1
        send_ref[pl.ds(owner * CAP + rank, 1)] = cache[page : page + 1]


def attention_kernel(
    pages, me_ref, owner_ref, slot_ref, fill_ref, q_ref, cache_ref, fresh_ref, out_ref
):
    owners = owner_ref.shape[0]
    slots, _, heads, page_len, width = cache_ref.shape
    requests, steps, q_heads, _ = q_ref.shape
    group = q_heads // heads
    rows = requests * steps * group
    mine = (owner_ref[...] == me_ref[0]).astype(jnp.float32)
    before = (
        lax.broadcasted_iota(jnp.int32, (pages, pages), 0)
        < lax.broadcasted_iota(jnp.int32, (pages, pages), 1)
    ).astype(jnp.float32)
    rank = jnp.dot(mine, before, preferred_element_type=jnp.float32)
    code = (slot_ref[...] * (page_len + 1) + fill_ref[...]).astype(jnp.float32)
    columns = slots * page_len
    place = lax.broadcasted_iota(jnp.int32, (owners, columns), 1)
    source = lax.broadcasted_iota(jnp.int32, (owners, columns), 0)
    spread = jnp.zeros((owners, columns), jnp.float32)
    for c in range(CAP):
        held = jnp.sum(
            jnp.where((mine > 0.0) & (rank == float(c)), code, 0.0), axis=1, keepdims=True
        )
        spread = jnp.where(place // page_len == source * CAP + c, held, spread)
    line = jnp.sum(spread, axis=0, keepdims=True).astype(jnp.int32)
    request_of = line // (page_len + 1)
    fill_of = line - request_of * (page_len + 1)
    position = lax.broadcasted_iota(jnp.int32, (1, columns), 1) % page_len
    request_of = jnp.where(position < fill_of, request_of, -1)
    row_request = lax.broadcasted_iota(jnp.int32, (rows, 1), 0) // (steps * group)
    visible = row_request == request_of
    token = lax.broadcasted_iota(jnp.int32, (rows, 1), 0) // group
    first = row_request * steps
    fresh_at = lax.broadcasted_iota(jnp.int32, (1, fresh_ref.shape[2]), 1)
    fresh_visible = (fresh_at >= first) & (fresh_at <= token)
    factor = 1.0 / math.sqrt(width)
    contract = (((1,), (1,)), ((), ()))
    for head in range(heads):
        q = q_ref[:, :, head * group : (head + 1) * group, :].reshape(rows, width)
        keys = cache_ref[:, 0, head].reshape(columns, width)
        values = cache_ref[:, 1, head].reshape(columns, width)
        scores = lax.dot_general(q, keys, contract, preferred_element_type=jnp.float32) * factor
        fresh = (
            lax.dot_general(q, fresh_ref[0, head], contract, preferred_element_type=jnp.float32)
            * factor
        )
        scores = jnp.where(visible, scores, -jnp.inf)
        fresh = jnp.where(fresh_visible, fresh, -jnp.inf)
        peak = jnp.maximum(
            jnp.max(scores, axis=1, keepdims=True), jnp.max(fresh, axis=1, keepdims=True)
        )
        weight = jnp.exp(scores - peak)
        fresh_weight = jnp.exp(fresh - peak)
        total = jnp.sum(weight, axis=1, keepdims=True) + jnp.sum(
            fresh_weight, axis=1, keepdims=True
        )
        mixed = jnp.dot(
            weight.astype(jnp.bfloat16), values, preferred_element_type=jnp.float32
        ) + jnp.dot(
            fresh_weight.astype(jnp.bfloat16), fresh_ref[1, head], preferred_element_type=jnp.float32
        )
        out_ref[:, :, head * group : (head + 1) * group, :] = (
            (mixed / total).astype(out_ref.dtype).reshape(requests, steps, group, width)
        )


def front_kernel(blocks, x_ref, gate_ref, up_ref, hidden_ref, gate_sum, up_sum):
    k = pl.program_id(0)
    gate = jnp.dot(x_ref[...], gate_ref[0], preferred_element_type=jnp.float32)
    up = jnp.dot(x_ref[...], up_ref[0], preferred_element_type=jnp.float32)

    @pl.when(k == 0)
    def _():
        gate_sum[...] = gate
        up_sum[...] = up

    @pl.when((k > 0) & (k < blocks - 1))
    def _():
        gate_sum[...] += gate
        up_sum[...] += up

    @pl.when(k == blocks - 1)
    def _():
        whole = gate_sum[...] + gate
        hidden_ref[...] = (
            whole / (1.0 + jnp.exp(-whole)) * (up_sum[...] + up)
        ).astype(hidden_ref.dtype)


def down_kernel(me_ref, hidden_ref, down_ref, probs_ref, out_ref):
    half = hidden_ref.shape[2]
    total = jnp.dot(hidden_ref[0], down_ref[0, :half], preferred_element_type=jnp.float32)
    total += jnp.dot(hidden_ref[1], down_ref[0, half:], preferred_element_type=jnp.float32)
    probs = probs_ref[...]
    mine = lax.broadcasted_iota(jnp.int32, probs.shape, 1) == me_ref[0]
    weight = jnp.sum(jnp.where(mine, probs, 0.0), axis=1, keepdims=True)
    out_ref[...] = (total * weight).astype(out_ref.dtype)


def expert_front(x, w_gate, w_up):
    tokens = x.shape[0] // 2
    half, d, f = x.shape[1], w_gate.shape[1], w_gate.shape[2]
    depth = min(half, 1024)
    per_half = half // depth
    blocks = d // depth
    return pl.pallas_call(
        functools.partial(front_kernel, blocks),
        grid=(blocks,),
        out_shape=jax.ShapeDtypeStruct((tokens, f), jnp.bfloat16),
        in_specs=[
            pl.BlockSpec((tokens, depth), lambda k: (k // per_half, k % per_half)),
            pl.BlockSpec((1, depth, f), lambda k: (0, k, 0)),
            pl.BlockSpec((1, depth, f), lambda k: (0, k, 0)),
        ],
        out_specs=pl.BlockSpec((tokens, f), lambda k: (0, 0)),
        scratch_shapes=[pltpu.VMEM((tokens, f), jnp.float32)] * 2,
        compiler_params=pltpu.CompilerParams(vmem_limit_bytes=40 * MIB),
        cost_estimate=pl.CostEstimate(
            flops=4 * tokens * d * f,
            bytes_accessed=2 * (tokens * d + 2 * d * f + tokens * f),
            transcendentals=tokens * f,
        ),
        name="expert_front",
    )(x, w_gate, w_up)


def expert_back(me, hidden, w_down, probs):
    _, tokens, f = hidden.shape
    width = w_down.shape[2]
    block = min(width, 512)
    return pl.pallas_call(
        down_kernel,
        grid=(width // block,),
        out_shape=jax.ShapeDtypeStruct((tokens, width), jnp.bfloat16),
        in_specs=[
            smem(),
            pl.BlockSpec((2, tokens, f), lambda n: (0, 0, 0)),
            pl.BlockSpec((1, 2 * f, block), lambda n: (0, 0, n)),
            pl.BlockSpec(probs.shape, lambda n: (0, 0)),
        ],
        out_specs=pl.BlockSpec((tokens, block), lambda n: (0, n)),
        compiler_params=pltpu.CompilerParams(vmem_limit_bytes=40 * MIB),
        cost_estimate=pl.CostEstimate(
            flops=4 * tokens * f * width,
            bytes_accessed=2 * (2 * tokens * f + 2 * f * width + tokens * width),
            transcendentals=0,
        ),
        name="expert_back",
    )(me, hidden, w_down, probs)


def body(
    prompt_kv,
    page_owner,
    page_slot,
    page_fill,
    queries,
    new_kv,
    moe_input,
    expert_routes,
    route_probs,
    w_gate,
    w_up,
    w_down,
):
    owners = lax.axis_size("ep")
    me = lax.axis_index("ep").astype(jnp.int32)
    me_ref = me.reshape(1)
    core = lax.axis_index("pd")
    pages, _, page_len, heads, width = prompt_kv.shape
    requests, steps, q_heads, _ = queries.shape
    d = moe_input.shape[2]
    tokens = requests * steps
    slots = owners * CAP

    mine = lax.dynamic_slice_in_dim(
        moe_input.transpose(1, 0, 2).reshape(tokens, d), core * (d // 2), d // 2, axis=1
    )
    x = lax.all_gather(mine, ("pd", "ep"), axis=0, tiled=True)
    hot = expert_routes[..., None] == jnp.arange(owners, dtype=jnp.int32)
    own_probs = jnp.sum(
        jnp.where(hot, route_probs.transpose(1, 0, 2)[..., None], 0.0), axis=2
    ).reshape(tokens, owners)
    probs = lax.all_gather(own_probs, "ep", axis=0, tiled=True)

    send = pl.pallas_call(
        functools.partial(page_kernel, pages),
        out_shape=jax.ShapeDtypeStruct((slots, 2, heads, page_len, width), jnp.bfloat16),
        in_specs=[smem(), smem(), vmem()],
        out_specs=vmem(),
        scratch_shapes=[pltpu.SMEM((owners,), jnp.int32)],
        compiler_params=pltpu.CompilerParams(vmem_limit_bytes=40 * MIB),
        name="quantize_pages",
    )(me_ref, page_owner.reshape(-1), prompt_kv.transpose(0, 1, 3, 2, 4))
    cache = lax.all_to_all(send, "ep", split_axis=0, concat_axis=0, tiled=True)

    hidden = expert_front(x, w_gate, w_up)
    hidden = lax.all_gather(hidden, "pd", axis=0)
    parts = expert_back(me_ref, hidden, w_down, probs)
    moe = lax.psum_scatter(parts, "ep", scatter_dimension=0, tiled=True)
    moe_out = moe.reshape(steps, requests, d // 2).transpose(1, 0, 2)

    fresh = new_kv.transpose(2, 3, 0, 1, 4).reshape(2, heads, tokens, width)
    fresh = jnp.pad(fresh, ((0, 0), (0, 0), (0, 128 - tokens), (0, 0)))
    attn_out = pl.pallas_call(
        functools.partial(attention_kernel, pages),
        out_shape=jax.ShapeDtypeStruct(queries.shape, jnp.bfloat16),
        in_specs=[smem()] + [vmem()] * 6,
        out_specs=vmem(),
        compiler_params=pltpu.CompilerParams(vmem_limit_bytes=48 * MIB),
        name="attention",
    )(
        me_ref,
        page_owner.reshape(owners, pages),
        page_slot.reshape(owners, pages),
        page_fill.reshape(owners, pages),
        queries,
        cache,
        fresh,
    )
    return (attn_out, moe_out)


def solution(mesh):
    return jax.shard_map(
        body,
        mesh=mesh,
        in_specs=(
            P(("grp", "ep"), None, None, "pd", None),
            P("grp", None),
            P("grp"),
            P("grp"),
            P(("grp", "ep"), None, "pd", None),
            P(("grp", "ep"), None, None, "pd", None),
            P(("grp", "ep"), None, None),
            P(None, ("grp", "ep"), None),
            P(("grp", "ep"), None, None),
            P("ep", None, "pd"),
            P("ep", None, "pd"),
            P("ep", None, "pd"),
        ),
        out_specs=(P(("grp", "ep"), None, "pd", None), P(("grp", "ep"), None, "pd")),
        check_vma=False,
    )
```

time: 205 us -> 222 us (1.083)
  waiting for transfers between devices: 61.9 us -> 132 us
  starting transfers between devices: 46.1 us -> 4.51 us
  blocking collectives: 5.84 us -> 45.7 us
  local copies, waits for them, and re-layouts: 41.5 us -> 8.22 us
  matrix products: 23.2 us -> 0 us
  other arithmetic: 23 us -> 1.51 us
  Pallas kernels: 0 us -> 15.1 us
  between operations: 1.12 us -> 14.1 us
    reduce_scatter x0 -> x1, waiting for transfers between devices: none -> 96.1 us  [body(): moe = lax.psum_scatter(parts, 'ep', scatter_dimension=0, tiled=True)]
    all_to_all x8 -> x1, waiting for transfers between devices: 61.9 us -> 16 us  [body(): cache = lax.all_to_all(send, 'ep', split_axis=0, concat_axis=0, tiled=True)]
    all_to_all x8 -> x1, starting transfers between devices: 46.1 us -> 4.43 us  [body(): cache = lax.all_to_all(send, 'ep', split_axis=0, concat_axis=0, tiled=True)]
    all_gather x3 -> x2, blocking collectives: 5.84 us -> 45.7 us  [the longest x1 43.4 us: body(): probs = lax.all_gather(own_probs, 'ep', axis=0, tiled=True)]
    dot_general x13 -> x0, matrix products: 23.2 us -> none  [the longest x3 8.21 us: expert_front(): jnp.einsum('nid,df->nif', received, w_gate[0], preferred_element_type=jnp...]
    all_gather x0 -> x1, waiting for transfers between devices: none -> 20.2 us  [body(): x = lax.all_gather(mine, ('pd', 'ep'), axis=0, tiled=True)]
    scatter x5 -> x0, local copies, waits for them, and re-layouts: 19.1 us -> none  [the longest x3 14.1 us: pack(): jnp.zeros((experts * capacity, rows.shape[1]), rows.dtype).at[target]]
    pallas_call x0 -> x4, Pallas kernels: none -> 15.1 us  [the longest x1 4.93 us: body(): pl.pallas_call(functools.partial(page_kernel, pages), out_shape=jax.Shape...]
  transfers between devices with their start and end apart: 8 -> 3, of which waited for: 7 -> 3; matrix products, arithmetic and copies ran while one was open for 36% -> 1% of each run, Pallas kernels for 0% -> 3%
where the time goes in v1:
time: 222 us; the launch traced here: 221 us
  waiting for transfers between devices  132 us (59%)
  blocking collectives  45.7 us (21%)
  Pallas kernels  15.1 us (7%)
  between operations  14.1 us (6%)
  local copies, waits for them, and re-layouts  8.22 us (4%)
  starting transfers between devices  4.51 us (2%)
    reduce_scatter x1, waiting for transfers between devices, body(): moe = lax.psum_scatter(parts, 'ep', scatter_dimension=0, tiled=True)  96.1 us
    all_gather x1, blocking collectives, body(): probs = lax.all_gather(own_probs, 'ep', axis=0, tiled=True)  43.4 us
    all_gather x1, waiting for transfers between devices, body(): x = lax.all_gather(mine, ('pd', 'ep'), axis=0, tiled=True)  20.2 us
    all_to_all x1, waiting for transfers between devices, body(): cache = lax.all_to_all(send, 'ep', split_axis=0, concat_axis=0, tiled=True)  16 us
    unnamed x25, local copies, waits for them, and re-layouts  7.19 us
    pallas_call x1, Pallas kernels, body(): pl.pallas_call(functools.partial(page_kernel, pages), out_shape=jax.Shape...  4.93 us
    pallas_call x1, Pallas kernels, expert_front(): pl.pallas_call(functools.partial(front_kernel, blocks), grid=(blocks,), o...  4.78 us
  transfers between devices with their start and end apart: 3, of which 3 were waited for; matrix products, arithmetic and copies ran while one was open for 1% of the time, Pallas kernels for 3%

profile of v1, /device:TPU:0, one launch (start us, length us, event | category | flops | bytes accessed | tf_op | source)
XLA Modules:
  0.0 221.5 jit_solution(12174045463399090459)
XLA Ops:
  7.2 0.0 copy-start
  7.2 0.0 all-gather.4.cloned.1.call-start
  7.2 0.9 copy-done
  8.1 0.6 constant_dynamic-slice_fusion
  8.7 0.0 all-gather.4.cloned.1.call-update
  8.8 0.0 reduce-scatter.2.cloned.1.call-start
  8.8 0.9 select_reduce_fusion
  9.7 0.1 copy.31
  9.8 43.4 %all-gather.1 = f32[16,24,16]{1,2,0:T(8,128)S(1)} all-gather(f32[1,24,16]{1,2,0:T(8,128)S(1)} %copy.31), channel_id=1, replica_groups=mesh['grp'=1,'ep'=16,'pd'=2] {'ep'}, dimensions={0}, use_global_device_ids=true | all-gather | bytes 26112 | tf_op jit(solution)/shard_map/all_gather | solution.py:242
  53.2 0.1 copy.32
  53.3 20.2 %all-gather.4.cloned.1.call-done.x_ref = bf16[768,2048]{1,0:T(8,128)(2,1)} async-done(((bf16[24,2048]{1,0:T(8,128)(2,1)}), bf16[768,2048]{1,0:T(8,128)(2,1)}) %all-gather.4.cloned.1.call-update) | async-done | bytes 3145744 | tf_op jit(solution)/shard_map/all_gather | solution.py:237
  73.5 1.9 copy-done.1
  75.4 1.9 copy-done.2
  77.3 1.9 copy-done.4
  79.2 4.8 %expert_front.1 = bf16[384,384]{1,0:T(8,128)(2,1)S(1)} custom-call(bf16[768,2048]{1,0:T(8,128)(2,1)S(1)} %copy-done.4, bf16[1,4096,384]{2,1,0:T(8,128)(2,1)S(1)} %copy-done.1, bf16[1,4096,384]{2,1,0:T(8,128)(2,1)S(1)} %copy-done.2), custom_call_target="tpu_custom_call" | custom-call | flops 2415919104 | bytes 9732096 | tf_op jit(solution)/shard_map/expert_front/pallas_call | solution.py:164
  83.9 2.2 %all-gather = bf16[768,384]{1,0:T(8,128)(2,1)S(1)} all-gather(bf16[384,384]{1,0:T(8,128)(2,1)S(1)} %expert_front.1), channel_id=2, replica_groups=mesh['grp'=1,'ep'=16,'pd'=2] {'pd'}, dimensions={0}, use_global_device_ids=true | all-gather | bytes 884736 | tf_op jit(solution)/shard_map/all_gather | solution.py:256
  86.2 0.0 copy-done.3
  86.2 3.5 %expert_back.1 = bf16[384,2048]{1,0:T(8,128)(2,1)} custom-call(s32[1]{0:T(128)} %bitcast.me_ref, bf16[2,384,384]{2,1,0:T(8,128)(2,1)S(1)} %bitcast.20, bf16[1,768,2048]{2,1,0:T(8,128)(2,1)S(1)} %copy-done.3, f32[384,16]{1,0:T(8,128)S(1)} %bitcast.22), custom_call_target="tpu_custom_call" | custom-call | flops 1207959552 | bytes 5308416 | tf_op jit(solution)/shard_map/expert_back/pallas_call | solution.py:189
  89.7 0.0 reduce-scatter.2.cloned.1.call-update
  89.7 0.0 copy-done.7
  89.8 0.0 copy-done.6
  89.8 4.9 %quantize_pages.1 = bf16[32,2,2,16,128]{4,3,2,1,0:T(8,128)(2,1)} custom-call(s32[1]{0:T(128)} %bitcast.me_ref, s32[256]{0:T(256)S(1)} %bitcast.23, bf16[16,2,2,16,128]{4,3,2,1,0:T(8,128)(2,1)S(1)} %bitcast.21), custom_call_target="tpu_custom_call" | custom-call | tf_op jit(solution)/shard_map/quantize_pages/pallas_call | solution.py:244
  94.7 4.4 %all-to-all-start = ((bf16[32,2,2,16,128]{4,3,2,1,0:T(8,128)(2,1)}), bf16[32,2,2,16,128]{4,3,2,1,0:T(8,128)(2,1)S(1)}, u32[]{:S(2)}, u32[]{:S(2)}) async-start(bf16[32,2,2,16,128]{4,3,2,1,0:T(8,128)(2,1)} %quantize_pages.1), calls=%async_computation | async-start | bytes 1048576 | tf_op jit(solution)/shard_map/all_to_all | solution.py:253
  99.2 0.0 copy-done.8
  99.2 0.5 broadcast.7
  99.7 0.7 reduce.3
  100.4 0.1 reshape.34.owner_ref
  100.5 0.1 reshape.35.slot_ref
  100.5 0.1 reshape.36.fill_ref
  100.6 16.0 %all-to-all-done.cache_ref = bf16[32,2,2,16,128]{4,3,2,1,0:T(8,128)(2,1)S(1)} async-done(((bf16[32,2,2,16,128]{4,3,2,1,0:T(8,128)(2,1)}), bf16[32,2,2,16,128]{4,3,2,1,0:T(8,128)(2,1)S(1)}, u32[]{:S(2)}, u32[]{:S(2)}) %all-to-all-start) | async-done | bytes 524320 | tf_op jit(solution)/shard_map/all_to_all | solution.py:253
  116.7 1.9 attention.1
  118.6 96.1 %reduce-scatter.2.cloned.1.call-done = bf16[24,2048]{1,0:T(8,128)(2,1)} async-done(((bf16[384,2048]{1,0:T(8,128)(2,1)}), bf16[24,2048]{1,0:T(8,128)(2,1)}) %reduce-scatter.2.cloned.1.call-update) | async-done | bytes 98320 | tf_op jit(solution)/shard_map/reduce_scatter | solution.py:258
  (16 shorter events, 0.1 us)
Async XLA Ops:
  7.2 0.9 copy-start
  7.2 66.3 %all-gather.4.cloned.1.call-start = ((), (), s32[]{:S(2)}) async-start(), calls=%async_computation.2 | async-start | bytes 3244032 | tf_op jit(solution)/shard_map/all_gather | solution.py:237
  8.8 205.9 %reduce-scatter.2.cloned.1.call-start = ((), (), s32[]{:S(2)}) async-start(), calls=%async_computation.3 | async-start | bytes 1671168 | tf_op jit(solution)/shard_map/reduce_scatter | solution.py:258
  73.5 1.9 copy-start.1
  75.4 1.9 copy-start.2
  77.3 1.9 copy-start.4
  79.2 7.0 %copy-start.3 = (bf16[1,768,2048]{2,1,0:T(8,128)(2,1)S(1)}, bf16[1,768,2048]{2,1,0:T(8,128)(2,1)}, u32[]{:S(2)}) copy-start(bf16[1,768,2048]{2,1,0:T(8,128)(2,1)} %down_ref.1) | copy-start | bytes 9437188
  86.2 3.5 %copy-start.7 = (bf16[16,2,16,2,128]{4,3,2,1,0:T(2,128)(2,1)S(1)}, bf16[16,2,16,2,128]{4,3,2,1,0:T(2,128)(2,1)}, u32[]{:S(2)}) copy-start(bf16[16,2,16,2,128]{4,3,2,1,0:T(2,128)(2,1)} %param.12) | copy-start | bytes 786436
  86.2 3.6 %copy-start.6 = (s32[256,1]{0,1:T(1,128)S(1)}, s32[256,1]{0,1:T(1,128)}, u32[]{:S(2)}) copy-start(s32[256,1]{0,1:T(1,128)} %param.13) | copy-start | bytes 3076
  89.7 9.5 %copy-start.8 = (bf16[8,3,2,2,128]{4,3,2,1,0:T(2,128)(2,1)S(1)}, bf16[8,3,2,2,128]{4,3,2,1,0:T(2,128)(2,1)}, u32[]{:S(2)}) copy-start(bf16[8,3,2,2,128]{4,3,2,1,0:T(2,128)(2,1)} %param.17) | copy-start | bytes 73732
  89.7 10.8 %copy-start.9 = (s32[256]{0:T(256)S(1)}, s32[256]{0:T(256)}, u32[]{:S(2)}) copy-start(s32[256]{0:T(256)} %param.14) | copy-start | bytes 3076
  89.7 10.8 %copy-start.10 = (s32[256]{0:T(256)S(1)}, s32[256]{0:T(256)}, u32[]{:S(2)}) copy-start(s32[256]{0:T(256)} %param.15) | copy-start | bytes 3076
  89.7 27.0 %copy-start.5 = (bf16[8,3,32,128]{3,2,1,0:T(8,128)(2,1)S(1)}, bf16[8,3,32,128]{3,2,1,0:T(8,128)(2,1)}, u32[]{:S(2)}) copy-start(bf16[8,3,32,128]{3,2,1,0:T(8,128)(2,1)} %q_ref.1) | copy-start | bytes 589828
  94.7 21.9 %all-to-all-start = ((bf16[32,2,2,16,128]{4,3,2,1,0:T(8,128)(2,1)}), bf16[32,2,2,16,128]{4,3,2,1,0:T(8,128)(2,1)S(1)}, u32[]{:S(2)}, u32[]{:S(2)}) async-start(bf16[32,2,2,16,128]{4,3,2,1,0:T(8,128)(2,1)} %quantize_pages.1), calls=%async_computation | async-start | bytes 1048576 | tf_op jit(solution)/shard_map/all_to_all | solution.py:253
Sparse Core Ops, SparseCore 0:
  11.5 61.9 all-gather.3
  89.8 124.7 reduce-scatter.1

commit v2 on v1

--- a/solution.py
+++ b/solution.py
@@ -122,89 +122,180 @@
         )
 
 
-def front_kernel(blocks, x_ref, gate_ref, up_ref, hidden_ref, gate_sum, up_sum):
+def pack_kernel(experts, core_ref, x_ref, route_ref, prob_ref, out_ref):
+    half = x_ref.shape[1] // 2
+    begin = pl.multiple_of(core_ref[0] * half, 128)
+    out_ref[:, :half] = x_ref[:, pl.ds(begin, half)]
+    shape = (x_ref.shape[0], out_ref.shape[1] - half)
+    lane = lax.broadcasted_iota(jnp.int32, shape, 1)
+    expert = lane % experts
+    part = lane // experts
+    dense = jnp.zeros(shape, jnp.float32)
+    for k in range(route_ref.shape[1]):
+        dense += jnp.where(route_ref[:, k : k + 1] == expert, prob_ref[:, k : k + 1], 0.0)
+    high = dense.astype(jnp.bfloat16).astype(jnp.float32)
+    middle = (dense - high).astype(jnp.bfloat16).astype(jnp.float32)
+    low = dense - high - middle
+    chosen = jnp.where(part == 0, high, jnp.where(part == 1, middle, low))
+    out_ref[:, half:] = jnp.where(part < 3, chosen, 0.0).astype(out_ref.dtype)
+
+
+def partial_kernel(blocks, core_ref, sr_ref, r2_ref, gate_ref, up_ref, gate_sum, up_sum):
     k = pl.program_id(0)
-    gate = jnp.dot(x_ref[...], gate_ref[0], preferred_element_type=jnp.float32)
-    up = jnp.dot(x_ref[...], up_ref[0], preferred_element_type=jnp.float32)
+    x = jnp.concatenate([sr_ref[...], r2_ref[...]], axis=0)
+    gate = jnp.dot(x, gate_ref[0], preferred_element_type=jnp.float32)
+    up = jnp.dot(x, up_ref[0], preferred_element_type=jnp.float32)
 
     @pl.when(k == 0)
     def _():
         gate_sum[...] = gate
         up_sum[...] = up
 
-    @pl.when((k > 0) & (k < blocks - 1))
+    @pl.when(k > 0)
     def _():
         gate_sum[...] += gate
         up_sum[...] += up
 
+
+def hidden_kernel(
+    blocks, core_ref, sr_ref, r2_ref, gate_ref, up_ref, gate_part, up_part, out_ref, gate_sum, up_sum
+):
+    k = pl.program_id(0)
+    group = sr_ref.shape[0] // 2
+    x = jnp.concatenate(
+        [sr_ref[:group], r2_ref[:group], sr_ref[group:], r2_ref[group:]], axis=0
+    )
+    gate = jnp.dot(x, gate_ref[0], preferred_element_type=jnp.float32)
+    up = jnp.dot(x, up_ref[0], preferred_element_type=jnp.float32)
+
+    @pl.when(k == 0)
+    def _():
+        gate_sum[...] = gate_part[...] + gate
+        up_sum[...] = up_part[...] + up
+
+    @pl.when(k > 0)
+    def _():
+        gate_sum[...] += gate
+        up_sum[...] += up
+
     @pl.when(k == blocks - 1)
     def _():
-        whole = gate_sum[...] + gate
-        hidden_ref[...] = (
-            whole / (1.0 + jnp.exp(-whole)) * (up_sum[...] + up)
-        ).astype(hidden_ref.dtype)
-
-
-def down_kernel(me_ref, hidden_ref, down_ref, probs_ref, out_ref):
-    half = hidden_ref.shape[2]
-    total = jnp.dot(hidden_ref[0], down_ref[0, :half], preferred_element_type=jnp.float32)
-    total += jnp.dot(hidden_ref[1], down_ref[0, half:], preferred_element_type=jnp.float32)
-    probs = probs_ref[...]
-    mine = lax.broadcasted_iota(jnp.int32, probs.shape, 1) == me_ref[0]
+        whole = gate_sum[...]
+        out_ref[...] = (whole / (1.0 + jnp.exp(-whole)) * up_sum[...]).astype(out_ref.dtype)
+
+
+def expert_front(core, own, other, w_gate, w_up, parts):
+    group2 = own[0].shape[0]
+    tokens = 2 * group2
+    d, f = w_gate.shape[1:]
+    depth = min(d // 2, 512)
+    blocks = d // 2 // depth
+    last = parts is not None
+    rows = pl.BlockSpec((group2, depth), lambda k, core: (0, k))
+    if last:
+        weight = pl.BlockSpec((1, depth, f), lambda k, core: (0, (1 - core[0]) * blocks + k, 0))
+    else:
+        weight = pl.BlockSpec((1, depth, f), lambda k, core: (0, core[0] * blocks + k, 0))
+    whole = pl.BlockSpec((tokens, f), lambda k, core: (0, 0))
+    total = jax.ShapeDtypeStruct((tokens, f), jnp.float32)
+    return pl.pallas_call(
+        functools.partial(hidden_kernel if last else partial_kernel, blocks),
+        grid_spec=pltpu.PrefetchScalarGridSpec(
+            num_scalar_prefetch=1,
+            grid=(blocks,),
+            in_specs=[rows, rows, weight, weight] + ([whole, whole] if last else []),
+            out_specs=whole if last else [whole, whole],
+            scratch_shapes=[pltpu.VMEM((tokens, f), jnp.float32)] * 2 if last else [],
+        ),
+        out_shape=jax.ShapeDtypeStruct((tokens, f), jnp.bfloat16) if last else [total, total],
+        compiler_params=pltpu.CompilerParams(vmem_limit_bytes=40 * MIB),
+        cost_estimate=pl.CostEstimate(
+            flops=2 * tokens * d * f,
+            bytes_accessed=tokens * d + 2 * d * f + 8 * tokens * f,
+            transcendentals=tokens * f if last else 0,
+        ),
+        name="expert_hidden" if last else "expert_partial",
+    )(core, *(other if last else own), w_gate, w_up, *(parts or ()))
+
+
+def back_kernel(send, experts, at_ref, own_ref, other_ref, down_ref, sr_ref, r2_ref, out_ref):
+    f = own_ref.shape[1]
+    group = sr_ref.shape[0] // 2
+    core = at_ref[1]
+    first = int(send)
+
+    def rows(ref, a, b):
+        return jnp.concatenate(
+            [ref[a * group : (a + 1) * group], ref[b * group : (b + 1) * group]], axis=0
+        )
+
+    own = rows(own_ref, 1, 3) if send else rows(own_ref, 0, 2)
+    other = rows(other_ref, 2, 3) if send else rows(other_ref, 0, 1)
+    begin = pl.multiple_of(core * f, 128)
+    rest = pl.multiple_of((1 - core) * f, 128)
+    total = jnp.dot(own, down_ref[0, pl.ds(begin, f), :], preferred_element_type=jnp.float32)
+    total += jnp.dot(other, down_ref[0, pl.ds(rest, f), :], preferred_element_type=jnp.float32)
+    probs = jnp.concatenate(
+        [
+            sr_ref[first * group : (first + 1) * group].astype(jnp.float32),
+            r2_ref[first * group : (first + 1) * group].astype(jnp.float32),
+        ],
+        axis=0,
+    )
+    lane = lax.broadcasted_iota(jnp.int32, probs.shape, 1)
+    mine = lane % experts == at_ref[0]
     weight = jnp.sum(jnp.where(mine, probs, 0.0), axis=1, keepdims=True)
     out_ref[...] = (total * weight).astype(out_ref.dtype)
 
 
-def expert_front(x, w_gate, w_up):
-    tokens = x.shape[0] // 2
-    half, d, f = x.shape[1], w_gate.shape[1], w_gate.shape[2]
-    depth = min(half, 1024)
-    per_half = half // depth
-    blocks = d // depth
+def expert_back(send, experts, at, own, other, w_down, sr, r2, lanes):
+    tokens, f = own.shape
+    group2 = sr.shape[0]
+    width = w_down.shape[2]
+    block = min(width, 512)
+    begin = (sr.shape[1] - lanes) // lanes
     return pl.pallas_call(
-        functools.partial(front_kernel, blocks),
-        grid=(blocks,),
-        out_shape=jax.ShapeDtypeStruct((tokens, f), jnp.bfloat16),
+        functools.partial(back_kernel, send, experts),
+        grid=(width // block,),
+        out_shape=jax.ShapeDtypeStruct((group2, width), jnp.bfloat16 if send else jnp.float32),
         in_specs=[
-            pl.BlockSpec((tokens, depth), lambda k: (k // per_half, k % per_half)),
-            pl.BlockSpec((1, depth, f), lambda k: (0, k, 0)),
-            pl.BlockSpec((1, depth, f), lambda k: (0, k, 0)),
+            smem(),
+            pl.BlockSpec((tokens, f), lambda n: (0, 0)),
+            pl.BlockSpec((tokens, f), lambda n: (0, 0)),
+            pl.BlockSpec((1, 2 * f, block), lambda n: (0, 0, n)),
+            pl.BlockSpec((group2, lanes), lambda n: (0, begin)),
+            pl.BlockSpec((group2, lanes), lambda n: (0, begin)),
         ],
-        out_specs=pl.BlockSpec((tokens, f), lambda k: (0, 0)),
-        scratch_shapes=[pltpu.VMEM((tokens, f), jnp.float32)] * 2,
+        out_specs=pl.BlockSpec((group2, block), lambda n: (0, n)),
         compiler_params=pltpu.CompilerParams(vmem_limit_bytes=40 * MIB),
         cost_estimate=pl.CostEstimate(
-            flops=4 * tokens * d * f,
-            bytes_accessed=2 * (tokens * d + 2 * d * f + tokens * f),
-            transcendentals=tokens * f,
-        ),
-        name="expert_front",
-    )(x, w_gate, w_up)
-
-
-def expert_back(me, hidden, w_down, probs):
-    _, tokens, f = hidden.shape
-    width = w_down.shape[2]
-    block = min(width, 512)
-    return pl.pallas_call(
-        down_kernel,
-        grid=(width // block,),
-        out_shape=jax.ShapeDtypeStruct((tokens, width), jnp.bfloat16),
-        in_specs=[
-            smem(),
-            pl.BlockSpec((2, tokens, f), lambda n: (0, 0, 0)),
-            pl.BlockSpec((1, 2 * f, block), lambda n: (0, 0, n)),
-            pl.BlockSpec(probs.shape, lambda n: (0, 0)),
-        ],
-        out_specs=pl.BlockSpec((tokens, block), lambda n: (0, n)),
-        compiler_params=pltpu.CompilerParams(vmem_limit_bytes=40 * MIB),
-        cost_estimate=pl.CostEstimate(
-            flops=4 * tokens * f * width,
-            bytes_accessed=2 * (2 * tokens * f + 2 * f * width + tokens * width),
+            flops=2 * tokens * f * width,
+            bytes_accessed=2 * (2 * tokens * f + 2 * f * width + 2 * group2 * width),
             transcendentals=0,
         ),
-        name="expert_back",
-    )(me, hidden, w_down, probs)
+        name="expert_back_send" if send else "expert_back_keep",
+    )(at, own, other, w_down, sr, r2)
+
+
+class Moves:
+    def __init__(self, owners):
+        self.owners = owners
+        self.lines = owners // 4
+
+    def go(self, x, where):
+        perm = [
+            (ep * 2 + core, where(ep, core)) for ep in range(self.owners) for core in range(2)
+        ]
+        return lax.ppermute(x, ("ep", "pd"), perm)
+
+    def along_z(self, x, shift):
+        return self.go(x, lambda ep, core: (ep + 4 * shift) % self.owners * 2 + core)
+
+    def flip(self, x, turn):
+        return self.go(x, lambda ep, core: (ep ^ (1 << ((core + turn) % 2))) * 2 + core)
+
+    def cores(self, x):
+        return self.go(x, lambda ep, core: ep * 2 + 1 - core)
 
 
 def body(
@@ -224,22 +315,35 @@
     owners = lax.axis_size("ep")
     me = lax.axis_index("ep").astype(jnp.int32)
     me_ref = me.reshape(1)
-    core = lax.axis_index("pd")
+    core = lax.axis_index("pd").astype(jnp.int32)
     pages, _, page_len, heads, width = prompt_kv.shape
     requests, steps, q_heads, _ = queries.shape
     d = moe_input.shape[2]
     tokens = requests * steps
     slots = owners * CAP
 
-    mine = lax.dynamic_slice_in_dim(
-        moe_input.transpose(1, 0, 2).reshape(tokens, d), core * (d // 2), d // 2, axis=1
+    moves = Moves(owners)
+    top = expert_routes.shape[2]
+    lanes = -(-3 * owners // 128) * 128
+    at = jnp.stack([me, core])
+    own_core = core.reshape(1)
+    mine = pl.pallas_call(
+        functools.partial(pack_kernel, owners),
+        out_shape=jax.ShapeDtypeStruct((tokens, d // 2 + lanes), jnp.bfloat16),
+        in_specs=[smem()] + [vmem()] * 3,
+        out_specs=vmem(),
+        name="pack_tokens",
+    )(
+        own_core,
+        moe_input.transpose(1, 0, 2).reshape(tokens, d),
+        expert_routes.reshape(tokens, top),
+        route_probs.transpose(1, 0, 2).reshape(tokens, top),
     )
-    x = lax.all_gather(mine, ("pd", "ep"), axis=0, tiled=True)
-    hot = expert_routes[..., None] == jnp.arange(owners, dtype=jnp.int32)
-    own_probs = jnp.sum(
-        jnp.where(hot, route_probs.transpose(1, 0, 2)[..., None], 0.0), axis=2
-    ).reshape(tokens, owners)
-    probs = lax.all_gather(own_probs, "ep", axis=0, tiled=True)
+    line = [mine] + [moves.along_z(mine, -shift) for shift in range(1, moves.lines)]
+    line = jnp.concatenate(line, axis=0)
+    sr = jnp.concatenate([line, moves.flip(line, 0)], axis=0)
+    r2 = moves.flip(sr, 1)
+    other_sr, other_r2 = moves.cores(sr), moves.cores(r2)
 
     send = pl.pallas_call(
         functools.partial(page_kernel, pages),
@@ -252,10 +356,19 @@
     )(me_ref, page_owner.reshape(-1), prompt_kv.transpose(0, 1, 3, 2, 4))
     cache = lax.all_to_all(send, "ep", split_axis=0, concat_axis=0, tiled=True)
 
-    hidden = expert_front(x, w_gate, w_up)
-    hidden = lax.all_gather(hidden, "pd", axis=0)
-    parts = expert_back(me_ref, hidden, w_down, probs)
-    moe = lax.psum_scatter(parts, "ep", scatter_dimension=0, tiled=True)
+    parts = expert_front(own_core, (sr, r2), None, w_gate, w_up, None)
+    hidden = expert_front(own_core, (sr, r2), (other_sr, other_r2), w_gate, w_up, parts)
+    other_hidden = moves.cores(hidden)
+    sent = expert_back(True, owners, at, hidden, other_hidden, w_down, sr, r2, lanes)
+    kept = expert_back(False, owners, at, hidden, other_hidden, w_down, sr, r2, lanes)
+    group = moves.lines * tokens
+    kept = kept + moves.flip(sent, 0).astype(jnp.float32)
+    kept = kept[:group] + moves.flip(kept[group:].astype(jnp.bfloat16), 1).astype(jnp.float32)
+    moe = kept[:tokens]
+    for shift in range(1, moves.lines):
+        block = kept[shift * tokens : (shift + 1) * tokens].astype(jnp.bfloat16)
+        moe = moe + moves.along_z(block, shift).astype(jnp.float32)
+    moe = moe.astype(jnp.bfloat16)
     moe_out = moe.reshape(steps, requests, d // 2).transpose(1, 0, 2)
 
     fresh = new_kv.transpose(2, 3, 0, 1, 4).reshape(2, heads, tokens, width)

time: 222 us -> 103 us (0.46)
  waiting for transfers between devices: 132 us -> 45.6 us
  blocking collectives: 45.7 us -> 0 us
  starting transfers between devices: 4.51 us -> 23 us
  between operations: 14.1 us -> 0.88 us
  Pallas kernels: 15.1 us -> 20.8 us
    reduce_scatter x1 -> x0, waiting for transfers between devices: 96.1 us -> none  [body(): moe = lax.psum_scatter(parts, 'ep', scatter_dimension=0, tiled=True)]
    all_gather x2 -> x0, blocking collectives: 45.7 us -> none  [the longest x1 43.4 us: body(): probs = lax.all_gather(own_probs, 'ep', axis=0, tiled=True)]
    ppermute x0 -> x13, waiting for transfers between devices: none -> 35.7 us  [go(): return lax.ppermute(x, ('ep', 'pd'), perm)]
    all_gather x1 -> x0, waiting for transfers between devices: 20.2 us -> none  [body(): x = lax.all_gather(mine, ('pd', 'ep'), axis=0, tiled=True)]
    ppermute x0 -> x13, starting transfers between devices: none -> 18.4 us  [go(): return lax.ppermute(x, ('ep', 'pd'), perm)]
    all_to_all x1, waiting for transfers between devices: 16 us -> 9.96 us  [body(): cache = lax.all_to_all(send, 'ep', split_axis=0, concat_axis=0, tiled=True)]
    pallas_call x2 -> x5, Pallas kernels: 8.29 us -> 13.9 us  [the longest x2 6.56 us: expert_front(): pl.pallas_call(functools.partial(hidden_kernel if last else partial_kerne...]
    unnamed x25 -> x36, local copies, waits for them, and re-layouts: 7.19 us -> 7.97 us
  transfers between devices with their start and end apart: 3 -> 14, of which waited for: 3 -> 8; matrix products, arithmetic and copies ran while one was open for 1% -> 3% of each run, Pallas kernels for 3% -> 13%
where the time goes in v2:
time: 103 us; the launch traced here: 102 us
  waiting for transfers between devices  45.6 us (44%)
  starting transfers between devices  23 us (22%)
  Pallas kernels  20.8 us (20%)
  local copies, waits for them, and re-layouts  9.1 us (9%)
  other arithmetic  2.63 us (3%)
    ppermute x13, waiting for transfers between devices, go(): return lax.ppermute(x, ('ep', 'pd'), perm)  35.7 us
    ppermute x13, starting transfers between devices, go(): return lax.ppermute(x, ('ep', 'pd'), perm)  18.4 us
    all_to_all x1, waiting for transfers between devices, body(): cache = lax.all_to_all(send, 'ep', split_axis=0, concat_axis=0, tiled=True)  9.96 us
    unnamed x36, local copies, waits for them, and re-layouts  7.97 us
    pallas_call x2, Pallas kernels, expert_front(): pl.pallas_call(functools.partial(hidden_kernel if last else partial_kerne...  6.56 us
    pallas_call x2, Pallas kernels, expert_back(): pl.pallas_call(functools.partial(back_kernel, send, experts), grid=(width...  5.62 us
    pallas_call x1, Pallas kernels, body(): pl.pallas_call(functools.partial(page_kernel, pages), out_shape=jax.Shape...  4.96 us
    all_to_all x1, starting transfers between devices, body(): cache = lax.all_to_all(send, 'ep', split_axis=0, concat_axis=0, tiled=True)  4.66 us
  transfers between devices with their start and end apart: 14, of which 8 were waited for; matrix products, arithmetic and copies ran while one was open for 3% of the time, Pallas kernels for 13%

profile of v2, /device:TPU:0, one launch (start us, length us, event | category | flops | bytes accessed | tf_op | source)
XLA Modules:
  0.0 102.0 jit_solution(11666585654729921837)
XLA Ops:
  0.6 1.7 %pack_tokens.1 = bf16[24,2176]{1,0:T(8,128)(2,1)} custom-call(s32[1]{0:T(128)} %bitcast.5.core_ref, bf16[24,4096]{1,0:T(8,128)(2,1)} %bitcast.23, s32[24,8]{1,0:T(8,128)} %bitcast.25, f32[24,8]{1,0:T(8,128)} %bitcast.26), custom_call_target="tpu_custom_call" | custom-call | tf_op jit(solution)/shard_map/pack_tokens/pallas_call | solution.py:330
  2.4 5.0 %collective-permute-start = (bf16[24,2176]{1,0:T(8,128)(2,1)}, bf16[24,2176]{1,0:T(8,128)(2,1)S(1)}, u32[]{:S(2)}, u32[]{:S(2)}) collective-permute-start(bf16[24,2176]{1,0:T(8,128)(2,1)} %pack_tokens.1), channel_id=1, source_target_pairs={{0,24},{1,25},{2,26},{3,27},{4,28},{5,29},{6,30},{7,31},{8,0},{9,1... | collective-permute-start | bytes 313352 | tf_op jit(solution)/shard_map/ppermute | solution.py:289
  7.4 1.0 collective-permute-start.2
  8.4 0.9 constant_dynamic-update-slice_fusion.4
  9.4 1.7 %collective-permute-done = bf16[24,2176]{1,0:T(8,128)(2,1)S(1)} collective-permute-done((bf16[24,2176]{1,0:T(8,128)(2,1)}, bf16[24,2176]{1,0:T(8,128)(2,1)S(1)}, u32[]{:S(2)}, u32[]{:S(2)}) %collective-permute-start) | collective-permute-done | bytes 104480 | tf_op jit(solution)/shard_map/ppermute | solution.py:289
  11.1 5.8 %collective-permute-done.1 = bf16[24,2176]{1,0:T(8,128)(2,1)S(1)} collective-permute-done((bf16[24,2176]{1,0:T(8,128)(2,1)}, bf16[24,2176]{1,0:T(8,128)(2,1)S(1)}, u32[]{:S(2)}, u32[]{:S(2)}) %collective-permute-start.1) | collective-permute-done | bytes 104480 | tf_op jit(solution)/shard_map/ppermute | solution.py:289
  16.8 0.9 pad_maximum_fusion
  17.8 1.6 %collective-permute-start.3 = (bf16[96,2176]{1,0:T(8,128)(2,1)S(1)}, bf16[96,2176]{1,0:T(8,128)(2,1)S(1)}, u32[]{:S(2)}, u32[]{:S(2)}) collective-permute-start(bf16[96,2176]{1,0:T(8,128)(2,1)S(1)} %pad_maximum_fusion), channel_id=1, source_target_pairs={{0,2},{1,5},{2,0},{3,7},{4,6},{5,1},{6,4},{7,3},{8,10},{9,13},{10,... | collective-permute-start | bytes 1253384 | tf_op jit(solution)/shard_map/ppermute | solution.py:289
  19.4 6.5 %collective-permute-done.3 = bf16[96,2176]{1,0:T(8,128)(2,1)S(1)} collective-permute-done((bf16[96,2176]{1,0:T(8,128)(2,1)S(1)}, bf16[96,2176]{1,0:T(8,128)(2,1)S(1)}, u32[]{:S(2)}, u32[]{:S(2)}) %collective-permute-start.3) | collective-permute-done | bytes 417824 | tf_op jit(solution)/shard_map/ppermute | solution.py:289
  25.9 1.6 %collective-permute-start.5 = (bf16[192,2176]{1,0:T(8,128)(2,1)S(1)}, bf16[192,2176]{1,0:T(8,128)(2,1)S(1)}, u32[]{:S(2)}, u32[]{:S(2)}) collective-permute-start(bf16[192,2176]{1,0:T(8,128)(2,1)S(1)} %constant_dynamic-update-slice_fusion.sr_ref), channel_id=1, source_target_pairs={{0,4},{1,3},{2,6},{3,1},{4,0},{5,7},{6,2},{7,5},{8,12},{9,11},{10,... | collective-permute-start | bytes 2506760 | tf_op jit(solution)/shard_map/ppermute | solution.py:289
  27.5 11.0 %collective-permute-done.5.r2_ref = bf16[192,2176]{1,0:T(8,128)(2,1)S(1)} collective-permute-done((bf16[192,2176]{1,0:T(8,128)(2,1)S(1)}, bf16[192,2176]{1,0:T(8,128)(2,1)S(1)}, u32[]{:S(2)}, u32[]{:S(2)}) %collective-permute-start.5) | collective-permute-done | bytes 835616 | tf_op jit(solution)/shard_map/ppermute | solution.py:289
  38.5 2.2 %copy-done.1 = bf16[1,4096,384]{2,1,0:T(8,128)(2,1)S(1)} copy-done((bf16[1,4096,384]{2,1,0:T(8,128)(2,1)S(1)}, bf16[1,4096,384]{2,1,0:T(8,128)(2,1)}, u32[]{:S(2)}) %copy-start.1) | copy-done | bytes 3145752
  40.7 1.9 %copy-done.3 = bf16[1,4096,384]{2,1,0:T(8,128)(2,1)S(1)} copy-done((bf16[1,4096,384]{2,1,0:T(8,128)(2,1)S(1)}, bf16[1,4096,384]{2,1,0:T(8,128)(2,1)}, u32[]{:S(2)}) %copy-start.3) | copy-done | bytes 3145752
  42.6 3.2 %expert_partial.1 = (f32[384,384]{1,0:T(8,128)S(1)}, f32[384,384]{1,0:T(8,128)S(1)}) custom-call(s32[1]{0:T(128)} %bitcast.5.core_ref, bf16[192,2176]{1,0:T(8,128)(2,1)S(1)} %constant_dynamic-update-slice_fusion.sr_ref, bf16[192,2176]{1,0:T(8,128)(2,1)S(1)} %collective-permute-done.5.r2_ref, bf16[1,4096,384]{2,1,0:T(8,128)(2,1)S(1)} %copy-done.1, ...), custom_call_target="tpu_custom_call" | custom-call | flops 1207959552 | bytes 5898240 | tf_op jit(solution)/shard_map/expert_partial/pallas_call | solution.py:201
  45.8 3.4 %expert_hidden.1.own_ref = bf16[384,384]{1,0:T(8,128)(2,1)S(1)} custom-call(s32[1]{0:T(128)} %bitcast.5.core_ref, bf16[192,2176]{1,0:T(8,128)(2,1)S(1)} %collective-permute-done.4.sr_ref, bf16[192,2176]{1,0:T(8,128)(2,1)S(1)} %collective-permute-done.6.r2_ref, bf16[1,4096,384]{2,1,0:T(8,128)(2,1)S(1)} %copy-done.2, bf16[1,4096,384]{2,1,0:T(8,128)(2,1)S(1)} %copy-done.4, ...), custom_call_target="tpu_custom_call" | custom-call | flops 1207959552 | bytes 5898240 | tf_op jit(solution)/shard_map/expert_hidden/pallas_call | solution.py:201
  49.6 1.4 %collective-permute-done.7.other_ref = bf16[384,384]{1,0:T(8,128)(2,1)} collective-permute-done((bf16[384,384]{1,0:T(8,128)(2,1)S(1)}, bf16[384,384]{1,0:T(8,128)(2,1)}, u32[]{:S(2)}, u32[]{:S(2)}) %collective-permute-start.7) | collective-permute-done | bytes 294944 | tf_op jit(solution)/shard_map/ppermute | solution.py:289
  51.0 1.1 %copy-done.6 = bf16[192,2176]{1,0:T(8,128)(2,1)S(1)} copy-done((bf16[192,2176]{1,0:T(8,128)(2,1)S(1)}, bf16[192,2176]{1,0:T(8,128)(2,1)}, u32[]{:S(2)}) %copy-start.6) | copy-done | bytes 835608
  52.2 1.1 %copy-done.8 = bf16[192,2176]{1,0:T(8,128)(2,1)S(1)} copy-done((bf16[192,2176]{1,0:T(8,128)(2,1)S(1)}, bf16[192,2176]{1,0:T(8,128)(2,1)}, u32[]{:S(2)}) %copy-start.8) | copy-done | bytes 835608
  53.3 2.8 %expert_back_send.1 = bf16[192,2048]{1,0:T(8,128)(2,1)S(1)} custom-call(s32[2]{0:T(128)S(1)} %pad_add_fusion.at_ref, bf16[384,384]{1,0:T(8,128)(2,1)S(1)} %expert_hidden.1.own_ref, bf16[384,384]{1,0:T(8,128)(2,1)} %collective-permute-done.7.other_ref, bf16[1,768,2048]{2,1,0:T(8,128)(2,1)S(1)} %copy-done, bf16[192,2176]{1,0:T(8,128)(2,1)S(1)} %copy-done.6, ...), custom_call_target="tpu_custom_call" | custom-call | flops 603979776 | bytes 5308416 | tf_op jit(solution)/shard_map/expert_back_send/pallas_call | solution.py:257
  56.1 1.6 %collective-permute-start.8 = (bf16[192,2048]{1,0:T(8,128)(2,1)S(1)}, bf16[192,2048]{1,0:T(8,128)(2,1)S(1)}, u32[]{:S(2)}, u32[]{:S(2)}) collective-permute-start(bf16[192,2048]{1,0:T(8,128)(2,1)S(1)} %expert_back_send.1), channel_id=1, source_target_pairs={{0,2},{1,5},{2,0},{3,7},{4,6},{5,1},{6,4},{7,3},{8,10},{9,13},{10,... | collective-permute-start | bytes 2359304 | tf_op jit(solution)/shard_map/ppermute | solution.py:289
  57.7 2.8 %expert_back_keep.1 = f32[192,2048]{1,0:T(8,128)S(1)} custom-call(s32[2]{0:T(128)S(1)} %pad_add_fusion.at_ref, bf16[384,384]{1,0:T(8,128)(2,1)S(1)} %expert_hidden.1.own_ref, bf16[384,384]{1,0:T(8,128)(2,1)} %collective-permute-done.7.other_ref, bf16[1,768,2048]{2,1,0:T(8,128)(2,1)S(1)} %copy-done, bf16[192,2176]{1,0:T(8,128)(2,1)S(1)} %copy-done.6, ...), custom_call_target="tpu_custom_call" | custom-call | flops 603979776 | bytes 5308416 | tf_op jit(solution)/shard_map/expert_back_keep/pallas_call | solution.py:257
  60.5 7.6 %collective-permute-done.8 = bf16[192,2048]{1,0:T(8,128)(2,1)S(1)} collective-permute-done((bf16[192,2048]{1,0:T(8,128)(2,1)S(1)}, bf16[192,2048]{1,0:T(8,128)(2,1)S(1)}, u32[]{:S(2)}, u32[]{:S(2)}) %collective-permute-start.8) | collective-permute-done | bytes 786464 | tf_op jit(solution)/shard_map/ppermute | solution.py:289
  68.3 0.8 slice.45
  69.1 1.5 %collective-permute-start.9 = (bf16[96,2048]{1,0:T(8,128)(2,1)}, bf16[96,2048]{1,0:T(8,128)(2,1)S(1)}, u32[]{:S(2)}, u32[]{:S(2)}) collective-permute-start(bf16[96,2048]{1,0:T(8,128)(2,1)} %slice.45), channel_id=1, source_target_pairs={{0,4},{1,3},{2,6},{3,1},{4,0},{5,7},{6,2},{7,5},{8,12},{9,11},{10,... | collective-permute-start | bytes 1179656 | tf_op jit(solution)/shard_map/ppermute | solution.py:289
  70.7 5.0 %quantize_pages.1 = bf16[32,2,2,16,128]{4,3,2,1,0:T(8,128)(2,1)} custom-call(s32[1]{0:T(128)} %bitcast.me_ref, s32[256]{0:T(256)S(1)} %bitcast.22, bf16[16,2,2,16,128]{4,3,2,1,0:T(8,128)(2,1)S(1)} %bitcast.21), custom_call_target="tpu_custom_call" | custom-call | tf_op jit(solution)/shard_map/quantize_pages/pallas_call | solution.py:348
  75.7 4.7 %all-to-all-start = ((bf16[32,2,2,16,128]{4,3,2,1,0:T(8,128)(2,1)}), bf16[32,2,2,16,128]{4,3,2,1,0:T(8,128)(2,1)S(1)}, u32[]{:S(2)}, u32[]{:S(2)}) async-start(bf16[32,2,2,16,128]{4,3,2,1,0:T(8,128)(2,1)} %quantize_pages.1), calls=%async_computation | async-start | bytes 1048576 | tf_op jit(solution)/shard_map/all_to_all | solution.py:357
  80.6 2.0 %collective-permute-start.10 = (bf16[24,2048]{1,0:T(8,128)(2,1)S(1)}, bf16[24,2048]{1,0:T(8,128)(2,1)S(1)}, u32[]{:S(2)}, u32[]{:S(2)}) collective-permute-start(bf16[24,2048]{1,0:T(8,128)(2,1)S(1)} %get-tuple-element.8), channel_id=1, source_target_pairs={{0,8},{1,9},{2,10},{3,11},{4,12},{5,13},{6,14},{7,15},{8,16},{9,17... | collective-permute-start | bytes 294920 | tf_op jit(solution)/shard_map/ppermute | solution.py:289
  82.5 2.4 %collective-permute-start.11 = (bf16[24,2048]{1,0:T(8,128)(2,1)S(1)}, bf16[24,2048]{1,0:T(8,128)(2,1)S(1)}, u32[]{:S(2)}, u32[]{:S(2)}) collective-permute-start(bf16[24,2048]{1,0:T(8,128)(2,1)S(1)} %get-tuple-element.10), channel_id=1, source_target_pairs={{0,16},{1,17},{2,18},{3,19},{4,20},{5,21},{6,22},{7,23},{8,24},{9,... | collective-permute-start | bytes 294920 | tf_op jit(solution)/shard_map/ppermute | solution.py:289
  84.9 1.5 %collective-permute-start.12 = (bf16[24,2048]{1,0:T(8,128)(2,1)S(1)}, bf16[24,2048]{1,0:T(8,128)(2,1)S(1)}, u32[]{:S(2)}, u32[]{:S(2)}) collective-permute-start(bf16[24,2048]{1,0:T(8,128)(2,1)S(1)} %get-tuple-element.9), channel_id=1, source_target_pairs={{0,24},{1,25},{2,26},{3,27},{4,28},{5,29},{6,30},{7,31},{8,0},{9,1... | collective-permute-start | bytes 294920 | tf_op jit(solution)/shard_map/ppermute | solution.py:289
  87.8 10.0 %all-to-all-done.cache_ref = bf16[32,2,2,16,128]{4,3,2,1,0:T(8,128)(2,1)S(1)} async-done(((bf16[32,2,2,16,128]{4,3,2,1,0:T(8,128)(2,1)}), bf16[32,2,2,16,128]{4,3,2,1,0:T(8,128)(2,1)S(1)}, u32[]{:S(2)}, u32[]{:S(2)}) %all-to-all-start) | async-done | bytes 524320 | tf_op jit(solution)/shard_map/all_to_all | solution.py:357
  97.8 1.9 %attention.1 = bf16[8,3,32,128]{3,2,1,0:T(8,128)(2,1)} custom-call(s32[1]{0:T(128)} %bitcast.me_ref, s32[16,16]{1,0:T(8,128)S(1)} %reshape.36.owner_ref, s32[16,16]{1,0:T(8,128)S(1)} %reshape.37.slot_ref, s32[16,16]{1,0:T(8,128)S(1)} %reshape.38.fill_ref, bf16[8,3,32,128]{3,2,1,0:T(8,128)(2,1)S(1)} %copy-done.9, ...), custom_call_target="tpu_custom_call" | custom-call | tf_op jit(solution)/shard_map/attention/pallas_call | solution.py:376
  99.7 1.6 %collective-permute-done.11 = bf16[24,2048]{1,0:T(8,128)(2,1)S(1)} collective-permute-done((bf16[24,2048]{1,0:T(8,128)(2,1)S(1)}, bf16[24,2048]{1,0:T(8,128)(2,1)S(1)}, u32[]{:S(2)}, u32[]{:S(2)}) %collective-permute-start.11) | collective-permute-done | bytes 98336 | tf_op jit(solution)/shard_map/ppermute | solution.py:289
  (53 shorter events, 3.0 us)
Async XLA Ops:
  2.4 8.7 %collective-permute-start = (bf16[24,2176]{1,0:T(8,128)(2,1)}, bf16[24,2176]{1,0:T(8,128)(2,1)S(1)}, u32[]{:S(2)}, u32[]{:S(2)}) collective-permute-start(bf16[24,2176]{1,0:T(8,128)(2,1)} %pack_tokens.1), channel_id=1, source_target_pairs={{0,24},{1,25},{2,26},{3,27},{4,28},{5,29},{6,30},{7,31},{8,0},{9,1... | collective-permute-start | bytes 313352 | tf_op jit(solution)/shard_map/ppermute | solution.py:289
  7.4 9.4 %collective-permute-start.1 = (bf16[24,2176]{1,0:T(8,128)(2,1)}, bf16[24,2176]{1,0:T(8,128)(2,1)S(1)}, u32[]{:S(2)}, u32[]{:S(2)}) collective-permute-start(bf16[24,2176]{1,0:T(8,128)(2,1)} %pack_tokens.1), channel_id=1, source_target_pairs={{0,16},{1,17},{2,18},{3,19},{4,20},{5,21},{6,22},{7,23},{8,24},{9,... | collective-permute-start | bytes 313352 | tf_op jit(solution)/shard_map/ppermute | solution.py:289
  7.4 9.4 %collective-permute-start.2 = (bf16[24,2176]{1,0:T(8,128)(2,1)}, bf16[24,2176]{1,0:T(8,128)(2,1)S(1)}, u32[]{:S(2)}, u32[]{:S(2)}) collective-permute-start(bf16[24,2176]{1,0:T(8,128)(2,1)} %pack_tokens.1), channel_id=1, source_target_pairs={{0,8},{1,9},{2,10},{3,11},{4,12},{5,13},{6,14},{7,15},{8,16},{9,17... | collective-permute-start | bytes 313352 | tf_op jit(solution)/shard_map/ppermute | solution.py:289
  17.8 8.1 %collective-permute-start.3 = (bf16[96,2176]{1,0:T(8,128)(2,1)S(1)}, bf16[96,2176]{1,0:T(8,128)(2,1)S(1)}, u32[]{:S(2)}, u32[]{:S(2)}) collective-permute-start(bf16[96,2176]{1,0:T(8,128)(2,1)S(1)} %pad_maximum_fusion), channel_id=1, source_target_pairs={{0,2},{1,5},{2,0},{3,7},{4,6},{5,1},{6,4},{7,3},{8,10},{9,13},{10,... | collective-permute-start | bytes 1253384 | tf_op jit(solution)/shard_map/ppermute | solution.py:289
  25.9 19.9 %copy-start.5 = (bf16[192,2176]{1,0:T(8,128)(2,1)}, bf16[192,2176]{1,0:T(8,128)(2,1)S(1)}, u32[]{:S(2)}) copy-start(bf16[192,2176]{1,0:T(8,128)(2,1)S(1)} %constant_dynamic-update-slice_fusion.sr_ref) | copy-start | bytes 2506756
  25.9 12.6 %collective-permute-start.5 = (bf16[192,2176]{1,0:T(8,128)(2,1)S(1)}, bf16[192,2176]{1,0:T(8,128)(2,1)S(1)}, u32[]{:S(2)}, u32[]{:S(2)}) collective-permute-start(bf16[192,2176]{1,0:T(8,128)(2,1)S(1)} %constant_dynamic-update-slice_fusion.sr_ref), channel_id=1, source_target_pairs={{0,4},{1,3},{2,6},{3,1},{4,0},{5,7},{6,2},{7,5},{8,12},{9,11},{10,... | collective-permute-start | bytes 2506760 | tf_op jit(solution)/shard_map/ppermute | solution.py:289
  27.5 18.3 %collective-permute-start.4 = (bf16[192,2176]{1,0:T(8,128)(2,1)S(1)}, bf16[192,2176]{1,0:T(8,128)(2,1)S(1)}, u32[]{:S(2)}, u32[]{:S(2)}) collective-permute-start(bf16[192,2176]{1,0:T(8,128)(2,1)S(1)} %constant_dynamic-update-slice_fusion.sr_ref), channel_id=1, source_target_pairs={{0,1},{1,0},{2,3},{3,2},{4,5},{5,4},{6,7},{7,6},{8,9},{9,8},{10,11... | collective-permute-start | bytes 2506760 | tf_op jit(solution)/shard_map/ppermute | solution.py:289
  38.5 7.3 %copy-start.7 = (bf16[192,2176]{1,0:T(8,128)(2,1)}, bf16[192,2176]{1,0:T(8,128)(2,1)S(1)}, u32[]{:S(2)}) copy-start(bf16[192,2176]{1,0:T(8,128)(2,1)S(1)} %collective-permute-done.5.r2_ref) | copy-start | bytes 2506756
  38.5 7.3 %collective-permute-start.6 = (bf16[192,2176]{1,0:T(8,128)(2,1)S(1)}, bf16[192,2176]{1,0:T(8,128)(2,1)S(1)}, u32[]{:S(2)}, u32[]{:S(2)}) collective-permute-start(bf16[192,2176]{1,0:T(8,128)(2,1)S(1)} %collective-permute-done.5.r2_ref), channel_id=1, source_target_pairs={{0,1},{1,0},{2,3},{3,2},{4,5},{5,4},{6,7},{7,6},{8,9},{9,8},{10,11... | collective-permute-start | bytes 2506760 | tf_op jit(solution)/shard_map/ppermute | solution.py:289
  38.5 2.2 %copy-start.1 = (bf16[1,4096,384]{2,1,0:T(8,128)(2,1)S(1)}, bf16[1,4096,384]{2,1,0:T(8,128)(2,1)}, u32[]{:S(2)}) copy-start(bf16[1,4096,384]{2,1,0:T(8,128)(2,1)} %gate_ref.3) | copy-start | bytes 9437188
  40.7 1.9 %copy-start.3 = (bf16[1,4096,384]{2,1,0:T(8,128)(2,1)S(1)}, bf16[1,4096,384]{2,1,0:T(8,128)(2,1)}, u32[]{:S(2)}) copy-start(bf16[1,4096,384]{2,1,0:T(8,128)(2,1)} %up_ref.3) | copy-start | bytes 9437188
  42.6 3.2 %copy-start.2 = (bf16[1,4096,384]{2,1,0:T(8,128)(2,1)S(1)}, bf16[1,4096,384]{2,1,0:T(8,128)(2,1)}, u32[]{:S(2)}) copy-start(bf16[1,4096,384]{2,1,0:T(8,128)(2,1)} %gate_ref.3) | copy-start | bytes 9437188
  42.6 3.2 %copy-start.4 = (bf16[1,4096,384]{2,1,0:T(8,128)(2,1)S(1)}, bf16[1,4096,384]{2,1,0:T(8,128)(2,1)}, u32[]{:S(2)}) copy-start(bf16[1,4096,384]{2,1,0:T(8,128)(2,1)} %up_ref.3) | copy-start | bytes 9437188
  45.8 5.2 %copy-start = (bf16[1,768,2048]{2,1,0:T(8,128)(2,1)S(1)}, bf16[1,768,2048]{2,1,0:T(8,128)(2,1)}, u32[]{:S(2)}) copy-start(bf16[1,768,2048]{2,1,0:T(8,128)(2,1)} %down_ref.3) | copy-start | bytes 9437188
  49.2 1.8 %collective-permute-start.7 = (bf16[384,384]{1,0:T(8,128)(2,1)S(1)}, bf16[384,384]{1,0:T(8,128)(2,1)}, u32[]{:S(2)}, u32[]{:S(2)}) collective-permute-start(bf16[384,384]{1,0:T(8,128)(2,1)S(1)} %expert_hidden.1.own_ref), channel_id=1, source_target_pairs={{0,1},{1,0},{2,3},{3,2},{4,5},{5,4},{6,7},{7,6},{8,9},{9,8},{10,11... | collective-permute-start | bytes 884744 | tf_op jit(solution)/shard_map/ppermute | solution.py:289
  51.0 1.2 %copy-start.6 = (bf16[192,2176]{1,0:T(8,128)(2,1)S(1)}, bf16[192,2176]{1,0:T(8,128)(2,1)}, u32[]{:S(2)}) copy-start(bf16[192,2176]{1,0:T(8,128)(2,1)} %copy-done.5) | copy-start | bytes 2506756
  52.2 1.1 %copy-start.8 = (bf16[192,2176]{1,0:T(8,128)(2,1)S(1)}, bf16[192,2176]{1,0:T(8,128)(2,1)}, u32[]{:S(2)}) copy-start(bf16[192,2176]{1,0:T(8,128)(2,1)} %copy-done.7) | copy-start | bytes 2506756
  56.1 12.1 %collective-permute-start.8 = (bf16[192,2048]{1,0:T(8,128)(2,1)S(1)}, bf16[192,2048]{1,0:T(8,128)(2,1)S(1)}, u32[]{:S(2)}, u32[]{:S(2)}) collective-permute-start(bf16[192,2048]{1,0:T(8,128)(2,1)S(1)} %expert_back_send.1), channel_id=1, source_target_pairs={{0,2},{1,5},{2,0},{3,7},{4,6},{5,1},{6,4},{7,3},{8,10},{9,13},{10,... | collective-permute-start | bytes 2359304 | tf_op jit(solution)/shard_map/ppermute | solution.py:289
  60.5 10.2 %copy-start.11 = (bf16[16,2,16,2,128]{4,3,2,1,0:T(2,128)(2,1)S(1)}, bf16[16,2,16,2,128]{4,3,2,1,0:T(2,128)(2,1)}, u32[]{:S(2)}) copy-start(bf16[16,2,16,2,128]{4,3,2,1,0:T(2,128)(2,1)} %param.12) | copy-start | bytes 786436
  60.5 10.2 %copy-start.10 = (s32[256,1]{0,1:T(1,128)S(1)}, s32[256,1]{0,1:T(1,128)}, u32[]{:S(2)}) copy-start(s32[256,1]{0,1:T(1,128)} %param.13) | copy-start | bytes 3076
  69.1 11.3 %collective-permute-start.9 = (bf16[96,2048]{1,0:T(8,128)(2,1)}, bf16[96,2048]{1,0:T(8,128)(2,1)S(1)}, u32[]{:S(2)}, u32[]{:S(2)}) collective-permute-start(bf16[96,2048]{1,0:T(8,128)(2,1)} %slice.45), channel_id=1, source_target_pairs={{0,4},{1,3},{2,6},{3,1},{4,0},{5,7},{6,2},{7,5},{8,12},{9,11},{10,... | collective-permute-start | bytes 1179656 | tf_op jit(solution)/shard_map/ppermute | solution.py:289
  75.7 22.1 %all-to-all-start = ((bf16[32,2,2,16,128]{4,3,2,1,0:T(8,128)(2,1)}), bf16[32,2,2,16,128]{4,3,2,1,0:T(8,128)(2,1)S(1)}, u32[]{:S(2)}, u32[]{:S(2)}) async-start(bf16[32,2,2,16,128]{4,3,2,1,0:T(8,128)(2,1)} %quantize_pages.1), calls=%async_computation | async-start | bytes 1048576 | tf_op jit(solution)/shard_map/all_to_all | solution.py:357
  80.4 6.0 %copy-start.12 = (bf16[8,3,2,2,128]{4,3,2,1,0:T(2,128)(2,1)S(1)}, bf16[8,3,2,2,128]{4,3,2,1,0:T(2,128)(2,1)}, u32[]{:S(2)}) copy-start(bf16[8,3,2,2,128]{4,3,2,1,0:T(2,128)(2,1)} %param.17) | copy-start | bytes 73732
  80.4 7.3 %copy-start.13 = (s32[256]{0:T(256)S(1)}, s32[256]{0:T(256)}, u32[]{:S(2)}) copy-start(s32[256]{0:T(256)} %param.14) | copy-start | bytes 3076
  80.4 7.3 %copy-start.14 = (s32[256]{0:T(256)S(1)}, s32[256]{0:T(256)}, u32[]{:S(2)}) copy-start(s32[256]{0:T(256)} %param.15) | copy-start | bytes 3076
  80.4 17.4 %copy-start.9 = (bf16[8,3,32,128]{3,2,1,0:T(8,128)(2,1)S(1)}, bf16[8,3,32,128]{3,2,1,0:T(8,128)(2,1)}, u32[]{:S(2)}) copy-start(bf16[8,3,32,128]{3,2,1,0:T(8,128)(2,1)} %q_ref.1) | copy-start | bytes 589828
  80.6 19.2 %collective-permute-start.10 = (bf16[24,2048]{1,0:T(8,128)(2,1)S(1)}, bf16[24,2048]{1,0:T(8,128)(2,1)S(1)}, u32[]{:S(2)}, u32[]{:S(2)}) collective-permute-start(bf16[24,2048]{1,0:T(8,128)(2,1)S(1)} %get-tuple-element.8), channel_id=1, source_target_pairs={{0,8},{1,9},{2,10},{3,11},{4,12},{5,13},{6,14},{7,15},{8,16},{9,17... | collective-permute-start | bytes 294920 | tf_op jit(solution)/shard_map/ppermute | solution.py:289
  82.5 18.8 %collective-permute-start.11 = (bf16[24,2048]{1,0:T(8,128)(2,1)S(1)}, bf16[24,2048]{1,0:T(8,128)(2,1)S(1)}, u32[]{:S(2)}, u32[]{:S(2)}) collective-permute-start(bf16[24,2048]{1,0:T(8,128)(2,1)S(1)} %get-tuple-element.10), channel_id=1, source_target_pairs={{0,16},{1,17},{2,18},{3,19},{4,20},{5,21},{6,22},{7,23},{8,24},{9,... | collective-permute-start | bytes 294920 | tf_op jit(solution)/shard_map/ppermute | solution.py:289
  84.9 16.4 %collective-permute-start.12 = (bf16[24,2048]{1,0:T(8,128)(2,1)S(1)}, bf16[24,2048]{1,0:T(8,128)(2,1)S(1)}, u32[]{:S(2)}, u32[]{:S(2)}) collective-permute-start(bf16[24,2048]{1,0:T(8,128)(2,1)S(1)} %get-tuple-element.9), channel_id=1, source_target_pairs={{0,24},{1,25},{2,26},{3,27},{4,28},{5,29},{6,30},{7,31},{8,0},{9,1... | collective-permute-start | bytes 294920 | tf_op jit(solution)/shard_map/ppermute | solution.py:289

commit v3 on v2

--- a/solution.py
+++ b/solution.py
@@ -19,6 +19,10 @@
 
 def smem():
     return pl.BlockSpec(memory_space=pltpu.SMEM)
+
+
+def hbm():
+    return pl.BlockSpec(memory_space=pltpu.HBM)
 
 
 def page_kernel(pages, me_ref, owner_ref, kv_ref, send_ref, count_ref):
@@ -140,73 +144,69 @@
     out_ref[:, half:] = jnp.where(part < 3, chosen, 0.0).astype(out_ref.dtype)
 
 
-def partial_kernel(blocks, core_ref, sr_ref, r2_ref, gate_ref, up_ref, gate_sum, up_sum):
-    k = pl.program_id(0)
-    x = jnp.concatenate([sr_ref[...], r2_ref[...]], axis=0)
-    gate = jnp.dot(x, gate_ref[0], preferred_element_type=jnp.float32)
-    up = jnp.dot(x, up_ref[0], preferred_element_type=jnp.float32)
-
-    @pl.when(k == 0)
-    def _():
-        gate_sum[...] = gate
-        up_sum[...] = up
-
-    @pl.when(k > 0)
-    def _():
-        gate_sum[...] += gate
-        up_sum[...] += up
+def weight_copies(half, core, gate_ref, up_ref, held, sems):
+    depth = half // sems.shape[1]
+    pairs = []
+    for c in range(sems.shape[1]):
+        rows = pl.ds(pl.multiple_of(core * half + c * depth, 128), depth)
+        pairs.append(
+            [
+                pltpu.make_async_copy(
+                    ref.at[0, rows], held.at[i, pl.ds(c * depth, depth)], sems.at[i, c]
+                )
+                for i, ref in enumerate((gate_ref, up_ref))
+            ]
+        )
+    for pair in pairs:
+        for copy in pair:
+            copy.start()
+    return pairs, depth
+
+
+def partial_kernel(core_ref, sr_ref, r2_ref, gate_ref, up_ref, gate_sum, up_sum, held, sems):
+    half = held.shape[1]
+    pairs, depth = weight_copies(half, core_ref[0], gate_ref, up_ref, held, sems)
+    for c, pair in enumerate(pairs):
+        at = slice(c * depth, (c + 1) * depth)
+        x = jnp.concatenate([sr_ref[:, at], r2_ref[:, at]], axis=0)
+        for i, total in enumerate((gate_sum, up_sum)):
+            pair[i].wait()
+            part = jnp.dot(x, held[i, at], preferred_element_type=jnp.float32)
+            total[...] = part if c == 0 else total[...] + part
 
 
 def hidden_kernel(
-    blocks, core_ref, sr_ref, r2_ref, gate_ref, up_ref, gate_part, up_part, out_ref, gate_sum, up_sum
+    core_ref, sr_ref, r2_ref, gate_ref, up_ref, gate_part, up_part, out_ref, held, sems, sums
 ):
-    k = pl.program_id(0)
+    half = held.shape[1]
     group = sr_ref.shape[0] // 2
-    x = jnp.concatenate(
-        [sr_ref[:group], r2_ref[:group], sr_ref[group:], r2_ref[group:]], axis=0
-    )
-    gate = jnp.dot(x, gate_ref[0], preferred_element_type=jnp.float32)
-    up = jnp.dot(x, up_ref[0], preferred_element_type=jnp.float32)
-
-    @pl.when(k == 0)
-    def _():
-        gate_sum[...] = gate_part[...] + gate
-        up_sum[...] = up_part[...] + up
-
-    @pl.when(k > 0)
-    def _():
-        gate_sum[...] += gate
-        up_sum[...] += up
-
-    @pl.when(k == blocks - 1)
-    def _():
-        whole = gate_sum[...]
-        out_ref[...] = (whole / (1.0 + jnp.exp(-whole)) * up_sum[...]).astype(out_ref.dtype)
-
-
-def expert_front(core, own, other, w_gate, w_up, parts):
-    group2 = own[0].shape[0]
-    tokens = 2 * group2
+    pairs, depth = weight_copies(half, 1 - core_ref[0], gate_ref, up_ref, held, sems)
+    last = len(pairs) - 1
+    for c, pair in enumerate(pairs):
+        at = slice(c * depth, (c + 1) * depth)
+        x = jnp.concatenate(
+            [sr_ref[:group, at], r2_ref[:group, at], sr_ref[group:, at], r2_ref[group:, at]],
+            axis=0,
+        )
+        for i, start in enumerate((gate_part, up_part)):
+            pair[i].wait()
+            part = jnp.dot(x, held[i, at], preferred_element_type=jnp.float32)
+            sums[i] = (start[...] if c == 0 else sums[i]) + part
+    gate = sums[0]
+    out_ref[...] = (gate / (1.0 + jnp.exp(-gate)) * sums[1]).astype(out_ref.dtype)
+
+
+def expert_front(core, rows, w_gate, w_up, parts):
+    tokens = 2 * rows[0].shape[0]
     d, f = w_gate.shape[1:]
-    depth = min(d // 2, 512)
-    blocks = d // 2 // depth
     last = parts is not None
-    rows = pl.BlockSpec((group2, depth), lambda k, core: (0, k))
-    if last:
-        weight = pl.BlockSpec((1, depth, f), lambda k, core: (0, (1 - core[0]) * blocks + k, 0))
-    else:
-        weight = pl.BlockSpec((1, depth, f), lambda k, core: (0, core[0] * blocks + k, 0))
-    whole = pl.BlockSpec((tokens, f), lambda k, core: (0, 0))
     total = jax.ShapeDtypeStruct((tokens, f), jnp.float32)
+    scratch = [pltpu.VMEM((2, d // 2, f), jnp.bfloat16), pltpu.SemaphoreType.DMA((2, 4))]
     return pl.pallas_call(
-        functools.partial(hidden_kernel if last else partial_kernel, blocks),
-        grid_spec=pltpu.PrefetchScalarGridSpec(
-            num_scalar_prefetch=1,
-            grid=(blocks,),
-            in_specs=[rows, rows, weight, weight] + ([whole, whole] if last else []),
-            out_specs=whole if last else [whole, whole],
-            scratch_shapes=[pltpu.VMEM((tokens, f), jnp.float32)] * 2 if last else [],
-        ),
+        hidden_kernel if last else partial_kernel,
+        in_specs=[smem(), vmem(), vmem(), hbm(), hbm()] + ([vmem(), vmem()] if last else []),
+        out_specs=vmem() if last else [vmem(), vmem()],
+        scratch_shapes=scratch + ([pltpu.VMEM((2, tokens, f), jnp.float32)] if last else []),
         out_shape=jax.ShapeDtypeStruct((tokens, f), jnp.bfloat16) if last else [total, total],
         compiler_params=pltpu.CompilerParams(vmem_limit_bytes=40 * MIB),
         cost_estimate=pl.CostEstimate(
@@ -215,10 +215,24 @@
             transcendentals=tokens * f if last else 0,
         ),
         name="expert_hidden" if last else "expert_partial",
-    )(core, *(other if last else own), w_gate, w_up, *(parts or ()))
-
-
-def back_kernel(send, experts, at_ref, own_ref, other_ref, down_ref, sr_ref, r2_ref, out_ref):
+    )(core, *rows, w_gate, w_up, *(parts or ()))
+
+
+def back_kernel(
+    send, experts, lanes, at_ref, own_ref, other_ref, sr_ref, r2_ref, down_ref, out_ref, held, sems
+):
+    chunks = sems.shape[0]
+    block = held.shape[1] // chunks
+    copies = [
+        pltpu.make_async_copy(
+            down_ref.at[0, :, pl.ds(c * block, block)],
+            held.at[:, pl.ds(c * block, block)],
+            sems.at[c],
+        )
+        for c in range(chunks)
+    ]
+    for copy in copies:
+        copy.start()
     f = own_ref.shape[1]
     group = sr_ref.shape[0] // 2
     core = at_ref[1]
@@ -233,40 +247,36 @@
     other = rows(other_ref, 2, 3) if send else rows(other_ref, 0, 1)
     begin = pl.multiple_of(core * f, 128)
     rest = pl.multiple_of((1 - core) * f, 128)
-    total = jnp.dot(own, down_ref[0, pl.ds(begin, f), :], preferred_element_type=jnp.float32)
-    total += jnp.dot(other, down_ref[0, pl.ds(rest, f), :], preferred_element_type=jnp.float32)
+    tail = slice(sr_ref.shape[1] - lanes, sr_ref.shape[1])
+    picked = slice(first * group, (first + 1) * group)
     probs = jnp.concatenate(
-        [
-            sr_ref[first * group : (first + 1) * group].astype(jnp.float32),
-            r2_ref[first * group : (first + 1) * group].astype(jnp.float32),
-        ],
+        [sr_ref[picked, tail].astype(jnp.float32), r2_ref[picked, tail].astype(jnp.float32)],
         axis=0,
     )
     lane = lax.broadcasted_iota(jnp.int32, probs.shape, 1)
     mine = lane % experts == at_ref[0]
     weight = jnp.sum(jnp.where(mine, probs, 0.0), axis=1, keepdims=True)
-    out_ref[...] = (total * weight).astype(out_ref.dtype)
+    for c, copy in enumerate(copies):
+        at = slice(c * block, (c + 1) * block)
+        copy.wait()
+        total = jnp.dot(own, held[pl.ds(begin, f), at], preferred_element_type=jnp.float32)
+        total += jnp.dot(other, held[pl.ds(rest, f), at], preferred_element_type=jnp.float32)
+        out_ref[:, at] = (total * weight).astype(out_ref.dtype)
 
 
 def expert_back(send, experts, at, own, other, w_down, sr, r2, lanes):
     tokens, f = own.shape
     group2 = sr.shape[0]
     width = w_down.shape[2]
-    block = min(width, 512)
-    begin = (sr.shape[1] - lanes) // lanes
     return pl.pallas_call(
-        functools.partial(back_kernel, send, experts),
-        grid=(width // block,),
+        functools.partial(back_kernel, send, experts, lanes),
         out_shape=jax.ShapeDtypeStruct((group2, width), jnp.bfloat16 if send else jnp.float32),
-        in_specs=[
-            smem(),
-            pl.BlockSpec((tokens, f), lambda n: (0, 0)),
-            pl.BlockSpec((tokens, f), lambda n: (0, 0)),
-            pl.BlockSpec((1, 2 * f, block), lambda n: (0, 0, n)),
-            pl.BlockSpec((group2, lanes), lambda n: (0, begin)),
-            pl.BlockSpec((group2, lanes), lambda n: (0, begin)),
+        in_specs=[smem()] + [vmem()] * 4 + [hbm()],
+        out_specs=vmem(),
+        scratch_shapes=[
+            pltpu.VMEM(w_down.shape[1:], jnp.bfloat16),
+            pltpu.SemaphoreType.DMA((4,)),
         ],
-        out_specs=pl.BlockSpec((group2, block), lambda n: (0, n)),
         compiler_params=pltpu.CompilerParams(vmem_limit_bytes=40 * MIB),
         cost_estimate=pl.CostEstimate(
             flops=2 * tokens * f * width,
@@ -274,7 +284,7 @@
             transcendentals=0,
         ),
         name="expert_back_send" if send else "expert_back_keep",
-    )(at, own, other, w_down, sr, r2)
+    )(at, own, other, sr, r2, w_down)
 
 
 class Moves:
@@ -339,12 +349,6 @@
         expert_routes.reshape(tokens, top),
         route_probs.transpose(1, 0, 2).reshape(tokens, top),
     )
-    line = [mine] + [moves.along_z(mine, -shift) for shift in range(1, moves.lines)]
-    line = jnp.concatenate(line, axis=0)
-    sr = jnp.concatenate([line, moves.flip(line, 0)], axis=0)
-    r2 = moves.flip(sr, 1)
-    other_sr, other_r2 = moves.cores(sr), moves.cores(r2)
-
     send = pl.pallas_call(
         functools.partial(page_kernel, pages),
         out_shape=jax.ShapeDtypeStruct((slots, 2, heads, page_len, width), jnp.bfloat16),
@@ -354,25 +358,22 @@
         compiler_params=pltpu.CompilerParams(vmem_limit_bytes=40 * MIB),
         name="quantize_pages",
     )(me_ref, page_owner.reshape(-1), prompt_kv.transpose(0, 1, 3, 2, 4))
+    line = [mine] + [moves.along_z(mine, -shift) for shift in range(1, moves.lines)]
+    line = jnp.concatenate(line, axis=0)
+    fresh = new_kv.transpose(2, 3, 0, 1, 4).reshape(2, heads, tokens, width)
+    fresh = jnp.pad(fresh, ((0, 0), (0, 0), (0, 128 - tokens), (0, 0)))
+    tables = [t.reshape(owners, pages) for t in (page_owner, page_slot, page_fill)]
+    line, send, fresh, tables = lax.optimization_barrier((line, send, fresh, tables))
+    sr = jnp.concatenate([line, moves.flip(line, 0)], axis=0)
+    r2 = moves.flip(sr, 1)
     cache = lax.all_to_all(send, "ep", split_axis=0, concat_axis=0, tiled=True)
-
-    parts = expert_front(own_core, (sr, r2), None, w_gate, w_up, None)
-    hidden = expert_front(own_core, (sr, r2), (other_sr, other_r2), w_gate, w_up, parts)
+    other_sr, other_r2 = moves.cores(sr), moves.cores(r2)
+
+    parts = expert_front(own_core, (sr, r2), w_gate, w_up, None)
+    hidden = expert_front(own_core, (other_sr, other_r2), w_gate, w_up, parts)
     other_hidden = moves.cores(hidden)
     sent = expert_back(True, owners, at, hidden, other_hidden, w_down, sr, r2, lanes)
     kept = expert_back(False, owners, at, hidden, other_hidden, w_down, sr, r2, lanes)
-    group = moves.lines * tokens
-    kept = kept + moves.flip(sent, 0).astype(jnp.float32)
-    kept = kept[:group] + moves.flip(kept[group:].astype(jnp.bfloat16), 1).astype(jnp.float32)
-    moe = kept[:tokens]
-    for shift in range(1, moves.lines):
-        block = kept[shift * tokens : (shift + 1) * tokens].astype(jnp.bfloat16)
-        moe = moe + moves.along_z(block, shift).astype(jnp.float32)
-    moe = moe.astype(jnp.bfloat16)
-    moe_out = moe.reshape(steps, requests, d // 2).transpose(1, 0, 2)
-
-    fresh = new_kv.transpose(2, 3, 0, 1, 4).reshape(2, heads, tokens, width)
-    fresh = jnp.pad(fresh, ((0, 0), (0, 0), (0, 128 - tokens), (0, 0)))
     attn_out = pl.pallas_call(
         functools.partial(attention_kernel, pages),
         out_shape=jax.ShapeDtypeStruct(queries.shape, jnp.bfloat16),
@@ -382,13 +383,22 @@
         name="attention",
     )(
         me_ref,
-        page_owner.reshape(owners, pages),
-        page_slot.reshape(owners, pages),
-        page_fill.reshape(owners, pages),
+        *tables,
         queries,
         cache,
         fresh,
     )
+    group = moves.lines * tokens
+    kept = kept + moves.flip(sent, 0).astype(jnp.float32)
+    kept, attn_out = lax.optimization_barrier((kept, attn_out))
+    kept = kept[:group] + moves.flip(kept[group:].astype(jnp.bfloat16), 1).astype(jnp.float32)
+    moe = kept[:tokens]
+    for shift in range(1, moves.lines):
+        block = kept[shift * tokens : (shift + 1) * tokens].astype(jnp.bfloat16)
+        moe = moe + moves.along_z(block, shift).astype(jnp.float32)
+    moe = moe.astype(jnp.bfloat16)
+    moe_out = moe.reshape(steps, requests, d // 2).transpose(1, 0, 2)
+
     return (attn_out, moe_out)
 
 

time: 103 us -> 102 us (level)
  waiting for transfers between devices: 45.6 us -> 37.7 us
  local copies, waits for them, and re-layouts: 9.1 us -> 13.5 us
  Pallas kernels: 20.8 us -> 23.8 us
  starting transfers between devices: 23 us -> 21.6 us
    ppermute x13, waiting for transfers between devices: 35.7 us -> 30.4 us  [go(): return lax.ppermute(x, ('ep', 'pd'), perm)]
    pallas_call x4, Pallas kernels: 12.2 us -> 14.9 us  [the longest x2 7.99 us: expert_front(): pl.pallas_call(hidden_kernel if last else partial_kernel, in_specs=[smem(...]
    all_to_all x1, waiting for transfers between devices: 9.96 us -> 7.33 us  [body(): cache = lax.all_to_all(send, 'ep', split_axis=0, concat_axis=0, tiled=True)]
    unnamed x36 -> x31, local copies, waits for them, and re-layouts: 7.97 us -> 10.4 us
    reshape x3, local copies, waits for them, and re-layouts: 0.23 us -> 1.6 us  [body(): t.reshape(owners, pages)]
    ppermute x13, starting transfers between devices: 18.4 us -> 17.2 us  [go(): return lax.ppermute(x, ('ep', 'pd'), perm)]
    add x1, other arithmetic: 0.17 us -> 1.31 us  [body(): kept = kept + moves.flip(sent, 0).astype(jnp.float32)]
    pallas_call x1, Pallas kernels: 1.93 us -> 3.04 us  [body(): pl.pallas_call(functools.partial(attention_kernel, pages), out_shape=jax....]
  transfers between devices with their start and end apart: 14 -> 14, of which waited for: 8 -> 7; matrix products, arithmetic and copies ran while one was open for 3% -> 6% of each run, Pallas kernels for 13% -> 18%
where the time goes in v3:
time: 102 us; the launch traced here: 101 us
  waiting for transfers between devices  37.7 us (37%)
  Pallas kernels  23.8 us (23%)
  starting transfers between devices  21.6 us (21%)
  local copies, waits for them, and re-layouts  13.5 us (13%)
  other arithmetic  3.58 us (4%)
    ppermute x13, waiting for transfers between devices, go(): return lax.ppermute(x, ('ep', 'pd'), perm)  30.4 us
    ppermute x13, starting transfers between devices, go(): return lax.ppermute(x, ('ep', 'pd'), perm)  17.2 us
    unnamed x31, local copies, waits for them, and re-layouts  10.4 us
    pallas_call x2, Pallas kernels, expert_front(): pl.pallas_call(hidden_kernel if last else partial_kernel, in_specs=[smem(...  7.99 us
    all_to_all x1, waiting for transfers between devices, body(): cache = lax.all_to_all(send, 'ep', split_axis=0, concat_axis=0, tiled=True)  7.33 us
    pallas_call x2, Pallas kernels, expert_back(): pl.pallas_call(functools.partial(back_kernel, send, experts, lanes), out_...  6.9 us
    all_to_all x1, starting transfers between devices, body(): cache = lax.all_to_all(send, 'ep', split_axis=0, concat_axis=0, tiled=True)  4.42 us
    pallas_call x1, Pallas kernels, body(): pl.pallas_call(functools.partial(page_kernel, pages), out_shape=jax.Shape...  4.13 us
  transfers between devices with their start and end apart: 14, of which 7 were waited for; matrix products, arithmetic and copies ran while one was open for 6% of the time, Pallas kernels for 18%

profile of v3, /device:TPU:0, one launch (start us, length us, event | category | flops | bytes accessed | tf_op | source)
XLA Modules:
  0.0 101.1 jit_solution(8914840343038829318)
XLA Ops:
  0.6 1.7 %pack_tokens.1 = bf16[24,2176]{1,0:T(8,128)(2,1)} custom-call(s32[1]{0:T(128)} %bitcast.1.core_ref, bf16[24,4096]{1,0:T(8,128)(2,1)} %bitcast.23, s32[24,8]{1,0:T(8,128)} %bitcast.25, f32[24,8]{1,0:T(8,128)} %bitcast.26), custom_call_target="tpu_custom_call" | custom-call | tf_op jit(solution)/shard_map/pack_tokens/pallas_call | solution.py:340
  2.4 3.0 %collective-permute-start.2 = (bf16[24,2176]{1,0:T(8,128)(2,1)}, bf16[24,2176]{1,0:T(8,128)(2,1)S(1)}, u32[]{:S(2)}, u32[]{:S(2)}) collective-permute-start(bf16[24,2176]{1,0:T(8,128)(2,1)} %pack_tokens.1), channel_id=1, source_target_pairs={{0,8},{1,9},{2,10},{3,11},{4,12},{5,13},{6,14},{7,15},{8,16},{9,17... | collective-permute-start | bytes 313352 | tf_op jit(solution)/shard_map/ppermute | solution.py:299
  5.4 2.6 %collective-permute-start.1 = (bf16[24,2176]{1,0:T(8,128)(2,1)}, bf16[24,2176]{1,0:T(8,128)(2,1)S(1)}, u32[]{:S(2)}, u32[]{:S(2)}) collective-permute-start(bf16[24,2176]{1,0:T(8,128)(2,1)} %pack_tokens.1), channel_id=1, source_target_pairs={{0,16},{1,17},{2,18},{3,19},{4,20},{5,21},{6,22},{7,23},{8,24},{9,... | collective-permute-start | bytes 313352 | tf_op jit(solution)/shard_map/ppermute | solution.py:299
  8.0 1.3 %collective-permute-start = (bf16[24,2176]{1,0:T(8,128)(2,1)}, bf16[24,2176]{1,0:T(8,128)(2,1)S(1)}, u32[]{:S(2)}, u32[]{:S(2)}) collective-permute-start(bf16[24,2176]{1,0:T(8,128)(2,1)} %pack_tokens.1), channel_id=1, source_target_pairs={{0,24},{1,25},{2,26},{3,27},{4,28},{5,29},{6,30},{7,31},{8,0},{9,1... | collective-permute-start | bytes 313352 | tf_op jit(solution)/shard_map/ppermute | solution.py:299
  9.8 1.3 %reduce.3 = s32[256]{0:T(256)S(1)} reduce(s32[256,1]{0,1:T(1,128)} %param.13, s32[]{:T(128)} %broadcast.5), dimensions={1}, to_apply=%param.13.reduce_sub_computation.3 | reduce | bytes 2052 | tf_op args[1]
  13.5 1.0 copy.22
  15.9 4.1 %quantize_pages.1 = bf16[32,2,2,16,128]{4,3,2,1,0:T(8,128)(2,1)S(1)} custom-call(s32[1]{0:T(128)} %bitcast.me_ref, s32[256]{0:T(256)S(1)} %bitcast.22, bf16[16,2,2,16,128]{4,3,2,1,0:T(8,128)(2,1)S(1)} %bitcast.21), custom_call_target="tpu_custom_call" | custom-call | tf_op jit(solution)/shard_map/quantize_pages/pallas_call | solution.py:352
  20.8 1.5 %collective-permute-start.3 = (bf16[96,2176]{1,0:T(8,128)(2,1)S(1)}, bf16[96,2176]{1,0:T(8,128)(2,1)S(1)}, u32[]{:S(2)}, u32[]{:S(2)}) collective-permute-start(bf16[96,2176]{1,0:T(8,128)(2,1)S(1)} %pad_maximum_fusion), channel_id=1, source_target_pairs={{0,2},{1,5},{2,0},{3,7},{4,6},{5,1},{6,4},{7,3},{8,10},{9,13},{10,... | collective-permute-start | bytes 1253384 | tf_op jit(solution)/shard_map/ppermute | solution.py:299
  22.3 6.5 %collective-permute-done.3 = bf16[96,2176]{1,0:T(8,128)(2,1)S(1)} collective-permute-done((bf16[96,2176]{1,0:T(8,128)(2,1)S(1)}, bf16[96,2176]{1,0:T(8,128)(2,1)S(1)}, u32[]{:S(2)}, u32[]{:S(2)}) %collective-permute-start.3) | collective-permute-done | bytes 417824 | tf_op jit(solution)/shard_map/ppermute | solution.py:299
  28.9 1.6 %collective-permute-start.5 = (bf16[192,2176]{1,0:T(8,128)(2,1)S(1)}, bf16[192,2176]{1,0:T(8,128)(2,1)S(1)}, u32[]{:S(2)}, u32[]{:S(2)}) collective-permute-start(bf16[192,2176]{1,0:T(8,128)(2,1)S(1)} %constant_dynamic-update-slice_fusion.sr_ref), channel_id=1, source_target_pairs={{0,4},{1,3},{2,6},{3,1},{4,0},{5,7},{6,2},{7,5},{8,12},{9,11},{10,... | collective-permute-start | bytes 2506760 | tf_op jit(solution)/shard_map/ppermute | solution.py:299
  30.5 11.0 %collective-permute-done.5.r2_ref = bf16[192,2176]{1,0:T(8,128)(2,1)S(1)} collective-permute-done((bf16[192,2176]{1,0:T(8,128)(2,1)S(1)}, bf16[192,2176]{1,0:T(8,128)(2,1)S(1)}, u32[]{:S(2)}, u32[]{:S(2)}) %collective-permute-start.5) | collective-permute-done | bytes 835616 | tf_op jit(solution)/shard_map/ppermute | solution.py:299
  41.5 2.2 %copy-done.2 = bf16[1,4096,384]{2,1,0:T(8,128)(2,1)S(1)} copy-done((bf16[1,4096,384]{2,1,0:T(8,128)(2,1)S(1)}, bf16[1,4096,384]{2,1,0:T(8,128)(2,1)}, u32[]{:S(2)}) %copy-start.2) | copy-done | bytes 3145752
  43.7 3.9 %expert_partial.1 = (f32[384,384]{1,0:T(8,128)S(1)}, f32[384,384]{1,0:T(8,128)S(1)}) custom-call(s32[1]{0:T(128)} %bitcast.1.core_ref, bf16[192,2176]{1,0:T(8,128)(2,1)S(1)} %constant_dynamic-update-slice_fusion.sr_ref, bf16[192,2176]{1,0:T(8,128)(2,1)S(1)} %collective-permute-done.5.r2_ref, bf16[1,4096,384]{2,1,0:T(8,128)(2,1)S(1)} %copy-done.1, ...), custom_call_target="tpu_custom_call" | custom-call | flops 1207959552 | bytes 5898240 | tf_op jit(solution)/shard_map/expert_partial/pallas_call | solution.py:205
  47.7 4.0 %expert_hidden.1.own_ref = bf16[384,384]{1,0:T(8,128)(2,1)S(1)} custom-call(s32[1]{0:T(128)} %bitcast.1.core_ref, bf16[192,2176]{1,0:T(8,128)(2,1)S(1)} %collective-permute-done.4.sr_ref, bf16[192,2176]{1,0:T(8,128)(2,1)S(1)} %collective-permute-done.6.r2_ref, bf16[1,4096,384]{2,1,0:T(8,128)(2,1)S(1)} %copy-done.1, bf16[1,4096,384]{2,1,0:T(8,128)(2,1)S(1)} %copy-done.2, ...), custom_call_target="tpu_custom_call" | custom-call | flops 1207959552 | bytes 5898240 | tf_op jit(solution)/shard_map/expert_hidden/pallas_call | solution.py:205
  52.0 4.4 %all-to-all-start = ((bf16[32,2,2,16,128]{4,3,2,1,0:T(8,128)(2,1)}), bf16[32,2,2,16,128]{4,3,2,1,0:T(8,128)(2,1)}, u32[]{:S(2)}, u32[]{:S(2)}) async-start(bf16[32,2,2,16,128]{4,3,2,1,0:T(8,128)(2,1)} %copy-done.9), calls=%async_computation | async-start | bytes 1048576 | tf_op jit(solution)/shard_map/all_to_all | solution.py:369
  56.5 1.1 %copy-done.4 = bf16[192,2176]{1,0:T(8,128)(2,1)S(1)} copy-done((bf16[192,2176]{1,0:T(8,128)(2,1)S(1)}, bf16[192,2176]{1,0:T(8,128)(2,1)}, u32[]{:S(2)}) %copy-start.4) | copy-done | bytes 835608
  57.7 1.1 %copy-done.7 = bf16[192,2176]{1,0:T(8,128)(2,1)S(1)} copy-done((bf16[192,2176]{1,0:T(8,128)(2,1)S(1)}, bf16[192,2176]{1,0:T(8,128)(2,1)}, u32[]{:S(2)}) %copy-start.7) | copy-done | bytes 835608
  58.8 3.9 %expert_back_send.1 = bf16[192,2048]{1,0:T(8,128)(2,1)} custom-call(s32[2]{0:T(128)S(1)} %pad_add_fusion.at_ref, bf16[384,384]{1,0:T(8,128)(2,1)S(1)} %expert_hidden.1.own_ref, bf16[384,384]{1,0:T(8,128)(2,1)} %collective-permute-done.7.other_ref, bf16[192,2176]{1,0:T(8,128)(2,1)S(1)} %copy-done.4, bf16[192,2176]{1,0:T(8,128)(2,1)S(1)} %copy-done.7, ...), custom_call_target="tpu_custom_call" | custom-call | flops 603979776 | bytes 5308416 | tf_op jit(solution)/shard_map/expert_back_send/pallas_call | solution.py:271
  62.7 1.6 %collective-permute-start.8 = (bf16[192,2048]{1,0:T(8,128)(2,1)}, bf16[192,2048]{1,0:T(8,128)(2,1)}, u32[]{:S(2)}, u32[]{:S(2)}) collective-permute-start(bf16[192,2048]{1,0:T(8,128)(2,1)} %expert_back_send.1), channel_id=1, source_target_pairs={{0,2},{1,5},{2,0},{3,7},{4,6},{5,1},{6,4},{7,3},{8,10},{9,13},{10,... | collective-permute-start | bytes 2359304 | tf_op jit(solution)/shard_map/ppermute | solution.py:299
  64.4 7.3 %all-to-all-done.cache_ref = bf16[32,2,2,16,128]{4,3,2,1,0:T(8,128)(2,1)} async-done(((bf16[32,2,2,16,128]{4,3,2,1,0:T(8,128)(2,1)}), bf16[32,2,2,16,128]{4,3,2,1,0:T(8,128)(2,1)}, u32[]{:S(2)}, u32[]{:S(2)}) %all-to-all-start) | async-done | bytes 524320 | tf_op jit(solution)/shard_map/all_to_all | solution.py:369
  72.6 0.9 copy-done.11
  73.5 3.0 %attention.1 = bf16[8,3,32,128]{3,2,1,0:T(8,128)(2,1)} custom-call(s32[1]{0:T(128)} %bitcast.me_ref, s32[16,16]{1,0:T(8,128)S(1)} %reshape.38.owner_ref, s32[16,16]{1,0:T(8,128)S(1)} %reshape.39.slot_ref, s32[16,16]{1,0:T(8,128)S(1)} %reshape.40.fill_ref, bf16[8,3,32,128]{3,2,1,0:T(8,128)(2,1)S(1)} %copy-done.11, ...), custom_call_target="tpu_custom_call" | custom-call | tf_op jit(solution)/shard_map/attention/pallas_call | solution.py:377
  76.6 1.1 %copy-done.8 = bf16[192,2176]{1,0:T(8,128)(2,1)S(1)} copy-done((bf16[192,2176]{1,0:T(8,128)(2,1)S(1)}, bf16[192,2176]{1,0:T(8,128)(2,1)}, u32[]{:S(2)}) %copy-start.8) | copy-done | bytes 835608
  77.7 3.0 %expert_back_keep.1 = f32[192,2048]{1,0:T(8,128)S(1)} custom-call(s32[2]{0:T(128)S(1)} %pad_add_fusion.at_ref, bf16[384,384]{1,0:T(8,128)(2,1)S(1)} %expert_hidden.1.own_ref, bf16[384,384]{1,0:T(8,128)(2,1)} %collective-permute-done.7.other_ref, bf16[192,2176]{1,0:T(8,128)(2,1)S(1)} %copy-done.5, bf16[192,2176]{1,0:T(8,128)(2,1)S(1)} %copy-done.8, ...), custom_call_target="tpu_custom_call" | custom-call | flops 603979776 | bytes 5308416 | tf_op jit(solution)/shard_map/expert_back_keep/pallas_call | solution.py:271
  80.8 1.3 %convert_add_fusion = f32[192,2048]{1,0:T(8,128)S(1)} fusion(f32[192,2048]{1,0:T(8,128)S(1)} %expert_back_keep.1, bf16[192,2048]{1,0:T(8,128)(2,1)} %collective-permute-done.8), kind=kLoop, calls=%fused_computation | loop fusion | flops 786432 | bytes 3932160 | tf_op jit(solution)/shard_map/add | solution.py:392
  82.1 1.3 %collective-permute-start.9 = (bf16[96,2048]{1,0:T(8,128)(2,1)S(1)}, bf16[96,2048]{1,0:T(8,128)(2,1)S(1)}, u32[]{:S(2)}, u32[]{:S(2)}) collective-permute-start(bf16[96,2048]{1,0:T(8,128)(2,1)S(1)} %slice.44), channel_id=1, source_target_pairs={{0,4},{1,3},{2,6},{3,1},{4,0},{5,7},{6,2},{7,5},{8,12},{9,11},{10,... | collective-permute-start | bytes 1179656 | tf_op jit(solution)/shard_map/ppermute | solution.py:299
  83.5 6.5 %collective-permute-done.9 = bf16[96,2048]{1,0:T(8,128)(2,1)S(1)} collective-permute-done((bf16[96,2048]{1,0:T(8,128)(2,1)S(1)}, bf16[96,2048]{1,0:T(8,128)(2,1)S(1)}, u32[]{:S(2)}, u32[]{:S(2)}) %collective-permute-start.9) | collective-permute-done | bytes 393248 | tf_op jit(solution)/shard_map/ppermute | solution.py:299
  90.1 2.0 %collective-permute-start.10 = (bf16[24,2048]{1,0:T(8,128)(2,1)S(1)}, bf16[24,2048]{1,0:T(8,128)(2,1)S(1)}, u32[]{:S(2)}, u32[]{:S(2)}) collective-permute-start(bf16[24,2048]{1,0:T(8,128)(2,1)S(1)} %get-tuple-element.24), channel_id=1, source_target_pairs={{0,8},{1,9},{2,10},{3,11},{4,12},{5,13},{6,14},{7,15},{8,16},{9,17... | collective-permute-start | bytes 294920 | tf_op jit(solution)/shard_map/ppermute | solution.py:299
  92.1 1.9 %collective-permute-start.12 = (bf16[24,2048]{1,0:T(8,128)(2,1)S(1)}, bf16[24,2048]{1,0:T(8,128)(2,1)S(1)}, u32[]{:S(2)}, u32[]{:S(2)}) collective-permute-start(bf16[24,2048]{1,0:T(8,128)(2,1)S(1)} %get-tuple-element.25), channel_id=1, source_target_pairs={{0,24},{1,25},{2,26},{3,27},{4,28},{5,29},{6,30},{7,31},{8,0},{9,1... | collective-permute-start | bytes 294920 | tf_op jit(solution)/shard_map/ppermute | solution.py:299
  94.0 2.7 %collective-permute-done.10 = bf16[24,2048]{1,0:T(8,128)(2,1)S(1)} collective-permute-done((bf16[24,2048]{1,0:T(8,128)(2,1)S(1)}, bf16[24,2048]{1,0:T(8,128)(2,1)S(1)}, u32[]{:S(2)}, u32[]{:S(2)}) %collective-permute-start.10) | collective-permute-done | bytes 98336 | tf_op jit(solution)/shard_map/ppermute | solution.py:299
  96.7 1.6 %collective-permute-done.12 = bf16[24,2048]{1,0:T(8,128)(2,1)S(1)} collective-permute-done((bf16[24,2048]{1,0:T(8,128)(2,1)S(1)}, bf16[24,2048]{1,0:T(8,128)(2,1)S(1)}, u32[]{:S(2)}, u32[]{:S(2)}) %collective-permute-start.12) | collective-permute-done | bytes 98336 | tf_op jit(solution)/shard_map/ppermute | solution.py:299
  98.3 2.0 %collective-permute-done.11 = bf16[24,2048]{1,0:T(8,128)(2,1)S(1)} collective-permute-done((bf16[24,2048]{1,0:T(8,128)(2,1)S(1)}, bf16[24,2048]{1,0:T(8,128)(2,1)S(1)}, u32[]{:S(2)}, u32[]{:S(2)}) %collective-permute-start.11) | collective-permute-done | bytes 98336 | tf_op jit(solution)/shard_map/ppermute | solution.py:299
  (48 shorter events, 7.2 us)
Async XLA Ops:
  2.4 17.7 %copy-start.13 = (bf16[24,2176]{1,0:T(8,128)(2,1)S(1)}, bf16[24,2176]{1,0:T(8,128)(2,1)}, u32[]{:S(2)}) copy-start(bf16[24,2176]{1,0:T(8,128)(2,1)} %pack_tokens.1) | copy-start | bytes 313348
  2.4 17.7 %collective-permute-start.2 = (bf16[24,2176]{1,0:T(8,128)(2,1)}, bf16[24,2176]{1,0:T(8,128)(2,1)S(1)}, u32[]{:S(2)}, u32[]{:S(2)}) collective-permute-start(bf16[24,2176]{1,0:T(8,128)(2,1)} %pack_tokens.1), channel_id=1, source_target_pairs={{0,8},{1,9},{2,10},{3,11},{4,12},{5,13},{6,14},{7,15},{8,16},{9,17... | collective-permute-start | bytes 313352 | tf_op jit(solution)/shard_map/ppermute | solution.py:299
  5.4 14.7 %collective-permute-start.1 = (bf16[24,2176]{1,0:T(8,128)(2,1)}, bf16[24,2176]{1,0:T(8,128)(2,1)S(1)}, u32[]{:S(2)}, u32[]{:S(2)}) collective-permute-start(bf16[24,2176]{1,0:T(8,128)(2,1)} %pack_tokens.1), channel_id=1, source_target_pairs={{0,16},{1,17},{2,18},{3,19},{4,20},{5,21},{6,22},{7,23},{8,24},{9,... | collective-permute-start | bytes 313352 | tf_op jit(solution)/shard_map/ppermute | solution.py:299
  8.0 12.1 %collective-permute-start = (bf16[24,2176]{1,0:T(8,128)(2,1)}, bf16[24,2176]{1,0:T(8,128)(2,1)S(1)}, u32[]{:S(2)}, u32[]{:S(2)}) collective-permute-start(bf16[24,2176]{1,0:T(8,128)(2,1)} %pack_tokens.1), channel_id=1, source_target_pairs={{0,24},{1,25},{2,26},{3,27},{4,28},{5,29},{6,30},{7,31},{8,0},{9,1... | collective-permute-start | bytes 313352 | tf_op jit(solution)/shard_map/ppermute | solution.py:299
  15.2 0.7 copy-start.12
  15.9 25.6 %copy-start.1 = (bf16[1,4096,384]{2,1,0:T(8,128)(2,1)S(1)}, bf16[1,4096,384]{2,1,0:T(8,128)(2,1)}, u32[]{:S(2)}) copy-start(bf16[1,4096,384]{2,1,0:T(8,128)(2,1)} %gate_ref.3) | copy-start | bytes 9437188
  20.0 0.8 copy-start.9
  20.8 8.0 %collective-permute-start.3 = (bf16[96,2176]{1,0:T(8,128)(2,1)S(1)}, bf16[96,2176]{1,0:T(8,128)(2,1)S(1)}, u32[]{:S(2)}, u32[]{:S(2)}) collective-permute-start(bf16[96,2176]{1,0:T(8,128)(2,1)S(1)} %pad_maximum_fusion), channel_id=1, source_target_pairs={{0,2},{1,5},{2,0},{3,7},{4,6},{5,1},{6,4},{7,3},{8,10},{9,13},{10,... | collective-permute-start | bytes 1253384 | tf_op jit(solution)/shard_map/ppermute | solution.py:299
  28.9 18.8 %copy-start.3 = (bf16[192,2176]{1,0:T(8,128)(2,1)}, bf16[192,2176]{1,0:T(8,128)(2,1)S(1)}, u32[]{:S(2)}) copy-start(bf16[192,2176]{1,0:T(8,128)(2,1)S(1)} %constant_dynamic-update-slice_fusion.sr_ref) | copy-start | bytes 2506756
  28.9 12.6 %collective-permute-start.5 = (bf16[192,2176]{1,0:T(8,128)(2,1)S(1)}, bf16[192,2176]{1,0:T(8,128)(2,1)S(1)}, u32[]{:S(2)}, u32[]{:S(2)}) collective-permute-start(bf16[192,2176]{1,0:T(8,128)(2,1)S(1)} %constant_dynamic-update-slice_fusion.sr_ref), channel_id=1, source_target_pairs={{0,4},{1,3},{2,6},{3,1},{4,0},{5,7},{6,2},{7,5},{8,12},{9,11},{10,... | collective-permute-start | bytes 2506760 | tf_op jit(solution)/shard_map/ppermute | solution.py:299
  30.5 17.2 %collective-permute-start.4 = (bf16[192,2176]{1,0:T(8,128)(2,1)S(1)}, bf16[192,2176]{1,0:T(8,128)(2,1)S(1)}, u32[]{:S(2)}, u32[]{:S(2)}) collective-permute-start(bf16[192,2176]{1,0:T(8,128)(2,1)S(1)} %constant_dynamic-update-slice_fusion.sr_ref), channel_id=1, source_target_pairs={{0,1},{1,0},{2,3},{3,2},{4,5},{5,4},{6,7},{7,6},{8,9},{9,8},{10,11... | collective-permute-start | bytes 2506760 | tf_op jit(solution)/shard_map/ppermute | solution.py:299
  41.5 6.2 %copy-start.6 = (bf16[192,2176]{1,0:T(8,128)(2,1)}, bf16[192,2176]{1,0:T(8,128)(2,1)S(1)}, u32[]{:S(2)}) copy-start(bf16[192,2176]{1,0:T(8,128)(2,1)S(1)} %collective-permute-done.5.r2_ref) | copy-start | bytes 2506756
  41.5 6.2 %collective-permute-start.6 = (bf16[192,2176]{1,0:T(8,128)(2,1)S(1)}, bf16[192,2176]{1,0:T(8,128)(2,1)S(1)}, u32[]{:S(2)}, u32[]{:S(2)}) collective-permute-start(bf16[192,2176]{1,0:T(8,128)(2,1)S(1)} %collective-permute-done.5.r2_ref), channel_id=1, source_target_pairs={{0,1},{1,0},{2,3},{3,2},{4,5},{5,4},{6,7},{7,6},{8,9},{9,8},{10,11... | collective-permute-start | bytes 2506760 | tf_op jit(solution)/shard_map/ppermute | solution.py:299
  41.5 2.2 %copy-start.2 = (bf16[1,4096,384]{2,1,0:T(8,128)(2,1)S(1)}, bf16[1,4096,384]{2,1,0:T(8,128)(2,1)}, u32[]{:S(2)}) copy-start(bf16[1,4096,384]{2,1,0:T(8,128)(2,1)} %up_ref.3) | copy-start | bytes 9437188
  47.7 8.8 %copy-start = (bf16[1,768,2048]{2,1,0:T(8,128)(2,1)S(1)}, bf16[1,768,2048]{2,1,0:T(8,128)(2,1)}, u32[]{:S(2)}) copy-start(bf16[1,768,2048]{2,1,0:T(8,128)(2,1)} %down_ref.3) | copy-start | bytes 9437188
  51.7 4.8 %collective-permute-start.7 = (bf16[384,384]{1,0:T(8,128)(2,1)S(1)}, bf16[384,384]{1,0:T(8,128)(2,1)}, u32[]{:S(2)}, u32[]{:S(2)}) collective-permute-start(bf16[384,384]{1,0:T(8,128)(2,1)S(1)} %expert_hidden.1.own_ref), channel_id=1, source_target_pairs={{0,1},{1,0},{2,3},{3,2},{4,5},{5,4},{6,7},{7,6},{8,9},{9,8},{10,11... | collective-permute-start | bytes 884744 | tf_op jit(solution)/shard_map/ppermute | solution.py:299
  52.0 19.7 %all-to-all-start = ((bf16[32,2,2,16,128]{4,3,2,1,0:T(8,128)(2,1)}), bf16[32,2,2,16,128]{4,3,2,1,0:T(8,128)(2,1)}, u32[]{:S(2)}, u32[]{:S(2)}) async-start(bf16[32,2,2,16,128]{4,3,2,1,0:T(8,128)(2,1)} %copy-done.9), calls=%async_computation | async-start | bytes 1048576 | tf_op jit(solution)/shard_map/all_to_all | solution.py:369
  56.5 1.2 %copy-start.4 = (bf16[192,2176]{1,0:T(8,128)(2,1)S(1)}, bf16[192,2176]{1,0:T(8,128)(2,1)}, u32[]{:S(2)}) copy-start(bf16[192,2176]{1,0:T(8,128)(2,1)} %copy-done.3) | copy-start | bytes 2506756
  57.7 1.1 %copy-start.7 = (bf16[192,2176]{1,0:T(8,128)(2,1)S(1)}, bf16[192,2176]{1,0:T(8,128)(2,1)}, u32[]{:S(2)}) copy-start(bf16[192,2176]{1,0:T(8,128)(2,1)} %copy-done.6) | copy-start | bytes 2506756
  62.7 18.0 %collective-permute-start.8 = (bf16[192,2048]{1,0:T(8,128)(2,1)}, bf16[192,2048]{1,0:T(8,128)(2,1)}, u32[]{:S(2)}, u32[]{:S(2)}) collective-permute-start(bf16[192,2048]{1,0:T(8,128)(2,1)} %expert_back_send.1), channel_id=1, source_target_pairs={{0,2},{1,5},{2,0},{3,7},{4,6},{5,1},{6,4},{7,3},{8,10},{9,13},{10,... | collective-permute-start | bytes 2359304 | tf_op jit(solution)/shard_map/ppermute | solution.py:299
  71.7 0.9 copy-start.10
  72.6 0.9 copy-start.11
  73.5 3.0 %copy-start.5 = (bf16[192,2176]{1,0:T(8,128)(2,1)S(1)}, bf16[192,2176]{1,0:T(8,128)(2,1)}, u32[]{:S(2)}) copy-start(bf16[192,2176]{1,0:T(8,128)(2,1)} %copy-done.3) | copy-start | bytes 2506756
  76.6 1.2 %copy-start.8 = (bf16[192,2176]{1,0:T(8,128)(2,1)S(1)}, bf16[192,2176]{1,0:T(8,128)(2,1)}, u32[]{:S(2)}) copy-start(bf16[192,2176]{1,0:T(8,128)(2,1)} %copy-done.6) | copy-start | bytes 2506756
  82.1 7.8 %collective-permute-start.9 = (bf16[96,2048]{1,0:T(8,128)(2,1)S(1)}, bf16[96,2048]{1,0:T(8,128)(2,1)S(1)}, u32[]{:S(2)}, u32[]{:S(2)}) collective-permute-start(bf16[96,2048]{1,0:T(8,128)(2,1)S(1)} %slice.44), channel_id=1, source_target_pairs={{0,4},{1,3},{2,6},{3,1},{4,0},{5,7},{6,2},{7,5},{8,12},{9,11},{10,... | collective-permute-start | bytes 1179656 | tf_op jit(solution)/shard_map/ppermute | solution.py:299
  90.1 6.6 %collective-permute-start.10 = (bf16[24,2048]{1,0:T(8,128)(2,1)S(1)}, bf16[24,2048]{1,0:T(8,128)(2,1)S(1)}, u32[]{:S(2)}, u32[]{:S(2)}) collective-permute-start(bf16[24,2048]{1,0:T(8,128)(2,1)S(1)} %get-tuple-element.24), channel_id=1, source_target_pairs={{0,8},{1,9},{2,10},{3,11},{4,12},{5,13},{6,14},{7,15},{8,16},{9,17... | collective-permute-start | bytes 294920 | tf_op jit(solution)/shard_map/ppermute | solution.py:299
  92.1 6.2 %collective-permute-start.12 = (bf16[24,2048]{1,0:T(8,128)(2,1)S(1)}, bf16[24,2048]{1,0:T(8,128)(2,1)S(1)}, u32[]{:S(2)}, u32[]{:S(2)}) collective-permute-start(bf16[24,2048]{1,0:T(8,128)(2,1)S(1)} %get-tuple-element.25), channel_id=1, source_target_pairs={{0,24},{1,25},{2,26},{3,27},{4,28},{5,29},{6,30},{7,31},{8,0},{9,1... | collective-permute-start | bytes 294920 | tf_op jit(solution)/shard_map/ppermute | solution.py:299
  94.0 6.4 %collective-permute-start.11 = (bf16[24,2048]{1,0:T(8,128)(2,1)S(1)}, bf16[24,2048]{1,0:T(8,128)(2,1)S(1)}, u32[]{:S(2)}, u32[]{:S(2)}) collective-permute-start(bf16[24,2048]{1,0:T(8,128)(2,1)S(1)} %get-tuple-element.26), channel_id=1, source_target_pairs={{0,16},{1,17},{2,18},{3,19},{4,20},{5,21},{6,22},{7,23},{8,24},{9,... | collective-permute-start | bytes 294920 | tf_op jit(solution)/shard_map/ppermute | solution.py:299

commit v4 on v3

--- a/solution.py
+++ b/solution.py
@@ -19,10 +19,6 @@
 
 def smem():
     return pl.BlockSpec(memory_space=pltpu.SMEM)
-
-
-def hbm():
-    return pl.BlockSpec(memory_space=pltpu.HBM)
 
 
 def page_kernel(pages, me_ref, owner_ref, kv_ref, send_ref, count_ref):
@@ -144,56 +140,40 @@
     out_ref[:, half:] = jnp.where(part < 3, chosen, 0.0).astype(out_ref.dtype)
 
 
-def weight_copies(half, core, gate_ref, up_ref, held, sems):
-    depth = half // sems.shape[1]
-    pairs = []
-    for c in range(sems.shape[1]):
-        rows = pl.ds(pl.multiple_of(core * half + c * depth, 128), depth)
-        pairs.append(
-            [
-                pltpu.make_async_copy(
-                    ref.at[0, rows], held.at[i, pl.ds(c * depth, depth)], sems.at[i, c]
-                )
-                for i, ref in enumerate((gate_ref, up_ref))
-            ]
-        )
-    for pair in pairs:
-        for copy in pair:
-            copy.start()
-    return pairs, depth
-
-
-def partial_kernel(core_ref, sr_ref, r2_ref, gate_ref, up_ref, gate_sum, up_sum, held, sems):
-    half = held.shape[1]
-    pairs, depth = weight_copies(half, core_ref[0], gate_ref, up_ref, held, sems)
-    for c, pair in enumerate(pairs):
+def partial_kernel(chunks, core_ref, sr_ref, r2_ref, gate_ref, up_ref, gate_sum, up_sum):
+    half = gate_ref.shape[1] // 2
+    depth = half // chunks
+    for c in range(chunks):
         at = slice(c * depth, (c + 1) * depth)
+        rows = pl.ds(pl.multiple_of(core_ref[0] * half + c * depth, 128), depth)
         x = jnp.concatenate([sr_ref[:, at], r2_ref[:, at]], axis=0)
-        for i, total in enumerate((gate_sum, up_sum)):
-            pair[i].wait()
-            part = jnp.dot(x, held[i, at], preferred_element_type=jnp.float32)
+        for weight, total in ((gate_ref, gate_sum), (up_ref, up_sum)):
+            part = jnp.dot(x, weight[0, rows], preferred_element_type=jnp.float32)
             total[...] = part if c == 0 else total[...] + part
 
 
 def hidden_kernel(
-    core_ref, sr_ref, r2_ref, gate_ref, up_ref, gate_part, up_part, out_ref, held, sems, sums
+    chunks, core_ref, sr_ref, r2_ref, gate_ref, up_ref, gate_part, up_part, out_ref, sums
 ):
-    half = held.shape[1]
+    half = gate_ref.shape[1] // 2
+    depth = half // chunks
     group = sr_ref.shape[0] // 2
-    pairs, depth = weight_copies(half, 1 - core_ref[0], gate_ref, up_ref, held, sems)
-    last = len(pairs) - 1
-    for c, pair in enumerate(pairs):
+    for c in range(chunks):
         at = slice(c * depth, (c + 1) * depth)
+        rows = pl.ds(pl.multiple_of((1 - core_ref[0]) * half + c * depth, 128), depth)
         x = jnp.concatenate(
             [sr_ref[:group, at], r2_ref[:group, at], sr_ref[group:, at], r2_ref[group:, at]],
             axis=0,
         )
-        for i, start in enumerate((gate_part, up_part)):
-            pair[i].wait()
-            part = jnp.dot(x, held[i, at], preferred_element_type=jnp.float32)
+        for i, (weight, start) in enumerate(((gate_ref, gate_part), (up_ref, up_part))):
+            part = jnp.dot(x, weight[0, rows], preferred_element_type=jnp.float32)
             sums[i] = (start[...] if c == 0 else sums[i]) + part
     gate = sums[0]
     out_ref[...] = (gate / (1.0 + jnp.exp(-gate)) * sums[1]).astype(out_ref.dtype)
+
+
+def room(*arrays):
+    return sum(math.prod(a.shape) * a.dtype.itemsize for a in arrays) * 9 // 8 + 4 * MIB
 
 
 def expert_front(core, rows, w_gate, w_up, parts):
@@ -201,14 +181,16 @@
     d, f = w_gate.shape[1:]
     last = parts is not None
     total = jax.ShapeDtypeStruct((tokens, f), jnp.float32)
-    scratch = [pltpu.VMEM((2, d // 2, f), jnp.bfloat16), pltpu.SemaphoreType.DMA((2, 4))]
+    scratch = [pltpu.VMEM((2, tokens, f), jnp.float32)] if last else []
     return pl.pallas_call(
-        hidden_kernel if last else partial_kernel,
-        in_specs=[smem(), vmem(), vmem(), hbm(), hbm()] + ([vmem(), vmem()] if last else []),
+        functools.partial(hidden_kernel if last else partial_kernel, 4),
+        in_specs=[smem()] + [vmem()] * (6 if last else 4),
         out_specs=vmem() if last else [vmem(), vmem()],
-        scratch_shapes=scratch + ([pltpu.VMEM((2, tokens, f), jnp.float32)] if last else []),
+        scratch_shapes=scratch,
         out_shape=jax.ShapeDtypeStruct((tokens, f), jnp.bfloat16) if last else [total, total],
-        compiler_params=pltpu.CompilerParams(vmem_limit_bytes=40 * MIB),
+        compiler_params=pltpu.CompilerParams(
+            vmem_limit_bytes=room(*rows, w_gate, w_up, *[total] * (5 if last else 2))
+        ),
         cost_estimate=pl.CostEstimate(
             flops=2 * tokens * d * f,
             bytes_accessed=tokens * d + 2 * d * f + 8 * tokens * f,
@@ -219,20 +201,9 @@
 
 
 def back_kernel(
-    send, experts, lanes, at_ref, own_ref, other_ref, sr_ref, r2_ref, down_ref, out_ref, held, sems
+    send, experts, lanes, chunks, at_ref, own_ref, other_ref, sr_ref, r2_ref, down_ref, out_ref
 ):
-    chunks = sems.shape[0]
-    block = held.shape[1] // chunks
-    copies = [
-        pltpu.make_async_copy(
-            down_ref.at[0, :, pl.ds(c * block, block)],
-            held.at[:, pl.ds(c * block, block)],
-            sems.at[c],
-        )
-        for c in range(chunks)
-    ]
-    for copy in copies:
-        copy.start()
+    block = down_ref.shape[2] // chunks
     f = own_ref.shape[1]
     group = sr_ref.shape[0] // 2
     core = at_ref[1]
@@ -256,11 +227,12 @@
     lane = lax.broadcasted_iota(jnp.int32, probs.shape, 1)
     mine = lane % experts == at_ref[0]
     weight = jnp.sum(jnp.where(mine, probs, 0.0), axis=1, keepdims=True)
-    for c, copy in enumerate(copies):
+    for c in range(chunks):
         at = slice(c * block, (c + 1) * block)
-        copy.wait()
-        total = jnp.dot(own, held[pl.ds(begin, f), at], preferred_element_type=jnp.float32)
-        total += jnp.dot(other, held[pl.ds(rest, f), at], preferred_element_type=jnp.float32)
+        total = jnp.dot(own, down_ref[0, pl.ds(begin, f), at], preferred_element_type=jnp.float32)
+        total += jnp.dot(
+            other, down_ref[0, pl.ds(rest, f), at], preferred_element_type=jnp.float32
+        )
         out_ref[:, at] = (total * weight).astype(out_ref.dtype)
 
 
@@ -268,16 +240,15 @@
     tokens, f = own.shape
     group2 = sr.shape[0]
     width = w_down.shape[2]
+    out = jax.ShapeDtypeStruct((group2, width), jnp.bfloat16 if send else jnp.float32)
     return pl.pallas_call(
-        functools.partial(back_kernel, send, experts, lanes),
-        out_shape=jax.ShapeDtypeStruct((group2, width), jnp.bfloat16 if send else jnp.float32),
-        in_specs=[smem()] + [vmem()] * 4 + [hbm()],
+        functools.partial(back_kernel, send, experts, lanes, 4),
+        out_shape=out,
+        in_specs=[smem()] + [vmem()] * 5,
         out_specs=vmem(),
-        scratch_shapes=[
-            pltpu.VMEM(w_down.shape[1:], jnp.bfloat16),
-            pltpu.SemaphoreType.DMA((4,)),
-        ],
-        compiler_params=pltpu.CompilerParams(vmem_limit_bytes=40 * MIB),
+        compiler_params=pltpu.CompilerParams(
+            vmem_limit_bytes=room(own, other, w_down, sr, r2, out, out)
+        ),
         cost_estimate=pl.CostEstimate(
             flops=2 * tokens * f * width,
             bytes_accessed=2 * (2 * tokens * f + 2 * f * width + 2 * group2 * width),
@@ -355,7 +326,7 @@
         in_specs=[smem(), smem(), vmem()],
         out_specs=vmem(),
         scratch_shapes=[pltpu.SMEM((owners,), jnp.int32)],
-        compiler_params=pltpu.CompilerParams(vmem_limit_bytes=40 * MIB),
+        compiler_params=pltpu.CompilerParams(vmem_limit_bytes=room(prompt_kv) * 4),
         name="quantize_pages",
     )(me_ref, page_owner.reshape(-1), prompt_kv.transpose(0, 1, 3, 2, 4))
     line = [mine] + [moves.along_z(mine, -shift) for shift in range(1, moves.lines)]
@@ -363,10 +334,12 @@
     fresh = new_kv.transpose(2, 3, 0, 1, 4).reshape(2, heads, tokens, width)
     fresh = jnp.pad(fresh, ((0, 0), (0, 0), (0, 128 - tokens), (0, 0)))
     tables = [t.reshape(owners, pages) for t in (page_owner, page_slot, page_fill)]
-    line, send, fresh, tables = lax.optimization_barrier((line, send, fresh, tables))
+    line, send = lax.optimization_barrier((line, send))
     sr = jnp.concatenate([line, moves.flip(line, 0)], axis=0)
+    sr, fresh, tables = lax.optimization_barrier((sr, fresh, tables))
     r2 = moves.flip(sr, 1)
     cache = lax.all_to_all(send, "ep", split_axis=0, concat_axis=0, tiled=True)
+    r2, cache = lax.optimization_barrier((r2, cache))
     other_sr, other_r2 = moves.cores(sr), moves.cores(r2)
 
     parts = expert_front(own_core, (sr, r2), w_gate, w_up, None)
@@ -379,7 +352,7 @@
         out_shape=jax.ShapeDtypeStruct(queries.shape, jnp.bfloat16),
         in_specs=[smem()] + [vmem()] * 6,
         out_specs=vmem(),
-        compiler_params=pltpu.CompilerParams(vmem_limit_bytes=48 * MIB),
+        compiler_params=pltpu.CompilerParams(vmem_limit_bytes=8 * MIB + 16 * slots * page_len * tokens * q_heads),
         name="attention",
     )(
         me_ref,

time: 102 us -> 85.9 us (0.84)
  Pallas kernels: 23.8 us -> 15.3 us
  local copies, waits for them, and re-layouts: 13.5 us -> 6.38 us
  starting transfers between devices: 21.6 us -> 23.3 us
    pallas_call x4, Pallas kernels: 14.9 us -> 6.68 us  [the longest x2 3.61 us: expert_front(): pl.pallas_call(functools.partial(hidden_kernel if last else partial_kerne...]
    ppermute x13, waiting for transfers between devices: 30.4 us -> 24.8 us  [go(): return lax.ppermute(x, ('ep', 'pd'), perm)]
    all_to_all x1, waiting for transfers between devices: 7.33 us -> 12.1 us  [body(): cache = lax.all_to_all(send, 'ep', split_axis=0, concat_axis=0, tiled=True)]
    unnamed x31 -> x22, local copies, waits for them, and re-layouts: 10.4 us -> 6.05 us
    reshape x3, local copies, waits for them, and re-layouts: 1.6 us -> 0.23 us  [body(): t.reshape(owners, pages)]
    add x1, other arithmetic: 1.31 us -> 0.17 us  [body(): kept = kept + moves.flip(sent, 0).astype(jnp.float32)]
    pallas_call x1, Pallas kernels: 3.04 us -> 1.93 us  [body(): pl.pallas_call(functools.partial(attention_kernel, pages), out_shape=jax....]
  transfers between devices with their start and end apart: 14 -> 14, of which waited for: 7 -> 7; matrix products, arithmetic and copies ran while one was open for 6% -> 3% of each run, Pallas kernels for 18% -> 12%
where the time goes in v4:
time: 85.9 us; the launch traced here: 85.4 us
  waiting for transfers between devices  36.9 us (43%)
  starting transfers between devices  23.3 us (27%)
  Pallas kernels  15.3 us (18%)
  local copies, waits for them, and re-layouts  6.38 us (7%)
  other arithmetic  2.73 us (3%)
    ppermute x13, waiting for transfers between devices, go(): return lax.ppermute(x, ('ep', 'pd'), perm)  24.8 us
    ppermute x13, starting transfers between devices, go(): return lax.ppermute(x, ('ep', 'pd'), perm)  18.1 us
    all_to_all x1, waiting for transfers between devices, body(): cache = lax.all_to_all(send, 'ep', split_axis=0, concat_axis=0, tiled=True)  12.1 us
    unnamed x22, local copies, waits for them, and re-layouts  6.05 us
    all_to_all x1, starting transfers between devices, body(): cache = lax.all_to_all(send, 'ep', split_axis=0, concat_axis=0, tiled=True)  5.29 us
    pallas_call x1, Pallas kernels, body(): pl.pallas_call(functools.partial(page_kernel, pages), out_shape=jax.Shape...  4.93 us
    pallas_call x2, Pallas kernels, expert_front(): pl.pallas_call(functools.partial(hidden_kernel if last else partial_kerne...  3.61 us
    pallas_call x2, Pallas kernels, expert_back(): pl.pallas_call(functools.partial(back_kernel, send, experts, lanes, 4), o...  3.07 us
  transfers between devices with their start and end apart: 14, of which 7 were waited for; matrix products, arithmetic and copies ran while one was open for 3% of the time, Pallas kernels for 12%

profile of v4, /device:TPU:0, one launch (start us, length us, event | category | flops | bytes accessed | tf_op | source)
XLA Modules:
  0.0 85.4 jit_solution(8106862029158836524)
XLA Ops:
  0.7 1.7 %pack_tokens.1 = bf16[24,2176]{1,0:T(8,128)(2,1)} custom-call(s32[1]{0:T(128)} %bitcast.1.core_ref, bf16[24,4096]{1,0:T(8,128)(2,1)} %bitcast.23, s32[24,8]{1,0:T(8,128)} %bitcast.25, f32[24,8]{1,0:T(8,128)} %bitcast.26), custom_call_target="tpu_custom_call" | custom-call | tf_op jit(solution)/shard_map/pack_tokens/pallas_call | solution.py:311
  2.4 3.0 %collective-permute-start.2 = (bf16[24,2176]{1,0:T(8,128)(2,1)}, bf16[24,2176]{1,0:T(8,128)(2,1)S(1)}, u32[]{:S(2)}, u32[]{:S(2)}) collective-permute-start(bf16[24,2176]{1,0:T(8,128)(2,1)} %pack_tokens.1), channel_id=1, source_target_pairs={{0,8},{1,9},{2,10},{3,11},{4,12},{5,13},{6,14},{7,15},{8,16},{9,17... | collective-permute-start | bytes 313352 | tf_op jit(solution)/shard_map/ppermute | solution.py:270
  5.4 2.6 %collective-permute-start.1 = (bf16[24,2176]{1,0:T(8,128)(2,1)}, bf16[24,2176]{1,0:T(8,128)(2,1)S(1)}, u32[]{:S(2)}, u32[]{:S(2)}) collective-permute-start(bf16[24,2176]{1,0:T(8,128)(2,1)} %pack_tokens.1), channel_id=1, source_target_pairs={{0,16},{1,17},{2,18},{3,19},{4,20},{5,21},{6,22},{7,23},{8,24},{9,... | collective-permute-start | bytes 313352 | tf_op jit(solution)/shard_map/ppermute | solution.py:270
  8.0 1.3 %collective-permute-start = (bf16[24,2176]{1,0:T(8,128)(2,1)}, bf16[24,2176]{1,0:T(8,128)(2,1)S(1)}, u32[]{:S(2)}, u32[]{:S(2)}) collective-permute-start(bf16[24,2176]{1,0:T(8,128)(2,1)} %pack_tokens.1), channel_id=1, source_target_pairs={{0,24},{1,25},{2,26},{3,27},{4,28},{5,29},{6,30},{7,31},{8,0},{9,1... | collective-permute-start | bytes 313352 | tf_op jit(solution)/shard_map/ppermute | solution.py:270
  9.4 1.0 %copy.22 = bf16[16,2,16,2,128]{4,2,3,1,0:T(8,128)(2,1)S(1)} copy(bf16[16,2,16,2,128]{4,3,2,1,0:T(2,128)(2,1)} %param.12) | data formatting | bytes 524288 | tf_op args[0]
  10.4 0.7 copy-done.5
  11.1 4.9 %quantize_pages.1 = bf16[32,2,2,16,128]{4,3,2,1,0:T(8,128)(2,1)} custom-call(s32[1]{0:T(128)} %bitcast.me_ref, s32[256]{0:T(256)S(1)} %bitcast.22, bf16[16,2,2,16,128]{4,3,2,1,0:T(8,128)(2,1)S(1)} %bitcast.21), custom_call_target="tpu_custom_call" | custom-call | tf_op jit(solution)/shard_map/quantize_pages/pallas_call | solution.py:323
  16.0 0.9 %pad_maximum_fusion.1 = bf16[96,2176]{1,0:T(8,128)(2,1)S(1)} fusion(bf16[24,2176]{1,0:T(8,128)(2,1)S(1)} %collective-permute-done.2, bf16[24,2176]{1,0:T(8,128)(2,1)S(1)} %collective-permute-done.1, bf16[24,2176]{1,0:T(8,128)(2,1)S(1)} %collective-permute-done, bf16[24,2176]{1,0:T(8,128)(2,1)} %pack_tokens.1), kind=kLoop, calls=%fused_computation.4 | loop fusion | flops 1671168 | bytes 835584 | tf_op jit(solution)/shard_map/concatenate | solution.py:333
  16.9 1.6 %collective-permute-start.3 = (bf16[96,2176]{1,0:T(8,128)(2,1)S(1)}, bf16[96,2176]{1,0:T(8,128)(2,1)S(1)}, u32[]{:S(2)}, u32[]{:S(2)}) collective-permute-start(bf16[96,2176]{1,0:T(8,128)(2,1)S(1)} %pad_maximum_fusion.1), channel_id=1, source_target_pairs={{0,2},{1,5},{2,0},{3,7},{4,6},{5,1},{6,4},{7,3},{8,10},{9,13},{10,... | collective-permute-start | bytes 1253384 | tf_op jit(solution)/shard_map/ppermute | solution.py:270
  19.0 0.7 reduce.3
  20.0 5.3 %all-to-all-start = ((bf16[32,2,2,16,128]{4,3,2,1,0:T(8,128)(2,1)}), bf16[32,2,2,16,128]{4,3,2,1,0:T(8,128)(2,1)S(1)}, u32[]{:S(2)}, u32[]{:S(2)}) async-start(bf16[32,2,2,16,128]{4,3,2,1,0:T(8,128)(2,1)} %quantize_pages.1), calls=%async_computation | async-start | bytes 1048576 | tf_op jit(solution)/shard_map/all_to_all | solution.py:341
  25.4 2.0 %collective-permute-start.5 = (bf16[192,2176]{1,0:T(8,128)(2,1)S(1)}, bf16[192,2176]{1,0:T(8,128)(2,1)S(1)}, u32[]{:S(2)}, u32[]{:S(2)}) collective-permute-start(bf16[192,2176]{1,0:T(8,128)(2,1)S(1)} %pad_maximum_fusion.sr_ref), channel_id=1, source_target_pairs={{0,4},{1,3},{2,6},{3,1},{4,0},{5,7},{6,2},{7,5},{8,12},{9,11},{10,... | collective-permute-start | bytes 2506760 | tf_op jit(solution)/shard_map/ppermute | solution.py:270
  27.3 12.1 %all-to-all-done.cache_ref = bf16[32,2,2,16,128]{4,3,2,1,0:T(8,128)(2,1)S(1)} async-done(((bf16[32,2,2,16,128]{4,3,2,1,0:T(8,128)(2,1)}), bf16[32,2,2,16,128]{4,3,2,1,0:T(8,128)(2,1)S(1)}, u32[]{:S(2)}, u32[]{:S(2)}) %all-to-all-start) | async-done | bytes 524320 | tf_op jit(solution)/shard_map/all_to_all | solution.py:341
  39.5 2.6 %collective-permute-done.5.r2_ref = bf16[192,2176]{1,0:T(8,128)(2,1)S(1)} collective-permute-done((bf16[192,2176]{1,0:T(8,128)(2,1)S(1)}, bf16[192,2176]{1,0:T(8,128)(2,1)S(1)}, u32[]{:S(2)}, u32[]{:S(2)}) %collective-permute-start.5) | collective-permute-done | bytes 835616 | tf_op jit(solution)/shard_map/ppermute | solution.py:270
  42.1 1.9 %copy-done.1 = bf16[1,4096,384]{2,1,0:T(8,128)(2,1)S(1)} copy-done((bf16[1,4096,384]{2,1,0:T(8,128)(2,1)S(1)}, bf16[1,4096,384]{2,1,0:T(8,128)(2,1)}, u32[]{:S(2)}) %copy-start.1) | copy-done | bytes 3145752
  44.0 1.9 %copy-done.3 = bf16[1,4096,384]{2,1,0:T(8,128)(2,1)S(1)} copy-done((bf16[1,4096,384]{2,1,0:T(8,128)(2,1)S(1)}, bf16[1,4096,384]{2,1,0:T(8,128)(2,1)}, u32[]{:S(2)}) %copy-start.3) | copy-done | bytes 3145752
  45.9 1.8 %expert_partial.1 = (f32[384,384]{1,0:T(8,128)S(1)}, f32[384,384]{1,0:T(8,128)S(1)}) custom-call(s32[1]{0:T(128)} %bitcast.1.core_ref, bf16[192,2176]{1,0:T(8,128)(2,1)S(1)} %pad_maximum_fusion.sr_ref, bf16[192,2176]{1,0:T(8,128)(2,1)S(1)} %collective-permute-done.5.r2_ref, bf16[1,4096,384]{2,1,0:T(8,128)(2,1)S(1)} %copy-done.1, ...), custom_call_target="tpu_custom_call" | custom-call | flops 1207959552 | bytes 5898240 | tf_op jit(solution)/shard_map/expert_partial/pallas_call | solution.py:185
  47.8 1.8 %expert_hidden.1.own_ref = bf16[384,384]{1,0:T(8,128)(2,1)S(1)} custom-call(s32[1]{0:T(128)} %bitcast.1.core_ref, bf16[192,2176]{1,0:T(8,128)(2,1)S(1)} %collective-permute-done.4.sr_ref, bf16[192,2176]{1,0:T(8,128)(2,1)S(1)} %collective-permute-done.6.r2_ref, bf16[1,4096,384]{2,1,0:T(8,128)(2,1)S(1)} %copy-done.2, bf16[1,4096,384]{2,1,0:T(8,128)(2,1)S(1)} %copy-done.3, ...), custom_call_target="tpu_custom_call" | custom-call | flops 1207959552 | bytes 5898240 | tf_op jit(solution)/shard_map/expert_hidden/pallas_call | solution.py:185
  50.3 1.1 %collective-permute-done.7.other_ref = bf16[384,384]{1,0:T(8,128)(2,1)S(1)} collective-permute-done((bf16[384,384]{1,0:T(8,128)(2,1)S(1)}, bf16[384,384]{1,0:T(8,128)(2,1)S(1)}, u32[]{:S(2)}, u32[]{:S(2)}) %collective-permute-start.7) | collective-permute-done | bytes 294944 | tf_op jit(solution)/shard_map/ppermute | solution.py:270
  51.4 1.5 %expert_back_send.1 = bf16[192,2048]{1,0:T(8,128)(2,1)S(1)} custom-call(s32[2]{0:T(128)S(1)} %pad_add_fusion.at_ref, bf16[384,384]{1,0:T(8,128)(2,1)S(1)} %expert_hidden.1.own_ref, bf16[384,384]{1,0:T(8,128)(2,1)S(1)} %collective-permute-done.7.other_ref, bf16[192,2176]{1,0:T(8,128)(2,1)S(1)} %pad_maximum_fusion.sr_ref, ...), custom_call_target="tpu_custom_call" | custom-call | flops 603979776 | bytes 5308416 | tf_op jit(solution)/shard_map/expert_back_send/pallas_call | solution.py:244
  52.9 1.3 %collective-permute-start.8 = (bf16[192,2048]{1,0:T(8,128)(2,1)S(1)}, bf16[192,2048]{1,0:T(8,128)(2,1)S(1)}, u32[]{:S(2)}, u32[]{:S(2)}) collective-permute-start(bf16[192,2048]{1,0:T(8,128)(2,1)S(1)} %expert_back_send.1), channel_id=1, source_target_pairs={{0,2},{1,5},{2,0},{3,7},{4,6},{5,1},{6,4},{7,3},{8,10},{9,13},{10,... | collective-permute-start | bytes 2359304 | tf_op jit(solution)/shard_map/ppermute | solution.py:270
  54.3 1.9 %attention.1 = bf16[8,3,32,128]{3,2,1,0:T(8,128)(2,1)} custom-call(s32[1]{0:T(128)} %bitcast.me_ref, s32[16,16]{1,0:T(8,128)S(1)} %reshape.38.owner_ref, s32[16,16]{1,0:T(8,128)S(1)} %reshape.39.slot_ref, s32[16,16]{1,0:T(8,128)S(1)} %reshape.40.fill_ref, bf16[8,3,32,128]{3,2,1,0:T(8,128)(2,1)S(1)} %copy-done.4, ...), custom_call_target="tpu_custom_call" | custom-call | tf_op jit(solution)/shard_map/attention/pallas_call | solution.py:350
  56.2 1.5 %expert_back_keep.1 = f32[192,2048]{1,0:T(8,128)S(1)} custom-call(s32[2]{0:T(128)S(1)} %pad_add_fusion.at_ref, bf16[384,384]{1,0:T(8,128)(2,1)S(1)} %expert_hidden.1.own_ref, bf16[384,384]{1,0:T(8,128)(2,1)S(1)} %collective-permute-done.7.other_ref, bf16[192,2176]{1,0:T(8,128)(2,1)S(1)} %pad_maximum_fusion.sr_ref, ...), custom_call_target="tpu_custom_call" | custom-call | flops 603979776 | bytes 5308416 | tf_op jit(solution)/shard_map/expert_back_keep/pallas_call | solution.py:244
  57.7 7.3 %collective-permute-done.8 = bf16[192,2048]{1,0:T(8,128)(2,1)S(1)} collective-permute-done((bf16[192,2048]{1,0:T(8,128)(2,1)S(1)}, bf16[192,2048]{1,0:T(8,128)(2,1)S(1)}, u32[]{:S(2)}, u32[]{:S(2)}) %collective-permute-start.8) | collective-permute-done | bytes 786464 | tf_op jit(solution)/shard_map/ppermute | solution.py:270
  65.2 1.1 %collective-permute-start.9 = (bf16[96,2048]{1,0:T(8,128)(2,1)S(1)}, bf16[96,2048]{1,0:T(8,128)(2,1)S(1)}, u32[]{:S(2)}, u32[]{:S(2)}) collective-permute-start(bf16[96,2048]{1,0:T(8,128)(2,1)S(1)} %slice.44), channel_id=1, source_target_pairs={{0,4},{1,3},{2,6},{3,1},{4,0},{5,7},{6,2},{7,5},{8,12},{9,11},{10,... | collective-permute-start | bytes 1179656 | tf_op jit(solution)/shard_map/ppermute | solution.py:270
  66.3 6.8 %collective-permute-done.9 = bf16[96,2048]{1,0:T(8,128)(2,1)S(1)} collective-permute-done((bf16[96,2048]{1,0:T(8,128)(2,1)S(1)}, bf16[96,2048]{1,0:T(8,128)(2,1)S(1)}, u32[]{:S(2)}, u32[]{:S(2)}) %collective-permute-start.9) | collective-permute-done | bytes 393248 | tf_op jit(solution)/shard_map/ppermute | solution.py:270
  73.2 1.6 %collective-permute-start.10 = (bf16[24,2048]{1,0:T(8,128)(2,1)S(1)}, bf16[24,2048]{1,0:T(8,128)(2,1)S(1)}, u32[]{:S(2)}, u32[]{:S(2)}) collective-permute-start(bf16[24,2048]{1,0:T(8,128)(2,1)S(1)} %get-tuple-element.30), channel_id=1, source_target_pairs={{0,8},{1,9},{2,10},{3,11},{4,12},{5,13},{6,14},{7,15},{8,16},{9,17... | collective-permute-start | bytes 294920 | tf_op jit(solution)/shard_map/ppermute | solution.py:270
  74.9 2.2 %collective-permute-start.12 = (bf16[24,2048]{1,0:T(8,128)(2,1)S(1)}, bf16[24,2048]{1,0:T(8,128)(2,1)S(1)}, u32[]{:S(2)}, u32[]{:S(2)}) collective-permute-start(bf16[24,2048]{1,0:T(8,128)(2,1)S(1)} %get-tuple-element.31), channel_id=1, source_target_pairs={{0,24},{1,25},{2,26},{3,27},{4,28},{5,29},{6,30},{7,31},{8,0},{9,1... | collective-permute-start | bytes 294920 | tf_op jit(solution)/shard_map/ppermute | solution.py:270
  77.1 0.7 collective-permute-start.11
  77.8 2.8 %collective-permute-done.10 = bf16[24,2048]{1,0:T(8,128)(2,1)S(1)} collective-permute-done((bf16[24,2048]{1,0:T(8,128)(2,1)S(1)}, bf16[24,2048]{1,0:T(8,128)(2,1)S(1)}, u32[]{:S(2)}, u32[]{:S(2)}) %collective-permute-start.10) | collective-permute-done | bytes 98336 | tf_op jit(solution)/shard_map/ppermute | solution.py:270
  80.6 4.1 %collective-permute-done.11 = bf16[24,2048]{1,0:T(8,128)(2,1)S(1)} collective-permute-done((bf16[24,2048]{1,0:T(8,128)(2,1)S(1)}, bf16[24,2048]{1,0:T(8,128)(2,1)S(1)}, u32[]{:S(2)}, u32[]{:S(2)}) %collective-permute-start.11) | collective-permute-done | bytes 98336 | tf_op jit(solution)/shard_map/ppermute | solution.py:270
  84.8 0.7 fusion.3
  (39 shorter events, 2.0 us)
Async XLA Ops:
  0.6 18.4 %copy-start.6 = (s32[256,1]{0,1:T(1,128)S(1)}, s32[256,1]{0,1:T(1,128)}, u32[]{:S(2)}) copy-start(s32[256,1]{0,1:T(1,128)} %param.13) | copy-start | bytes 3076
  0.6 19.1 %copy-start.8 = (s32[256]{0:T(256)S(1)}, s32[256]{0:T(256)}, u32[]{:S(2)}) copy-start(s32[256]{0:T(256)} %param.14) | copy-start | bytes 3076
  0.7 19.2 %copy-start.9 = (s32[256]{0:T(256)S(1)}, s32[256]{0:T(256)}, u32[]{:S(2)}) copy-start(s32[256]{0:T(256)} %param.15) | copy-start | bytes 3076
  0.7 19.3 %copy-start.7 = (bf16[8,3,2,2,128]{4,3,2,1,0:T(2,128)(2,1)S(1)}, bf16[8,3,2,2,128]{4,3,2,1,0:T(2,128)(2,1)}, u32[]{:S(2)}) copy-start(bf16[8,3,2,2,128]{4,3,2,1,0:T(2,128)(2,1)} %param.17) | copy-start | bytes 73732
  2.4 13.6 %collective-permute-start.2 = (bf16[24,2176]{1,0:T(8,128)(2,1)}, bf16[24,2176]{1,0:T(8,128)(2,1)S(1)}, u32[]{:S(2)}, u32[]{:S(2)}) collective-permute-start(bf16[24,2176]{1,0:T(8,128)(2,1)} %pack_tokens.1), channel_id=1, source_target_pairs={{0,8},{1,9},{2,10},{3,11},{4,12},{5,13},{6,14},{7,15},{8,16},{9,17... | collective-permute-start | bytes 313352 | tf_op jit(solution)/shard_map/ppermute | solution.py:270
  5.4 10.6 %collective-permute-start.1 = (bf16[24,2176]{1,0:T(8,128)(2,1)}, bf16[24,2176]{1,0:T(8,128)(2,1)S(1)}, u32[]{:S(2)}, u32[]{:S(2)}) collective-permute-start(bf16[24,2176]{1,0:T(8,128)(2,1)} %pack_tokens.1), channel_id=1, source_target_pairs={{0,16},{1,17},{2,18},{3,19},{4,20},{5,21},{6,22},{7,23},{8,24},{9,... | collective-permute-start | bytes 313352 | tf_op jit(solution)/shard_map/ppermute | solution.py:270
  8.0 8.0 %collective-permute-start = (bf16[24,2176]{1,0:T(8,128)(2,1)}, bf16[24,2176]{1,0:T(8,128)(2,1)S(1)}, u32[]{:S(2)}, u32[]{:S(2)}) collective-permute-start(bf16[24,2176]{1,0:T(8,128)(2,1)} %pack_tokens.1), channel_id=1, source_target_pairs={{0,24},{1,25},{2,26},{3,27},{4,28},{5,29},{6,30},{7,31},{8,0},{9,1... | collective-permute-start | bytes 313352 | tf_op jit(solution)/shard_map/ppermute | solution.py:270
  10.4 0.7 copy-start.5
  16.9 8.3 %collective-permute-start.3 = (bf16[96,2176]{1,0:T(8,128)(2,1)S(1)}, bf16[96,2176]{1,0:T(8,128)(2,1)S(1)}, u32[]{:S(2)}, u32[]{:S(2)}) collective-permute-start(bf16[96,2176]{1,0:T(8,128)(2,1)S(1)} %pad_maximum_fusion.1), channel_id=1, source_target_pairs={{0,2},{1,5},{2,0},{3,7},{4,6},{5,1},{6,4},{7,3},{8,10},{9,13},{10,... | collective-permute-start | bytes 1253384 | tf_op jit(solution)/shard_map/ppermute | solution.py:270
  20.0 19.5 %all-to-all-start = ((bf16[32,2,2,16,128]{4,3,2,1,0:T(8,128)(2,1)}), bf16[32,2,2,16,128]{4,3,2,1,0:T(8,128)(2,1)S(1)}, u32[]{:S(2)}, u32[]{:S(2)}) async-start(bf16[32,2,2,16,128]{4,3,2,1,0:T(8,128)(2,1)} %quantize_pages.1), calls=%async_computation | async-start | bytes 1048576 | tf_op jit(solution)/shard_map/all_to_all | solution.py:341
  25.4 16.7 %collective-permute-start.5 = (bf16[192,2176]{1,0:T(8,128)(2,1)S(1)}, bf16[192,2176]{1,0:T(8,128)(2,1)S(1)}, u32[]{:S(2)}, u32[]{:S(2)}) collective-permute-start(bf16[192,2176]{1,0:T(8,128)(2,1)S(1)} %pad_maximum_fusion.sr_ref), channel_id=1, source_target_pairs={{0,4},{1,3},{2,6},{3,1},{4,0},{5,7},{6,2},{7,5},{8,12},{9,11},{10,... | collective-permute-start | bytes 2506760 | tf_op jit(solution)/shard_map/ppermute | solution.py:270
  27.3 20.3 %collective-permute-start.4 = (bf16[192,2176]{1,0:T(8,128)(2,1)S(1)}, bf16[192,2176]{1,0:T(8,128)(2,1)S(1)}, u32[]{:S(2)}, u32[]{:S(2)}) collective-permute-start(bf16[192,2176]{1,0:T(8,128)(2,1)S(1)} %pad_maximum_fusion.sr_ref), channel_id=1, source_target_pairs={{0,1},{1,0},{2,3},{3,2},{4,5},{5,4},{6,7},{7,6},{8,9},{9,8},{10,11... | collective-permute-start | bytes 2506760 | tf_op jit(solution)/shard_map/ppermute | solution.py:270
  42.1 5.6 %collective-permute-start.6 = (bf16[192,2176]{1,0:T(8,128)(2,1)S(1)}, bf16[192,2176]{1,0:T(8,128)(2,1)S(1)}, u32[]{:S(2)}, u32[]{:S(2)}) collective-permute-start(bf16[192,2176]{1,0:T(8,128)(2,1)S(1)} %collective-permute-done.5.r2_ref), channel_id=1, source_target_pairs={{0,1},{1,0},{2,3},{3,2},{4,5},{5,4},{6,7},{7,6},{8,9},{9,8},{10,11... | collective-permute-start | bytes 2506760 | tf_op jit(solution)/shard_map/ppermute | solution.py:270
  42.1 1.9 %copy-start.1 = (bf16[1,4096,384]{2,1,0:T(8,128)(2,1)S(1)}, bf16[1,4096,384]{2,1,0:T(8,128)(2,1)}, u32[]{:S(2)}) copy-start(bf16[1,4096,384]{2,1,0:T(8,128)(2,1)} %gate_ref.3) | copy-start | bytes 9437188
  44.0 1.9 %copy-start.3 = (bf16[1,4096,384]{2,1,0:T(8,128)(2,1)S(1)}, bf16[1,4096,384]{2,1,0:T(8,128)(2,1)}, u32[]{:S(2)}) copy-start(bf16[1,4096,384]{2,1,0:T(8,128)(2,1)} %up_ref.3) | copy-start | bytes 9437188
  45.9 1.9 %copy-start.2 = (bf16[1,4096,384]{2,1,0:T(8,128)(2,1)S(1)}, bf16[1,4096,384]{2,1,0:T(8,128)(2,1)}, u32[]{:S(2)}) copy-start(bf16[1,4096,384]{2,1,0:T(8,128)(2,1)} %gate_ref.3) | copy-start | bytes 9437188
  47.8 3.6 %copy-start = (bf16[1,768,2048]{2,1,0:T(8,128)(2,1)S(1)}, bf16[1,768,2048]{2,1,0:T(8,128)(2,1)}, u32[]{:S(2)}) copy-start(bf16[1,768,2048]{2,1,0:T(8,128)(2,1)} %down_ref.3) | copy-start | bytes 9437188
  49.6 1.8 %collective-permute-start.7 = (bf16[384,384]{1,0:T(8,128)(2,1)S(1)}, bf16[384,384]{1,0:T(8,128)(2,1)S(1)}, u32[]{:S(2)}, u32[]{:S(2)}) collective-permute-start(bf16[384,384]{1,0:T(8,128)(2,1)S(1)} %expert_hidden.1.own_ref), channel_id=1, source_target_pairs={{0,1},{1,0},{2,3},{3,2},{4,5},{5,4},{6,7},{7,6},{8,9},{9,8},{10,11... | collective-permute-start | bytes 884744 | tf_op jit(solution)/shard_map/ppermute | solution.py:270
  50.3 4.0 %copy-start.4 = (bf16[8,3,32,128]{3,2,1,0:T(8,128)(2,1)S(1)}, bf16[8,3,32,128]{3,2,1,0:T(8,128)(2,1)}, u32[]{:S(2)}) copy-start(bf16[8,3,32,128]{3,2,1,0:T(8,128)(2,1)} %q_ref.1) | copy-start | bytes 589828
  52.9 12.1 %collective-permute-start.8 = (bf16[192,2048]{1,0:T(8,128)(2,1)S(1)}, bf16[192,2048]{1,0:T(8,128)(2,1)S(1)}, u32[]{:S(2)}, u32[]{:S(2)}) collective-permute-start(bf16[192,2048]{1,0:T(8,128)(2,1)S(1)} %expert_back_send.1), channel_id=1, source_target_pairs={{0,2},{1,5},{2,0},{3,7},{4,6},{5,1},{6,4},{7,3},{8,10},{9,13},{10,... | collective-permute-start | bytes 2359304 | tf_op jit(solution)/shard_map/ppermute | solution.py:270
  65.2 7.8 %collective-permute-start.9 = (bf16[96,2048]{1,0:T(8,128)(2,1)S(1)}, bf16[96,2048]{1,0:T(8,128)(2,1)S(1)}, u32[]{:S(2)}, u32[]{:S(2)}) collective-permute-start(bf16[96,2048]{1,0:T(8,128)(2,1)S(1)} %slice.44), channel_id=1, source_target_pairs={{0,4},{1,3},{2,6},{3,1},{4,0},{5,7},{6,2},{7,5},{8,12},{9,11},{10,... | collective-permute-start | bytes 1179656 | tf_op jit(solution)/shard_map/ppermute | solution.py:270
  73.2 7.4 %collective-permute-start.10 = (bf16[24,2048]{1,0:T(8,128)(2,1)S(1)}, bf16[24,2048]{1,0:T(8,128)(2,1)S(1)}, u32[]{:S(2)}, u32[]{:S(2)}) collective-permute-start(bf16[24,2048]{1,0:T(8,128)(2,1)S(1)} %get-tuple-element.30), channel_id=1, source_target_pairs={{0,8},{1,9},{2,10},{3,11},{4,12},{5,13},{6,14},{7,15},{8,16},{9,17... | collective-permute-start | bytes 294920 | tf_op jit(solution)/shard_map/ppermute | solution.py:270
  74.9 5.8 %collective-permute-start.12 = (bf16[24,2048]{1,0:T(8,128)(2,1)S(1)}, bf16[24,2048]{1,0:T(8,128)(2,1)S(1)}, u32[]{:S(2)}, u32[]{:S(2)}) collective-permute-start(bf16[24,2048]{1,0:T(8,128)(2,1)S(1)} %get-tuple-element.31), channel_id=1, source_target_pairs={{0,24},{1,25},{2,26},{3,27},{4,28},{5,29},{6,30},{7,31},{8,0},{9,1... | collective-permute-start | bytes 294920 | tf_op jit(solution)/shard_map/ppermute | solution.py:270
  77.1 7.6 %collective-permute-start.11 = (bf16[24,2048]{1,0:T(8,128)(2,1)S(1)}, bf16[24,2048]{1,0:T(8,128)(2,1)S(1)}, u32[]{:S(2)}, u32[]{:S(2)}) collective-permute-start(bf16[24,2048]{1,0:T(8,128)(2,1)S(1)} %get-tuple-element.32), channel_id=1, source_target_pairs={{0,16},{1,17},{2,18},{3,19},{4,20},{5,21},{6,22},{7,23},{8,24},{9,... | collective-permute-start | bytes 294920 | tf_op jit(solution)/shard_map/ppermute | solution.py:270

commit v5 on v4

--- a/solution.py
+++ b/solution.py
@@ -201,27 +201,27 @@
 
 
 def back_kernel(
-    send, experts, lanes, chunks, at_ref, own_ref, other_ref, sr_ref, r2_ref, down_ref, out_ref
+    experts, lanes, chunks, at_ref, own_ref, other_ref, sr_ref, r2_ref, down_ref, send_ref, keep_ref
 ):
     block = down_ref.shape[2] // chunks
     f = own_ref.shape[1]
     group = sr_ref.shape[0] // 2
     core = at_ref[1]
-    first = int(send)
-
-    def rows(ref, a, b):
-        return jnp.concatenate(
-            [ref[a * group : (a + 1) * group], ref[b * group : (b + 1) * group]], axis=0
-        )
-
-    own = rows(own_ref, 1, 3) if send else rows(own_ref, 0, 2)
-    other = rows(other_ref, 2, 3) if send else rows(other_ref, 0, 1)
+
+    def rows(ref, order):
+        return jnp.concatenate([ref[i * group : (i + 1) * group] for i in order], axis=0)
+
+    own = rows(own_ref, (1, 3, 0, 2))
+    other = rows(other_ref, (2, 3, 0, 1))
     begin = pl.multiple_of(core * f, 128)
     rest = pl.multiple_of((1 - core) * f, 128)
     tail = slice(sr_ref.shape[1] - lanes, sr_ref.shape[1])
-    picked = slice(first * group, (first + 1) * group)
     probs = jnp.concatenate(
-        [sr_ref[picked, tail].astype(jnp.float32), r2_ref[picked, tail].astype(jnp.float32)],
+        [
+            ref[i * group : (i + 1) * group, tail].astype(jnp.float32)
+            for i in (1, 0)
+            for ref in (sr_ref, r2_ref)
+        ],
         axis=0,
     )
     lane = lax.broadcasted_iota(jnp.int32, probs.shape, 1)
@@ -233,29 +233,62 @@
         total += jnp.dot(
             other, down_ref[0, pl.ds(rest, f), at], preferred_element_type=jnp.float32
         )
-        out_ref[:, at] = (total * weight).astype(out_ref.dtype)
-
-
-def expert_back(send, experts, at, own, other, w_down, sr, r2, lanes):
+        total = total * weight
+        send_ref[:, at] = total[: 2 * group].astype(send_ref.dtype)
+        keep_ref[:, at] = total[2 * group :]
+
+
+def expert_back(experts, at, own, other, w_down, sr, r2, lanes):
     tokens, f = own.shape
     group2 = sr.shape[0]
     width = w_down.shape[2]
-    out = jax.ShapeDtypeStruct((group2, width), jnp.bfloat16 if send else jnp.float32)
+    send = jax.ShapeDtypeStruct((group2, width), jnp.bfloat16)
+    keep = jax.ShapeDtypeStruct((group2, width), jnp.float32)
     return pl.pallas_call(
-        functools.partial(back_kernel, send, experts, lanes, 4),
-        out_shape=out,
+        functools.partial(back_kernel, experts, lanes, 4),
+        out_shape=[send, keep],
         in_specs=[smem()] + [vmem()] * 5,
-        out_specs=vmem(),
+        out_specs=[vmem(), vmem()],
         compiler_params=pltpu.CompilerParams(
-            vmem_limit_bytes=room(own, other, w_down, sr, r2, out, out)
+            vmem_limit_bytes=room(own, other, w_down, sr, r2, send, keep, keep)
         ),
         cost_estimate=pl.CostEstimate(
-            flops=2 * tokens * f * width,
-            bytes_accessed=2 * (2 * tokens * f + 2 * f * width + 2 * group2 * width),
+            flops=4 * tokens * f * width,
+            bytes_accessed=2 * (2 * tokens * f + 2 * f * width + 3 * group2 * width),
             transcendentals=0,
         ),
-        name="expert_back_send" if send else "expert_back_keep",
+        name="expert_back",
     )(at, own, other, sr, r2, w_down)
+
+
+def stage_kernel(pieces, *refs):
+    count = len(refs) // 2
+    sems = refs[-1]
+    copies = []
+    for i in range(count):
+        source, target = refs[i], refs[count + i]
+        depth = source.shape[1] // pieces
+        for c in range(pieces):
+            rows = pl.ds(c * depth, depth)
+            copies.append(
+                pltpu.make_async_copy(source.at[:, rows], target.at[:, rows], sems.at[i, c])
+            )
+    for copy in copies:
+        copy.start()
+    for copy in copies:
+        copy.wait()
+
+
+def stage(*weights):
+    return pl.pallas_call(
+        functools.partial(stage_kernel, 4),
+        out_shape=[jax.ShapeDtypeStruct(w.shape, w.dtype) for w in weights],
+        in_specs=[pl.BlockSpec(memory_space=pltpu.HBM)] * len(weights),
+        out_specs=[vmem()] * len(weights),
+        scratch_shapes=[pltpu.SemaphoreType.DMA((len(weights), 4))],
+        compiler_params=pltpu.CompilerParams(vmem_limit_bytes=48 * MIB),
+        name="stage_weights",
+    )(*weights)
 
 
 class Moves:
@@ -269,8 +302,8 @@
         ]
         return lax.ppermute(x, ("ep", "pd"), perm)
 
-    def along_z(self, x, shift):
-        return self.go(x, lambda ep, core: (ep + 4 * shift) % self.owners * 2 + core)
+    def along_z(self, x, turn):
+        return self.go(x, lambda ep, core: (ep ^ (4 * turn)) * 2 + core)
 
     def flip(self, x, turn):
         return self.go(x, lambda ep, core: (ep ^ (1 << ((core + turn) % 2))) * 2 + core)
@@ -329,24 +362,37 @@
         compiler_params=pltpu.CompilerParams(vmem_limit_bytes=room(prompt_kv) * 4),
         name="quantize_pages",
     )(me_ref, page_owner.reshape(-1), prompt_kv.transpose(0, 1, 3, 2, 4))
-    line = [mine] + [moves.along_z(mine, -shift) for shift in range(1, moves.lines)]
-    line = jnp.concatenate(line, axis=0)
     fresh = new_kv.transpose(2, 3, 0, 1, 4).reshape(2, heads, tokens, width)
     fresh = jnp.pad(fresh, ((0, 0), (0, 0), (0, 128 - tokens), (0, 0)))
     tables = [t.reshape(owners, pages) for t in (page_owner, page_slot, page_fill)]
-    line, send = lax.optimization_barrier((line, send))
-    sr = jnp.concatenate([line, moves.flip(line, 0)], axis=0)
+
+    mine, w_gate, w_up = lax.optimization_barrier((mine, w_gate, w_up))
+    w_gate, w_up = stage(w_gate, w_up)
+
+    chunks = [range(0, moves.lines, 2), range(1, moves.lines, 2)]
+    line = [
+        jnp.concatenate([moves.along_z(mine, turn) if turn else mine for turn in chunk], axis=0)
+        for chunk in chunks
+    ]
+    near, w_gate, w_up = lax.optimization_barrier((line[0], w_gate, w_up))
+    sr = jnp.concatenate([near, moves.flip(near, 0)], axis=0)
+    cache = lax.all_to_all(send, "ep", split_axis=0, concat_axis=0, tiled=True)
+    gathered = [(sr, moves.flip(sr, 1))]
+    sr = jnp.concatenate([line[1], moves.flip(line[1], 0)], axis=0)
     sr, fresh, tables = lax.optimization_barrier((sr, fresh, tables))
     r2 = moves.flip(sr, 1)
-    cache = lax.all_to_all(send, "ep", split_axis=0, concat_axis=0, tiled=True)
     r2, cache = lax.optimization_barrier((r2, cache))
-    other_sr, other_r2 = moves.cores(sr), moves.cores(r2)
-
-    parts = expert_front(own_core, (sr, r2), w_gate, w_up, None)
-    hidden = expert_front(own_core, (other_sr, other_r2), w_gate, w_up, parts)
-    other_hidden = moves.cores(hidden)
-    sent = expert_back(True, owners, at, hidden, other_hidden, w_down, sr, r2, lanes)
-    kept = expert_back(False, owners, at, hidden, other_hidden, w_down, sr, r2, lanes)
+    gathered.append((sr, r2))
+
+    kept = []
+    for sr, r2 in gathered:
+        others = moves.cores(sr), moves.cores(r2)
+        parts = expert_front(own_core, (sr, r2), w_gate, w_up, None)
+        hidden = expert_front(own_core, others, w_gate, w_up, parts)
+        sent, keep = expert_back(
+            owners, at, hidden, moves.cores(hidden), w_down, sr, r2, lanes
+        )
+        kept.append(keep + moves.flip(sent, 0).astype(jnp.float32))
     attn_out = pl.pallas_call(
         functools.partial(attention_kernel, pages),
         out_shape=jax.ShapeDtypeStruct(queries.shape, jnp.bfloat16),
@@ -361,14 +407,17 @@
         cache,
         fresh,
     )
-    group = moves.lines * tokens
-    kept = kept + moves.flip(sent, 0).astype(jnp.float32)
-    kept, attn_out = lax.optimization_barrier((kept, attn_out))
-    kept = kept[:group] + moves.flip(kept[group:].astype(jnp.bfloat16), 1).astype(jnp.float32)
-    moe = kept[:tokens]
-    for shift in range(1, moves.lines):
-        block = kept[shift * tokens : (shift + 1) * tokens].astype(jnp.bfloat16)
-        moe = moe + moves.along_z(block, shift).astype(jnp.float32)
+    kept[1], attn_out = lax.optimization_barrier((kept[1], attn_out))
+    moe = None
+    for chunk, keep in zip(chunks, kept):
+        group = len(chunk) * tokens
+        back = moves.flip(keep[group:].astype(jnp.bfloat16), 1)
+        keep = keep[:group] + back.astype(jnp.float32)
+        for i, turn in enumerate(chunk):
+            block = keep[i * tokens : (i + 1) * tokens]
+            if turn:
+                block = moves.along_z(block.astype(jnp.bfloat16), turn).astype(jnp.float32)
+            moe = block if moe is None else moe + block
     moe = moe.astype(jnp.bfloat16)
     moe_out = moe.reshape(steps, requests, d // 2).transpose(1, 0, 2)
 

time: 85.9 us -> 97 us (1.13)
  Pallas kernels: 15.3 us -> 27.1 us
  waiting for transfers between devices: 36.9 us -> 30.3 us
  starting transfers between devices: 23.3 us -> 28.2 us
  other arithmetic: 2.73 us -> 4.14 us
    all_to_all x1, waiting for transfers between devices: 12.1 us -> 0.01 us  [body(): cache = lax.all_to_all(send, 'ep', split_axis=0, concat_axis=0, tiled=True)]
    pallas_call x2 -> x3, Pallas kernels: 3.07 us -> 8.8 us  [the longest x1 4.54 us: stage(): pl.pallas_call(functools.partial(stage_kernel, 4), out_shape=[jax.ShapeDt...]
    ppermute x13 -> x20, waiting for transfers between devices: 24.8 us -> 30.3 us  [go(): return lax.ppermute(x, ('ep', 'pd'), perm)]
    pallas_call x2 -> x4, Pallas kernels: 3.61 us -> 8.7 us  [expert_front(): pl.pallas_call(functools.partial(hidden_kernel if last else partial_kerne...]
    ppermute x13 -> x20, starting transfers between devices: 18.1 us -> 21 us  [go(): return lax.ppermute(x, ('ep', 'pd'), perm)]
    all_to_all x1, starting transfers between devices: 5.29 us -> 7.15 us  [body(): cache = lax.all_to_all(send, 'ep', split_axis=0, concat_axis=0, tiled=True)]
    concatenate x2 -> x3, other arithmetic: 1 us -> 2.48 us  [the longest x1 1.75 us: body(): sr = jnp.concatenate([line[1], moves.flip(line[1], 0)], axis=0)]
    unnamed x22 -> x23, local copies, waits for them, and re-layouts: 6.05 us -> 4.81 us
  transfers between devices with their start and end apart: 14 -> 21, of which waited for: 7 -> 8; matrix products, arithmetic and copies ran while one was open for 3% -> 7% of each run, Pallas kernels for 12% -> 26%
where the time goes in v5:
time: 97 us; the launch traced here: 96.5 us
  waiting for transfers between devices  30.3 us (31%)
  starting transfers between devices  28.2 us (29%)
  Pallas kernels  27.1 us (28%)
  local copies, waits for them, and re-layouts  5.85 us (6%)
  other arithmetic  4.14 us (4%)
    ppermute x20, waiting for transfers between devices, go(): return lax.ppermute(x, ('ep', 'pd'), perm)  30.3 us
    ppermute x20, starting transfers between devices, go(): return lax.ppermute(x, ('ep', 'pd'), perm)  21 us
    pallas_call x4, Pallas kernels, expert_front(): pl.pallas_call(functools.partial(hidden_kernel if last else partial_kerne...  8.7 us
    all_to_all x1, starting transfers between devices, body(): cache = lax.all_to_all(send, 'ep', split_axis=0, concat_axis=0, tiled=True)  7.15 us
    pallas_call x1, Pallas kernels, body(): pl.pallas_call(functools.partial(page_kernel, pages), out_shape=jax.Shape...  4.93 us
    unnamed x23, local copies, waits for them, and re-layouts  4.81 us
    pallas_call x1, Pallas kernels, stage(): pl.pallas_call(functools.partial(stage_kernel, 4), out_shape=[jax.ShapeDt...  4.54 us
    pallas_call x2, Pallas kernels, expert_back(): pl.pallas_call(functools.partial(back_kernel, experts, lanes, 4), out_sha...  4.26 us
  transfers between devices with their start and end apart: 21, of which 8 were waited for; matrix products, arithmetic and copies ran while one was open for 7% of the time, Pallas kernels for 26%

profile of v5, /device:TPU:0, one launch (start us, length us, event | category | flops | bytes accessed | tf_op | source)
XLA Modules:
  0.0 96.5 jit_solution(17795360192095699593)
XLA Ops:
  0.6 1.7 %pack_tokens.1 = bf16[24,2176]{1,0:T(8,128)(2,1)} custom-call(s32[1]{0:T(128)} %bitcast.1.core_ref, bf16[24,4096]{1,0:T(8,128)(2,1)} %bitcast.23, s32[24,8]{1,0:T(8,128)} %bitcast.25, f32[24,8]{1,0:T(8,128)} %bitcast.26), custom_call_target="tpu_custom_call" | custom-call | tf_op jit(solution)/shard_map/pack_tokens/pallas_call | solution.py:344
  2.4 5.0 %collective-permute-start.1 = (bf16[24,2176]{1,0:T(8,128)(2,1)}, bf16[24,2176]{1,0:T(8,128)(2,1)S(1)}, u32[]{:S(2)}, u32[]{:S(2)}) collective-permute-start(bf16[24,2176]{1,0:T(8,128)(2,1)} %pack_tokens.1), channel_id=1, source_target_pairs={{0,24},{1,25},{2,26},{3,27},{4,28},{5,29},{6,30},{7,31},{8,16},{9,... | collective-permute-start | bytes 313352 | tf_op jit(solution)/shard_map/ppermute | solution.py:303
  8.0 1.0 %copy.22 = bf16[16,2,16,2,128]{4,2,3,1,0:T(8,128)(2,1)S(1)} copy(bf16[16,2,16,2,128]{4,3,2,1,0:T(2,128)(2,1)} %param.12) | data formatting | bytes 524288 | tf_op args[0]
  9.7 4.9 %quantize_pages.1 = bf16[32,2,2,16,128]{4,3,2,1,0:T(8,128)(2,1)} custom-call(s32[1]{0:T(128)} %bitcast.me_ref, s32[256]{0:T(256)S(1)} %bitcast.22, bf16[16,2,2,16,128]{4,3,2,1,0:T(8,128)(2,1)S(1)} %bitcast.21), custom_call_target="tpu_custom_call" | custom-call | tf_op jit(solution)/shard_map/quantize_pages/pallas_call | solution.py:356
  14.6 7.1 %all-to-all-start = ((bf16[32,2,2,16,128]{4,3,2,1,0:T(8,128)(2,1)}), bf16[32,2,2,16,128]{4,3,2,1,0:T(8,128)(2,1)}, u32[]{:S(2)}, u32[]{:S(2)}) async-start(bf16[32,2,2,16,128]{4,3,2,1,0:T(8,128)(2,1)} %quantize_pages.1), calls=%async_computation | async-start | bytes 1048576 | tf_op jit(solution)/shard_map/all_to_all | solution.py:379
  21.8 4.5 %stage_weights.1 = (bf16[1,4096,384]{2,1,0:T(8,128)(2,1)S(1)}, bf16[1,4096,384]{2,1,0:T(8,128)(2,1)}) custom-call(bf16[1,4096,384]{2,1,0:T(8,128)(2,1)} %refs_0_, bf16[1,4096,384]{2,1,0:T(8,128)(2,1)} %refs_1_), custom_call_target="tpu_custom_call" | custom-call | tf_op jit(solution)/shard_map/stage_weights/pallas_call | solution.py:283
  27.1 1.9 %collective-permute-start.2 = (bf16[48,2176]{1,0:T(8,128)(2,1)}, bf16[48,2176]{1,0:T(8,128)(2,1)}, u32[]{:S(2)}, u32[]{:S(2)}) collective-permute-start(bf16[48,2176]{1,0:T(8,128)(2,1)} %pad_maximum_fusion.1), channel_id=1, source_target_pairs={{0,2},{1,5},{2,0},{3,7},{4,6},{5,1},{6,4},{7,3},{8,10},{9,13},{10,... | collective-permute-start | bytes 626696 | tf_op jit(solution)/shard_map/ppermute | solution.py:303
  29.9 7.5 %collective-permute-done.9 = bf16[48,2176]{1,0:T(8,128)(2,1)S(1)} collective-permute-done((bf16[48,2176]{1,0:T(8,128)(2,1)S(1)}, bf16[48,2176]{1,0:T(8,128)(2,1)S(1)}, u32[]{:S(2)}, u32[]{:S(2)}) %collective-permute-start.9) | collective-permute-done | bytes 208928 | tf_op jit(solution)/shard_map/ppermute | solution.py:303
  38.1 1.3 %collective-permute-start.11 = (bf16[96,2176]{1,0:T(8,128)(2,1)}, bf16[96,2176]{1,0:T(8,128)(2,1)}, u32[]{:S(2)}, u32[]{:S(2)}) collective-permute-start(bf16[96,2176]{1,0:T(8,128)(2,1)} %constant_dynamic-update-slice_fusion.sr_ref), channel_id=1, source_target_pairs={{0,4},{1,3},{2,6},{3,1},{4,0},{5,7},{6,2},{7,5},{8,12},{9,11},{10,... | collective-permute-start | bytes 1253384 | tf_op jit(solution)/shard_map/ppermute | solution.py:303
  40.8 1.7 %pad_maximum_fusion.sr_ref = bf16[96,2176]{1,0:T(8,128)(2,1)} fusion(bf16[48,2176]{1,0:T(8,128)(2,1)} %collective-permute-done.2, bf16[24,2176]{1,0:T(8,128)(2,1)S(1)} %collective-permute-done.1, bf16[24,2176]{1,0:T(8,128)(2,1)S(1)} %collective-permute-done), kind=kLoop, calls=%fused_computation.2 | loop fusion | flops 1253376 | bytes 835584 | tf_op jit(solution)/shard_map/concatenate | solution.py:381
  42.6 0.8 collective-permute-start.4
  43.4 3.1 %collective-permute-done.11.r2_ref = bf16[96,2176]{1,0:T(8,128)(2,1)} collective-permute-done((bf16[96,2176]{1,0:T(8,128)(2,1)}, bf16[96,2176]{1,0:T(8,128)(2,1)}, u32[]{:S(2)}, u32[]{:S(2)}) %collective-permute-start.11) | collective-permute-done | bytes 417824 | tf_op jit(solution)/shard_map/ppermute | solution.py:303
  47.0 4.0 %collective-permute-done.4.r2_ref = bf16[96,2176]{1,0:T(8,128)(2,1)} collective-permute-done((bf16[96,2176]{1,0:T(8,128)(2,1)}, bf16[96,2176]{1,0:T(8,128)(2,1)}, u32[]{:S(2)}, u32[]{:S(2)}) %collective-permute-start.4) | collective-permute-done | bytes 417824 | tf_op jit(solution)/shard_map/ppermute | solution.py:303
  51.0 1.9 %copy-done = bf16[1,4096,384]{2,1,0:T(8,128)(2,1)S(1)} copy-done((bf16[1,4096,384]{2,1,0:T(8,128)(2,1)S(1)}, bf16[1,4096,384]{2,1,0:T(8,128)(2,1)}, u32[]{:S(2)}) %copy-start) | copy-done | bytes 3145752
  52.9 2.3 %expert_partial.3 = (f32[192,384]{1,0:T(8,128)S(1)}, f32[192,384]{1,0:T(8,128)S(1)}) custom-call(s32[1]{0:T(128)} %bitcast.1.core_ref, bf16[96,2176]{1,0:T(8,128)(2,1)} %constant_dynamic-update-slice_fusion.sr_ref, bf16[96,2176]{1,0:T(8,128)(2,1)} %collective-permute-done.11.r2_ref, bf16[1,4096,384]{2,1,0:T(8,128)(2,1)S(1)} %get-tuple-element.34.gate_ref, ...), custom_call_target="tpu_custom_call" | custom-call | flops 603979776 | bytes 4521984 | tf_op jit(solution)/shard_map/expert_partial/pallas_call | solution.py:185
  55.2 2.3 %expert_hidden.3.own_ref = bf16[192,384]{1,0:T(8,128)(2,1)S(1)} custom-call(s32[1]{0:T(128)} %bitcast.1.core_ref, bf16[96,2176]{1,0:T(8,128)(2,1)} %collective-permute-done.10.sr_ref, bf16[96,2176]{1,0:T(8,128)(2,1)} %collective-permute-done.12.r2_ref, bf16[1,4096,384]{2,1,0:T(8,128)(2,1)S(1)} %get-tuple-element.34.gate_ref, ...), custom_call_target="tpu_custom_call" | custom-call | flops 603979776 | bytes 4521984 | tf_op jit(solution)/shard_map/expert_hidden/pallas_call | solution.py:185
  58.1 0.9 collective-permute-done.13.other_ref
  59.0 2.1 %expert_back.3 = (bf16[96,2048]{1,0:T(8,128)(2,1)S(1)}, f32[96,2048]{1,0:T(8,128)S(1)}) custom-call(s32[2]{0:T(128)S(1)} %pad_add_fusion.at_ref, bf16[192,384]{1,0:T(8,128)(2,1)S(1)} %expert_hidden.3.own_ref, bf16[192,384]{1,0:T(8,128)(2,1)S(1)} %collective-permute-done.13.other_ref, bf16[96,2176]{1,0:T(8,128)(2,1)} %constant_dynamic-update-slice_fusion.sr_ref, ...), custom_call_target="tpu_custom_call" | custom-call | flops 603979776 | bytes 4620288 | tf_op jit(solution)/shard_map/expert_back/pallas_call | solution.py:247
  61.2 1.3 %collective-permute-start.14 = (bf16[96,2048]{1,0:T(8,128)(2,1)S(1)}, bf16[96,2048]{1,0:T(8,128)(2,1)S(1)}, u32[]{:S(2)}, u32[]{:S(2)}) collective-permute-start(bf16[96,2048]{1,0:T(8,128)(2,1)S(1)} %get-tuple-element.50), channel_id=1, source_target_pairs={{0,2},{1,5},{2,0},{3,7},{4,6},{5,1},{6,4},{7,3},{8,10},{9,13},{10,... | collective-permute-start | bytes 1179656 | tf_op jit(solution)/shard_map/ppermute | solution.py:303
  62.5 2.1 %expert_partial.2 = (f32[192,384]{1,0:T(8,128)S(1)}, f32[192,384]{1,0:T(8,128)S(1)}) custom-call(s32[1]{0:T(128)} %bitcast.1.core_ref, bf16[96,2176]{1,0:T(8,128)(2,1)} %pad_maximum_fusion.sr_ref, bf16[96,2176]{1,0:T(8,128)(2,1)} %collective-permute-done.4.r2_ref, bf16[1,4096,384]{2,1,0:T(8,128)(2,1)S(1)} %get-tuple-element.34.gate_ref, ...), custom_call_target="tpu_custom_call" | custom-call | flops 603979776 | bytes 4521984 | tf_op jit(solution)/shard_map/expert_partial/pallas_call | solution.py:185
  64.6 2.1 %expert_hidden.2.own_ref = bf16[192,384]{1,0:T(8,128)(2,1)S(1)} custom-call(s32[1]{0:T(128)} %bitcast.1.core_ref, bf16[96,2176]{1,0:T(8,128)(2,1)} %collective-permute-done.3.sr_ref, bf16[96,2176]{1,0:T(8,128)(2,1)S(1)} %collective-permute-done.5.r2_ref, bf16[1,4096,384]{2,1,0:T(8,128)(2,1)S(1)} %get-tuple-element.34.gate_ref, ...), custom_call_target="tpu_custom_call" | custom-call | flops 603979776 | bytes 4521984 | tf_op jit(solution)/shard_map/expert_hidden/pallas_call | solution.py:185
  66.8 3.0 %attention.1 = bf16[8,3,32,128]{3,2,1,0:T(8,128)(2,1)} custom-call(s32[1]{0:T(128)} %bitcast.me_ref, s32[16,16]{1,0:T(8,128)S(1)} %reshape.37.owner_ref, s32[16,16]{1,0:T(8,128)S(1)} %reshape.38.slot_ref, s32[16,16]{1,0:T(8,128)S(1)} %reshape.39.fill_ref, bf16[8,3,32,128]{3,2,1,0:T(8,128)(2,1)S(1)} %copy-done.3, ...), custom_call_target="tpu_custom_call" | custom-call | tf_op jit(solution)/shard_map/attention/pallas_call | solution.py:396
  69.8 2.1 %expert_back.2 = (bf16[96,2048]{1,0:T(8,128)(2,1)S(1)}, f32[96,2048]{1,0:T(8,128)S(1)}) custom-call(s32[2]{0:T(128)S(1)} %pad_add_fusion.at_ref, bf16[192,384]{1,0:T(8,128)(2,1)S(1)} %expert_hidden.2.own_ref, bf16[192,384]{1,0:T(8,128)(2,1)S(1)} %collective-permute-done.7.other_ref, bf16[96,2176]{1,0:T(8,128)(2,1)} %pad_maximum_fusion.sr_ref, ...), custom_call_target="tpu_custom_call" | custom-call | flops 603979776 | bytes 4620288 | tf_op jit(solution)/shard_map/expert_back/pallas_call | solution.py:247
  72.0 1.3 %collective-permute-start.8 = (bf16[96,2048]{1,0:T(8,128)(2,1)S(1)}, bf16[96,2048]{1,0:T(8,128)(2,1)S(1)}, u32[]{:S(2)}, u32[]{:S(2)}) collective-permute-start(bf16[96,2048]{1,0:T(8,128)(2,1)S(1)} %get-tuple-element.39), channel_id=1, source_target_pairs={{0,2},{1,5},{2,0},{3,7},{4,6},{5,1},{6,4},{7,3},{8,10},{9,13},{10,... | collective-permute-start | bytes 1179656 | tf_op jit(solution)/shard_map/ppermute | solution.py:303
  73.4 0.8 collective-permute-start.15
  74.2 7.7 %collective-permute-done.8 = bf16[96,2048]{1,0:T(8,128)(2,1)S(1)} collective-permute-done((bf16[96,2048]{1,0:T(8,128)(2,1)S(1)}, bf16[96,2048]{1,0:T(8,128)(2,1)S(1)}, u32[]{:S(2)}, u32[]{:S(2)}) %collective-permute-start.8) | collective-permute-done | bytes 393248 | tf_op jit(solution)/shard_map/ppermute | solution.py:303
  82.0 1.2 %collective-permute-start.17 = (bf16[48,2048]{1,0:T(8,128)(2,1)S(1)}, bf16[48,2048]{1,0:T(8,128)(2,1)S(1)}, u32[]{:S(2)}, u32[]{:S(2)}) collective-permute-start(bf16[48,2048]{1,0:T(8,128)(2,1)S(1)} %slice.58), channel_id=1, source_target_pairs={{0,4},{1,3},{2,6},{3,1},{4,0},{5,7},{6,2},{7,5},{8,12},{9,11},{10,... | collective-permute-start | bytes 589832 | tf_op jit(solution)/shard_map/ppermute | solution.py:303
  83.3 2.0 %collective-permute-start.16 = (bf16[24,2048]{1,0:T(8,128)(2,1)S(1)}, bf16[24,2048]{1,0:T(8,128)(2,1)S(1)}, u32[]{:S(2)}, u32[]{:S(2)}) collective-permute-start(bf16[24,2048]{1,0:T(8,128)(2,1)S(1)} %slice.60), channel_id=1, source_target_pairs={{0,16},{1,17},{2,18},{3,19},{4,20},{5,21},{6,22},{7,23},{8,24},{9,... | collective-permute-start | bytes 294920 | tf_op jit(solution)/shard_map/ppermute | solution.py:303
  85.3 2.4 %collective-permute-done.17 = bf16[48,2048]{1,0:T(8,128)(2,1)S(1)} collective-permute-done((bf16[48,2048]{1,0:T(8,128)(2,1)S(1)}, bf16[48,2048]{1,0:T(8,128)(2,1)S(1)}, u32[]{:S(2)}, u32[]{:S(2)}) %collective-permute-start.17) | collective-permute-done | bytes 196640 | tf_op jit(solution)/shard_map/ppermute | solution.py:303
  87.8 3.4 %collective-permute-start.19 = (bf16[24,2048]{1,0:T(8,128)(2,1)S(1)}, bf16[24,2048]{1,0:T(8,128)(2,1)S(1)}, u32[]{:S(2)}, u32[]{:S(2)}) collective-permute-start(bf16[24,2048]{1,0:T(8,128)(2,1)S(1)} %get-tuple-element.53), channel_id=1, source_target_pairs={{0,24},{1,25},{2,26},{3,27},{4,28},{5,29},{6,30},{7,31},{8,16},{9,... | collective-permute-start | bytes 294920 | tf_op jit(solution)/shard_map/ppermute | solution.py:303
  91.2 3.2 %collective-permute-done.19 = bf16[24,2048]{1,0:T(8,128)(2,1)S(1)} collective-permute-done((bf16[24,2048]{1,0:T(8,128)(2,1)S(1)}, bf16[24,2048]{1,0:T(8,128)(2,1)S(1)}, u32[]{:S(2)}, u32[]{:S(2)}) %collective-permute-start.19) | collective-permute-done | bytes 98336 | tf_op jit(solution)/shard_map/ppermute | solution.py:303
  94.4 1.4 %collective-permute-done.18 = bf16[24,2048]{1,0:T(8,128)(2,1)S(1)} collective-permute-done((bf16[24,2048]{1,0:T(8,128)(2,1)S(1)}, bf16[24,2048]{1,0:T(8,128)(2,1)S(1)}, u32[]{:S(2)}, u32[]{:S(2)}) %collective-permute-start.18) | collective-permute-done | bytes 98336 | tf_op jit(solution)/shard_map/ppermute | solution.py:303
  (63 shorter events, 7.5 us)
Async XLA Ops:
  2.4 24.0 %collective-permute-start.1 = (bf16[24,2176]{1,0:T(8,128)(2,1)}, bf16[24,2176]{1,0:T(8,128)(2,1)S(1)}, u32[]{:S(2)}, u32[]{:S(2)}) collective-permute-start(bf16[24,2176]{1,0:T(8,128)(2,1)} %pack_tokens.1), channel_id=1, source_target_pairs={{0,24},{1,25},{2,26},{3,27},{4,28},{5,29},{6,30},{7,31},{8,16},{9,... | collective-permute-start | bytes 313352 | tf_op jit(solution)/shard_map/ppermute | solution.py:303
  7.4 19.0 %collective-permute-start = (bf16[24,2176]{1,0:T(8,128)(2,1)}, bf16[24,2176]{1,0:T(8,128)(2,1)S(1)}, u32[]{:S(2)}, u32[]{:S(2)}) collective-permute-start(bf16[24,2176]{1,0:T(8,128)(2,1)} %pack_tokens.1), channel_id=1, source_target_pairs={{0,8},{1,9},{2,10},{3,11},{4,12},{5,13},{6,14},{7,15},{8,0},{9,1},... | collective-permute-start | bytes 313352 | tf_op jit(solution)/shard_map/ppermute | solution.py:303
  7.4 21.5 %collective-permute-start.6 = (bf16[24,2176]{1,0:T(8,128)(2,1)}, bf16[24,2176]{1,0:T(8,128)(2,1)S(1)}, u32[]{:S(2)}, u32[]{:S(2)}) collective-permute-start(bf16[24,2176]{1,0:T(8,128)(2,1)} %pack_tokens.1), channel_id=1, source_target_pairs={{0,16},{1,17},{2,18},{3,19},{4,20},{5,21},{6,22},{7,23},{8,24},{9,... | collective-permute-start | bytes 313352 | tf_op jit(solution)/shard_map/ppermute | solution.py:303
  9.0 0.7 copy-start.4
  14.6 36.4 %all-to-all-start = ((bf16[32,2,2,16,128]{4,3,2,1,0:T(8,128)(2,1)}), bf16[32,2,2,16,128]{4,3,2,1,0:T(8,128)(2,1)}, u32[]{:S(2)}, u32[]{:S(2)}) async-start(bf16[32,2,2,16,128]{4,3,2,1,0:T(8,128)(2,1)} %quantize_pages.1), calls=%async_computation | async-start | bytes 1048576 | tf_op jit(solution)/shard_map/all_to_all | solution.py:379
  21.7 7.2 %copy-start.6 = (bf16[24,2176]{1,0:T(8,128)(2,1)S(1)}, bf16[24,2176]{1,0:T(8,128)(2,1)}, u32[]{:S(2)}) copy-start(bf16[24,2176]{1,0:T(8,128)(2,1)} %pack_tokens.1) | copy-start | bytes 313348
  21.8 17.6 %copy-start.7 = (bf16[8,3,2,2,128]{4,3,2,1,0:T(2,128)(2,1)S(1)}, bf16[8,3,2,2,128]{4,3,2,1,0:T(2,128)(2,1)}, u32[]{:S(2)}) copy-start(bf16[8,3,2,2,128]{4,3,2,1,0:T(2,128)(2,1)} %param.17) | copy-start | bytes 73732
  21.8 18.1 %copy-start.5 = (s32[256,1]{0,1:T(1,128)S(1)}, s32[256,1]{0,1:T(1,128)}, u32[]{:S(2)}) copy-start(s32[256,1]{0,1:T(1,128)} %param.13) | copy-start | bytes 3076
  21.8 18.9 %copy-start.8 = (s32[256]{0:T(256)S(1)}, s32[256]{0:T(256)}, u32[]{:S(2)}) copy-start(s32[256]{0:T(256)} %param.14) | copy-start | bytes 3076
  21.8 18.9 %copy-start.9 = (s32[256]{0:T(256)S(1)}, s32[256]{0:T(256)}, u32[]{:S(2)}) copy-start(s32[256]{0:T(256)} %param.15) | copy-start | bytes 3076
  27.1 13.8 %collective-permute-start.2 = (bf16[48,2176]{1,0:T(8,128)(2,1)}, bf16[48,2176]{1,0:T(8,128)(2,1)}, u32[]{:S(2)}, u32[]{:S(2)}) collective-permute-start(bf16[48,2176]{1,0:T(8,128)(2,1)} %pad_maximum_fusion.1), channel_id=1, source_target_pairs={{0,2},{1,5},{2,0},{3,7},{4,6},{5,1},{6,4},{7,3},{8,10},{9,13},{10,... | collective-permute-start | bytes 626696 | tf_op jit(solution)/shard_map/ppermute | solution.py:303
  29.0 8.4 %collective-permute-start.9 = (bf16[48,2176]{1,0:T(8,128)(2,1)S(1)}, bf16[48,2176]{1,0:T(8,128)(2,1)S(1)}, u32[]{:S(2)}, u32[]{:S(2)}) collective-permute-start(bf16[48,2176]{1,0:T(8,128)(2,1)S(1)} %pad_maximum_fusion.2), channel_id=1, source_target_pairs={{0,2},{1,5},{2,0},{3,7},{4,6},{5,1},{6,4},{7,3},{8,10},{9,13},{10,... | collective-permute-start | bytes 626696 | tf_op jit(solution)/shard_map/ppermute | solution.py:303
  38.1 8.4 %collective-permute-start.11 = (bf16[96,2176]{1,0:T(8,128)(2,1)}, bf16[96,2176]{1,0:T(8,128)(2,1)}, u32[]{:S(2)}, u32[]{:S(2)}) collective-permute-start(bf16[96,2176]{1,0:T(8,128)(2,1)} %constant_dynamic-update-slice_fusion.sr_ref), channel_id=1, source_target_pairs={{0,4},{1,3},{2,6},{3,1},{4,0},{5,7},{6,2},{7,5},{8,12},{9,11},{10,... | collective-permute-start | bytes 1253384 | tf_op jit(solution)/shard_map/ppermute | solution.py:303
  42.6 8.4 %collective-permute-start.4 = (bf16[96,2176]{1,0:T(8,128)(2,1)}, bf16[96,2176]{1,0:T(8,128)(2,1)}, u32[]{:S(2)}, u32[]{:S(2)}) collective-permute-start(bf16[96,2176]{1,0:T(8,128)(2,1)} %pad_maximum_fusion.sr_ref), channel_id=1, source_target_pairs={{0,4},{1,3},{2,6},{3,1},{4,0},{5,7},{6,2},{7,5},{8,12},{9,11},{10,... | collective-permute-start | bytes 1253384 | tf_op jit(solution)/shard_map/ppermute | solution.py:303
  43.4 11.8 %collective-permute-start.10 = (bf16[96,2176]{1,0:T(8,128)(2,1)}, bf16[96,2176]{1,0:T(8,128)(2,1)}, u32[]{:S(2)}, u32[]{:S(2)}) collective-permute-start(bf16[96,2176]{1,0:T(8,128)(2,1)} %constant_dynamic-update-slice_fusion.sr_ref), channel_id=1, source_target_pairs={{0,1},{1,0},{2,3},{3,2},{4,5},{5,4},{6,7},{7,6},{8,9},{9,8},{10,11... | collective-permute-start | bytes 1253384 | tf_op jit(solution)/shard_map/ppermute | solution.py:303
  46.5 8.7 %collective-permute-start.12 = (bf16[96,2176]{1,0:T(8,128)(2,1)}, bf16[96,2176]{1,0:T(8,128)(2,1)}, u32[]{:S(2)}, u32[]{:S(2)}) collective-permute-start(bf16[96,2176]{1,0:T(8,128)(2,1)} %collective-permute-done.11.r2_ref), channel_id=1, source_target_pairs={{0,1},{1,0},{2,3},{3,2},{4,5},{5,4},{6,7},{7,6},{8,9},{9,8},{10,11... | collective-permute-start | bytes 1253384 | tf_op jit(solution)/shard_map/ppermute | solution.py:303
  46.5 18.1 %collective-permute-start.3 = (bf16[96,2176]{1,0:T(8,128)(2,1)}, bf16[96,2176]{1,0:T(8,128)(2,1)}, u32[]{:S(2)}, u32[]{:S(2)}) collective-permute-start(bf16[96,2176]{1,0:T(8,128)(2,1)} %pad_maximum_fusion.sr_ref), channel_id=1, source_target_pairs={{0,1},{1,0},{2,3},{3,2},{4,5},{5,4},{6,7},{7,6},{8,9},{9,8},{10,11... | collective-permute-start | bytes 1253384 | tf_op jit(solution)/shard_map/ppermute | solution.py:303
  51.0 13.6 %collective-permute-start.5 = (bf16[96,2176]{1,0:T(8,128)(2,1)}, bf16[96,2176]{1,0:T(8,128)(2,1)S(1)}, u32[]{:S(2)}, u32[]{:S(2)}) collective-permute-start(bf16[96,2176]{1,0:T(8,128)(2,1)} %collective-permute-done.4.r2_ref), channel_id=1, source_target_pairs={{0,1},{1,0},{2,3},{3,2},{4,5},{5,4},{6,7},{7,6},{8,9},{9,8},{10,11... | collective-permute-start | bytes 1253384 | tf_op jit(solution)/shard_map/ppermute | solution.py:303
  51.0 1.9 %copy-start = (bf16[1,4096,384]{2,1,0:T(8,128)(2,1)S(1)}, bf16[1,4096,384]{2,1,0:T(8,128)(2,1)}, u32[]{:S(2)}) copy-start(bf16[1,4096,384]{2,1,0:T(8,128)(2,1)} %get-tuple-element.35.up_ref) | copy-start | bytes 9437188
  52.8 2.3 %copy-start.1 = (bf16[1,4096,384]{2,1,0:T(8,128)(2,1)S(1)}, bf16[1,4096,384]{2,1,0:T(8,128)(2,1)}, u32[]{:S(2)}) copy-start(bf16[1,4096,384]{2,1,0:T(8,128)(2,1)} %get-tuple-element.35.up_ref) | copy-start | bytes 9437188
  55.1 3.9 %copy-start.2 = (bf16[1,768,2048]{2,1,0:T(8,128)(2,1)S(1)}, bf16[1,768,2048]{2,1,0:T(8,128)(2,1)}, u32[]{:S(2)}) copy-start(bf16[1,768,2048]{2,1,0:T(8,128)(2,1)} %down_ref.3) | copy-start | bytes 9437188
  57.4 1.6 %collective-permute-start.13 = (bf16[192,384]{1,0:T(8,128)(2,1)S(1)}, bf16[192,384]{1,0:T(8,128)(2,1)S(1)}, u32[]{:S(2)}, u32[]{:S(2)}) collective-permute-start(bf16[192,384]{1,0:T(8,128)(2,1)S(1)} %expert_hidden.3.own_ref), channel_id=1, source_target_pairs={{0,1},{1,0},{2,3},{3,2},{4,5},{5,4},{6,7},{7,6},{8,9},{9,8},{10,11... | collective-permute-start | bytes 442376 | tf_op jit(solution)/shard_map/ppermute | solution.py:303
  61.2 12.1 %collective-permute-start.14 = (bf16[96,2048]{1,0:T(8,128)(2,1)S(1)}, bf16[96,2048]{1,0:T(8,128)(2,1)S(1)}, u32[]{:S(2)}, u32[]{:S(2)}) collective-permute-start(bf16[96,2048]{1,0:T(8,128)(2,1)S(1)} %get-tuple-element.50), channel_id=1, source_target_pairs={{0,2},{1,5},{2,0},{3,7},{4,6},{5,1},{6,4},{7,3},{8,10},{9,13},{10,... | collective-permute-start | bytes 1179656 | tf_op jit(solution)/shard_map/ppermute | solution.py:303
  64.6 2.2 %copy-start.3 = (bf16[8,3,32,128]{3,2,1,0:T(8,128)(2,1)S(1)}, bf16[8,3,32,128]{3,2,1,0:T(8,128)(2,1)}, u32[]{:S(2)}) copy-start(bf16[8,3,32,128]{3,2,1,0:T(8,128)(2,1)} %q_ref.1) | copy-start | bytes 589828
  66.7 3.1 %collective-permute-start.7 = (bf16[192,384]{1,0:T(8,128)(2,1)S(1)}, bf16[192,384]{1,0:T(8,128)(2,1)S(1)}, u32[]{:S(2)}, u32[]{:S(2)}) collective-permute-start(bf16[192,384]{1,0:T(8,128)(2,1)S(1)} %expert_hidden.2.own_ref), channel_id=1, source_target_pairs={{0,1},{1,0},{2,3},{3,2},{4,5},{5,4},{6,7},{7,6},{8,9},{9,8},{10,11... | collective-permute-start | bytes 442376 | tf_op jit(solution)/shard_map/ppermute | solution.py:303
  72.0 9.9 %collective-permute-start.8 = (bf16[96,2048]{1,0:T(8,128)(2,1)S(1)}, bf16[96,2048]{1,0:T(8,128)(2,1)S(1)}, u32[]{:S(2)}, u32[]{:S(2)}) collective-permute-start(bf16[96,2048]{1,0:T(8,128)(2,1)S(1)} %get-tuple-element.39), channel_id=1, source_target_pairs={{0,2},{1,5},{2,0},{3,7},{4,6},{5,1},{6,4},{7,3},{8,10},{9,13},{10,... | collective-permute-start | bytes 1179656 | tf_op jit(solution)/shard_map/ppermute | solution.py:303
  73.4 9.9 %collective-permute-start.15 = (bf16[48,2048]{1,0:T(8,128)(2,1)S(1)}, bf16[48,2048]{1,0:T(8,128)(2,1)S(1)}, u32[]{:S(2)}, u32[]{:S(2)}) collective-permute-start(bf16[48,2048]{1,0:T(8,128)(2,1)S(1)} %slice.59), channel_id=1, source_target_pairs={{0,4},{1,3},{2,6},{3,1},{4,0},{5,7},{6,2},{7,5},{8,12},{9,11},{10,... | collective-permute-start | bytes 589832 | tf_op jit(solution)/shard_map/ppermute | solution.py:303
  82.0 5.7 %collective-permute-start.17 = (bf16[48,2048]{1,0:T(8,128)(2,1)S(1)}, bf16[48,2048]{1,0:T(8,128)(2,1)S(1)}, u32[]{:S(2)}, u32[]{:S(2)}) collective-permute-start(bf16[48,2048]{1,0:T(8,128)(2,1)S(1)} %slice.58), channel_id=1, source_target_pairs={{0,4},{1,3},{2,6},{3,1},{4,0},{5,7},{6,2},{7,5},{8,12},{9,11},{10,... | collective-permute-start | bytes 589832 | tf_op jit(solution)/shard_map/ppermute | solution.py:303
  83.3 7.9 %collective-permute-start.16 = (bf16[24,2048]{1,0:T(8,128)(2,1)S(1)}, bf16[24,2048]{1,0:T(8,128)(2,1)S(1)}, u32[]{:S(2)}, u32[]{:S(2)}) collective-permute-start(bf16[24,2048]{1,0:T(8,128)(2,1)S(1)} %slice.60), channel_id=1, source_target_pairs={{0,16},{1,17},{2,18},{3,19},{4,20},{5,21},{6,22},{7,23},{8,24},{9,... | collective-permute-start | bytes 294920 | tf_op jit(solution)/shard_map/ppermute | solution.py:303
  87.8 6.6 %collective-permute-start.19 = (bf16[24,2048]{1,0:T(8,128)(2,1)S(1)}, bf16[24,2048]{1,0:T(8,128)(2,1)S(1)}, u32[]{:S(2)}, u32[]{:S(2)}) collective-permute-start(bf16[24,2048]{1,0:T(8,128)(2,1)S(1)} %get-tuple-element.53), channel_id=1, source_target_pairs={{0,24},{1,25},{2,26},{3,27},{4,28},{5,29},{6,30},{7,31},{8,16},{9,... | collective-permute-start | bytes 294920 | tf_op jit(solution)/shard_map/ppermute | solution.py:303
  91.2 4.6 %collective-permute-start.18 = (bf16[24,2048]{1,0:T(8,128)(2,1)S(1)}, bf16[24,2048]{1,0:T(8,128)(2,1)S(1)}, u32[]{:S(2)}, u32[]{:S(2)}) collective-permute-start(bf16[24,2048]{1,0:T(8,128)(2,1)S(1)} %get-tuple-element.52), channel_id=1, source_target_pairs={{0,8},{1,9},{2,10},{3,11},{4,12},{5,13},{6,14},{7,15},{8,0},{9,1},... | collective-permute-start | bytes 294920 | tf_op jit(solution)/shard_map/ppermute | solution.py:303

commit v6 on v4

--- a/solution.py
+++ b/solution.py
@@ -21,7 +21,7 @@
     return pl.BlockSpec(memory_space=pltpu.SMEM)
 
 
-def page_kernel(pages, me_ref, owner_ref, kv_ref, send_ref, count_ref):
+def page_kernel(pages, me_ref, owner_ref, kv_ref, gate_ref, up_ref, send_ref, count_ref):
     values = kv_ref[...].astype(jnp.float32)
     largest = jnp.max(jnp.abs(values), axis=(3, 4), keepdims=True)
     scale = jnp.full(largest.shape, 2.0 ** (-16), jnp.float32)
@@ -140,31 +140,28 @@
     out_ref[:, half:] = jnp.where(part < 3, chosen, 0.0).astype(out_ref.dtype)
 
 
-def partial_kernel(chunks, core_ref, sr_ref, r2_ref, gate_ref, up_ref, gate_sum, up_sum):
+def partial_kernel(chunks, count, core_ref, *refs):
+    x_refs, (gate_ref, up_ref, gate_sum, up_sum) = refs[:count], refs[count:]
     half = gate_ref.shape[1] // 2
     depth = half // chunks
     for c in range(chunks):
         at = slice(c * depth, (c + 1) * depth)
         rows = pl.ds(pl.multiple_of(core_ref[0] * half + c * depth, 128), depth)
-        x = jnp.concatenate([sr_ref[:, at], r2_ref[:, at]], axis=0)
+        x = jnp.concatenate([ref[:, at] for ref in x_refs], axis=0)
         for weight, total in ((gate_ref, gate_sum), (up_ref, up_sum)):
             part = jnp.dot(x, weight[0, rows], preferred_element_type=jnp.float32)
             total[...] = part if c == 0 else total[...] + part
 
 
-def hidden_kernel(
-    chunks, core_ref, sr_ref, r2_ref, gate_ref, up_ref, gate_part, up_part, out_ref, sums
-):
+def hidden_kernel(chunks, count, core_ref, *refs):
+    x_refs = refs[:count]
+    gate_ref, up_ref, gate_part, up_part, out_ref, sums = refs[count:]
     half = gate_ref.shape[1] // 2
     depth = half // chunks
-    group = sr_ref.shape[0] // 2
     for c in range(chunks):
         at = slice(c * depth, (c + 1) * depth)
         rows = pl.ds(pl.multiple_of((1 - core_ref[0]) * half + c * depth, 128), depth)
-        x = jnp.concatenate(
-            [sr_ref[:group, at], r2_ref[:group, at], sr_ref[group:, at], r2_ref[group:, at]],
-            axis=0,
-        )
+        x = jnp.concatenate([ref[:, at] for ref in x_refs], axis=0)
         for i, (weight, start) in enumerate(((gate_ref, gate_part), (up_ref, up_part))):
             part = jnp.dot(x, weight[0, rows], preferred_element_type=jnp.float32)
             sums[i] = (start[...] if c == 0 else sums[i]) + part
@@ -177,14 +174,14 @@
 
 
 def expert_front(core, rows, w_gate, w_up, parts):
-    tokens = 2 * rows[0].shape[0]
+    tokens = sum(x.shape[0] for x in rows)
     d, f = w_gate.shape[1:]
     last = parts is not None
     total = jax.ShapeDtypeStruct((tokens, f), jnp.float32)
     scratch = [pltpu.VMEM((2, tokens, f), jnp.float32)] if last else []
     return pl.pallas_call(
-        functools.partial(hidden_kernel if last else partial_kernel, 4),
-        in_specs=[smem()] + [vmem()] * (6 if last else 4),
+        functools.partial(hidden_kernel if last else partial_kernel, 4, len(rows)),
+        in_specs=[smem()] + [vmem()] * (len(rows) + (4 if last else 2)),
         out_specs=vmem() if last else [vmem(), vmem()],
         scratch_shapes=scratch,
         out_shape=jax.ShapeDtypeStruct((tokens, f), jnp.bfloat16) if last else [total, total],
@@ -200,62 +197,57 @@
     )(core, *rows, w_gate, w_up, *(parts or ()))
 
 
-def back_kernel(
-    send, experts, lanes, chunks, at_ref, own_ref, other_ref, sr_ref, r2_ref, down_ref, out_ref
-):
+def back_kernel(experts, begin, count, chunks, at_ref, own_ref, other_ref, *refs):
+    prob_refs, (down_ref, keep_ref, *send_refs) = refs[:count], refs[count:]
     block = down_ref.shape[2] // chunks
     f = own_ref.shape[1]
-    group = sr_ref.shape[0] // 2
+    piece = keep_ref.shape[0]
+    rows = (len(send_refs) + 1) * piece
+    lanes = 128 * (-(-3 * experts // 128))
     core = at_ref[1]
-    first = int(send)
-
-    def rows(ref, a, b):
-        return jnp.concatenate(
-            [ref[a * group : (a + 1) * group], ref[b * group : (b + 1) * group]], axis=0
-        )
-
-    own = rows(own_ref, 1, 3) if send else rows(own_ref, 0, 2)
-    other = rows(other_ref, 2, 3) if send else rows(other_ref, 0, 1)
-    begin = pl.multiple_of(core * f, 128)
+    own = own_ref[begin : begin + rows]
+    other = other_ref[begin : begin + rows]
+    first = pl.multiple_of(core * f, 128)
     rest = pl.multiple_of((1 - core) * f, 128)
-    tail = slice(sr_ref.shape[1] - lanes, sr_ref.shape[1])
-    picked = slice(first * group, (first + 1) * group)
     probs = jnp.concatenate(
-        [sr_ref[picked, tail].astype(jnp.float32), r2_ref[picked, tail].astype(jnp.float32)],
-        axis=0,
+        [ref[:, ref.shape[1] - lanes :].astype(jnp.float32) for ref in prob_refs], axis=0
     )
     lane = lax.broadcasted_iota(jnp.int32, probs.shape, 1)
     mine = lane % experts == at_ref[0]
     weight = jnp.sum(jnp.where(mine, probs, 0.0), axis=1, keepdims=True)
     for c in range(chunks):
         at = slice(c * block, (c + 1) * block)
-        total = jnp.dot(own, down_ref[0, pl.ds(begin, f), at], preferred_element_type=jnp.float32)
+        total = jnp.dot(own, down_ref[0, pl.ds(first, f), at], preferred_element_type=jnp.float32)
         total += jnp.dot(
             other, down_ref[0, pl.ds(rest, f), at], preferred_element_type=jnp.float32
         )
-        out_ref[:, at] = (total * weight).astype(out_ref.dtype)
-
-
-def expert_back(send, experts, at, own, other, w_down, sr, r2, lanes):
-    tokens, f = own.shape
-    group2 = sr.shape[0]
+        total = total * weight
+        keep_ref[:, at] = total[:piece]
+        for i, ref in enumerate(send_refs):
+            ref[:, at] = total[(i + 1) * piece : (i + 2) * piece].astype(ref.dtype)
+
+
+def expert_back(experts, begin, at, own, other, w_down, pieces):
+    rows = sum(x.shape[0] for x in pieces)
+    f = own.shape[1]
     width = w_down.shape[2]
-    out = jax.ShapeDtypeStruct((group2, width), jnp.bfloat16 if send else jnp.float32)
+    send = jax.ShapeDtypeStruct((rows // 4, width), jnp.bfloat16)
+    keep = jax.ShapeDtypeStruct((rows // 4, width), jnp.float32)
     return pl.pallas_call(
-        functools.partial(back_kernel, send, experts, lanes, 4),
-        out_shape=out,
-        in_specs=[smem()] + [vmem()] * 5,
-        out_specs=vmem(),
+        functools.partial(back_kernel, experts, begin, len(pieces), 4),
+        out_shape=[keep, send, send, send],
+        in_specs=[smem()] + [vmem()] * (3 + len(pieces)),
+        out_specs=[vmem()] * 4,
         compiler_params=pltpu.CompilerParams(
-            vmem_limit_bytes=room(own, other, w_down, sr, r2, out, out)
+            vmem_limit_bytes=room(own, other, w_down, *pieces, *[keep] * 4)
         ),
         cost_estimate=pl.CostEstimate(
-            flops=2 * tokens * f * width,
-            bytes_accessed=2 * (2 * tokens * f + 2 * f * width + 2 * group2 * width),
+            flops=4 * rows * f * width,
+            bytes_accessed=2 * (4 * rows * f + 2 * f * width + 2 * rows * width),
             transcendentals=0,
         ),
-        name="expert_back_send" if send else "expert_back_keep",
-    )(at, own, other, sr, r2, w_down)
+        name="expert_back",
+    )(at, own, other, *pieces, w_down)
 
 
 class Moves:
@@ -269,11 +261,11 @@
         ]
         return lax.ppermute(x, ("ep", "pd"), perm)
 
-    def along_z(self, x, shift):
-        return self.go(x, lambda ep, core: (ep + 4 * shift) % self.owners * 2 + core)
-
-    def flip(self, x, turn):
-        return self.go(x, lambda ep, core: (ep ^ (1 << ((core + turn) % 2))) * 2 + core)
+    def along_z(self, x, turn):
+        return self.go(x, lambda ep, core: (ep ^ (4 * turn)) * 2 + core)
+
+    def across(self, x, turn):
+        return self.go(x, lambda ep, core: (ep ^ turn) * 2 + core)
 
     def cores(self, x):
         return self.go(x, lambda ep, core: ep * 2 + 1 - core)
@@ -320,39 +312,56 @@
         expert_routes.reshape(tokens, top),
         route_probs.transpose(1, 0, 2).reshape(tokens, top),
     )
+    fresh = new_kv.transpose(2, 3, 0, 1, 4).reshape(2, heads, tokens, width)
+    fresh = jnp.pad(fresh, ((0, 0), (0, 0), (0, 128 - tokens), (0, 0)))
+    tables = [t.reshape(owners, pages) for t in (page_owner, page_slot, page_fill)]
+
+    sets = [range(0, moves.lines, 2), range(1, moves.lines, 2)]
+    line = [
+        jnp.concatenate([moves.along_z(mine, turn) if turn else mine for turn in chips], axis=0)
+        for chips in sets
+    ]
+    line[1], prompt_kv = lax.optimization_barrier((line[1], prompt_kv))
     send = pl.pallas_call(
         functools.partial(page_kernel, pages),
         out_shape=jax.ShapeDtypeStruct((slots, 2, heads, page_len, width), jnp.bfloat16),
-        in_specs=[smem(), smem(), vmem()],
+        in_specs=[smem(), smem()] + [vmem()] * 3,
         out_specs=vmem(),
         scratch_shapes=[pltpu.SMEM((owners,), jnp.int32)],
-        compiler_params=pltpu.CompilerParams(vmem_limit_bytes=room(prompt_kv) * 4),
+        compiler_params=pltpu.CompilerParams(vmem_limit_bytes=room(*[prompt_kv] * 5, w_gate, w_up)),
         name="quantize_pages",
-    )(me_ref, page_owner.reshape(-1), prompt_kv.transpose(0, 1, 3, 2, 4))
-    line = [mine] + [moves.along_z(mine, -shift) for shift in range(1, moves.lines)]
-    line = jnp.concatenate(line, axis=0)
-    fresh = new_kv.transpose(2, 3, 0, 1, 4).reshape(2, heads, tokens, width)
-    fresh = jnp.pad(fresh, ((0, 0), (0, 0), (0, 128 - tokens), (0, 0)))
-    tables = [t.reshape(owners, pages) for t in (page_owner, page_slot, page_fill)]
-    line, send = lax.optimization_barrier((line, send))
-    sr = jnp.concatenate([line, moves.flip(line, 0)], axis=0)
-    sr, fresh, tables = lax.optimization_barrier((sr, fresh, tables))
-    r2 = moves.flip(sr, 1)
+    )(me_ref, page_owner.reshape(-1), prompt_kv.transpose(0, 1, 3, 2, 4), w_gate, w_up)
     cache = lax.all_to_all(send, "ep", split_axis=0, concat_axis=0, tiled=True)
-    r2, cache = lax.optimization_barrier((r2, cache))
-    other_sr, other_r2 = moves.cores(sr), moves.cores(r2)
-
-    parts = expert_front(own_core, (sr, r2), w_gate, w_up, None)
-    hidden = expert_front(own_core, (other_sr, other_r2), w_gate, w_up, parts)
+    near = [line[0]] + [moves.across(line[0], turn) for turn in (1, 2, 3)]
+    far = [line[1]] + [moves.across(line[1], turn) for turn in (1, 2, 3)]
+    near = [jnp.concatenate(near, axis=0)]
+    others = [moves.cores(x) for x in near + far]
+    parts = expert_front(own_core, near + far, w_gate, w_up, None)
+    others, cache = lax.optimization_barrier((others, cache))
+    hidden = expert_front(own_core, others, w_gate, w_up, parts)
     other_hidden = moves.cores(hidden)
-    sent = expert_back(True, owners, at, hidden, other_hidden, w_down, sr, r2, lanes)
-    kept = expert_back(False, owners, at, hidden, other_hidden, w_down, sr, r2, lanes)
+
+    half = near[0].shape[0]
+    sums = []
+    for begin, pieces in ((half, far), (0, near)):
+        keep, *send = expert_back(owners, begin, at, hidden, other_hidden, w_down, pieces)
+        for turn, rows in zip((1, 2, 3), send):
+            keep = keep + moves.across(rows, turn).astype(jnp.float32)
+        sums.append(keep)
+    moe = sums[1][:tokens]
+    for chips, rows in zip(sets, reversed(sums)):
+        for i, turn in enumerate(chips):
+            if turn:
+                block = rows[i * tokens : (i + 1) * tokens].astype(jnp.bfloat16)
+                moe = moe + moves.along_z(block, turn).astype(jnp.float32)
     attn_out = pl.pallas_call(
         functools.partial(attention_kernel, pages),
         out_shape=jax.ShapeDtypeStruct(queries.shape, jnp.bfloat16),
         in_specs=[smem()] + [vmem()] * 6,
         out_specs=vmem(),
-        compiler_params=pltpu.CompilerParams(vmem_limit_bytes=8 * MIB + 16 * slots * page_len * tokens * q_heads),
+        compiler_params=pltpu.CompilerParams(
+            vmem_limit_bytes=8 * MIB + 16 * slots * page_len * tokens * q_heads
+        ),
         name="attention",
     )(
         me_ref,
@@ -361,14 +370,6 @@
         cache,
         fresh,
     )
-    group = moves.lines * tokens
-    kept = kept + moves.flip(sent, 0).astype(jnp.float32)
-    kept, attn_out = lax.optimization_barrier((kept, attn_out))
-    kept = kept[:group] + moves.flip(kept[group:].astype(jnp.bfloat16), 1).astype(jnp.float32)
-    moe = kept[:tokens]
-    for shift in range(1, moves.lines):
-        block = kept[shift * tokens : (shift + 1) * tokens].astype(jnp.bfloat16)
-        moe = moe + moves.along_z(block, shift).astype(jnp.float32)
     moe = moe.astype(jnp.bfloat16)
     moe_out = moe.reshape(steps, requests, d // 2).transpose(1, 0, 2)
 

time: 85.9 us -> 111 us (1.29)
  local copies, waits for them, and re-layouts: 6.38 us -> 29.4 us
  waiting for transfers between devices: 36.9 us -> 27.8 us
  starting transfers between devices: 23.3 us -> 32.3 us
  Pallas kernels: 15.3 us -> 16.8 us
    unnamed x22 -> x71, local copies, waits for them, and re-layouts: 6.05 us -> 26.5 us
    all_to_all x1, waiting for transfers between devices: 12.1 us -> 0.01 us  [body(): cache = lax.all_to_all(send, 'ep', split_axis=0, concat_axis=0, tiled=True)]
    ppermute x13 -> x24, starting transfers between devices: 18.1 us -> 26.5 us  [go(): return lax.ppermute(x, ('ep', 'pd'), perm)]
    ppermute x13 -> x24, waiting for transfers between devices: 24.8 us -> 27.8 us  [go(): return lax.ppermute(x, ('ep', 'pd'), perm)]
    concatenate x0 -> x1, local copies, waits for them, and re-layouts: none -> 1.63 us  [body(): near = [jnp.concatenate(near, axis=0)]]
    pallas_call x2, Pallas kernels: 3.61 us -> 4.94 us  [expert_front(): pl.pallas_call(functools.partial(hidden_kernel if last else partial_kerne...]
  transfers between devices with their start and end apart: 14 -> 25, of which waited for: 7 -> 8; matrix products, arithmetic and copies ran while one was open for 3% -> 10% of each run, Pallas kernels for 12% -> 9%
where the time goes in v6:
time: 111 us; the launch traced here: 110 us
  starting transfers between devices  32.3 us (29%)
  local copies, waits for them, and re-layouts  29.4 us (26%)
  waiting for transfers between devices  27.8 us (25%)
  Pallas kernels  16.8 us (15%)
  other arithmetic  3.22 us (3%)
    ppermute x24, waiting for transfers between devices, go(): return lax.ppermute(x, ('ep', 'pd'), perm)  27.8 us
    ppermute x24, starting transfers between devices, go(): return lax.ppermute(x, ('ep', 'pd'), perm)  26.5 us
    unnamed x71, local copies, waits for them, and re-layouts  26.5 us
    all_to_all x1, starting transfers between devices, body(): cache = lax.all_to_all(send, 'ep', split_axis=0, concat_axis=0, tiled=True)  5.81 us
    pallas_call x2, Pallas kernels, expert_front(): pl.pallas_call(functools.partial(hidden_kernel if last else partial_kerne...  4.94 us
    pallas_call x1, Pallas kernels, body(): pl.pallas_call(functools.partial(page_kernel, pages), out_shape=jax.Shape...  4.13 us
    pallas_call x2, Pallas kernels, expert_back(): pl.pallas_call(functools.partial(back_kernel, experts, begin, len(pieces)...  3.04 us
    pallas_call x1, Pallas kernels, body(): pl.pallas_call(functools.partial(attention_kernel, pages), out_shape=jax....  2.97 us
  transfers between devices with their start and end apart: 25, of which 8 were waited for; matrix products, arithmetic and copies ran while one was open for 10% of the time, Pallas kernels for 9%

profile of v6, /device:TPU:0, one launch (start us, length us, event | category | flops | bytes accessed | tf_op | source)
XLA Modules:
  0.0 110.5 jit_solution(3498720280267304013)
XLA Ops:
  0.6 1.7 %pack_tokens.1 = bf16[24,2176]{1,0:T(8,128)(2,1)} custom-call(s32[1]{0:T(128)} %bitcast.1.core_ref, bf16[24,4096]{1,0:T(8,128)(2,1)} %bitcast.23, s32[24,8]{1,0:T(8,128)} %bitcast.25, f32[24,8]{1,0:T(8,128)} %bitcast.26), custom_call_target="tpu_custom_call" | custom-call | tf_op jit(solution)/shard_map/pack_tokens/pallas_call | solution.py:303
  2.4 5.0 %collective-permute-start.6 = (bf16[24,2176]{1,0:T(8,128)(2,1)}, bf16[24,2176]{1,0:T(8,128)(2,1)S(1)}, u32[]{:S(2)}, u32[]{:S(2)}) collective-permute-start(bf16[24,2176]{1,0:T(8,128)(2,1)} %pack_tokens.1), channel_id=1, source_target_pairs={{0,24},{1,25},{2,26},{3,27},{4,28},{5,29},{6,30},{7,31},{8,16},{9,... | collective-permute-start | bytes 313352 | tf_op jit(solution)/shard_map/ppermute | solution.py:262
  8.0 1.6 %constant_dynamic-update-slice_fusion.4 = bf16[192,2176]{1,0:T(8,128)(2,1)} fusion(bf16[24,2176]{1,0:T(8,128)(2,1)} %pack_tokens.1), kind=kLoop, calls=%fused_computation.15 | loop fusion | bytes 208896
  9.5 6.9 %collective-permute-done = bf16[24,2176]{1,0:T(8,128)(2,1)S(1)} collective-permute-done((bf16[24,2176]{1,0:T(8,128)(2,1)}, bf16[24,2176]{1,0:T(8,128)(2,1)S(1)}, u32[]{:S(2)}, u32[]{:S(2)}) %collective-permute-start) | collective-permute-done | bytes 104480 | tf_op jit(solution)/shard_map/ppermute | solution.py:262
  16.4 1.6 %pad_maximum_fusion = bf16[48,2176]{1,0:T(8,128)(2,1)} fusion(bf16[24,2176]{1,0:T(8,128)(2,1)S(1)} %collective-permute-done, bf16[24,2176]{1,0:T(8,128)(2,1)} %pack_tokens.1), kind=kLoop, calls=%fused_computation.3 | loop fusion | flops 417792 | bytes 417792 | tf_op jit(solution)/shard_map/concatenate | solution.py:321
  18.0 2.4 %collective-permute-start.3 = (bf16[48,2176]{1,0:T(8,128)(2,1)}, bf16[48,2176]{1,0:T(8,128)(2,1)}, u32[]{:S(2)}, u32[]{:S(2)}) collective-permute-start(bf16[48,2176]{1,0:T(8,128)(2,1)} %pad_maximum_fusion), channel_id=1, source_target_pairs={{0,6},{1,7},{2,4},{3,5},{4,2},{5,3},{6,0},{7,1},{8,14},{9,15},{10,... | collective-permute-start | bytes 626696 | tf_op jit(solution)/shard_map/ppermute | solution.py:262
  22.5 1.9 %copy-done = bf16[1,4096,384]{2,1,0:T(8,128)(2,1)S(1)} copy-done((bf16[1,4096,384]{2,1,0:T(8,128)(2,1)S(1)}, bf16[1,4096,384]{2,1,0:T(8,128)(2,1)}, u32[]{:S(2)}) %copy-start) | copy-done | bytes 3145752
  24.4 1.9 %copy-done.2 = bf16[1,4096,384]{2,1,0:T(8,128)(2,1)S(1)} copy-done((bf16[1,4096,384]{2,1,0:T(8,128)(2,1)S(1)}, bf16[1,4096,384]{2,1,0:T(8,128)(2,1)}, u32[]{:S(2)}) %copy-start.2) | copy-done | bytes 3145752
  27.0 4.1 %quantize_pages.1 = bf16[32,2,2,16,128]{4,3,2,1,0:T(8,128)(2,1)S(1)} custom-call(s32[1]{0:T(128)} %bitcast.me_ref, s32[256]{0:T(256)S(1)} %bitcast.22, bf16[16,2,2,16,128]{4,3,2,1,0:T(8,128)(2,1)S(1)} %bitcast.21, bf16[1,4096,384]{2,1,0:T(8,128)(2,1)S(1)} %copy-done, bf16[1,4096,384]{2,1,0:T(8,128)(2,1)S(1)} %copy-done.2), custom_call_target="tpu_custom_call" | custom-call | tf_op jit(solution)/shard_map/quantize_pages/pallas_call | solution.py:325
  31.9 5.8 %all-to-all-start = ((bf16[32,2,2,16,128]{4,3,2,1,0:T(8,128)(2,1)}), bf16[32,2,2,16,128]{4,3,2,1,0:T(8,128)(2,1)}, u32[]{:S(2)}, u32[]{:S(2)}) async-start(bf16[32,2,2,16,128]{4,3,2,1,0:T(8,128)(2,1)} %copy-done.8), calls=%async_computation | async-start | bytes 1048576 | tf_op jit(solution)/shard_map/all_to_all | solution.py:334
  38.4 1.6 %constant_dynamic-update-slice_fusion.2 = bf16[192,2176]{1,0:T(8,128)(2,1)} fusion(bf16[192,2176]{1,0:T(8,128)(2,1)} %constant_dynamic-update-slice_fusion.3, bf16[48,2176]{1,0:T(8,128)(2,1)} %collective-permute-done.1), kind=kLoop, calls=%fused_computation.13 | loop fusion | bytes 417792
  40.1 1.6 %constant_dynamic-update-slice_fusion.1 = bf16[192,2176]{1,0:T(8,128)(2,1)} fusion(bf16[192,2176]{1,0:T(8,128)(2,1)} %constant_dynamic-update-slice_fusion.2, bf16[48,2176]{1,0:T(8,128)(2,1)} %collective-permute-done.2), kind=kLoop, calls=%fused_computation.12 | loop fusion | bytes 417792
  41.7 1.6 %constant_dynamic-update-slice_fusion.refs_0_ = bf16[192,2176]{1,0:T(8,128)(2,1)} fusion(bf16[192,2176]{1,0:T(8,128)(2,1)} %constant_dynamic-update-slice_fusion.1, bf16[48,2176]{1,0:T(8,128)(2,1)} %collective-permute-done.3), kind=kLoop, calls=%fused_computation.11 | loop fusion | bytes 417792 | tf_op jit(solution)/shard_map/concatenate | solution.py:337
  43.3 2.8 %collective-permute-start.12 = (bf16[48,2176]{1,0:T(8,128)(2,1)S(1)}, bf16[48,2176]{1,0:T(8,128)(2,1)S(1)}, u32[]{:S(2)}, u32[]{:S(2)}) collective-permute-start(bf16[48,2176]{1,0:T(8,128)(2,1)S(1)} %pad_maximum_fusion.1.refs_1_.refs_0_), channel_id=1, source_target_pairs={{0,6},{1,7},{2,4},{3,5},{4,2},{5,3},{6,0},{7,1},{8,14},{9,15},{10,... | collective-permute-start | bytes 626696 | tf_op jit(solution)/shard_map/ppermute | solution.py:262
  46.8 7.5 %collective-permute-done.12.refs_4_.refs_3_ = bf16[48,2176]{1,0:T(8,128)(2,1)S(1)} collective-permute-done((bf16[48,2176]{1,0:T(8,128)(2,1)S(1)}, bf16[48,2176]{1,0:T(8,128)(2,1)S(1)}, u32[]{:S(2)}, u32[]{:S(2)}) %collective-permute-start.12) | collective-permute-done | bytes 208928 | tf_op jit(solution)/shard_map/ppermute | solution.py:262
  54.3 3.6 %collective-permute-done.10.refs_3_.refs_2_ = bf16[48,2176]{1,0:T(8,128)(2,1)S(1)} collective-permute-done((bf16[48,2176]{1,0:T(8,128)(2,1)S(1)}, bf16[48,2176]{1,0:T(8,128)(2,1)S(1)}, u32[]{:S(2)}, u32[]{:S(2)}) %collective-permute-start.10) | collective-permute-done | bytes 208928 | tf_op jit(solution)/shard_map/ppermute | solution.py:262
  58.5 1.9 %copy-done.3 = bf16[1,4096,384]{2,1,0:T(8,128)(2,1)S(1)} copy-done((bf16[1,4096,384]{2,1,0:T(8,128)(2,1)S(1)}, bf16[1,4096,384]{2,1,0:T(8,128)(2,1)}, u32[]{:S(2)}) %copy-start.3) | copy-done | bytes 3145752
  61.5 1.8 %expert_partial.1 = (f32[384,384]{1,0:T(8,128)S(1)}, f32[384,384]{1,0:T(8,128)S(1)}) custom-call(s32[1]{0:T(128)} %bitcast.1.core_ref, bf16[192,2176]{1,0:T(8,128)(2,1)S(1)} %copy-done.6, bf16[48,2176]{1,0:T(8,128)(2,1)S(1)} %pad_maximum_fusion.1.refs_1_.refs_0_, bf16[48,2176]{1,0:T(8,128)(2,1)S(1)} %collective-permute-done.8.refs_2_.refs_1_, ...), custom_call_target="tpu_custom_call" | custom-call | flops 1207959552 | bytes 5898240 | tf_op jit(solution)/shard_map/expert_partial/pallas_call | solution.py:182
  67.8 1.9 %copy-done.4 = bf16[1,4096,384]{2,1,0:T(8,128)(2,1)S(1)} copy-done((bf16[1,4096,384]{2,1,0:T(8,128)(2,1)S(1)}, bf16[1,4096,384]{2,1,0:T(8,128)(2,1)}, u32[]{:S(2)}) %copy-start.4) | copy-done | bytes 3145752
  75.5 3.1 %expert_hidden.1.own_ref = bf16[384,384]{1,0:T(8,128)(2,1)S(1)} custom-call(s32[1]{0:T(128)} %bitcast.1.core_ref, bf16[192,2176]{1,0:T(8,128)(2,1)} %collective-permute-done.4.refs_0_, bf16[48,2176]{1,0:T(8,128)(2,1)S(1)} %copy-done.20, bf16[48,2176]{1,0:T(8,128)(2,1)S(1)} %copy-done.26, bf16[48,2176]{1,0:T(8,128)(2,1)S(1)} %copy-done.24, ...), custom_call_target="tpu_custom_call" | custom-call | flops 1207959552 | bytes 5898240 | tf_op jit(solution)/shard_map/expert_hidden/pallas_call | solution.py:182
  80.4 1.5 %expert_back.3 = (f32[48,2048]{1,0:T(8,128)S(1)}, bf16[48,2048]{1,0:T(8,128)(2,1)S(1)}, bf16[48,2048]{1,0:T(8,128)(2,1)S(1)}, bf16[48,2048]{1,0:T(8,128)(2,1)S(1)}) custom-call(s32[2]{0:T(128)S(1)} %pad_add_fusion.at_ref, bf16[384,384]{1,0:T(8,128)(2,1)S(1)} %expert_hidden.1.own_ref, bf16[384,384]{1,0:T(8,128)(2,1)S(1)} %collective-permute-done.14.other_ref, ...), custom_call_target="tpu_custom_call" | custom-call | flops 603979776 | bytes 5308416 | tf_op jit(solution)/shard_map/expert_back/pallas_call | solution.py:236
  81.9 1.5 %collective-permute-start.19 = (bf16[48,2048]{1,0:T(8,128)(2,1)S(1)}, bf16[48,2048]{1,0:T(8,128)(2,1)S(1)}, u32[]{:S(2)}, u32[]{:S(2)}) collective-permute-start(bf16[48,2048]{1,0:T(8,128)(2,1)S(1)} %get-tuple-element.35), channel_id=1, source_target_pairs={{0,2},{1,3},{2,0},{3,1},{4,6},{5,7},{6,4},{7,5},{8,10},{9,11},{10,... | collective-permute-start | bytes 589832 | tf_op jit(solution)/shard_map/ppermute | solution.py:262
  83.9 1.7 %collective-permute-start.21 = (bf16[48,2048]{1,0:T(8,128)(2,1)S(1)}, bf16[48,2048]{1,0:T(8,128)(2,1)S(1)}, u32[]{:S(2)}, u32[]{:S(2)}) collective-permute-start(bf16[48,2048]{1,0:T(8,128)(2,1)S(1)} %get-tuple-element.37), channel_id=1, source_target_pairs={{0,6},{1,7},{2,4},{3,5},{4,2},{5,3},{6,0},{7,1},{8,14},{9,15},{10,... | collective-permute-start | bytes 589832 | tf_op jit(solution)/shard_map/ppermute | solution.py:262
  85.6 1.5 %expert_back.2 = (f32[48,2048]{1,0:T(8,128)S(1)}, bf16[48,2048]{1,0:T(8,128)(2,1)S(1)}, bf16[48,2048]{1,0:T(8,128)(2,1)S(1)}, bf16[48,2048]{1,0:T(8,128)(2,1)S(1)}) custom-call(s32[2]{0:T(128)S(1)} %pad_add_fusion.at_ref, bf16[384,384]{1,0:T(8,128)(2,1)S(1)} %expert_hidden.1.own_ref, bf16[384,384]{1,0:T(8,128)(2,1)S(1)} %collective-permute-done.14.other_ref, ...), custom_call_target="tpu_custom_call" | custom-call | flops 603979776 | bytes 5308416 | tf_op jit(solution)/shard_map/expert_back/pallas_call | solution.py:236
  87.1 1.5 %collective-permute-start.15 = (bf16[48,2048]{1,0:T(8,128)(2,1)S(1)}, bf16[48,2048]{1,0:T(8,128)(2,1)S(1)}, u32[]{:S(2)}, u32[]{:S(2)}) collective-permute-start(bf16[48,2048]{1,0:T(8,128)(2,1)S(1)} %get-tuple-element.31), channel_id=1, source_target_pairs={{0,2},{1,3},{2,0},{3,1},{4,6},{5,7},{6,4},{7,5},{8,10},{9,11},{10,... | collective-permute-start | bytes 589832 | tf_op jit(solution)/shard_map/ppermute | solution.py:262
  89.7 1.3 %collective-permute-start.17 = (bf16[48,2048]{1,0:T(8,128)(2,1)S(1)}, bf16[48,2048]{1,0:T(8,128)(2,1)S(1)}, u32[]{:S(2)}, u32[]{:S(2)}) collective-permute-start(bf16[48,2048]{1,0:T(8,128)(2,1)S(1)} %get-tuple-element.33), channel_id=1, source_target_pairs={{0,6},{1,7},{2,4},{3,5},{4,2},{5,3},{6,0},{7,1},{8,14},{9,15},{10,... | collective-permute-start | bytes 589832 | tf_op jit(solution)/shard_map/ppermute | solution.py:262
  91.1 3.8 %collective-permute-done.20 = bf16[48,2048]{1,0:T(8,128)(2,1)S(1)} collective-permute-done((bf16[48,2048]{1,0:T(8,128)(2,1)S(1)}, bf16[48,2048]{1,0:T(8,128)(2,1)S(1)}, u32[]{:S(2)}, u32[]{:S(2)}) %collective-permute-start.20) | collective-permute-done | bytes 196640 | tf_op jit(solution)/shard_map/ppermute | solution.py:262
  95.0 1.8 %collective-permute-start.22 = (bf16[24,2048]{1,0:T(8,128)(2,1)S(1)}, bf16[24,2048]{1,0:T(8,128)(2,1)S(1)}, u32[]{:S(2)}, u32[]{:S(2)}) collective-permute-start(bf16[24,2048]{1,0:T(8,128)(2,1)S(1)} %get-tuple-element.38), channel_id=1, source_target_pairs={{0,8},{1,9},{2,10},{3,11},{4,12},{5,13},{6,14},{7,15},{8,0},{9,1},... | collective-permute-start | bytes 294920 | tf_op jit(solution)/shard_map/ppermute | solution.py:262
  96.7 2.2 %collective-permute-start.23 = (bf16[24,2048]{1,0:T(8,128)(2,1)S(1)}, bf16[24,2048]{1,0:T(8,128)(2,1)S(1)}, u32[]{:S(2)}, u32[]{:S(2)}) collective-permute-start(bf16[24,2048]{1,0:T(8,128)(2,1)S(1)} %get-tuple-element.39), channel_id=1, source_target_pairs={{0,24},{1,25},{2,26},{3,27},{4,28},{5,29},{6,30},{7,31},{8,16},{9,... | collective-permute-start | bytes 294920 | tf_op jit(solution)/shard_map/ppermute | solution.py:262
  99.0 3.8 %collective-permute-done.16 = bf16[48,2048]{1,0:T(8,128)(2,1)S(1)} collective-permute-done((bf16[48,2048]{1,0:T(8,128)(2,1)S(1)}, bf16[48,2048]{1,0:T(8,128)(2,1)S(1)}, u32[]{:S(2)}, u32[]{:S(2)}) %collective-permute-start.16) | collective-permute-done | bytes 196640 | tf_op jit(solution)/shard_map/ppermute | solution.py:262
  102.8 2.4 %collective-permute-start.18 = (bf16[24,2048]{1,0:T(8,128)(2,1)S(1)}, bf16[24,2048]{1,0:T(8,128)(2,1)S(1)}, u32[]{:S(2)}, u32[]{:S(2)}) collective-permute-start(bf16[24,2048]{1,0:T(8,128)(2,1)S(1)} %slice.33), channel_id=1, source_target_pairs={{0,16},{1,17},{2,18},{3,19},{4,20},{5,21},{6,22},{7,23},{8,24},{9,... | collective-permute-start | bytes 294920 | tf_op jit(solution)/shard_map/ppermute | solution.py:262
  106.8 3.0 %attention.1 = bf16[8,3,32,128]{3,2,1,0:T(8,128)(2,1)} custom-call(s32[1]{0:T(128)} %bitcast.me_ref, s32[16,16]{1,0:T(8,128)S(1)} %reshape.38.owner_ref, s32[16,16]{1,0:T(8,128)S(1)} %reshape.39.slot_ref, s32[16,16]{1,0:T(8,128)S(1)} %reshape.40.fill_ref, bf16[8,3,32,128]{3,2,1,0:T(8,128)(2,1)S(1)} %copy-done.27, ...), custom_call_target="tpu_custom_call" | custom-call | tf_op jit(solution)/shard_map/attention/pallas_call | solution.py:357
  (112 shorter events, 23.1 us)
Async XLA Ops:
  2.4 19.1 %collective-permute-start.6 = (bf16[24,2176]{1,0:T(8,128)(2,1)}, bf16[24,2176]{1,0:T(8,128)(2,1)S(1)}, u32[]{:S(2)}, u32[]{:S(2)}) collective-permute-start(bf16[24,2176]{1,0:T(8,128)(2,1)} %pack_tokens.1), channel_id=1, source_target_pairs={{0,24},{1,25},{2,26},{3,27},{4,28},{5,29},{6,30},{7,31},{8,16},{9,... | collective-permute-start | bytes 313352 | tf_op jit(solution)/shard_map/ppermute | solution.py:262
  7.4 14.1 %collective-permute-start.5 = (bf16[24,2176]{1,0:T(8,128)(2,1)}, bf16[24,2176]{1,0:T(8,128)(2,1)S(1)}, u32[]{:S(2)}, u32[]{:S(2)}) collective-permute-start(bf16[24,2176]{1,0:T(8,128)(2,1)} %pack_tokens.1), channel_id=1, source_target_pairs={{0,8},{1,9},{2,10},{3,11},{4,12},{5,13},{6,14},{7,15},{8,0},{9,1},... | collective-permute-start | bytes 313352 | tf_op jit(solution)/shard_map/ppermute | solution.py:262
  7.4 9.0 %collective-permute-start = (bf16[24,2176]{1,0:T(8,128)(2,1)}, bf16[24,2176]{1,0:T(8,128)(2,1)S(1)}, u32[]{:S(2)}, u32[]{:S(2)}) collective-permute-start(bf16[24,2176]{1,0:T(8,128)(2,1)} %pack_tokens.1), channel_id=1, source_target_pairs={{0,16},{1,17},{2,18},{3,19},{4,20},{5,21},{6,22},{7,23},{8,24},{9,... | collective-permute-start | bytes 313352 | tf_op jit(solution)/shard_map/ppermute | solution.py:262
  18.0 23.7 %collective-permute-start.3 = (bf16[48,2176]{1,0:T(8,128)(2,1)}, bf16[48,2176]{1,0:T(8,128)(2,1)}, u32[]{:S(2)}, u32[]{:S(2)}) collective-permute-start(bf16[48,2176]{1,0:T(8,128)(2,1)} %pad_maximum_fusion), channel_id=1, source_target_pairs={{0,6},{1,7},{2,4},{3,5},{4,2},{5,3},{6,0},{7,1},{8,14},{9,15},{10,... | collective-permute-start | bytes 626696 | tf_op jit(solution)/shard_map/ppermute | solution.py:262
  20.5 19.6 %collective-permute-start.2 = (bf16[48,2176]{1,0:T(8,128)(2,1)}, bf16[48,2176]{1,0:T(8,128)(2,1)}, u32[]{:S(2)}, u32[]{:S(2)}) collective-permute-start(bf16[48,2176]{1,0:T(8,128)(2,1)} %pad_maximum_fusion), channel_id=1, source_target_pairs={{0,4},{1,5},{2,6},{3,7},{4,0},{5,1},{6,2},{7,3},{8,12},{9,13},{10,... | collective-permute-start | bytes 626696 | tf_op jit(solution)/shard_map/ppermute | solution.py:262
  21.0 17.4 %collective-permute-start.1 = (bf16[48,2176]{1,0:T(8,128)(2,1)}, bf16[48,2176]{1,0:T(8,128)(2,1)}, u32[]{:S(2)}, u32[]{:S(2)}) collective-permute-start(bf16[48,2176]{1,0:T(8,128)(2,1)} %pad_maximum_fusion), channel_id=1, source_target_pairs={{0,2},{1,3},{2,0},{3,1},{4,6},{5,7},{6,4},{7,5},{8,10},{9,11},{10,... | collective-permute-start | bytes 626696 | tf_op jit(solution)/shard_map/ppermute | solution.py:262
  27.0 31.5 %copy-start.1 = (bf16[1,4096,384]{2,1,0:T(8,128)(2,1)S(1)}, bf16[1,4096,384]{2,1,0:T(8,128)(2,1)}, u32[]{:S(2)}) copy-start(bf16[1,4096,384]{2,1,0:T(8,128)(2,1)} %refs_5_.3) | copy-start | bytes 9437188
  31.9 35.8 %all-to-all-start = ((bf16[32,2,2,16,128]{4,3,2,1,0:T(8,128)(2,1)}), bf16[32,2,2,16,128]{4,3,2,1,0:T(8,128)(2,1)}, u32[]{:S(2)}, u32[]{:S(2)}) async-start(bf16[32,2,2,16,128]{4,3,2,1,0:T(8,128)(2,1)} %copy-done.8), calls=%async_computation | async-start | bytes 1048576 | tf_op jit(solution)/shard_map/all_to_all | solution.py:334
  43.3 24.5 %collective-permute-start.4 = (bf16[192,2176]{1,0:T(8,128)(2,1)}, bf16[192,2176]{1,0:T(8,128)(2,1)}, u32[]{:S(2)}, u32[]{:S(2)}) collective-permute-start(bf16[192,2176]{1,0:T(8,128)(2,1)} %constant_dynamic-update-slice_fusion.refs_0_), channel_id=1, source_target_pairs={{0,1},{1,0},{2,3},{3,2},{4,5},{5,4},{6,7},{7,6},{8,9},{9,8},{10,11... | collective-permute-start | bytes 2506760 | tf_op jit(solution)/shard_map/ppermute | solution.py:262
  43.3 11.0 %collective-permute-start.12 = (bf16[48,2176]{1,0:T(8,128)(2,1)S(1)}, bf16[48,2176]{1,0:T(8,128)(2,1)S(1)}, u32[]{:S(2)}, u32[]{:S(2)}) collective-permute-start(bf16[48,2176]{1,0:T(8,128)(2,1)S(1)} %pad_maximum_fusion.1.refs_1_.refs_0_), channel_id=1, source_target_pairs={{0,6},{1,7},{2,4},{3,5},{4,2},{5,3},{6,0},{7,1},{8,14},{9,15},{10,... | collective-permute-start | bytes 626696 | tf_op jit(solution)/shard_map/ppermute | solution.py:262
  46.1 11.9 %collective-permute-start.10 = (bf16[48,2176]{1,0:T(8,128)(2,1)S(1)}, bf16[48,2176]{1,0:T(8,128)(2,1)S(1)}, u32[]{:S(2)}, u32[]{:S(2)}) collective-permute-start(bf16[48,2176]{1,0:T(8,128)(2,1)S(1)} %pad_maximum_fusion.1.refs_1_.refs_0_), channel_id=1, source_target_pairs={{0,4},{1,5},{2,6},{3,7},{4,0},{5,1},{6,2},{7,3},{8,12},{9,13},{10,... | collective-permute-start | bytes 626696 | tf_op jit(solution)/shard_map/ppermute | solution.py:262
  46.6 11.7 %collective-permute-start.8 = (bf16[48,2176]{1,0:T(8,128)(2,1)S(1)}, bf16[48,2176]{1,0:T(8,128)(2,1)S(1)}, u32[]{:S(2)}, u32[]{:S(2)}) collective-permute-start(bf16[48,2176]{1,0:T(8,128)(2,1)S(1)} %pad_maximum_fusion.1.refs_1_.refs_0_), channel_id=1, source_target_pairs={{0,2},{1,3},{2,0},{3,1},{4,6},{5,7},{6,4},{7,5},{8,10},{9,11},{10,... | collective-permute-start | bytes 626696 | tf_op jit(solution)/shard_map/ppermute | solution.py:262
  46.8 18.2 %collective-permute-start.7 = (bf16[48,2176]{1,0:T(8,128)(2,1)S(1)}, bf16[48,2176]{1,0:T(8,128)(2,1)S(1)}, u32[]{:S(2)}, u32[]{:S(2)}) collective-permute-start(bf16[48,2176]{1,0:T(8,128)(2,1)S(1)} %pad_maximum_fusion.1.refs_1_.refs_0_), channel_id=1, source_target_pairs={{0,1},{1,0},{2,3},{3,2},{4,5},{5,4},{6,7},{7,6},{8,9},{9,8},{10,11... | collective-permute-start | bytes 626696 | tf_op jit(solution)/shard_map/ppermute | solution.py:262
  54.3 9.0 %copy-start.9 = (bf16[48,2176]{1,0:T(8,128)(2,1)}, bf16[48,2176]{1,0:T(8,128)(2,1)S(1)}, u32[]{:S(2)}) copy-start(bf16[48,2176]{1,0:T(8,128)(2,1)S(1)} %collective-permute-done.12.refs_4_.refs_3_) | copy-start | bytes 626692
  54.3 11.4 %collective-permute-start.13 = (bf16[48,2176]{1,0:T(8,128)(2,1)S(1)}, bf16[48,2176]{1,0:T(8,128)(2,1)S(1)}, u32[]{:S(2)}, u32[]{:S(2)}) collective-permute-start(bf16[48,2176]{1,0:T(8,128)(2,1)S(1)} %collective-permute-done.12.refs_4_.refs_3_), channel_id=1, source_target_pairs={{0,1},{1,0},{2,3},{3,2},{4,5},{5,4},{6,7},{7,6},{8,9},{9,8},{10,11... | collective-permute-start | bytes 626696 | tf_op jit(solution)/shard_map/ppermute | solution.py:262
  57.9 8.5 %collective-permute-start.11 = (bf16[48,2176]{1,0:T(8,128)(2,1)S(1)}, bf16[48,2176]{1,0:T(8,128)(2,1)S(1)}, u32[]{:S(2)}, u32[]{:S(2)}) collective-permute-start(bf16[48,2176]{1,0:T(8,128)(2,1)S(1)} %collective-permute-done.10.refs_3_.refs_2_), channel_id=1, source_target_pairs={{0,1},{1,0},{2,3},{3,2},{4,5},{5,4},{6,7},{7,6},{8,9},{9,8},{10,11... | collective-permute-start | bytes 626696 | tf_op jit(solution)/shard_map/ppermute | solution.py:262
  58.4 8.7 %collective-permute-start.9 = (bf16[48,2176]{1,0:T(8,128)(2,1)S(1)}, bf16[48,2176]{1,0:T(8,128)(2,1)S(1)}, u32[]{:S(2)}, u32[]{:S(2)}) collective-permute-start(bf16[48,2176]{1,0:T(8,128)(2,1)S(1)} %collective-permute-done.8.refs_2_.refs_1_), channel_id=1, source_target_pairs={{0,1},{1,0},{2,3},{3,2},{4,5},{5,4},{6,7},{7,6},{8,9},{9,8},{10,11... | collective-permute-start | bytes 626696 | tf_op jit(solution)/shard_map/ppermute | solution.py:262
  78.7 1.7 %collective-permute-start.14 = (bf16[384,384]{1,0:T(8,128)(2,1)S(1)}, bf16[384,384]{1,0:T(8,128)(2,1)S(1)}, u32[]{:S(2)}, u32[]{:S(2)}) collective-permute-start(bf16[384,384]{1,0:T(8,128)(2,1)S(1)} %expert_hidden.1.own_ref), channel_id=1, source_target_pairs={{0,1},{1,0},{2,3},{3,2},{4,5},{5,4},{6,7},{7,6},{8,9},{9,8},{10,11... | collective-permute-start | bytes 884744 | tf_op jit(solution)/shard_map/ppermute | solution.py:262
  81.9 7.8 %collective-permute-start.19 = (bf16[48,2048]{1,0:T(8,128)(2,1)S(1)}, bf16[48,2048]{1,0:T(8,128)(2,1)S(1)}, u32[]{:S(2)}, u32[]{:S(2)}) collective-permute-start(bf16[48,2048]{1,0:T(8,128)(2,1)S(1)} %get-tuple-element.35), channel_id=1, source_target_pairs={{0,2},{1,3},{2,0},{3,1},{4,6},{5,7},{6,4},{7,5},{8,10},{9,11},{10,... | collective-permute-start | bytes 589832 | tf_op jit(solution)/shard_map/ppermute | solution.py:262
  83.4 11.4 %collective-permute-start.20 = (bf16[48,2048]{1,0:T(8,128)(2,1)S(1)}, bf16[48,2048]{1,0:T(8,128)(2,1)S(1)}, u32[]{:S(2)}, u32[]{:S(2)}) collective-permute-start(bf16[48,2048]{1,0:T(8,128)(2,1)S(1)} %get-tuple-element.36), channel_id=1, source_target_pairs={{0,4},{1,5},{2,6},{3,7},{4,0},{5,1},{6,2},{7,3},{8,12},{9,13},{10,... | collective-permute-start | bytes 589832 | tf_op jit(solution)/shard_map/ppermute | solution.py:262
  83.9 21.9 %copy-start.29 = (s32[256,1]{0,1:T(1,128)S(1)}, s32[256,1]{0,1:T(1,128)}, u32[]{:S(2)}) copy-start(s32[256,1]{0,1:T(1,128)} %param.13) | copy-start | bytes 3076
  83.9 22.6 %copy-start.31 = (s32[256]{0:T(256)S(1)}, s32[256]{0:T(256)}, u32[]{:S(2)}) copy-start(s32[256]{0:T(256)} %param.14) | copy-start | bytes 3076
  83.9 22.7 %copy-start.32 = (s32[256]{0:T(256)S(1)}, s32[256]{0:T(256)}, u32[]{:S(2)}) copy-start(s32[256]{0:T(256)} %param.15) | copy-start | bytes 3076
  83.9 22.8 %copy-start.30 = (bf16[8,3,2,2,128]{4,3,2,1,0:T(2,128)(2,1)S(1)}, bf16[8,3,2,2,128]{4,3,2,1,0:T(2,128)(2,1)}, u32[]{:S(2)}) copy-start(bf16[8,3,2,2,128]{4,3,2,1,0:T(2,128)(2,1)} %param.17) | copy-start | bytes 73732
  83.9 22.8 %copy-start.27 = (bf16[8,3,32,128]{3,2,1,0:T(8,128)(2,1)S(1)}, bf16[8,3,32,128]{3,2,1,0:T(8,128)(2,1)}, u32[]{:S(2)}) copy-start(bf16[8,3,32,128]{3,2,1,0:T(8,128)(2,1)} %q_ref.1) | copy-start | bytes 589828
  83.9 10.9 %collective-permute-start.21 = (bf16[48,2048]{1,0:T(8,128)(2,1)S(1)}, bf16[48,2048]{1,0:T(8,128)(2,1)S(1)}, u32[]{:S(2)}, u32[]{:S(2)}) collective-permute-start(bf16[48,2048]{1,0:T(8,128)(2,1)S(1)} %get-tuple-element.37), channel_id=1, source_target_pairs={{0,6},{1,7},{2,4},{3,5},{4,2},{5,3},{6,0},{7,1},{8,14},{9,15},{10,... | collective-permute-start | bytes 589832 | tf_op jit(solution)/shard_map/ppermute | solution.py:262
  87.1 11.8 %collective-permute-start.15 = (bf16[48,2048]{1,0:T(8,128)(2,1)S(1)}, bf16[48,2048]{1,0:T(8,128)(2,1)S(1)}, u32[]{:S(2)}, u32[]{:S(2)}) collective-permute-start(bf16[48,2048]{1,0:T(8,128)(2,1)S(1)} %get-tuple-element.31), channel_id=1, source_target_pairs={{0,2},{1,3},{2,0},{3,1},{4,6},{5,7},{6,4},{7,5},{8,10},{9,11},{10,... | collective-permute-start | bytes 589832 | tf_op jit(solution)/shard_map/ppermute | solution.py:262
  88.6 14.1 %collective-permute-start.16 = (bf16[48,2048]{1,0:T(8,128)(2,1)S(1)}, bf16[48,2048]{1,0:T(8,128)(2,1)S(1)}, u32[]{:S(2)}, u32[]{:S(2)}) collective-permute-start(bf16[48,2048]{1,0:T(8,128)(2,1)S(1)} %get-tuple-element.32), channel_id=1, source_target_pairs={{0,4},{1,5},{2,6},{3,7},{4,0},{5,1},{6,2},{7,3},{8,12},{9,13},{10,... | collective-permute-start | bytes 589832 | tf_op jit(solution)/shard_map/ppermute | solution.py:262
  89.7 13.0 %collective-permute-start.17 = (bf16[48,2048]{1,0:T(8,128)(2,1)S(1)}, bf16[48,2048]{1,0:T(8,128)(2,1)S(1)}, u32[]{:S(2)}, u32[]{:S(2)}) collective-permute-start(bf16[48,2048]{1,0:T(8,128)(2,1)S(1)} %get-tuple-element.33), channel_id=1, source_target_pairs={{0,6},{1,7},{2,4},{3,5},{4,2},{5,3},{6,0},{7,1},{8,14},{9,15},{10,... | collective-permute-start | bytes 589832 | tf_op jit(solution)/shard_map/ppermute | solution.py:262
  95.0 14.7 %collective-permute-start.22 = (bf16[24,2048]{1,0:T(8,128)(2,1)S(1)}, bf16[24,2048]{1,0:T(8,128)(2,1)S(1)}, u32[]{:S(2)}, u32[]{:S(2)}) collective-permute-start(bf16[24,2048]{1,0:T(8,128)(2,1)S(1)} %get-tuple-element.38), channel_id=1, source_target_pairs={{0,8},{1,9},{2,10},{3,11},{4,12},{5,13},{6,14},{7,15},{8,0},{9,1},... | collective-permute-start | bytes 294920 | tf_op jit(solution)/shard_map/ppermute | solution.py:262
  96.7 13.0 %collective-permute-start.23 = (bf16[24,2048]{1,0:T(8,128)(2,1)S(1)}, bf16[24,2048]{1,0:T(8,128)(2,1)S(1)}, u32[]{:S(2)}, u32[]{:S(2)}) collective-permute-start(bf16[24,2048]{1,0:T(8,128)(2,1)S(1)} %get-tuple-element.39), channel_id=1, source_target_pairs={{0,24},{1,25},{2,26},{3,27},{4,28},{5,29},{6,30},{7,31},{8,16},{9,... | collective-permute-start | bytes 294920 | tf_op jit(solution)/shard_map/ppermute | solution.py:262
  102.8 6.9 %collective-permute-start.18 = (bf16[24,2048]{1,0:T(8,128)(2,1)S(1)}, bf16[24,2048]{1,0:T(8,128)(2,1)S(1)}, u32[]{:S(2)}, u32[]{:S(2)}) collective-permute-start(bf16[24,2048]{1,0:T(8,128)(2,1)S(1)} %slice.33), channel_id=1, source_target_pairs={{0,16},{1,17},{2,18},{3,19},{4,20},{5,21},{6,22},{7,23},{8,24},{9,... | collective-permute-start | bytes 294920 | tf_op jit(solution)/shard_map/ppermute | solution.py:262
  (26 other events, 57.2 us)

commit v7 on v4

--- a/solution.py
+++ b/solution.py
@@ -57,7 +57,7 @@
 
 
 def attention_kernel(
-    pages, me_ref, owner_ref, slot_ref, fill_ref, q_ref, cache_ref, fresh_ref, out_ref
+    pages, me_ref, owner_ref, slot_ref, fill_ref, q_ref, cache_ref, fresh_ref, after_ref, out_ref
 ):
     owners = owner_ref.shape[0]
     slots, _, heads, page_len, width = cache_ref.shape
@@ -140,20 +140,19 @@
     out_ref[:, half:] = jnp.where(part < 3, chosen, 0.0).astype(out_ref.dtype)
 
 
-def partial_kernel(chunks, core_ref, sr_ref, r2_ref, gate_ref, up_ref, gate_sum, up_sum):
+def partial_kernel(chunks, core_ref, x_ref, gate_ref, up_ref, gate_sum, up_sum):
     half = gate_ref.shape[1] // 2
     depth = half // chunks
     for c in range(chunks):
         at = slice(c * depth, (c + 1) * depth)
         rows = pl.ds(pl.multiple_of(core_ref[0] * half + c * depth, 128), depth)
-        x = jnp.concatenate([sr_ref[:, at], r2_ref[:, at]], axis=0)
         for weight, total in ((gate_ref, gate_sum), (up_ref, up_sum)):
-            part = jnp.dot(x, weight[0, rows], preferred_element_type=jnp.float32)
+            part = jnp.dot(x_ref[:, at], weight[0, rows], preferred_element_type=jnp.float32)
             total[...] = part if c == 0 else total[...] + part
 
 
 def hidden_kernel(
-    chunks, core_ref, sr_ref, r2_ref, gate_ref, up_ref, gate_part, up_part, out_ref, sums
+    chunks, core_ref, sr_ref, r2_ref, gate_ref, up_ref, g0_ref, u0_ref, g1_ref, u1_ref, out_ref, sums
 ):
     half = gate_ref.shape[1] // 2
     depth = half // chunks
@@ -165,9 +164,15 @@
             [sr_ref[:group, at], r2_ref[:group, at], sr_ref[group:, at], r2_ref[group:, at]],
             axis=0,
         )
-        for i, (weight, start) in enumerate(((gate_ref, gate_part), (up_ref, up_part))):
+        for i, (weight, early, late) in enumerate(
+            ((gate_ref, g0_ref, g1_ref), (up_ref, u0_ref, u1_ref))
+        ):
             part = jnp.dot(x, weight[0, rows], preferred_element_type=jnp.float32)
-            sums[i] = (start[...] if c == 0 else sums[i]) + part
+            if c == 0:
+                sums[i, : 2 * group] = early[...] + part[: 2 * group]
+                sums[i, 2 * group :] = late[...] + part[2 * group :]
+            else:
+                sums[i] += part
     gate = sums[0]
     out_ref[...] = (gate / (1.0 + jnp.exp(-gate)) * sums[1]).astype(out_ref.dtype)
 
@@ -176,52 +181,74 @@
     return sum(math.prod(a.shape) * a.dtype.itemsize for a in arrays) * 9 // 8 + 4 * MIB
 
 
-def expert_front(core, rows, w_gate, w_up, parts):
-    tokens = 2 * rows[0].shape[0]
+def expert_partial(core, x, w_gate, w_up):
+    tokens = x.shape[0]
     d, f = w_gate.shape[1:]
-    last = parts is not None
     total = jax.ShapeDtypeStruct((tokens, f), jnp.float32)
-    scratch = [pltpu.VMEM((2, tokens, f), jnp.float32)] if last else []
     return pl.pallas_call(
-        functools.partial(hidden_kernel if last else partial_kernel, 4),
-        in_specs=[smem()] + [vmem()] * (6 if last else 4),
-        out_specs=vmem() if last else [vmem(), vmem()],
-        scratch_shapes=scratch,
-        out_shape=jax.ShapeDtypeStruct((tokens, f), jnp.bfloat16) if last else [total, total],
-        compiler_params=pltpu.CompilerParams(
-            vmem_limit_bytes=room(*rows, w_gate, w_up, *[total] * (5 if last else 2))
-        ),
+        functools.partial(partial_kernel, 4),
+        in_specs=[smem()] + [vmem()] * 3,
+        out_specs=[vmem(), vmem()],
+        out_shape=[total, total],
+        compiler_params=pltpu.CompilerParams(vmem_limit_bytes=room(x, w_gate, w_up, total, total)),
         cost_estimate=pl.CostEstimate(
             flops=2 * tokens * d * f,
             bytes_accessed=tokens * d + 2 * d * f + 8 * tokens * f,
-            transcendentals=tokens * f if last else 0,
-        ),
-        name="expert_hidden" if last else "expert_partial",
-    )(core, *rows, w_gate, w_up, *(parts or ()))
+            transcendentals=0,
+        ),
+        name="expert_partial",
+    )(core, x, w_gate, w_up)
+
+
+def expert_hidden(core, sr, r2, w_gate, w_up, parts):
+    tokens = 2 * sr.shape[0]
+    d, f = w_gate.shape[1:]
+    total = jax.ShapeDtypeStruct((tokens, f), jnp.float32)
+    return pl.pallas_call(
+        functools.partial(hidden_kernel, 4),
+        in_specs=[smem()] + [vmem()] * 8,
+        out_specs=vmem(),
+        out_shape=jax.ShapeDtypeStruct((tokens, f), jnp.bfloat16),
+        scratch_shapes=[pltpu.VMEM((2, tokens, f), jnp.float32)],
+        compiler_params=pltpu.CompilerParams(
+            vmem_limit_bytes=room(sr, r2, w_gate, w_up, *[total] * 5)
+        ),
+        cost_estimate=pl.CostEstimate(
+            flops=2 * tokens * d * f,
+            bytes_accessed=tokens * d + 2 * d * f + 10 * tokens * f,
+            transcendentals=tokens * f,
+        ),
+        name="expert_hidden",
+    )(core, sr, r2, w_gate, w_up, *parts)
 
 
 def back_kernel(
-    send, experts, lanes, chunks, at_ref, own_ref, other_ref, sr_ref, r2_ref, down_ref, out_ref
+    experts, begin, chunks, at_ref, own_ref, other_ref, sr_ref, r2_ref, down_ref, keep_ref, *send_refs
 ):
     block = down_ref.shape[2] // chunks
     f = own_ref.shape[1]
+    piece = keep_ref.shape[0]
     group = sr_ref.shape[0] // 2
+    lanes = 128 * (-(-3 * experts // 128))
     core = at_ref[1]
-    first = int(send)
-
-    def rows(ref, a, b):
+
+    def rows(ref, order):
         return jnp.concatenate(
-            [ref[a * group : (a + 1) * group], ref[b * group : (b + 1) * group]], axis=0
-        )
-
-    own = rows(own_ref, 1, 3) if send else rows(own_ref, 0, 2)
-    other = rows(other_ref, 2, 3) if send else rows(other_ref, 0, 1)
-    begin = pl.multiple_of(core * f, 128)
+            [ref[i * group + begin : i * group + begin + piece] for i in order], axis=0
+        )
+
+    own = rows(own_ref, (0, 1, 2, 3))
+    other = rows(other_ref, (0, 2, 1, 3))
+    first = pl.multiple_of(core * f, 128)
     rest = pl.multiple_of((1 - core) * f, 128)
-    tail = slice(sr_ref.shape[1] - lanes, sr_ref.shape[1])
-    picked = slice(first * group, (first + 1) * group)
     probs = jnp.concatenate(
-        [sr_ref[picked, tail].astype(jnp.float32), r2_ref[picked, tail].astype(jnp.float32)],
+        [
+            ref[i * group + begin : i * group + begin + piece, ref.shape[1] - lanes :].astype(
+                jnp.float32
+            )
+            for ref in (sr_ref, r2_ref)
+            for i in (0, 1)
+        ],
         axis=0,
     )
     lane = lax.broadcasted_iota(jnp.int32, probs.shape, 1)
@@ -229,32 +256,36 @@
     weight = jnp.sum(jnp.where(mine, probs, 0.0), axis=1, keepdims=True)
     for c in range(chunks):
         at = slice(c * block, (c + 1) * block)
-        total = jnp.dot(own, down_ref[0, pl.ds(begin, f), at], preferred_element_type=jnp.float32)
+        total = jnp.dot(own, down_ref[0, pl.ds(first, f), at], preferred_element_type=jnp.float32)
         total += jnp.dot(
             other, down_ref[0, pl.ds(rest, f), at], preferred_element_type=jnp.float32
         )
-        out_ref[:, at] = (total * weight).astype(out_ref.dtype)
-
-
-def expert_back(send, experts, at, own, other, w_down, sr, r2, lanes):
-    tokens, f = own.shape
-    group2 = sr.shape[0]
+        total = total * weight
+        keep_ref[:, at] = total[:piece]
+        for i, ref in enumerate(send_refs):
+            ref[:, at] = total[(i + 1) * piece : (i + 2) * piece].astype(ref.dtype)
+
+
+def expert_back(experts, begin, piece, at, own, other, w_down, sr, r2):
+    f = own.shape[1]
     width = w_down.shape[2]
-    out = jax.ShapeDtypeStruct((group2, width), jnp.bfloat16 if send else jnp.float32)
+    rows = 4 * piece
+    send = jax.ShapeDtypeStruct((piece, width), jnp.bfloat16)
+    keep = jax.ShapeDtypeStruct((piece, width), jnp.float32)
     return pl.pallas_call(
-        functools.partial(back_kernel, send, experts, lanes, 4),
-        out_shape=out,
+        functools.partial(back_kernel, experts, begin, 4),
+        out_shape=[keep, send, send, send],
         in_specs=[smem()] + [vmem()] * 5,
-        out_specs=vmem(),
+        out_specs=[vmem()] * 4,
         compiler_params=pltpu.CompilerParams(
-            vmem_limit_bytes=room(own, other, w_down, sr, r2, out, out)
+            vmem_limit_bytes=room(own, other, w_down, sr, r2, *[keep] * 4)
         ),
         cost_estimate=pl.CostEstimate(
-            flops=2 * tokens * f * width,
-            bytes_accessed=2 * (2 * tokens * f + 2 * f * width + 2 * group2 * width),
+            flops=4 * rows * f * width,
+            bytes_accessed=2 * (4 * rows * f + 2 * f * width + 2 * rows * width),
             transcendentals=0,
         ),
-        name="expert_back_send" if send else "expert_back_keep",
+        name="expert_back",
     )(at, own, other, sr, r2, w_down)
 
 
@@ -269,11 +300,14 @@
         ]
         return lax.ppermute(x, ("ep", "pd"), perm)
 
-    def along_z(self, x, shift):
-        return self.go(x, lambda ep, core: (ep + 4 * shift) % self.owners * 2 + core)
+    def along_z(self, x, turn):
+        return self.go(x, lambda ep, core: (ep ^ (4 * turn)) * 2 + core)
 
     def flip(self, x, turn):
         return self.go(x, lambda ep, core: (ep ^ (1 << ((core + turn) % 2))) * 2 + core)
+
+    def diagonal(self, x):
+        return self.go(x, lambda ep, core: (ep ^ 3) * 2 + core)
 
     def cores(self, x):
         return self.go(x, lambda ep, core: ep * 2 + 1 - core)
@@ -323,36 +357,45 @@
     send = pl.pallas_call(
         functools.partial(page_kernel, pages),
         out_shape=jax.ShapeDtypeStruct((slots, 2, heads, page_len, width), jnp.bfloat16),
-        in_specs=[smem(), smem(), vmem()],
+        in_specs=[smem(), smem()] + [vmem()],
         out_specs=vmem(),
         scratch_shapes=[pltpu.SMEM((owners,), jnp.int32)],
-        compiler_params=pltpu.CompilerParams(vmem_limit_bytes=room(prompt_kv) * 4),
+        compiler_params=pltpu.CompilerParams(vmem_limit_bytes=room(*[prompt_kv] * 5)),
         name="quantize_pages",
     )(me_ref, page_owner.reshape(-1), prompt_kv.transpose(0, 1, 3, 2, 4))
-    line = [mine] + [moves.along_z(mine, -shift) for shift in range(1, moves.lines)]
+
+    sets = [range(0, moves.lines, 2), range(1, moves.lines, 2)]
+    line = [moves.along_z(mine, turn) if turn else mine for chips in sets for turn in chips]
     line = jnp.concatenate(line, axis=0)
+    line, send = lax.optimization_barrier((line, send))
     fresh = new_kv.transpose(2, 3, 0, 1, 4).reshape(2, heads, tokens, width)
     fresh = jnp.pad(fresh, ((0, 0), (0, 0), (0, 128 - tokens), (0, 0)))
     tables = [t.reshape(owners, pages) for t in (page_owner, page_slot, page_fill)]
-    line, send = lax.optimization_barrier((line, send))
     sr = jnp.concatenate([line, moves.flip(line, 0)], axis=0)
     sr, fresh, tables = lax.optimization_barrier((sr, fresh, tables))
     r2 = moves.flip(sr, 1)
+
     cache = lax.all_to_all(send, "ep", split_axis=0, concat_axis=0, tiled=True)
-    r2, cache = lax.optimization_barrier((r2, cache))
+
+    early = expert_partial(own_core, sr, w_gate, w_up)
+    r2, cache, early = lax.optimization_barrier((r2, cache, early))
     other_sr, other_r2 = moves.cores(sr), moves.cores(r2)
-
-    parts = expert_front(own_core, (sr, r2), w_gate, w_up, None)
-    hidden = expert_front(own_core, (other_sr, other_r2), w_gate, w_up, parts)
+    parts = early + expert_partial(own_core, r2, w_gate, w_up)
+    hidden = expert_hidden(own_core, other_sr, other_r2, w_gate, w_up, parts)
     other_hidden = moves.cores(hidden)
-    sent = expert_back(True, owners, at, hidden, other_hidden, w_down, sr, r2, lanes)
-    kept = expert_back(False, owners, at, hidden, other_hidden, w_down, sr, r2, lanes)
+    piece = line.shape[0] // 2
+    backs = [
+        expert_back(owners, begin, piece, at, hidden, other_hidden, w_down, sr, r2)
+        for begin in (piece, 0)
+    ]
     attn_out = pl.pallas_call(
         functools.partial(attention_kernel, pages),
         out_shape=jax.ShapeDtypeStruct(queries.shape, jnp.bfloat16),
-        in_specs=[smem()] + [vmem()] * 6,
+        in_specs=[smem()] + [vmem()] * 6 + [pl.BlockSpec(memory_space=pl.ANY)],
         out_specs=vmem(),
-        compiler_params=pltpu.CompilerParams(vmem_limit_bytes=8 * MIB + 16 * slots * page_len * tokens * q_heads),
+        compiler_params=pltpu.CompilerParams(
+            vmem_limit_bytes=8 * MIB + 16 * slots * page_len * tokens * q_heads
+        ),
         name="attention",
     )(
         me_ref,
@@ -360,15 +403,20 @@
         queries,
         cache,
         fresh,
+        backs[1][1],
     )
-    group = moves.lines * tokens
-    kept = kept + moves.flip(sent, 0).astype(jnp.float32)
-    kept, attn_out = lax.optimization_barrier((kept, attn_out))
-    kept = kept[:group] + moves.flip(kept[group:].astype(jnp.bfloat16), 1).astype(jnp.float32)
-    moe = kept[:tokens]
-    for shift in range(1, moves.lines):
-        block = kept[shift * tokens : (shift + 1) * tokens].astype(jnp.bfloat16)
-        moe = moe + moves.along_z(block, shift).astype(jnp.float32)
+    sums = []
+    for total, *send in backs:
+        for rows in (moves.flip(send[0], 0), moves.flip(send[1], 1), moves.diagonal(send[2])):
+            total = total + rows.astype(jnp.float32)
+        sums.append(total)
+    sums[0], attn_out = lax.optimization_barrier((sums[0], attn_out))
+    moe = sums[1][:tokens]
+    for chips, rows in zip(sets, reversed(sums)):
+        for i, turn in enumerate(chips):
+            if turn:
+                block = rows[i * tokens : (i + 1) * tokens].astype(jnp.bfloat16)
+                moe = moe + moves.along_z(block, turn).astype(jnp.float32)
     moe = moe.astype(jnp.bfloat16)
     moe_out = moe.reshape(steps, requests, d // 2).transpose(1, 0, 2)
 

time: 85.9 us -> 90 us (1.048)
  waiting for transfers between devices: 36.9 us -> 20.7 us
  starting transfers between devices: 23.3 us -> 29.8 us
  Pallas kernels: 15.3 us -> 21.3 us
  local copies, waits for them, and re-layouts: 6.38 us -> 10.6 us
  other arithmetic: 2.73 us -> 6.09 us
    ppermute x13 -> x17, waiting for transfers between devices: 24.8 us -> 14.9 us  [go(): return lax.ppermute(x, ('ep', 'pd'), perm)]
    all_to_all x1, waiting for transfers between devices: 12.1 us -> 5.76 us  [body(): cache = lax.all_to_all(send, 'ep', split_axis=0, concat_axis=0, tiled=True)]
    pallas_call x4 -> x5, Pallas kernels: 6.68 us -> 12.3 us  [the longest x2 4.8 us: expert_back(): pl.pallas_call(functools.partial(back_kernel, experts, begin, 4), out_sha...]
    ppermute x13 -> x17, starting transfers between devices: 18.1 us -> 23.7 us  [go(): return lax.ppermute(x, ('ep', 'pd'), perm)]
    unnamed x22 -> x26, local copies, waits for them, and re-layouts: 6.05 us -> 8.19 us
    concatenate x1, other arithmetic: 0.06 us -> 2.1 us  [body(): sr = jnp.concatenate([line, moves.flip(line, 0)], axis=0)]
    reshape x3, local copies, waits for them, and re-layouts: 0.23 us -> 1.6 us  [body(): t.reshape(owners, pages)]
    pallas_call x1, Pallas kernels: 1.93 us -> 2.97 us  [body(): pl.pallas_call(functools.partial(attention_kernel, pages), out_shape=jax....]
  transfers between devices with their start and end apart: 14 -> 18, of which waited for: 7 -> 10; matrix products, arithmetic and copies ran while one was open for 3% -> 8% of each run, Pallas kernels for 12% -> 16%
where the time goes in v7:
time: 90 us; the launch traced here: 89.3 us
  starting transfers between devices  29.8 us (33%)
  Pallas kernels  21.3 us (24%)
  waiting for transfers between devices  20.7 us (23%)
  local copies, waits for them, and re-layouts  10.6 us (12%)
  other arithmetic  6.09 us (7%)
    ppermute x17, starting transfers between devices, go(): return lax.ppermute(x, ('ep', 'pd'), perm)  23.7 us
    ppermute x17, waiting for transfers between devices, go(): return lax.ppermute(x, ('ep', 'pd'), perm)  14.9 us
    unnamed x26, local copies, waits for them, and re-layouts  8.19 us
    all_to_all x1, starting transfers between devices, body(): cache = lax.all_to_all(send, 'ep', split_axis=0, concat_axis=0, tiled=True)  6.11 us
    all_to_all x1, waiting for transfers between devices, body(): cache = lax.all_to_all(send, 'ep', split_axis=0, concat_axis=0, tiled=True)  5.76 us
    pallas_call x2, Pallas kernels, expert_back(): pl.pallas_call(functools.partial(back_kernel, experts, begin, 4), out_sha...  4.8 us
    pallas_call x2, Pallas kernels, expert_partial(): pl.pallas_call(functools.partial(partial_kernel, 4), in_specs=[smem()] +...  4.41 us
    pallas_call x1, Pallas kernels, body(): pl.pallas_call(functools.partial(page_kernel, pages), out_shape=jax.Shape...  4.13 us
  transfers between devices with their start and end apart: 18, of which 10 were waited for; matrix products, arithmetic and copies ran while one was open for 8% of the time, Pallas kernels for 16%

profile of v7, /device:TPU:0, one launch (start us, length us, event | category | flops | bytes accessed | tf_op | source)
XLA Modules:
  0.0 89.3 jit_solution(13100576010955198277)
XLA Ops:
  0.6 1.9 %pack_tokens.1 = bf16[24,2176]{1,0:T(8,128)(2,1)} custom-call(s32[1]{0:T(128)} %bitcast.1.core_ref, bf16[24,4096]{1,0:T(8,128)(2,1)} %bitcast.23, s32[24,8]{1,0:T(8,128)} %bitcast.25, f32[24,8]{1,0:T(8,128)} %bitcast.26), custom_call_target="tpu_custom_call" | custom-call | tf_op jit(solution)/shard_map/pack_tokens/pallas_call | solution.py:345
  2.5 4.0 %collective-permute-start = (bf16[24,2176]{1,0:T(8,128)(2,1)}, bf16[24,2176]{1,0:T(8,128)(2,1)S(1)}, u32[]{:S(2)}, u32[]{:S(2)}) collective-permute-start(bf16[24,2176]{1,0:T(8,128)(2,1)} %pack_tokens.1), channel_id=1, source_target_pairs={{0,16},{1,17},{2,18},{3,19},{4,20},{5,21},{6,22},{7,23},{8,24},{9,... | collective-permute-start | bytes 313352 | tf_op jit(solution)/shard_map/ppermute | solution.py:301
  6.6 1.6 %collective-permute-start.1 = (bf16[24,2176]{1,0:T(8,128)(2,1)}, bf16[24,2176]{1,0:T(8,128)(2,1)S(1)}, u32[]{:S(2)}, u32[]{:S(2)}) collective-permute-start(bf16[24,2176]{1,0:T(8,128)(2,1)} %pack_tokens.1), channel_id=1, source_target_pairs={{0,8},{1,9},{2,10},{3,11},{4,12},{5,13},{6,14},{7,15},{8,0},{9,1},... | collective-permute-start | bytes 313352 | tf_op jit(solution)/shard_map/ppermute | solution.py:301
  8.1 1.0 %copy.22 = bf16[16,2,16,2,128]{4,2,3,1,0:T(8,128)(2,1)S(1)} copy(bf16[16,2,16,2,128]{4,3,2,1,0:T(2,128)(2,1)} %param.12) | data formatting | bytes 524288 | tf_op args[0]
  9.8 4.1 %quantize_pages.1 = bf16[32,2,2,16,128]{4,3,2,1,0:T(8,128)(2,1)S(1)} custom-call(s32[1]{0:T(128)} %bitcast.me_ref, s32[256]{0:T(256)S(1)} %bitcast.22, bf16[16,2,2,16,128]{4,3,2,1,0:T(8,128)(2,1)S(1)} %bitcast.21), custom_call_target="tpu_custom_call" | custom-call | tf_op jit(solution)/shard_map/quantize_pages/pallas_call | solution.py:357
  15.3 1.7 %pad_maximum_fusion.1 = bf16[96,2176]{1,0:T(8,128)(2,1)} fusion(bf16[24,2176]{1,0:T(8,128)(2,1)S(1)} %collective-permute-done.2, bf16[24,2176]{1,0:T(8,128)(2,1)S(1)} %collective-permute-done.1, bf16[24,2176]{1,0:T(8,128)(2,1)S(1)} %collective-permute-done, bf16[24,2176]{1,0:T(8,128)(2,1)} %pack_tokens.1), kind=kLoop, calls=%fused_computation.1 | loop fusion | flops 1671168 | bytes 835584 | tf_op jit(solution)/shard_map/concatenate | solution.py:369
  17.0 1.5 %collective-permute-start.3 = (bf16[96,2176]{1,0:T(8,128)(2,1)}, bf16[96,2176]{1,0:T(8,128)(2,1)}, u32[]{:S(2)}, u32[]{:S(2)}) collective-permute-start(bf16[96,2176]{1,0:T(8,128)(2,1)} %pad_maximum_fusion.1), channel_id=1, source_target_pairs={{0,2},{1,5},{2,0},{3,7},{4,6},{5,1},{6,4},{7,3},{8,10},{9,13},{10,... | collective-permute-start | bytes 1253384 | tf_op jit(solution)/shard_map/ppermute | solution.py:301
  19.8 1.3 %reduce.3 = s32[256]{0:T(256)S(1)} reduce(s32[256,1]{0,1:T(1,128)} %param.13, s32[]{:T(128)} %broadcast.5), dimensions={1}, to_apply=%param.13.reduce_sub_computation.3 | reduce | bytes 2052 | tf_op args[1]
  22.8 6.1 %all-to-all-start = ((bf16[32,2,2,16,128]{4,3,2,1,0:T(8,128)(2,1)}), bf16[32,2,2,16,128]{4,3,2,1,0:T(8,128)(2,1)}, u32[]{:S(2)}, u32[]{:S(2)}) async-start(bf16[32,2,2,16,128]{4,3,2,1,0:T(8,128)(2,1)} %copy-done.5), calls=%async_computation | async-start | bytes 1048576 | tf_op jit(solution)/shard_map/all_to_all | solution.py:378
  28.9 2.1 %pad_maximum_fusion.x_ref.sr_ref = bf16[192,2176]{1,0:T(8,128)(2,1)} fusion(bf16[96,2176]{1,0:T(8,128)(2,1)} %collective-permute-done.3, bf16[96,2176]{1,0:T(8,128)(2,1)} %pad_maximum_fusion.1), kind=kLoop, calls=%fused_computation | loop fusion | flops 1671168 | bytes 1671168 | tf_op jit(solution)/shard_map/concatenate | solution.py:374
  31.0 1.9 %collective-permute-start.5 = (bf16[192,2176]{1,0:T(8,128)(2,1)}, bf16[192,2176]{1,0:T(8,128)(2,1)}, u32[]{:S(2)}, u32[]{:S(2)}) collective-permute-start(bf16[192,2176]{1,0:T(8,128)(2,1)} %pad_maximum_fusion.x_ref.sr_ref), channel_id=1, source_target_pairs={{0,4},{1,3},{2,6},{3,1},{4,0},{5,7},{6,2},{7,5},{8,12},{9,11},{10,... | collective-permute-start | bytes 2506760 | tf_op jit(solution)/shard_map/ppermute | solution.py:301
  32.9 1.9 %copy-done.1 = bf16[1,4096,384]{2,1,0:T(8,128)(2,1)S(1)} copy-done((bf16[1,4096,384]{2,1,0:T(8,128)(2,1)S(1)}, bf16[1,4096,384]{2,1,0:T(8,128)(2,1)}, u32[]{:S(2)}) %copy-start.1) | copy-done | bytes 3145752
  34.8 2.1 %expert_partial.2 = (f32[192,384]{1,0:T(8,128)S(1)}, f32[192,384]{1,0:T(8,128)S(1)}) custom-call(s32[1]{0:T(128)} %bitcast.1.core_ref, bf16[192,2176]{1,0:T(8,128)(2,1)} %pad_maximum_fusion.x_ref.sr_ref, bf16[1,4096,384]{2,1,0:T(8,128)(2,1)S(1)} %copy-done, bf16[1,4096,384]{2,1,0:T(8,128)(2,1)S(1)} %copy-done.1), custom_call_target="tpu_custom_call" | custom-call | flops 603979776 | bytes 4521984 | tf_op jit(solution)/shard_map/expert_partial/pallas_call | solution.py:188
  38.3 5.8 %all-to-all-done.cache_ref = bf16[32,2,2,16,128]{4,3,2,1,0:T(8,128)(2,1)} async-done(((bf16[32,2,2,16,128]{4,3,2,1,0:T(8,128)(2,1)}), bf16[32,2,2,16,128]{4,3,2,1,0:T(8,128)(2,1)}, u32[]{:S(2)}, u32[]{:S(2)}) %all-to-all-start) | async-done | bytes 524320 | tf_op jit(solution)/shard_map/all_to_all | solution.py:378
  44.1 2.6 %collective-permute-done.5.x_ref.r2_ref = bf16[192,2176]{1,0:T(8,128)(2,1)} collective-permute-done((bf16[192,2176]{1,0:T(8,128)(2,1)}, bf16[192,2176]{1,0:T(8,128)(2,1)}, u32[]{:S(2)}, u32[]{:S(2)}) %collective-permute-start.5) | collective-permute-done | bytes 835616 | tf_op jit(solution)/shard_map/ppermute | solution.py:301
  46.6 1.9 %copy-done.2 = bf16[1,4096,384]{2,1,0:T(8,128)(2,1)S(1)} copy-done((bf16[1,4096,384]{2,1,0:T(8,128)(2,1)S(1)}, bf16[1,4096,384]{2,1,0:T(8,128)(2,1)}, u32[]{:S(2)}) %copy-start.2) | copy-done | bytes 3145752
  48.5 2.3 %expert_partial.3 = (f32[192,384]{1,0:T(8,128)S(1)}, f32[192,384]{1,0:T(8,128)S(1)}) custom-call(s32[1]{0:T(128)} %bitcast.1.core_ref, bf16[192,2176]{1,0:T(8,128)(2,1)} %collective-permute-done.5.x_ref.r2_ref, bf16[1,4096,384]{2,1,0:T(8,128)(2,1)S(1)} %copy-done, bf16[1,4096,384]{2,1,0:T(8,128)(2,1)S(1)} %copy-done.2), custom_call_target="tpu_custom_call" | custom-call | flops 603979776 | bytes 4521984 | tf_op jit(solution)/shard_map/expert_partial/pallas_call | solution.py:188
  50.9 3.1 %expert_hidden.1.own_ref = bf16[384,384]{1,0:T(8,128)(2,1)S(1)} custom-call(s32[1]{0:T(128)} %bitcast.1.core_ref, bf16[192,2176]{1,0:T(8,128)(2,1)} %collective-permute-done.4.sr_ref, bf16[192,2176]{1,0:T(8,128)(2,1)S(1)} %collective-permute-done.6.r2_ref, bf16[1,4096,384]{2,1,0:T(8,128)(2,1)S(1)} %copy-done, bf16[1,4096,384]{2,1,0:T(8,128)(2,1)S(1)} %copy-done.3, ...), custom_call_target="tpu_custom_call" | custom-call | flops 1207959552 | bytes 6193152 | tf_op jit(solution)/shard_map/expert_hidden/pallas_call | solution.py:207
  54.7 1.1 %collective-permute-done.7.other_ref = bf16[384,384]{1,0:T(8,128)(2,1)S(1)} collective-permute-done((bf16[384,384]{1,0:T(8,128)(2,1)S(1)}, bf16[384,384]{1,0:T(8,128)(2,1)S(1)}, u32[]{:S(2)}, u32[]{:S(2)}) %collective-permute-start.7) | collective-permute-done | bytes 294944 | tf_op jit(solution)/shard_map/ppermute | solution.py:301
  55.8 2.4 %expert_back.3 = (f32[48,2048]{1,0:T(8,128)S(1)}, bf16[48,2048]{1,0:T(8,128)(2,1)S(1)}, bf16[48,2048]{1,0:T(8,128)(2,1)S(1)}, bf16[48,2048]{1,0:T(8,128)(2,1)S(1)}) custom-call(s32[2]{0:T(128)S(1)} %pad_add_fusion.at_ref, bf16[384,384]{1,0:T(8,128)(2,1)S(1)} %expert_hidden.1.own_ref, bf16[384,384]{1,0:T(8,128)(2,1)S(1)} %collective-permute-done.7.other_ref, ...), custom_call_target="tpu_custom_call" | custom-call | flops 603979776 | bytes 5308416 | tf_op jit(solution)/shard_map/expert_back/pallas_call | solution.py:275
  58.2 1.8 %collective-permute-start.11 = (bf16[48,2048]{1,0:T(8,128)(2,1)S(1)}, bf16[48,2048]{1,0:T(8,128)(2,1)S(1)}, u32[]{:S(2)}, u32[]{:S(2)}) collective-permute-start(bf16[48,2048]{1,0:T(8,128)(2,1)S(1)} %get-tuple-element.46.after_ref), channel_id=1, source_target_pairs={{0,2},{1,5},{2,0},{3,7},{4,6},{5,1},{6,4},{7,3},{8,10},{9,13},{10,... | collective-permute-start | bytes 589832 | tf_op jit(solution)/shard_map/ppermute | solution.py:301
  60.0 1.2 %collective-permute-start.12 = (bf16[48,2048]{1,0:T(8,128)(2,1)S(1)}, bf16[48,2048]{1,0:T(8,128)(2,1)S(1)}, u32[]{:S(2)}, u32[]{:S(2)}) collective-permute-start(bf16[48,2048]{1,0:T(8,128)(2,1)S(1)} %get-tuple-element.49), channel_id=1, source_target_pairs={{0,4},{1,3},{2,6},{3,1},{4,0},{5,7},{6,2},{7,5},{8,12},{9,11},{10,... | collective-permute-start | bytes 589832 | tf_op jit(solution)/shard_map/ppermute | solution.py:301
  61.8 2.4 %expert_back.2 = (f32[48,2048]{1,0:T(8,128)S(1)}, bf16[48,2048]{1,0:T(8,128)(2,1)S(1)}, bf16[48,2048]{1,0:T(8,128)(2,1)S(1)}, bf16[48,2048]{1,0:T(8,128)(2,1)S(1)}) custom-call(s32[2]{0:T(128)S(1)} %pad_add_fusion.at_ref, bf16[384,384]{1,0:T(8,128)(2,1)S(1)} %expert_hidden.1.own_ref, bf16[384,384]{1,0:T(8,128)(2,1)S(1)} %collective-permute-done.7.other_ref, ...), custom_call_target="tpu_custom_call" | custom-call | flops 603979776 | bytes 5308416 | tf_op jit(solution)/shard_map/expert_back/pallas_call | solution.py:275
  64.2 2.4 %collective-permute-start.10 = (bf16[48,2048]{1,0:T(8,128)(2,1)S(1)}, bf16[48,2048]{1,0:T(8,128)(2,1)S(1)}, u32[]{:S(2)}, u32[]{:S(2)}) collective-permute-start(bf16[48,2048]{1,0:T(8,128)(2,1)S(1)} %get-tuple-element.40), channel_id=1, source_target_pairs={{0,6},{1,7},{2,4},{3,5},{4,2},{5,3},{6,0},{7,1},{8,14},{9,15},{10,... | collective-permute-start | bytes 589832 | tf_op jit(solution)/shard_map/ppermute | solution.py:301
  67.2 3.0 %attention.1 = bf16[8,3,32,128]{3,2,1,0:T(8,128)(2,1)} custom-call(s32[1]{0:T(128)} %bitcast.me_ref, s32[16,16]{1,0:T(8,128)S(1)} %reshape.38.owner_ref, s32[16,16]{1,0:T(8,128)S(1)} %reshape.39.slot_ref, s32[16,16]{1,0:T(8,128)S(1)} %reshape.40.fill_ref, bf16[8,3,32,128]{3,2,1,0:T(8,128)(2,1)S(1)} %copy-done.10, ...), custom_call_target="tpu_custom_call" | custom-call | tf_op jit(solution)/shard_map/attention/pallas_call | solution.py:391
  71.4 2.6 %collective-permute-start.14 = (bf16[24,2048]{1,0:T(8,128)(2,1)S(1)}, bf16[24,2048]{1,0:T(8,128)(2,1)S(1)}, u32[]{:S(2)}, u32[]{:S(2)}) collective-permute-start(bf16[24,2048]{1,0:T(8,128)(2,1)S(1)} %slice.33), channel_id=1, source_target_pairs={{0,16},{1,17},{2,18},{3,19},{4,20},{5,21},{6,22},{7,23},{8,24},{9,... | collective-permute-start | bytes 294920 | tf_op jit(solution)/shard_map/ppermute | solution.py:301
  74.0 1.4 %collective-permute-done.10 = bf16[48,2048]{1,0:T(8,128)(2,1)S(1)} collective-permute-done((bf16[48,2048]{1,0:T(8,128)(2,1)S(1)}, bf16[48,2048]{1,0:T(8,128)(2,1)S(1)}, u32[]{:S(2)}, u32[]{:S(2)}) %collective-permute-start.10) | collective-permute-done | bytes 196640 | tf_op jit(solution)/shard_map/ppermute | solution.py:301
  75.4 2.8 %collective-permute-done.8 = bf16[48,2048]{1,0:T(8,128)(2,1)S(1)} collective-permute-done((bf16[48,2048]{1,0:T(8,128)(2,1)S(1)}, bf16[48,2048]{1,0:T(8,128)(2,1)S(1)}, u32[]{:S(2)}, u32[]{:S(2)}) %collective-permute-start.8) | collective-permute-done | bytes 196640 | tf_op jit(solution)/shard_map/ppermute | solution.py:301
  78.2 1.1 %collective-permute-done.9 = bf16[48,2048]{1,0:T(8,128)(2,1)S(1)} collective-permute-done((bf16[48,2048]{1,0:T(8,128)(2,1)S(1)}, bf16[48,2048]{1,0:T(8,128)(2,1)S(1)}, u32[]{:S(2)}, u32[]{:S(2)}) %collective-permute-start.9) | collective-permute-done | bytes 196640 | tf_op jit(solution)/shard_map/ppermute | solution.py:301
  79.4 1.9 %collective-permute-start.15 = (bf16[24,2048]{1,0:T(8,128)(2,1)S(1)}, bf16[24,2048]{1,0:T(8,128)(2,1)S(1)}, u32[]{:S(2)}, u32[]{:S(2)}) collective-permute-start(bf16[24,2048]{1,0:T(8,128)(2,1)S(1)} %get-tuple-element.52), channel_id=1, source_target_pairs={{0,8},{1,9},{2,10},{3,11},{4,12},{5,13},{6,14},{7,15},{8,0},{9,1},... | collective-permute-start | bytes 294920 | tf_op jit(solution)/shard_map/ppermute | solution.py:301
  81.4 2.5 %collective-permute-start.16 = (bf16[24,2048]{1,0:T(8,128)(2,1)S(1)}, bf16[24,2048]{1,0:T(8,128)(2,1)S(1)}, u32[]{:S(2)}, u32[]{:S(2)}) collective-permute-start(bf16[24,2048]{1,0:T(8,128)(2,1)S(1)} %get-tuple-element.53), channel_id=1, source_target_pairs={{0,24},{1,25},{2,26},{3,27},{4,28},{5,29},{6,30},{7,31},{8,16},{9,... | collective-permute-start | bytes 294920 | tf_op jit(solution)/shard_map/ppermute | solution.py:301
  84.3 4.3 %collective-permute-done.16 = bf16[24,2048]{1,0:T(8,128)(2,1)S(1)} collective-permute-done((bf16[24,2048]{1,0:T(8,128)(2,1)S(1)}, bf16[24,2048]{1,0:T(8,128)(2,1)S(1)}, u32[]{:S(2)}, u32[]{:S(2)}) %collective-permute-start.16) | collective-permute-done | bytes 98336 | tf_op jit(solution)/shard_map/ppermute | solution.py:301
  (52 shorter events, 10.7 us)
Async XLA Ops:
  0.6 32.2 %copy-start = (bf16[1,4096,384]{2,1,0:T(8,128)(2,1)S(1)}, bf16[1,4096,384]{2,1,0:T(8,128)(2,1)}, u32[]{:S(2)}) copy-start(bf16[1,4096,384]{2,1,0:T(8,128)(2,1)} %gate_ref.5) | copy-start | bytes 9437188
  2.5 12.2 %collective-permute-start = (bf16[24,2176]{1,0:T(8,128)(2,1)}, bf16[24,2176]{1,0:T(8,128)(2,1)S(1)}, u32[]{:S(2)}, u32[]{:S(2)}) collective-permute-start(bf16[24,2176]{1,0:T(8,128)(2,1)} %pack_tokens.1), channel_id=1, source_target_pairs={{0,16},{1,17},{2,18},{3,19},{4,20},{5,21},{6,22},{7,23},{8,24},{9,... | collective-permute-start | bytes 313352 | tf_op jit(solution)/shard_map/ppermute | solution.py:301
  6.6 8.2 %collective-permute-start.1 = (bf16[24,2176]{1,0:T(8,128)(2,1)}, bf16[24,2176]{1,0:T(8,128)(2,1)S(1)}, u32[]{:S(2)}, u32[]{:S(2)}) collective-permute-start(bf16[24,2176]{1,0:T(8,128)(2,1)} %pack_tokens.1), channel_id=1, source_target_pairs={{0,8},{1,9},{2,10},{3,11},{4,12},{5,13},{6,14},{7,15},{8,0},{9,1},... | collective-permute-start | bytes 313352 | tf_op jit(solution)/shard_map/ppermute | solution.py:301
  8.1 7.2 %collective-permute-start.2 = (bf16[24,2176]{1,0:T(8,128)(2,1)}, bf16[24,2176]{1,0:T(8,128)(2,1)S(1)}, u32[]{:S(2)}, u32[]{:S(2)}) collective-permute-start(bf16[24,2176]{1,0:T(8,128)(2,1)} %pack_tokens.1), channel_id=1, source_target_pairs={{0,24},{1,25},{2,26},{3,27},{4,28},{5,29},{6,30},{7,31},{8,16},{9,... | collective-permute-start | bytes 313352 | tf_op jit(solution)/shard_map/ppermute | solution.py:301
  9.1 0.7 copy-start.11
  14.0 0.8 copy-start.5
  17.0 11.8 %collective-permute-start.3 = (bf16[96,2176]{1,0:T(8,128)(2,1)}, bf16[96,2176]{1,0:T(8,128)(2,1)}, u32[]{:S(2)}, u32[]{:S(2)}) collective-permute-start(bf16[96,2176]{1,0:T(8,128)(2,1)} %pad_maximum_fusion.1), channel_id=1, source_target_pairs={{0,2},{1,5},{2,0},{3,7},{4,6},{5,1},{6,4},{7,3},{8,10},{9,13},{10,... | collective-permute-start | bytes 1253384 | tf_op jit(solution)/shard_map/ppermute | solution.py:301
  22.8 21.3 %all-to-all-start = ((bf16[32,2,2,16,128]{4,3,2,1,0:T(8,128)(2,1)}), bf16[32,2,2,16,128]{4,3,2,1,0:T(8,128)(2,1)}, u32[]{:S(2)}, u32[]{:S(2)}) async-start(bf16[32,2,2,16,128]{4,3,2,1,0:T(8,128)(2,1)} %copy-done.5), calls=%async_computation | async-start | bytes 1048576 | tf_op jit(solution)/shard_map/all_to_all | solution.py:378
  31.0 15.6 %collective-permute-start.5 = (bf16[192,2176]{1,0:T(8,128)(2,1)}, bf16[192,2176]{1,0:T(8,128)(2,1)}, u32[]{:S(2)}, u32[]{:S(2)}) collective-permute-start(bf16[192,2176]{1,0:T(8,128)(2,1)} %pad_maximum_fusion.x_ref.sr_ref), channel_id=1, source_target_pairs={{0,4},{1,3},{2,6},{3,1},{4,0},{5,7},{6,2},{7,5},{8,12},{9,11},{10,... | collective-permute-start | bytes 2506760 | tf_op jit(solution)/shard_map/ppermute | solution.py:301
  32.9 18.0 %collective-permute-start.4 = (bf16[192,2176]{1,0:T(8,128)(2,1)}, bf16[192,2176]{1,0:T(8,128)(2,1)}, u32[]{:S(2)}, u32[]{:S(2)}) collective-permute-start(bf16[192,2176]{1,0:T(8,128)(2,1)} %pad_maximum_fusion.x_ref.sr_ref), channel_id=1, source_target_pairs={{0,1},{1,0},{2,3},{3,2},{4,5},{5,4},{6,7},{7,6},{8,9},{9,8},{10,11... | collective-permute-start | bytes 2506760 | tf_op jit(solution)/shard_map/ppermute | solution.py:301
  32.9 1.9 %copy-start.1 = (bf16[1,4096,384]{2,1,0:T(8,128)(2,1)S(1)}, bf16[1,4096,384]{2,1,0:T(8,128)(2,1)}, u32[]{:S(2)}) copy-start(bf16[1,4096,384]{2,1,0:T(8,128)(2,1)} %up_ref.5) | copy-start | bytes 9437188
  36.9 0.7 copy-start.6
  37.6 0.7 copy-start.8
  46.6 4.2 %collective-permute-start.6 = (bf16[192,2176]{1,0:T(8,128)(2,1)}, bf16[192,2176]{1,0:T(8,128)(2,1)S(1)}, u32[]{:S(2)}, u32[]{:S(2)}) collective-permute-start(bf16[192,2176]{1,0:T(8,128)(2,1)} %collective-permute-done.5.x_ref.r2_ref), channel_id=1, source_target_pairs={{0,1},{1,0},{2,3},{3,2},{4,5},{5,4},{6,7},{7,6},{8,9},{9,8},{10,11... | collective-permute-start | bytes 2506760 | tf_op jit(solution)/shard_map/ppermute | solution.py:301
  46.6 1.9 %copy-start.2 = (bf16[1,4096,384]{2,1,0:T(8,128)(2,1)S(1)}, bf16[1,4096,384]{2,1,0:T(8,128)(2,1)}, u32[]{:S(2)}) copy-start(bf16[1,4096,384]{2,1,0:T(8,128)(2,1)} %up_ref.5) | copy-start | bytes 9437188
  48.5 2.3 %copy-start.3 = (bf16[1,4096,384]{2,1,0:T(8,128)(2,1)S(1)}, bf16[1,4096,384]{2,1,0:T(8,128)(2,1)}, u32[]{:S(2)}) copy-start(bf16[1,4096,384]{2,1,0:T(8,128)(2,1)} %up_ref.5) | copy-start | bytes 9437188
  48.5 2.3 %copy-start.7 = (f32[192,384]{1,0:T(8,128)S(1)}, f32[192,384]{1,0:T(8,128)}, u32[]{:S(2)}) copy-start(f32[192,384]{1,0:T(8,128)} %copy-done.6) | copy-start | bytes 884740
  48.5 2.3 %copy-start.9 = (f32[192,384]{1,0:T(8,128)S(1)}, f32[192,384]{1,0:T(8,128)}, u32[]{:S(2)}) copy-start(f32[192,384]{1,0:T(8,128)} %copy-done.8) | copy-start | bytes 884740
  50.9 4.9 %copy-start.4 = (bf16[1,768,2048]{2,1,0:T(8,128)(2,1)S(1)}, bf16[1,768,2048]{2,1,0:T(8,128)(2,1)}, u32[]{:S(2)}) copy-start(bf16[1,768,2048]{2,1,0:T(8,128)(2,1)} %down_ref.3) | copy-start | bytes 9437188
  54.0 1.8 %collective-permute-start.7 = (bf16[384,384]{1,0:T(8,128)(2,1)S(1)}, bf16[384,384]{1,0:T(8,128)(2,1)S(1)}, u32[]{:S(2)}, u32[]{:S(2)}) collective-permute-start(bf16[384,384]{1,0:T(8,128)(2,1)S(1)} %expert_hidden.1.own_ref), channel_id=1, source_target_pairs={{0,1},{1,0},{2,3},{3,2},{4,5},{5,4},{6,7},{7,6},{8,9},{9,8},{10,11... | collective-permute-start | bytes 884744 | tf_op jit(solution)/shard_map/ppermute | solution.py:301
  58.2 9.0 %copy-start.10 = (bf16[8,3,32,128]{3,2,1,0:T(8,128)(2,1)S(1)}, bf16[8,3,32,128]{3,2,1,0:T(8,128)(2,1)}, u32[]{:S(2)}) copy-start(bf16[8,3,32,128]{3,2,1,0:T(8,128)(2,1)} %q_ref.1) | copy-start | bytes 589828
  58.2 11.9 %collective-permute-start.11 = (bf16[48,2048]{1,0:T(8,128)(2,1)S(1)}, bf16[48,2048]{1,0:T(8,128)(2,1)S(1)}, u32[]{:S(2)}, u32[]{:S(2)}) collective-permute-start(bf16[48,2048]{1,0:T(8,128)(2,1)S(1)} %get-tuple-element.46.after_ref), channel_id=1, source_target_pairs={{0,2},{1,5},{2,0},{3,7},{4,6},{5,1},{6,4},{7,3},{8,10},{9,13},{10,... | collective-permute-start | bytes 589832 | tf_op jit(solution)/shard_map/ppermute | solution.py:301
  60.0 10.7 %collective-permute-start.12 = (bf16[48,2048]{1,0:T(8,128)(2,1)S(1)}, bf16[48,2048]{1,0:T(8,128)(2,1)S(1)}, u32[]{:S(2)}, u32[]{:S(2)}) collective-permute-start(bf16[48,2048]{1,0:T(8,128)(2,1)S(1)} %get-tuple-element.49), channel_id=1, source_target_pairs={{0,4},{1,3},{2,6},{3,1},{4,0},{5,7},{6,2},{7,5},{8,12},{9,11},{10,... | collective-permute-start | bytes 589832 | tf_op jit(solution)/shard_map/ppermute | solution.py:301
  61.2 10.1 %collective-permute-start.13 = (bf16[48,2048]{1,0:T(8,128)(2,1)S(1)}, bf16[48,2048]{1,0:T(8,128)(2,1)S(1)}, u32[]{:S(2)}, u32[]{:S(2)}) collective-permute-start(bf16[48,2048]{1,0:T(8,128)(2,1)S(1)} %get-tuple-element.50), channel_id=1, source_target_pairs={{0,6},{1,7},{2,4},{3,5},{4,2},{5,3},{6,0},{7,1},{8,14},{9,15},{10,... | collective-permute-start | bytes 589832 | tf_op jit(solution)/shard_map/ppermute | solution.py:301
  64.2 11.3 %collective-permute-start.10 = (bf16[48,2048]{1,0:T(8,128)(2,1)S(1)}, bf16[48,2048]{1,0:T(8,128)(2,1)S(1)}, u32[]{:S(2)}, u32[]{:S(2)}) collective-permute-start(bf16[48,2048]{1,0:T(8,128)(2,1)S(1)} %get-tuple-element.40), channel_id=1, source_target_pairs={{0,6},{1,7},{2,4},{3,5},{4,2},{5,3},{6,0},{7,1},{8,14},{9,15},{10,... | collective-permute-start | bytes 589832 | tf_op jit(solution)/shard_map/ppermute | solution.py:301
  66.6 11.6 %collective-permute-start.8 = (bf16[48,2048]{1,0:T(8,128)(2,1)S(1)}, bf16[48,2048]{1,0:T(8,128)(2,1)S(1)}, u32[]{:S(2)}, u32[]{:S(2)}) collective-permute-start(bf16[48,2048]{1,0:T(8,128)(2,1)S(1)} %get-tuple-element.38), channel_id=1, source_target_pairs={{0,2},{1,5},{2,0},{3,7},{4,6},{5,1},{6,4},{7,3},{8,10},{9,13},{10,... | collective-permute-start | bytes 589832 | tf_op jit(solution)/shard_map/ppermute | solution.py:301
  70.2 9.1 %collective-permute-start.9 = (bf16[48,2048]{1,0:T(8,128)(2,1)S(1)}, bf16[48,2048]{1,0:T(8,128)(2,1)S(1)}, u32[]{:S(2)}, u32[]{:S(2)}) collective-permute-start(bf16[48,2048]{1,0:T(8,128)(2,1)S(1)} %get-tuple-element.39), channel_id=1, source_target_pairs={{0,4},{1,3},{2,6},{3,1},{4,0},{5,7},{6,2},{7,5},{8,12},{9,11},{10,... | collective-permute-start | bytes 589832 | tf_op jit(solution)/shard_map/ppermute | solution.py:301
  71.4 12.5 %collective-permute-start.14 = (bf16[24,2048]{1,0:T(8,128)(2,1)S(1)}, bf16[24,2048]{1,0:T(8,128)(2,1)S(1)}, u32[]{:S(2)}, u32[]{:S(2)}) collective-permute-start(bf16[24,2048]{1,0:T(8,128)(2,1)S(1)} %slice.33), channel_id=1, source_target_pairs={{0,16},{1,17},{2,18},{3,19},{4,20},{5,21},{6,22},{7,23},{8,24},{9,... | collective-permute-start | bytes 294920 | tf_op jit(solution)/shard_map/ppermute | solution.py:301
  79.4 4.9 %collective-permute-start.15 = (bf16[24,2048]{1,0:T(8,128)(2,1)S(1)}, bf16[24,2048]{1,0:T(8,128)(2,1)S(1)}, u32[]{:S(2)}, u32[]{:S(2)}) collective-permute-start(bf16[24,2048]{1,0:T(8,128)(2,1)S(1)} %get-tuple-element.52), channel_id=1, source_target_pairs={{0,8},{1,9},{2,10},{3,11},{4,12},{5,13},{6,14},{7,15},{8,0},{9,1},... | collective-permute-start | bytes 294920 | tf_op jit(solution)/shard_map/ppermute | solution.py:301
  81.4 7.3 %collective-permute-start.16 = (bf16[24,2048]{1,0:T(8,128)(2,1)S(1)}, bf16[24,2048]{1,0:T(8,128)(2,1)S(1)}, u32[]{:S(2)}, u32[]{:S(2)}) collective-permute-start(bf16[24,2048]{1,0:T(8,128)(2,1)S(1)} %get-tuple-element.53), channel_id=1, source_target_pairs={{0,24},{1,25},{2,26},{3,27},{4,28},{5,29},{6,30},{7,31},{8,16},{9,... | collective-permute-start | bytes 294920 | tf_op jit(solution)/shard_map/ppermute | solution.py:301

commit v8 on v7

--- a/solution.py
+++ b/solution.py
@@ -347,6 +347,7 @@
         out_shape=jax.ShapeDtypeStruct((tokens, d // 2 + lanes), jnp.bfloat16),
         in_specs=[smem()] + [vmem()] * 3,
         out_specs=vmem(),
+        compiler_params=pltpu.CompilerParams(vmem_limit_bytes=room(moe_input, moe_input)),
         name="pack_tokens",
     )(
         own_core,

time: 90 us -> 90.7 us (level)
  local copies, waits for them, and re-layouts: 10.6 us -> 13 us
  Pallas kernels: 21.3 us -> 19.6 us
    unnamed x26 -> x32, local copies, waits for them, and re-layouts: 8.19 us -> 10.7 us
    pallas_call x1, Pallas kernels: 1.88 us -> 0.13 us  [body(): pl.pallas_call(functools.partial(pack_kernel, owners), out_shape=jax.Shap...]
  transfers between devices with their start and end apart: 18 -> 18, of which waited for: 10 -> 10; matrix products, arithmetic and copies ran while one was open for 8% -> 8% of each run, Pallas kernels for 16% -> 15%
where the time goes in v8:
time: 90.7 us; the launch traced here: 90 us
  starting transfers between devices  29.9 us (33%)
  waiting for transfers between devices  20.6 us (23%)
  Pallas kernels  19.6 us (22%)
  local copies, waits for them, and re-layouts  13 us (14%)
  other arithmetic  6.07 us (7%)
    ppermute x17, starting transfers between devices, go(): return lax.ppermute(x, ('ep', 'pd'), perm)  23.8 us
    ppermute x17, waiting for transfers between devices, go(): return lax.ppermute(x, ('ep', 'pd'), perm)  14.8 us
    unnamed x32, local copies, waits for them, and re-layouts  10.7 us
    all_to_all x1, starting transfers between devices, body(): cache = lax.all_to_all(send, 'ep', split_axis=0, concat_axis=0, tiled=True)  6.11 us
    all_to_all x1, waiting for transfers between devices, body(): cache = lax.all_to_all(send, 'ep', split_axis=0, concat_axis=0, tiled=True)  5.79 us
    pallas_call x2, Pallas kernels, expert_back(): pl.pallas_call(functools.partial(back_kernel, experts, begin, 4), out_sha...  4.81 us
    pallas_call x2, Pallas kernels, expert_partial(): pl.pallas_call(functools.partial(partial_kernel, 4), in_specs=[smem()] +...  4.41 us
    pallas_call x1, Pallas kernels, body(): pl.pallas_call(functools.partial(page_kernel, pages), out_shape=jax.Shape...  4.13 us
  transfers between devices with their start and end apart: 18, of which 10 were waited for; matrix products, arithmetic and copies ran while one was open for 8% of the time, Pallas kernels for 15%

profile of v8, /device:TPU:0, one launch (start us, length us, event | category | flops | bytes accessed | tf_op | source)
XLA Modules:
  0.0 90.0 jit_solution(3415876594952648163)
XLA Ops:
  0.7 1.1 %copy-done.11 = bf16[8,3,4096]{2,0,1:T(8,128)(2,1)S(1)} copy-done((bf16[8,3,4096]{2,0,1:T(8,128)(2,1)S(1)}, bf16[8,3,4096]{2,0,1:T(8,128)(2,1)}, u32[]{:S(2)}) %copy-start.11) | copy-done | bytes 196632
  3.3 4.1 %collective-permute-start = (bf16[24,2176]{1,0:T(8,128)(2,1)S(1)}, bf16[24,2176]{1,0:T(8,128)(2,1)S(1)}, u32[]{:S(2)}, u32[]{:S(2)}) collective-permute-start(bf16[24,2176]{1,0:T(8,128)(2,1)S(1)} %pack_tokens.1), channel_id=1, source_target_pairs={{0,16},{1,17},{2,18},{3,19},{4,20},{5,21},{6,22},{7,23},{8,24},{9,... | collective-permute-start | bytes 313352 | tf_op jit(solution)/shard_map/ppermute | solution.py:301
  7.4 1.6 %collective-permute-start.1 = (bf16[24,2176]{1,0:T(8,128)(2,1)S(1)}, bf16[24,2176]{1,0:T(8,128)(2,1)S(1)}, u32[]{:S(2)}, u32[]{:S(2)}) collective-permute-start(bf16[24,2176]{1,0:T(8,128)(2,1)S(1)} %pack_tokens.1), channel_id=1, source_target_pairs={{0,8},{1,9},{2,10},{3,11},{4,12},{5,13},{6,14},{7,15},{8,0},{9,1},... | collective-permute-start | bytes 313352 | tf_op jit(solution)/shard_map/ppermute | solution.py:301
  9.0 1.0 %copy.22 = bf16[16,2,16,2,128]{4,2,3,1,0:T(8,128)(2,1)S(1)} copy(bf16[16,2,16,2,128]{4,3,2,1,0:T(2,128)(2,1)} %param.12) | data formatting | bytes 524288 | tf_op args[0]
  10.6 4.1 %quantize_pages.1 = bf16[32,2,2,16,128]{4,3,2,1,0:T(8,128)(2,1)S(1)} custom-call(s32[1]{0:T(128)} %bitcast.me_ref, s32[256]{0:T(256)S(1)} %bitcast.25, bf16[16,2,2,16,128]{4,3,2,1,0:T(8,128)(2,1)S(1)} %bitcast.21), custom_call_target="tpu_custom_call" | custom-call | tf_op jit(solution)/shard_map/quantize_pages/pallas_call | solution.py:358
  16.1 1.7 %pad_maximum_fusion.1 = bf16[96,2176]{1,0:T(8,128)(2,1)} fusion(bf16[24,2176]{1,0:T(8,128)(2,1)} %collective-permute-done.2, bf16[24,2176]{1,0:T(8,128)(2,1)S(1)} %collective-permute-done.1, bf16[24,2176]{1,0:T(8,128)(2,1)S(1)} %collective-permute-done, bf16[24,2176]{1,0:T(8,128)(2,1)S(1)} %pack_tokens.1), kind=kLoop, calls=%fused_computation.1 | loop fusion | flops 1671168 | bytes 835584 | tf_op jit(solution)/shard_map/concatenate | solution.py:370
  17.7 1.5 %collective-permute-start.3 = (bf16[96,2176]{1,0:T(8,128)(2,1)}, bf16[96,2176]{1,0:T(8,128)(2,1)}, u32[]{:S(2)}, u32[]{:S(2)}) collective-permute-start(bf16[96,2176]{1,0:T(8,128)(2,1)} %pad_maximum_fusion.1), channel_id=1, source_target_pairs={{0,2},{1,5},{2,0},{3,7},{4,6},{5,1},{6,4},{7,3},{8,10},{9,13},{10,... | collective-permute-start | bytes 1253384 | tf_op jit(solution)/shard_map/ppermute | solution.py:301
  20.5 1.3 %reduce.3 = s32[256]{0:T(256)S(1)} reduce(s32[256,1]{0,1:T(1,128)} %param.13, s32[]{:T(128)} %broadcast.5), dimensions={1}, to_apply=%param.13.reduce_sub_computation.3 | reduce | bytes 2052 | tf_op args[1]
  23.5 6.1 %all-to-all-start = ((bf16[32,2,2,16,128]{4,3,2,1,0:T(8,128)(2,1)}), bf16[32,2,2,16,128]{4,3,2,1,0:T(8,128)(2,1)}, u32[]{:S(2)}, u32[]{:S(2)}) async-start(bf16[32,2,2,16,128]{4,3,2,1,0:T(8,128)(2,1)} %copy-done.5), calls=%async_computation | async-start | bytes 1048576 | tf_op jit(solution)/shard_map/all_to_all | solution.py:379
  29.6 2.1 %pad_maximum_fusion.x_ref.sr_ref = bf16[192,2176]{1,0:T(8,128)(2,1)} fusion(bf16[96,2176]{1,0:T(8,128)(2,1)} %collective-permute-done.3, bf16[96,2176]{1,0:T(8,128)(2,1)} %pad_maximum_fusion.1), kind=kLoop, calls=%fused_computation | loop fusion | flops 1671168 | bytes 1671168 | tf_op jit(solution)/shard_map/concatenate | solution.py:375
  31.7 1.9 %collective-permute-start.5 = (bf16[192,2176]{1,0:T(8,128)(2,1)}, bf16[192,2176]{1,0:T(8,128)(2,1)}, u32[]{:S(2)}, u32[]{:S(2)}) collective-permute-start(bf16[192,2176]{1,0:T(8,128)(2,1)} %pad_maximum_fusion.x_ref.sr_ref), channel_id=1, source_target_pairs={{0,4},{1,3},{2,6},{3,1},{4,0},{5,7},{6,2},{7,5},{8,12},{9,11},{10,... | collective-permute-start | bytes 2506760 | tf_op jit(solution)/shard_map/ppermute | solution.py:301
  33.6 1.9 %copy-done.1 = bf16[1,4096,384]{2,1,0:T(8,128)(2,1)S(1)} copy-done((bf16[1,4096,384]{2,1,0:T(8,128)(2,1)S(1)}, bf16[1,4096,384]{2,1,0:T(8,128)(2,1)}, u32[]{:S(2)}) %copy-start.1) | copy-done | bytes 3145752
  35.4 2.1 %expert_partial.2 = (f32[192,384]{1,0:T(8,128)S(1)}, f32[192,384]{1,0:T(8,128)S(1)}) custom-call(s32[1]{0:T(128)} %bitcast.1.core_ref, bf16[192,2176]{1,0:T(8,128)(2,1)} %pad_maximum_fusion.x_ref.sr_ref, bf16[1,4096,384]{2,1,0:T(8,128)(2,1)S(1)} %copy-done, bf16[1,4096,384]{2,1,0:T(8,128)(2,1)S(1)} %copy-done.1), custom_call_target="tpu_custom_call" | custom-call | flops 603979776 | bytes 4521984 | tf_op jit(solution)/shard_map/expert_partial/pallas_call | solution.py:188
  39.0 5.8 %all-to-all-done.cache_ref = bf16[32,2,2,16,128]{4,3,2,1,0:T(8,128)(2,1)} async-done(((bf16[32,2,2,16,128]{4,3,2,1,0:T(8,128)(2,1)}), bf16[32,2,2,16,128]{4,3,2,1,0:T(8,128)(2,1)}, u32[]{:S(2)}, u32[]{:S(2)}) %all-to-all-start) | async-done | bytes 524320 | tf_op jit(solution)/shard_map/all_to_all | solution.py:379
  44.8 2.5 %collective-permute-done.5.x_ref.r2_ref = bf16[192,2176]{1,0:T(8,128)(2,1)} collective-permute-done((bf16[192,2176]{1,0:T(8,128)(2,1)}, bf16[192,2176]{1,0:T(8,128)(2,1)}, u32[]{:S(2)}, u32[]{:S(2)}) %collective-permute-start.5) | collective-permute-done | bytes 835616 | tf_op jit(solution)/shard_map/ppermute | solution.py:301
  47.3 1.9 %copy-done.2 = bf16[1,4096,384]{2,1,0:T(8,128)(2,1)S(1)} copy-done((bf16[1,4096,384]{2,1,0:T(8,128)(2,1)S(1)}, bf16[1,4096,384]{2,1,0:T(8,128)(2,1)}, u32[]{:S(2)}) %copy-start.2) | copy-done | bytes 3145752
  49.2 2.3 %expert_partial.3 = (f32[192,384]{1,0:T(8,128)S(1)}, f32[192,384]{1,0:T(8,128)S(1)}) custom-call(s32[1]{0:T(128)} %bitcast.1.core_ref, bf16[192,2176]{1,0:T(8,128)(2,1)} %collective-permute-done.5.x_ref.r2_ref, bf16[1,4096,384]{2,1,0:T(8,128)(2,1)S(1)} %copy-done, bf16[1,4096,384]{2,1,0:T(8,128)(2,1)S(1)} %copy-done.2), custom_call_target="tpu_custom_call" | custom-call | flops 603979776 | bytes 4521984 | tf_op jit(solution)/shard_map/expert_partial/pallas_call | solution.py:188
  51.6 3.1 %expert_hidden.1.own_ref = bf16[384,384]{1,0:T(8,128)(2,1)S(1)} custom-call(s32[1]{0:T(128)} %bitcast.1.core_ref, bf16[192,2176]{1,0:T(8,128)(2,1)} %collective-permute-done.4.sr_ref, bf16[192,2176]{1,0:T(8,128)(2,1)S(1)} %collective-permute-done.6.r2_ref, bf16[1,4096,384]{2,1,0:T(8,128)(2,1)S(1)} %copy-done, bf16[1,4096,384]{2,1,0:T(8,128)(2,1)S(1)} %copy-done.3, ...), custom_call_target="tpu_custom_call" | custom-call | flops 1207959552 | bytes 6193152 | tf_op jit(solution)/shard_map/expert_hidden/pallas_call | solution.py:207
  55.4 1.1 %collective-permute-done.7.other_ref = bf16[384,384]{1,0:T(8,128)(2,1)S(1)} collective-permute-done((bf16[384,384]{1,0:T(8,128)(2,1)S(1)}, bf16[384,384]{1,0:T(8,128)(2,1)S(1)}, u32[]{:S(2)}, u32[]{:S(2)}) %collective-permute-start.7) | collective-permute-done | bytes 294944 | tf_op jit(solution)/shard_map/ppermute | solution.py:301
  56.5 2.4 %expert_back.3 = (f32[48,2048]{1,0:T(8,128)S(1)}, bf16[48,2048]{1,0:T(8,128)(2,1)S(1)}, bf16[48,2048]{1,0:T(8,128)(2,1)S(1)}, bf16[48,2048]{1,0:T(8,128)(2,1)S(1)}) custom-call(s32[2]{0:T(128)S(1)} %pad_add_fusion.at_ref, bf16[384,384]{1,0:T(8,128)(2,1)S(1)} %expert_hidden.1.own_ref, bf16[384,384]{1,0:T(8,128)(2,1)S(1)} %collective-permute-done.7.other_ref, ...), custom_call_target="tpu_custom_call" | custom-call | flops 603979776 | bytes 5308416 | tf_op jit(solution)/shard_map/expert_back/pallas_call | solution.py:275
  58.9 1.8 %collective-permute-start.11 = (bf16[48,2048]{1,0:T(8,128)(2,1)S(1)}, bf16[48,2048]{1,0:T(8,128)(2,1)S(1)}, u32[]{:S(2)}, u32[]{:S(2)}) collective-permute-start(bf16[48,2048]{1,0:T(8,128)(2,1)S(1)} %get-tuple-element.46.after_ref), channel_id=1, source_target_pairs={{0,2},{1,5},{2,0},{3,7},{4,6},{5,1},{6,4},{7,3},{8,10},{9,13},{10,... | collective-permute-start | bytes 589832 | tf_op jit(solution)/shard_map/ppermute | solution.py:301
  60.7 1.2 %collective-permute-start.12 = (bf16[48,2048]{1,0:T(8,128)(2,1)S(1)}, bf16[48,2048]{1,0:T(8,128)(2,1)S(1)}, u32[]{:S(2)}, u32[]{:S(2)}) collective-permute-start(bf16[48,2048]{1,0:T(8,128)(2,1)S(1)} %get-tuple-element.49), channel_id=1, source_target_pairs={{0,4},{1,3},{2,6},{3,1},{4,0},{5,7},{6,2},{7,5},{8,12},{9,11},{10,... | collective-permute-start | bytes 589832 | tf_op jit(solution)/shard_map/ppermute | solution.py:301
  62.5 2.4 %expert_back.2 = (f32[48,2048]{1,0:T(8,128)S(1)}, bf16[48,2048]{1,0:T(8,128)(2,1)S(1)}, bf16[48,2048]{1,0:T(8,128)(2,1)S(1)}, bf16[48,2048]{1,0:T(8,128)(2,1)S(1)}) custom-call(s32[2]{0:T(128)S(1)} %pad_add_fusion.at_ref, bf16[384,384]{1,0:T(8,128)(2,1)S(1)} %expert_hidden.1.own_ref, bf16[384,384]{1,0:T(8,128)(2,1)S(1)} %collective-permute-done.7.other_ref, ...), custom_call_target="tpu_custom_call" | custom-call | flops 603979776 | bytes 5308416 | tf_op jit(solution)/shard_map/expert_back/pallas_call | solution.py:275
  64.9 2.4 %collective-permute-start.10 = (bf16[48,2048]{1,0:T(8,128)(2,1)S(1)}, bf16[48,2048]{1,0:T(8,128)(2,1)S(1)}, u32[]{:S(2)}, u32[]{:S(2)}) collective-permute-start(bf16[48,2048]{1,0:T(8,128)(2,1)S(1)} %get-tuple-element.40), channel_id=1, source_target_pairs={{0,6},{1,7},{2,4},{3,5},{4,2},{5,3},{6,0},{7,1},{8,14},{9,15},{10,... | collective-permute-start | bytes 589832 | tf_op jit(solution)/shard_map/ppermute | solution.py:301
  67.9 3.0 %attention.1 = bf16[8,3,32,128]{3,2,1,0:T(8,128)(2,1)} custom-call(s32[1]{0:T(128)} %bitcast.me_ref, s32[16,16]{1,0:T(8,128)S(1)} %reshape.38.owner_ref, s32[16,16]{1,0:T(8,128)S(1)} %reshape.39.slot_ref, s32[16,16]{1,0:T(8,128)S(1)} %reshape.40.fill_ref, bf16[8,3,32,128]{3,2,1,0:T(8,128)(2,1)S(1)} %copy-done.10, ...), custom_call_target="tpu_custom_call" | custom-call | tf_op jit(solution)/shard_map/attention/pallas_call | solution.py:392
  72.1 2.6 %collective-permute-start.14 = (bf16[24,2048]{1,0:T(8,128)(2,1)S(1)}, bf16[24,2048]{1,0:T(8,128)(2,1)S(1)}, u32[]{:S(2)}, u32[]{:S(2)}) collective-permute-start(bf16[24,2048]{1,0:T(8,128)(2,1)S(1)} %slice.33), channel_id=1, source_target_pairs={{0,16},{1,17},{2,18},{3,19},{4,20},{5,21},{6,22},{7,23},{8,24},{9,... | collective-permute-start | bytes 294920 | tf_op jit(solution)/shard_map/ppermute | solution.py:301
  74.7 1.4 %collective-permute-done.10 = bf16[48,2048]{1,0:T(8,128)(2,1)S(1)} collective-permute-done((bf16[48,2048]{1,0:T(8,128)(2,1)S(1)}, bf16[48,2048]{1,0:T(8,128)(2,1)S(1)}, u32[]{:S(2)}, u32[]{:S(2)}) %collective-permute-start.10) | collective-permute-done | bytes 196640 | tf_op jit(solution)/shard_map/ppermute | solution.py:301
  76.2 2.8 %collective-permute-done.8 = bf16[48,2048]{1,0:T(8,128)(2,1)S(1)} collective-permute-done((bf16[48,2048]{1,0:T(8,128)(2,1)S(1)}, bf16[48,2048]{1,0:T(8,128)(2,1)S(1)}, u32[]{:S(2)}, u32[]{:S(2)}) %collective-permute-start.8) | collective-permute-done | bytes 196640 | tf_op jit(solution)/shard_map/ppermute | solution.py:301
  78.9 1.1 %collective-permute-done.9 = bf16[48,2048]{1,0:T(8,128)(2,1)S(1)} collective-permute-done((bf16[48,2048]{1,0:T(8,128)(2,1)S(1)}, bf16[48,2048]{1,0:T(8,128)(2,1)S(1)}, u32[]{:S(2)}, u32[]{:S(2)}) %collective-permute-start.9) | collective-permute-done | bytes 196640 | tf_op jit(solution)/shard_map/ppermute | solution.py:301
  80.1 1.9 %collective-permute-start.15 = (bf16[24,2048]{1,0:T(8,128)(2,1)S(1)}, bf16[24,2048]{1,0:T(8,128)(2,1)S(1)}, u32[]{:S(2)}, u32[]{:S(2)}) collective-permute-start(bf16[24,2048]{1,0:T(8,128)(2,1)S(1)} %get-tuple-element.52), channel_id=1, source_target_pairs={{0,8},{1,9},{2,10},{3,11},{4,12},{5,13},{6,14},{7,15},{8,0},{9,1},... | collective-permute-start | bytes 294920 | tf_op jit(solution)/shard_map/ppermute | solution.py:301
  82.1 2.5 %collective-permute-start.16 = (bf16[24,2048]{1,0:T(8,128)(2,1)S(1)}, bf16[24,2048]{1,0:T(8,128)(2,1)S(1)}, u32[]{:S(2)}, u32[]{:S(2)}) collective-permute-start(bf16[24,2048]{1,0:T(8,128)(2,1)S(1)} %get-tuple-element.53), channel_id=1, source_target_pairs={{0,24},{1,25},{2,26},{3,27},{4,28},{5,29},{6,30},{7,31},{8,16},{9,... | collective-permute-start | bytes 294920 | tf_op jit(solution)/shard_map/ppermute | solution.py:301
  85.0 4.3 %collective-permute-done.16 = bf16[24,2048]{1,0:T(8,128)(2,1)S(1)} collective-permute-done((bf16[24,2048]{1,0:T(8,128)(2,1)S(1)}, bf16[24,2048]{1,0:T(8,128)(2,1)S(1)}, u32[]{:S(2)}, u32[]{:S(2)}) %collective-permute-start.16) | collective-permute-done | bytes 98336 | tf_op jit(solution)/shard_map/ppermute | solution.py:301
  (58 shorter events, 12.1 us)
Async XLA Ops:
  0.6 32.9 %copy-start = (bf16[1,4096,384]{2,1,0:T(8,128)(2,1)S(1)}, bf16[1,4096,384]{2,1,0:T(8,128)(2,1)}, u32[]{:S(2)}) copy-start(bf16[1,4096,384]{2,1,0:T(8,128)(2,1)} %gate_ref.5) | copy-start | bytes 9437188
  0.6 1.1 %copy-start.11 = (bf16[8,3,4096]{2,0,1:T(8,128)(2,1)S(1)}, bf16[8,3,4096]{2,0,1:T(8,128)(2,1)}, u32[]{:S(2)}) copy-start(bf16[8,3,4096]{2,0,1:T(8,128)(2,1)} %param.18) | copy-start | bytes 589828
  1.7 0.7 copy-start.12
  2.4 0.7 copy-start.13
  3.3 12.3 %collective-permute-start = (bf16[24,2176]{1,0:T(8,128)(2,1)S(1)}, bf16[24,2176]{1,0:T(8,128)(2,1)S(1)}, u32[]{:S(2)}, u32[]{:S(2)}) collective-permute-start(bf16[24,2176]{1,0:T(8,128)(2,1)S(1)} %pack_tokens.1), channel_id=1, source_target_pairs={{0,16},{1,17},{2,18},{3,19},{4,20},{5,21},{6,22},{7,23},{8,24},{9,... | collective-permute-start | bytes 313352 | tf_op jit(solution)/shard_map/ppermute | solution.py:301
  7.4 8.2 %collective-permute-start.1 = (bf16[24,2176]{1,0:T(8,128)(2,1)S(1)}, bf16[24,2176]{1,0:T(8,128)(2,1)S(1)}, u32[]{:S(2)}, u32[]{:S(2)}) collective-permute-start(bf16[24,2176]{1,0:T(8,128)(2,1)S(1)} %pack_tokens.1), channel_id=1, source_target_pairs={{0,8},{1,9},{2,10},{3,11},{4,12},{5,13},{6,14},{7,15},{8,0},{9,1},... | collective-permute-start | bytes 313352 | tf_op jit(solution)/shard_map/ppermute | solution.py:301
  9.0 7.1 %collective-permute-start.2 = (bf16[24,2176]{1,0:T(8,128)(2,1)S(1)}, bf16[24,2176]{1,0:T(8,128)(2,1)}, u32[]{:S(2)}, u32[]{:S(2)}) collective-permute-start(bf16[24,2176]{1,0:T(8,128)(2,1)S(1)} %pack_tokens.1), channel_id=1, source_target_pairs={{0,24},{1,25},{2,26},{3,27},{4,28},{5,29},{6,30},{7,31},{8,16},{9,... | collective-permute-start | bytes 313352 | tf_op jit(solution)/shard_map/ppermute | solution.py:301
  14.8 0.8 copy-start.5
  17.7 11.8 %collective-permute-start.3 = (bf16[96,2176]{1,0:T(8,128)(2,1)}, bf16[96,2176]{1,0:T(8,128)(2,1)}, u32[]{:S(2)}, u32[]{:S(2)}) collective-permute-start(bf16[96,2176]{1,0:T(8,128)(2,1)} %pad_maximum_fusion.1), channel_id=1, source_target_pairs={{0,2},{1,5},{2,0},{3,7},{4,6},{5,1},{6,4},{7,3},{8,10},{9,13},{10,... | collective-permute-start | bytes 1253384 | tf_op jit(solution)/shard_map/ppermute | solution.py:301
  23.5 21.3 %all-to-all-start = ((bf16[32,2,2,16,128]{4,3,2,1,0:T(8,128)(2,1)}), bf16[32,2,2,16,128]{4,3,2,1,0:T(8,128)(2,1)}, u32[]{:S(2)}, u32[]{:S(2)}) async-start(bf16[32,2,2,16,128]{4,3,2,1,0:T(8,128)(2,1)} %copy-done.5), calls=%async_computation | async-start | bytes 1048576 | tf_op jit(solution)/shard_map/all_to_all | solution.py:379
  31.7 15.6 %collective-permute-start.5 = (bf16[192,2176]{1,0:T(8,128)(2,1)}, bf16[192,2176]{1,0:T(8,128)(2,1)}, u32[]{:S(2)}, u32[]{:S(2)}) collective-permute-start(bf16[192,2176]{1,0:T(8,128)(2,1)} %pad_maximum_fusion.x_ref.sr_ref), channel_id=1, source_target_pairs={{0,4},{1,3},{2,6},{3,1},{4,0},{5,7},{6,2},{7,5},{8,12},{9,11},{10,... | collective-permute-start | bytes 2506760 | tf_op jit(solution)/shard_map/ppermute | solution.py:301
  33.5 18.0 %collective-permute-start.4 = (bf16[192,2176]{1,0:T(8,128)(2,1)}, bf16[192,2176]{1,0:T(8,128)(2,1)}, u32[]{:S(2)}, u32[]{:S(2)}) collective-permute-start(bf16[192,2176]{1,0:T(8,128)(2,1)} %pad_maximum_fusion.x_ref.sr_ref), channel_id=1, source_target_pairs={{0,1},{1,0},{2,3},{3,2},{4,5},{5,4},{6,7},{7,6},{8,9},{9,8},{10,11... | collective-permute-start | bytes 2506760 | tf_op jit(solution)/shard_map/ppermute | solution.py:301
  33.6 1.9 %copy-start.1 = (bf16[1,4096,384]{2,1,0:T(8,128)(2,1)S(1)}, bf16[1,4096,384]{2,1,0:T(8,128)(2,1)}, u32[]{:S(2)}) copy-start(bf16[1,4096,384]{2,1,0:T(8,128)(2,1)} %up_ref.5) | copy-start | bytes 9437188
  37.6 0.7 copy-start.6
  38.3 0.7 copy-start.8
  47.3 4.2 %collective-permute-start.6 = (bf16[192,2176]{1,0:T(8,128)(2,1)}, bf16[192,2176]{1,0:T(8,128)(2,1)S(1)}, u32[]{:S(2)}, u32[]{:S(2)}) collective-permute-start(bf16[192,2176]{1,0:T(8,128)(2,1)} %collective-permute-done.5.x_ref.r2_ref), channel_id=1, source_target_pairs={{0,1},{1,0},{2,3},{3,2},{4,5},{5,4},{6,7},{7,6},{8,9},{9,8},{10,11... | collective-permute-start | bytes 2506760 | tf_op jit(solution)/shard_map/ppermute | solution.py:301
  47.3 1.9 %copy-start.2 = (bf16[1,4096,384]{2,1,0:T(8,128)(2,1)S(1)}, bf16[1,4096,384]{2,1,0:T(8,128)(2,1)}, u32[]{:S(2)}) copy-start(bf16[1,4096,384]{2,1,0:T(8,128)(2,1)} %up_ref.5) | copy-start | bytes 9437188
  49.2 2.3 %copy-start.3 = (bf16[1,4096,384]{2,1,0:T(8,128)(2,1)S(1)}, bf16[1,4096,384]{2,1,0:T(8,128)(2,1)}, u32[]{:S(2)}) copy-start(bf16[1,4096,384]{2,1,0:T(8,128)(2,1)} %up_ref.5) | copy-start | bytes 9437188
  49.2 2.3 %copy-start.7 = (f32[192,384]{1,0:T(8,128)S(1)}, f32[192,384]{1,0:T(8,128)}, u32[]{:S(2)}) copy-start(f32[192,384]{1,0:T(8,128)} %copy-done.6) | copy-start | bytes 884740
  49.2 2.3 %copy-start.9 = (f32[192,384]{1,0:T(8,128)S(1)}, f32[192,384]{1,0:T(8,128)}, u32[]{:S(2)}) copy-start(f32[192,384]{1,0:T(8,128)} %copy-done.8) | copy-start | bytes 884740
  51.6 4.9 %copy-start.4 = (bf16[1,768,2048]{2,1,0:T(8,128)(2,1)S(1)}, bf16[1,768,2048]{2,1,0:T(8,128)(2,1)}, u32[]{:S(2)}) copy-start(bf16[1,768,2048]{2,1,0:T(8,128)(2,1)} %down_ref.3) | copy-start | bytes 9437188
  54.7 1.8 %collective-permute-start.7 = (bf16[384,384]{1,0:T(8,128)(2,1)S(1)}, bf16[384,384]{1,0:T(8,128)(2,1)S(1)}, u32[]{:S(2)}, u32[]{:S(2)}) collective-permute-start(bf16[384,384]{1,0:T(8,128)(2,1)S(1)} %expert_hidden.1.own_ref), channel_id=1, source_target_pairs={{0,1},{1,0},{2,3},{3,2},{4,5},{5,4},{6,7},{7,6},{8,9},{9,8},{10,11... | collective-permute-start | bytes 884744 | tf_op jit(solution)/shard_map/ppermute | solution.py:301
  58.9 9.0 %copy-start.10 = (bf16[8,3,32,128]{3,2,1,0:T(8,128)(2,1)S(1)}, bf16[8,3,32,128]{3,2,1,0:T(8,128)(2,1)}, u32[]{:S(2)}) copy-start(bf16[8,3,32,128]{3,2,1,0:T(8,128)(2,1)} %q_ref.1) | copy-start | bytes 589828
  58.9 11.9 %collective-permute-start.11 = (bf16[48,2048]{1,0:T(8,128)(2,1)S(1)}, bf16[48,2048]{1,0:T(8,128)(2,1)S(1)}, u32[]{:S(2)}, u32[]{:S(2)}) collective-permute-start(bf16[48,2048]{1,0:T(8,128)(2,1)S(1)} %get-tuple-element.46.after_ref), channel_id=1, source_target_pairs={{0,2},{1,5},{2,0},{3,7},{4,6},{5,1},{6,4},{7,3},{8,10},{9,13},{10,... | collective-permute-start | bytes 589832 | tf_op jit(solution)/shard_map/ppermute | solution.py:301
  60.7 10.7 %collective-permute-start.12 = (bf16[48,2048]{1,0:T(8,128)(2,1)S(1)}, bf16[48,2048]{1,0:T(8,128)(2,1)S(1)}, u32[]{:S(2)}, u32[]{:S(2)}) collective-permute-start(bf16[48,2048]{1,0:T(8,128)(2,1)S(1)} %get-tuple-element.49), channel_id=1, source_target_pairs={{0,4},{1,3},{2,6},{3,1},{4,0},{5,7},{6,2},{7,5},{8,12},{9,11},{10,... | collective-permute-start | bytes 589832 | tf_op jit(solution)/shard_map/ppermute | solution.py:301
  61.9 10.1 %collective-permute-start.13 = (bf16[48,2048]{1,0:T(8,128)(2,1)S(1)}, bf16[48,2048]{1,0:T(8,128)(2,1)S(1)}, u32[]{:S(2)}, u32[]{:S(2)}) collective-permute-start(bf16[48,2048]{1,0:T(8,128)(2,1)S(1)} %get-tuple-element.50), channel_id=1, source_target_pairs={{0,6},{1,7},{2,4},{3,5},{4,2},{5,3},{6,0},{7,1},{8,14},{9,15},{10,... | collective-permute-start | bytes 589832 | tf_op jit(solution)/shard_map/ppermute | solution.py:301
  64.9 11.3 %collective-permute-start.10 = (bf16[48,2048]{1,0:T(8,128)(2,1)S(1)}, bf16[48,2048]{1,0:T(8,128)(2,1)S(1)}, u32[]{:S(2)}, u32[]{:S(2)}) collective-permute-start(bf16[48,2048]{1,0:T(8,128)(2,1)S(1)} %get-tuple-element.40), channel_id=1, source_target_pairs={{0,6},{1,7},{2,4},{3,5},{4,2},{5,3},{6,0},{7,1},{8,14},{9,15},{10,... | collective-permute-start | bytes 589832 | tf_op jit(solution)/shard_map/ppermute | solution.py:301
  67.3 11.6 %collective-permute-start.8 = (bf16[48,2048]{1,0:T(8,128)(2,1)S(1)}, bf16[48,2048]{1,0:T(8,128)(2,1)S(1)}, u32[]{:S(2)}, u32[]{:S(2)}) collective-permute-start(bf16[48,2048]{1,0:T(8,128)(2,1)S(1)} %get-tuple-element.38), channel_id=1, source_target_pairs={{0,2},{1,5},{2,0},{3,7},{4,6},{5,1},{6,4},{7,3},{8,10},{9,13},{10,... | collective-permute-start | bytes 589832 | tf_op jit(solution)/shard_map/ppermute | solution.py:301
  70.9 9.1 %collective-permute-start.9 = (bf16[48,2048]{1,0:T(8,128)(2,1)S(1)}, bf16[48,2048]{1,0:T(8,128)(2,1)S(1)}, u32[]{:S(2)}, u32[]{:S(2)}) collective-permute-start(bf16[48,2048]{1,0:T(8,128)(2,1)S(1)} %get-tuple-element.39), channel_id=1, source_target_pairs={{0,4},{1,3},{2,6},{3,1},{4,0},{5,7},{6,2},{7,5},{8,12},{9,11},{10,... | collective-permute-start | bytes 589832 | tf_op jit(solution)/shard_map/ppermute | solution.py:301
  72.1 12.4 %collective-permute-start.14 = (bf16[24,2048]{1,0:T(8,128)(2,1)S(1)}, bf16[24,2048]{1,0:T(8,128)(2,1)S(1)}, u32[]{:S(2)}, u32[]{:S(2)}) collective-permute-start(bf16[24,2048]{1,0:T(8,128)(2,1)S(1)} %slice.33), channel_id=1, source_target_pairs={{0,16},{1,17},{2,18},{3,19},{4,20},{5,21},{6,22},{7,23},{8,24},{9,... | collective-permute-start | bytes 294920 | tf_op jit(solution)/shard_map/ppermute | solution.py:301
  80.1 4.9 %collective-permute-start.15 = (bf16[24,2048]{1,0:T(8,128)(2,1)S(1)}, bf16[24,2048]{1,0:T(8,128)(2,1)S(1)}, u32[]{:S(2)}, u32[]{:S(2)}) collective-permute-start(bf16[24,2048]{1,0:T(8,128)(2,1)S(1)} %get-tuple-element.52), channel_id=1, source_target_pairs={{0,8},{1,9},{2,10},{3,11},{4,12},{5,13},{6,14},{7,15},{8,0},{9,1},... | collective-permute-start | bytes 294920 | tf_op jit(solution)/shard_map/ppermute | solution.py:301
  82.1 7.3 %collective-permute-start.16 = (bf16[24,2048]{1,0:T(8,128)(2,1)S(1)}, bf16[24,2048]{1,0:T(8,128)(2,1)S(1)}, u32[]{:S(2)}, u32[]{:S(2)}) collective-permute-start(bf16[24,2048]{1,0:T(8,128)(2,1)S(1)} %get-tuple-element.53), channel_id=1, source_target_pairs={{0,24},{1,25},{2,26},{3,27},{4,28},{5,29},{6,30},{7,31},{8,16},{9,... | collective-permute-start | bytes 294920 | tf_op jit(solution)/shard_map/ppermute | solution.py:301
  (1 other events, 0.7 us)

commit v9 on v8

--- a/solution.py
+++ b/solution.py
@@ -21,46 +21,60 @@
     return pl.BlockSpec(memory_space=pltpu.SMEM)
 
 
-def page_kernel(pages, me_ref, owner_ref, kv_ref, send_ref, count_ref):
+def page_kernel(pages, me_ref, owner_ref, kv_ref, *refs):
+    out_refs, placed_ref, count_ref = refs[:4], refs[4], refs[5]
     values = kv_ref[...].astype(jnp.float32)
     largest = jnp.max(jnp.abs(values), axis=(3, 4), keepdims=True)
     scale = jnp.full(largest.shape, 2.0 ** (-16), jnp.float32)
     inverse = jnp.full(largest.shape, 2.0**16, jnp.float32)
-    for exponent in range(-16, 4):
+    for exponent in range(-16, -6):
         exceeds = largest > LIMIT * 2.0**exponent
         scale = jnp.where(exceeds, scale * 2.0, scale)
         inverse = jnp.where(exceeds, inverse * 0.5, inverse)
     scaled = values * inverse
-    magnitude = jnp.abs(scaled)
+    rest = jnp.abs(scaled) * 2.0**6
     step = jnp.full(scaled.shape, 2.0 ** (-9), jnp.float32)
-    back = jnp.full(scaled.shape, 2.0**9, jnp.float32)
-    for exponent in range(-5, 9):
-        exceeds = magnitude >= 2.0**exponent
-        step = jnp.where(exceeds, step * 2.0, step)
-        back = jnp.where(exceeds, back * 0.5, back)
-    levels = jnp.minimum(jnp.floor(magnitude * back + 0.5) * step, LIMIT)
+    for bits in (8, 4, 2, 1):
+        exceeds = rest >= 2.0**bits
+        rest = jnp.where(exceeds, rest * 2.0**-bits, rest)
+        step = jnp.where(exceeds, step * 2.0**bits, step)
+    levels = jnp.minimum(jnp.floor(rest * 8.0 + 0.5) * step, LIMIT)
     cache = (jnp.where(scaled < 0.0, -levels, levels) * scale).astype(jnp.bfloat16)
 
-    send_ref[...] = jnp.zeros(send_ref.shape, send_ref.dtype)
+    placed_ref[...] = jnp.zeros(placed_ref.shape, placed_ref.dtype)
 
     def clear(o, carry):
         count_ref[o] = 0
         return carry
 
     lax.fori_loop(0, count_ref.shape[0], clear, 0)
-    first = me_ref[0] * pages
+    me = me_ref[0]
+    slots = out_refs[0].shape[0]
     for page in range(pages):
-        owner = owner_ref[first + page]
+        owner = owner_ref[me * pages + page]
         rank = count_ref[owner]
         count_ref[owner] = rank + 1
-        send_ref[pl.ds(owner * CAP + rank, 1)] = cache[page : page + 1]
+        apart = owner ^ me
+        slot = (apart & 3) * slots + (apart >> 2) * CAP + rank
+        placed_ref[pl.ds(slot, 1)] = cache[page : page + 1]
+    for k, ref in enumerate(out_refs):
+        ref[...] = placed_ref[k * slots : (k + 1) * slots]
+
+
+def regroup_kernel(*refs):
+    in_refs, out_refs = refs[:4], refs[4:]
+    for z, out in enumerate(out_refs):
+        for k, ref in enumerate(in_refs):
+            out[k * CAP : (k + 1) * CAP] = ref[z * CAP : (z + 1) * CAP]
 
 
 def attention_kernel(
-    pages, me_ref, owner_ref, slot_ref, fill_ref, q_ref, cache_ref, fresh_ref, after_ref, out_ref
+    pages, me_ref, owner_ref, slot_ref, fill_ref, q_ref, fresh_ref, after_ref, *refs
 ):
+    cache_refs, out_ref = refs[:-1], refs[-1]
     owners = owner_ref.shape[0]
-    slots, _, heads, page_len, width = cache_ref.shape
+    _, _, heads, page_len, width = cache_refs[0].shape
+    slots = owners * CAP
     requests, steps, q_heads, _ = q_ref.shape
     group = q_heads // heads
     rows = requests * steps * group
@@ -79,7 +93,7 @@
         held = jnp.sum(
             jnp.where((mine > 0.0) & (rank == float(c)), code, 0.0), axis=1, keepdims=True
         )
-        spread = jnp.where(place // page_len == source * CAP + c, held, spread)
+        spread = jnp.where(place // page_len == (source ^ me_ref[0]) * CAP + c, held, spread)
     line = jnp.sum(spread, axis=0, keepdims=True).astype(jnp.int32)
     request_of = line // (page_len + 1)
     fill_of = line - request_of * (page_len + 1)
@@ -95,8 +109,13 @@
     contract = (((1,), (1,)), ((), ()))
     for head in range(heads):
         q = q_ref[:, :, head * group : (head + 1) * group, :].reshape(rows, width)
-        keys = cache_ref[:, 0, head].reshape(columns, width)
-        values = cache_ref[:, 1, head].reshape(columns, width)
+        keys, values = (
+            jnp.concatenate(
+                [ref[:, i, head].reshape(ref.shape[0] * page_len, width) for ref in cache_refs],
+                axis=0,
+            )
+            for i in range(2)
+        )
         scores = lax.dot_general(q, keys, contract, preferred_element_type=jnp.float32) * factor
         fresh = (
             lax.dot_general(q, fresh_ref[0, head], contract, preferred_element_type=jnp.float32)
@@ -306,8 +325,8 @@
     def flip(self, x, turn):
         return self.go(x, lambda ep, core: (ep ^ (1 << ((core + turn) % 2))) * 2 + core)
 
-    def diagonal(self, x):
-        return self.go(x, lambda ep, core: (ep ^ 3) * 2 + core)
+    def across(self, x, turn):
+        return self.go(x, lambda ep, core: (ep ^ turn) * 2 + core)
 
     def cores(self, x):
         return self.go(x, lambda ep, core: ep * 2 + 1 - core)
@@ -355,13 +374,18 @@
         expert_routes.reshape(tokens, top),
         route_probs.transpose(1, 0, 2).reshape(tokens, top),
     )
+    page_shape = (moves.lines * CAP, 2, heads, page_len, width)
+    pages_out = jax.ShapeDtypeStruct(page_shape, jnp.bfloat16)
     send = pl.pallas_call(
         functools.partial(page_kernel, pages),
-        out_shape=jax.ShapeDtypeStruct((slots, 2, heads, page_len, width), jnp.bfloat16),
-        in_specs=[smem(), smem()] + [vmem()],
-        out_specs=vmem(),
-        scratch_shapes=[pltpu.SMEM((owners,), jnp.int32)],
-        compiler_params=pltpu.CompilerParams(vmem_limit_bytes=room(*[prompt_kv] * 5)),
+        out_shape=[pages_out] * 4,
+        in_specs=[smem(), smem(), vmem()],
+        out_specs=[vmem()] * 4,
+        scratch_shapes=[
+            pltpu.VMEM((slots,) + page_shape[1:], jnp.bfloat16),
+            pltpu.SMEM((owners,), jnp.int32),
+        ],
+        compiler_params=pltpu.CompilerParams(vmem_limit_bytes=room(*[prompt_kv] * 8)),
         name="quantize_pages",
     )(me_ref, page_owner.reshape(-1), prompt_kv.transpose(0, 1, 3, 2, 4))
 
@@ -369,20 +393,30 @@
     line = [moves.along_z(mine, turn) if turn else mine for chips in sets for turn in chips]
     line = jnp.concatenate(line, axis=0)
     line, send = lax.optimization_barrier((line, send))
+    held = [send[0]] + [moves.across(send[turn], turn) for turn in (1, 2, 3)]
+    held = pl.pallas_call(
+        regroup_kernel,
+        out_shape=[jax.ShapeDtypeStruct((4 * CAP,) + page_shape[1:], jnp.bfloat16)] * moves.lines,
+        in_specs=[vmem()] * 4,
+        out_specs=[vmem()] * moves.lines,
+        compiler_params=pltpu.CompilerParams(vmem_limit_bytes=room(*[pages_out] * 8)),
+        name="regroup_pages",
+    )(*held)
     fresh = new_kv.transpose(2, 3, 0, 1, 4).reshape(2, heads, tokens, width)
     fresh = jnp.pad(fresh, ((0, 0), (0, 0), (0, 128 - tokens), (0, 0)))
     tables = [t.reshape(owners, pages) for t in (page_owner, page_slot, page_fill)]
     sr = jnp.concatenate([line, moves.flip(line, 0)], axis=0)
-    sr, fresh, tables = lax.optimization_barrier((sr, fresh, tables))
+    sr, held, fresh, tables = lax.optimization_barrier((sr, held, fresh, tables))
+    cache = [moves.along_z(x, turn) if turn else x for turn, x in enumerate(held)]
     r2 = moves.flip(sr, 1)
 
-    cache = lax.all_to_all(send, "ep", split_axis=0, concat_axis=0, tiled=True)
 
     early = expert_partial(own_core, sr, w_gate, w_up)
-    r2, cache, early = lax.optimization_barrier((r2, cache, early))
+    r2, early = lax.optimization_barrier((r2, early))
     other_sr, other_r2 = moves.cores(sr), moves.cores(r2)
     parts = early + expert_partial(own_core, r2, w_gate, w_up)
-    hidden = expert_hidden(own_core, other_sr, other_r2, w_gate, w_up, parts)
+    core_then, cache = lax.optimization_barrier((own_core, cache))
+    hidden = expert_hidden(core_then, other_sr, other_r2, w_gate, w_up, parts)
     other_hidden = moves.cores(hidden)
     piece = line.shape[0] // 2
     backs = [
@@ -392,7 +426,10 @@
     attn_out = pl.pallas_call(
         functools.partial(attention_kernel, pages),
         out_shape=jax.ShapeDtypeStruct(queries.shape, jnp.bfloat16),
-        in_specs=[smem()] + [vmem()] * 6 + [pl.BlockSpec(memory_space=pl.ANY)],
+        in_specs=[smem()]
+        + [vmem()] * 5
+        + [pl.BlockSpec(memory_space=pl.ANY)]
+        + [vmem()] * moves.lines,
         out_specs=vmem(),
         compiler_params=pltpu.CompilerParams(
             vmem_limit_bytes=8 * MIB + 16 * slots * page_len * tokens * q_heads
@@ -402,13 +439,13 @@
         me_ref,
         *tables,
         queries,
-        cache,
         fresh,
         backs[1][1],
+        *cache,
     )
     sums = []
     for total, *send in backs:
-        for rows in (moves.flip(send[0], 0), moves.flip(send[1], 1), moves.diagonal(send[2])):
+        for rows in (moves.flip(send[0], 0), moves.flip(send[1], 1), moves.across(send[2], 3)):
             total = total + rows.astype(jnp.float32)
         sums.append(total)
     sums[0], attn_out = lax.optimization_barrier((sums[0], attn_out))

time: 90.7 us -> 100 us (1.10)
  waiting for transfers between devices: 20.6 us -> 36.8 us
  Pallas kernels: 19.6 us -> 12.6 us
  starting transfers between devices: 29.9 us -> 35.5 us
  local copies, waits for them, and re-layouts: 13 us -> 8.98 us
    ppermute x17 -> x23, waiting for transfers between devices: 14.8 us -> 36.8 us  [go(): return lax.ppermute(x, ('ep', 'pd'), perm)]
    ppermute x17 -> x23, starting transfers between devices: 23.8 us -> 35.5 us  [go(): return lax.ppermute(x, ('ep', 'pd'), perm)]
    all_to_all x1 -> x0, starting transfers between devices: 6.11 us -> none  [body(): cache = lax.all_to_all(send, 'ep', split_axis=0, concat_axis=0, tiled=True)]
    all_to_all x1 -> x0, waiting for transfers between devices: 5.79 us -> none  [body(): cache = lax.all_to_all(send, 'ep', split_axis=0, concat_axis=0, tiled=True)]
    unnamed x32 -> x20, local copies, waits for them, and re-layouts: 10.7 us -> 6.6 us
    pallas_call x2, Pallas kernels: 4.41 us -> 2.01 us  [expert_partial(): pl.pallas_call(functools.partial(partial_kernel, 4), in_specs=[smem()] +...]
    pallas_call x2, Pallas kernels: 4.81 us -> 3.05 us  [expert_back(): pl.pallas_call(functools.partial(back_kernel, experts, begin, 4), out_sha...]
    pallas_call x1, Pallas kernels: 3.13 us -> 1.83 us  [expert_hidden(): pl.pallas_call(functools.partial(hidden_kernel, 4), in_specs=[smem()] + [...]
  transfers between devices with their start and end apart: 18 -> 23, of which waited for: 10 -> 12; matrix products, arithmetic and copies ran while one was open for 8% -> 6% of each run, Pallas kernels for 15% -> 9%
where the time goes in v9:
time: 100 us; the launch traced here: 99.9 us
  waiting for transfers between devices  36.8 us (37%)
  starting transfers between devices  35.5 us (36%)
  Pallas kernels  12.6 us (13%)
  local copies, waits for them, and re-layouts  8.98 us (9%)
  other arithmetic  5.2 us (5%)
    ppermute x23, waiting for transfers between devices, go(): return lax.ppermute(x, ('ep', 'pd'), perm)  36.8 us
    ppermute x23, starting transfers between devices, go(): return lax.ppermute(x, ('ep', 'pd'), perm)  35.5 us
    unnamed x20, local copies, waits for them, and re-layouts  6.6 us
    pallas_call x2, Pallas kernels, expert_back(): pl.pallas_call(functools.partial(back_kernel, experts, begin, 4), out_sha...  3.05 us
    pallas_call x1, Pallas kernels, body(): pl.pallas_call(functools.partial(page_kernel, pages), out_shape=[pages_ou...  2.6 us
    pallas_call x2, Pallas kernels, expert_partial(): pl.pallas_call(functools.partial(partial_kernel, 4), in_specs=[smem()] +...  2.01 us
  transfers between devices with their start and end apart: 23, of which 12 were waited for; matrix products, arithmetic and copies ran while one was open for 6% of the time, Pallas kernels for 9%

profile of v9, /device:TPU:0, one launch (start us, length us, event | category | flops | bytes accessed | tf_op | source)
XLA Modules:
  0.0 99.9 jit_solution(11394191718449120202)
XLA Ops:
  3.3 4.1 %collective-permute-start = (bf16[24,2176]{1,0:T(8,128)(2,1)S(1)}, bf16[24,2176]{1,0:T(8,128)(2,1)S(1)}, u32[]{:S(2)}, u32[]{:S(2)}) collective-permute-start(bf16[24,2176]{1,0:T(8,128)(2,1)S(1)} %pack_tokens.1), channel_id=1, source_target_pairs={{0,16},{1,17},{2,18},{3,19},{4,20},{5,21},{6,22},{7,23},{8,24},{9,... | collective-permute-start | bytes 313352 | tf_op jit(solution)/shard_map/ppermute | solution.py:320
  7.4 1.6 %collective-permute-start.1 = (bf16[24,2176]{1,0:T(8,128)(2,1)S(1)}, bf16[24,2176]{1,0:T(8,128)(2,1)}, u32[]{:S(2)}, u32[]{:S(2)}) collective-permute-start(bf16[24,2176]{1,0:T(8,128)(2,1)S(1)} %pack_tokens.1), channel_id=1, source_target_pairs={{0,8},{1,9},{2,10},{3,11},{4,12},{5,13},{6,14},{7,15},{8,0},{9,1},... | collective-permute-start | bytes 313352 | tf_op jit(solution)/shard_map/ppermute | solution.py:320
  10.6 2.6 %quantize_pages.1 = (bf16[8,2,2,16,128]{4,3,2,1,0:T(8,128)(2,1)S(1)}, bf16[8,2,2,16,128]{4,3,2,1,0:T(8,128)(2,1)}, bf16[8,2,2,16,128]{4,3,2,1,0:T(8,128)(2,1)}, bf16[8,2,2,16,128]{4,3,2,1,0:T(8,128)(2,1)}) custom-call(s32[1]{0:T(128)} %bitcast.me_ref, s32[256]{0:T(256)S(1)} %bitcast.25, bf16[16,2,2,16,128]{4,3,2,1,0:T(8,128)(2,1)S(1)} %bitcast.21), custom_call_target="tpu_custom_call" | custom-call | tf_op jit(solution)/shard_map/quantize_pages/pallas_call | solution.py:379
  14.1 2.0 %collective-permute-done.2 = bf16[24,2176]{1,0:T(8,128)(2,1)} collective-permute-done((bf16[24,2176]{1,0:T(8,128)(2,1)S(1)}, bf16[24,2176]{1,0:T(8,128)(2,1)}, u32[]{:S(2)}, u32[]{:S(2)}) %collective-permute-start.2) | collective-permute-done | bytes 104480 | tf_op jit(solution)/shard_map/ppermute | solution.py:320
  16.1 1.7 %pad_maximum_fusion.1 = bf16[96,2176]{1,0:T(8,128)(2,1)} fusion(bf16[24,2176]{1,0:T(8,128)(2,1)} %collective-permute-done.2, bf16[24,2176]{1,0:T(8,128)(2,1)} %collective-permute-done.1, bf16[24,2176]{1,0:T(8,128)(2,1)S(1)} %collective-permute-done, bf16[24,2176]{1,0:T(8,128)(2,1)S(1)} %pack_tokens.1), kind=kLoop, calls=%fused_computation.1 | loop fusion | flops 1671168 | bytes 835584 | tf_op jit(solution)/shard_map/concatenate | solution.py:394
  17.8 1.5 %collective-permute-start.3 = (bf16[96,2176]{1,0:T(8,128)(2,1)}, bf16[96,2176]{1,0:T(8,128)(2,1)}, u32[]{:S(2)}, u32[]{:S(2)}) collective-permute-start(bf16[96,2176]{1,0:T(8,128)(2,1)} %pad_maximum_fusion.1), channel_id=1, source_target_pairs={{0,2},{1,5},{2,0},{3,7},{4,6},{5,1},{6,4},{7,3},{8,10},{9,13},{10,... | collective-permute-start | bytes 1253384 | tf_op jit(solution)/shard_map/ppermute | solution.py:320
  19.8 1.5 %collective-permute-start.5 = (bf16[8,2,2,16,128]{4,3,2,1,0:T(8,128)(2,1)}, bf16[8,2,2,16,128]{4,3,2,1,0:T(8,128)(2,1)}, u32[]{:S(2)}, u32[]{:S(2)}) collective-permute-start(bf16[8,2,2,16,128]{4,3,2,1,0:T(8,128)(2,1)} %get-tuple-element.53), channel_id=1, source_target_pairs={{0,4},{1,5},{2,6},{3,7},{4,0},{5,1},{6,2},{7,3},{8,12},{9,13},{10,... | collective-permute-start | bytes 393224 | tf_op jit(solution)/shard_map/ppermute | solution.py:320
  21.3 1.4 %collective-permute-start.6 = (bf16[8,2,2,16,128]{4,3,2,1,0:T(8,128)(2,1)}, bf16[8,2,2,16,128]{4,3,2,1,0:T(8,128)(2,1)}, u32[]{:S(2)}, u32[]{:S(2)}) collective-permute-start(bf16[8,2,2,16,128]{4,3,2,1,0:T(8,128)(2,1)} %get-tuple-element.54), channel_id=1, source_target_pairs={{0,6},{1,7},{2,4},{3,5},{4,2},{5,3},{6,0},{7,1},{8,14},{9,15},{10,... | collective-permute-start | bytes 393224 | tf_op jit(solution)/shard_map/ppermute | solution.py:320
  24.1 1.3 %reduce.3 = s32[256]{0:T(256)S(1)} reduce(s32[256,1]{0,1:T(1,128)} %param.13, s32[]{:T(128)} %broadcast.5), dimensions={1}, to_apply=%param.13.reduce_sub_computation.3 | reduce | bytes 2052 | tf_op args[1]
  27.0 2.6 %collective-permute-done.4.refs_1_ = bf16[8,2,2,16,128]{4,3,2,1,0:T(8,128)(2,1)S(1)} collective-permute-done((bf16[8,2,2,16,128]{4,3,2,1,0:T(8,128)(2,1)}, bf16[8,2,2,16,128]{4,3,2,1,0:T(8,128)(2,1)S(1)}, u32[]{:S(2)}, u32[]{:S(2)}) %collective-permute-start.4) | collective-permute-done | bytes 131104 | tf_op jit(solution)/shard_map/ppermute | solution.py:320
  29.6 1.7 %collective-permute-done.6.refs_3_ = bf16[8,2,2,16,128]{4,3,2,1,0:T(8,128)(2,1)} collective-permute-done((bf16[8,2,2,16,128]{4,3,2,1,0:T(8,128)(2,1)}, bf16[8,2,2,16,128]{4,3,2,1,0:T(8,128)(2,1)}, u32[]{:S(2)}, u32[]{:S(2)}) %collective-permute-start.6) | collective-permute-done | bytes 131104 | tf_op jit(solution)/shard_map/ppermute | solution.py:320
  33.5 1.3 %collective-permute-start.11 = (bf16[192,2176]{1,0:T(8,128)(2,1)S(1)}, bf16[192,2176]{1,0:T(8,128)(2,1)S(1)}, u32[]{:S(2)}, u32[]{:S(2)}) collective-permute-start(bf16[192,2176]{1,0:T(8,128)(2,1)S(1)} %pad_maximum_fusion.x_ref.sr_ref), channel_id=1, source_target_pairs={{0,4},{1,3},{2,6},{3,1},{4,0},{5,7},{6,2},{7,5},{8,12},{9,11},{10,... | collective-permute-start | bytes 2506760 | tf_op jit(solution)/shard_map/ppermute | solution.py:320
  34.9 1.9 %copy-done.1 = bf16[1,4096,384]{2,1,0:T(8,128)(2,1)S(1)} copy-done((bf16[1,4096,384]{2,1,0:T(8,128)(2,1)S(1)}, bf16[1,4096,384]{2,1,0:T(8,128)(2,1)}, u32[]{:S(2)}) %copy-start.1) | copy-done | bytes 3145752
  37.8 8.3 %collective-permute-done.11.x_ref.r2_ref = bf16[192,2176]{1,0:T(8,128)(2,1)S(1)} collective-permute-done((bf16[192,2176]{1,0:T(8,128)(2,1)S(1)}, bf16[192,2176]{1,0:T(8,128)(2,1)S(1)}, u32[]{:S(2)}, u32[]{:S(2)}) %collective-permute-start.11) | collective-permute-done | bytes 835616 | tf_op jit(solution)/shard_map/ppermute | solution.py:320
  46.1 2.4 %collective-permute-start.7 = (bf16[8,2,2,16,128]{4,3,2,1,0:T(8,128)(2,1)S(1)}, bf16[8,2,2,16,128]{4,3,2,1,0:T(8,128)(2,1)S(1)}, u32[]{:S(2)}, u32[]{:S(2)}) collective-permute-start(bf16[8,2,2,16,128]{4,3,2,1,0:T(8,128)(2,1)S(1)} %get-tuple-element.60), channel_id=1, source_target_pairs={{0,8},{1,9},{2,10},{3,11},{4,12},{5,13},{6,14},{7,15},{8,0},{9,1},... | collective-permute-start | bytes 393224 | tf_op jit(solution)/shard_map/ppermute | solution.py:320
  48.5 2.1 %collective-permute-start.8 = (bf16[8,2,2,16,128]{4,3,2,1,0:T(8,128)(2,1)S(1)}, bf16[8,2,2,16,128]{4,3,2,1,0:T(8,128)(2,1)S(1)}, u32[]{:S(2)}, u32[]{:S(2)}) collective-permute-start(bf16[8,2,2,16,128]{4,3,2,1,0:T(8,128)(2,1)S(1)} %get-tuple-element.61), channel_id=1, source_target_pairs={{0,16},{1,17},{2,18},{3,19},{4,20},{5,21},{6,22},{7,23},{8,24},{9,... | collective-permute-start | bytes 393224 | tf_op jit(solution)/shard_map/ppermute | solution.py:320
  50.6 1.4 %collective-permute-start.9 = (bf16[8,2,2,16,128]{4,3,2,1,0:T(8,128)(2,1)S(1)}, bf16[8,2,2,16,128]{4,3,2,1,0:T(8,128)(2,1)S(1)}, u32[]{:S(2)}, u32[]{:S(2)}) collective-permute-start(bf16[8,2,2,16,128]{4,3,2,1,0:T(8,128)(2,1)S(1)} %get-tuple-element.62), channel_id=1, source_target_pairs={{0,24},{1,25},{2,26},{3,27},{4,28},{5,29},{6,30},{7,31},{8,16},{9,... | collective-permute-start | bytes 393224 | tf_op jit(solution)/shard_map/ppermute | solution.py:320
  52.0 3.4 %collective-permute-done.7.refs_1_ = bf16[8,2,2,16,128]{4,3,2,1,0:T(8,128)(2,1)S(1)} collective-permute-done((bf16[8,2,2,16,128]{4,3,2,1,0:T(8,128)(2,1)S(1)}, bf16[8,2,2,16,128]{4,3,2,1,0:T(8,128)(2,1)S(1)}, u32[]{:S(2)}, u32[]{:S(2)}) %collective-permute-start.7) | collective-permute-done | bytes 131104 | tf_op jit(solution)/shard_map/ppermute | solution.py:320
  55.6 6.0 %collective-permute-done.9.refs_3_ = bf16[8,2,2,16,128]{4,3,2,1,0:T(8,128)(2,1)S(1)} collective-permute-done((bf16[8,2,2,16,128]{4,3,2,1,0:T(8,128)(2,1)S(1)}, bf16[8,2,2,16,128]{4,3,2,1,0:T(8,128)(2,1)S(1)}, u32[]{:S(2)}, u32[]{:S(2)}) %collective-permute-start.9) | collective-permute-done | bytes 131104 | tf_op jit(solution)/shard_map/ppermute | solution.py:320
  62.6 1.8 %expert_hidden.1.own_ref = bf16[384,384]{1,0:T(8,128)(2,1)S(1)} custom-call(s32[1]{0:T(128)} %bitcast.1.core_ref, bf16[192,2176]{1,0:T(8,128)(2,1)S(1)} %collective-permute-done.10.sr_ref, bf16[192,2176]{1,0:T(8,128)(2,1)S(1)} %collective-permute-done.12.r2_ref, bf16[1,4096,384]{2,1,0:T(8,128)(2,1)S(1)} %copy-done, bf16[1,4096,384]{2,1,0:T(8,128)(2,1)S(1)} %copy-done.2, ...), custom_call_target="tpu_custom_call" | custom-call | flops 1207959552 | bytes 6193152 | tf_op jit(solution)/shard_map/expert_hidden/pallas_call | solution.py:226
  64.6 1.5 %collective-permute-done.13.other_ref = bf16[384,384]{1,0:T(8,128)(2,1)S(1)} collective-permute-done((bf16[384,384]{1,0:T(8,128)(2,1)S(1)}, bf16[384,384]{1,0:T(8,128)(2,1)S(1)}, u32[]{:S(2)}, u32[]{:S(2)}) %collective-permute-start.13) | collective-permute-done | bytes 294944 | tf_op jit(solution)/shard_map/ppermute | solution.py:320
  66.1 1.5 %expert_back.3 = (f32[48,2048]{1,0:T(8,128)S(1)}, bf16[48,2048]{1,0:T(8,128)(2,1)S(1)}, bf16[48,2048]{1,0:T(8,128)(2,1)S(1)}, bf16[48,2048]{1,0:T(8,128)(2,1)S(1)}) custom-call(s32[2]{0:T(128)S(1)} %pad_add_fusion.at_ref, bf16[384,384]{1,0:T(8,128)(2,1)S(1)} %expert_hidden.1.own_ref, bf16[384,384]{1,0:T(8,128)(2,1)S(1)} %collective-permute-done.13.other_ref, ...), custom_call_target="tpu_custom_call" | custom-call | flops 603979776 | bytes 5308416 | tf_op jit(solution)/shard_map/expert_back/pallas_call | solution.py:294
  67.7 1.6 %collective-permute-start.17 = (bf16[48,2048]{1,0:T(8,128)(2,1)S(1)}, bf16[48,2048]{1,0:T(8,128)(2,1)S(1)}, u32[]{:S(2)}, u32[]{:S(2)}) collective-permute-start(bf16[48,2048]{1,0:T(8,128)(2,1)S(1)} %get-tuple-element.80.after_ref), channel_id=1, source_target_pairs={{0,2},{1,5},{2,0},{3,7},{4,6},{5,1},{6,4},{7,3},{8,10},{9,13},{10,... | collective-permute-start | bytes 589832 | tf_op jit(solution)/shard_map/ppermute | solution.py:320
  71.2 1.5 %expert_back.2 = (f32[48,2048]{1,0:T(8,128)S(1)}, bf16[48,2048]{1,0:T(8,128)(2,1)S(1)}, bf16[48,2048]{1,0:T(8,128)(2,1)S(1)}, bf16[48,2048]{1,0:T(8,128)(2,1)S(1)}) custom-call(s32[2]{0:T(128)S(1)} %pad_add_fusion.at_ref, bf16[384,384]{1,0:T(8,128)(2,1)S(1)} %expert_hidden.1.own_ref, bf16[384,384]{1,0:T(8,128)(2,1)S(1)} %collective-permute-done.13.other_ref, ...), custom_call_target="tpu_custom_call" | custom-call | flops 603979776 | bytes 5308416 | tf_op jit(solution)/shard_map/expert_back/pallas_call | solution.py:294
  72.8 1.6 %collective-permute-start.14 = (bf16[48,2048]{1,0:T(8,128)(2,1)S(1)}, bf16[48,2048]{1,0:T(8,128)(2,1)S(1)}, u32[]{:S(2)}, u32[]{:S(2)}) collective-permute-start(bf16[48,2048]{1,0:T(8,128)(2,1)S(1)} %get-tuple-element.73), channel_id=1, source_target_pairs={{0,2},{1,5},{2,0},{3,7},{4,6},{5,1},{6,4},{7,3},{8,10},{9,13},{10,... | collective-permute-start | bytes 589832 | tf_op jit(solution)/shard_map/ppermute | solution.py:320
  75.5 1.9 %attention.1 = bf16[8,3,32,128]{3,2,1,0:T(8,128)(2,1)} custom-call(s32[1]{0:T(128)} %bitcast.me_ref, s32[16,16]{1,0:T(8,128)S(1)} %reshape.38.owner_ref, s32[16,16]{1,0:T(8,128)S(1)} %reshape.39.slot_ref, s32[16,16]{1,0:T(8,128)S(1)} %reshape.40.fill_ref, bf16[8,3,32,128]{3,2,1,0:T(8,128)(2,1)S(1)} %copy-done.4, bf16[2,2,128,128]{3,2,1,0:T(8,128)(2,1)S(1)} %pad.4.fresh_ref, ...), custom_call_target="tpu_custom_call" | custom-call | tf_op jit(solution)/shard_map/attention/pallas_call | solution.py:426
  78.3 2.2 %collective-permute-done.19 = bf16[48,2048]{1,0:T(8,128)(2,1)S(1)} collective-permute-done((bf16[48,2048]{1,0:T(8,128)(2,1)S(1)}, bf16[48,2048]{1,0:T(8,128)(2,1)S(1)}, u32[]{:S(2)}, u32[]{:S(2)}) %collective-permute-start.19) | collective-permute-done | bytes 196640 | tf_op jit(solution)/shard_map/ppermute | solution.py:320
  80.6 4.5 %collective-permute-start.20 = (bf16[24,2048]{1,0:T(8,128)(2,1)S(1)}, bf16[24,2048]{1,0:T(8,128)(2,1)S(1)}, u32[]{:S(2)}, u32[]{:S(2)}) collective-permute-start(bf16[24,2048]{1,0:T(8,128)(2,1)S(1)} %slice.33), channel_id=1, source_target_pairs={{0,16},{1,17},{2,18},{3,19},{4,20},{5,21},{6,22},{7,23},{8,24},{9,... | collective-permute-start | bytes 294920 | tf_op jit(solution)/shard_map/ppermute | solution.py:320
  85.1 3.5 %collective-permute-done.16 = bf16[48,2048]{1,0:T(8,128)(2,1)S(1)} collective-permute-done((bf16[48,2048]{1,0:T(8,128)(2,1)S(1)}, bf16[48,2048]{1,0:T(8,128)(2,1)S(1)}, u32[]{:S(2)}, u32[]{:S(2)}) %collective-permute-start.16) | collective-permute-done | bytes 196640 | tf_op jit(solution)/shard_map/ppermute | solution.py:320
  88.7 2.6 %collective-permute-start.21 = (bf16[24,2048]{1,0:T(8,128)(2,1)S(1)}, bf16[24,2048]{1,0:T(8,128)(2,1)S(1)}, u32[]{:S(2)}, u32[]{:S(2)}) collective-permute-start(bf16[24,2048]{1,0:T(8,128)(2,1)S(1)} %get-tuple-element.90), channel_id=1, source_target_pairs={{0,8},{1,9},{2,10},{3,11},{4,12},{5,13},{6,14},{7,15},{8,0},{9,1},... | collective-permute-start | bytes 294920 | tf_op jit(solution)/shard_map/ppermute | solution.py:320
  91.3 3.4 %collective-permute-start.22 = (bf16[24,2048]{1,0:T(8,128)(2,1)S(1)}, bf16[24,2048]{1,0:T(8,128)(2,1)S(1)}, u32[]{:S(2)}, u32[]{:S(2)}) collective-permute-start(bf16[24,2048]{1,0:T(8,128)(2,1)S(1)} %get-tuple-element.91), channel_id=1, source_target_pairs={{0,24},{1,25},{2,26},{3,27},{4,28},{5,29},{6,30},{7,31},{8,16},{9,... | collective-permute-start | bytes 294920 | tf_op jit(solution)/shard_map/ppermute | solution.py:320
  94.6 4.6 %collective-permute-done.22 = bf16[24,2048]{1,0:T(8,128)(2,1)S(1)} collective-permute-done((bf16[24,2048]{1,0:T(8,128)(2,1)S(1)}, bf16[24,2048]{1,0:T(8,128)(2,1)S(1)}, u32[]{:S(2)}, u32[]{:S(2)}) %collective-permute-start.22) | collective-permute-done | bytes 98336 | tf_op jit(solution)/shard_map/ppermute | solution.py:320
  (57 shorter events, 18.1 us)
Async XLA Ops:
  0.6 34.2 %copy-start = (bf16[1,4096,384]{2,1,0:T(8,128)(2,1)S(1)}, bf16[1,4096,384]{2,1,0:T(8,128)(2,1)}, u32[]{:S(2)}) copy-start(bf16[1,4096,384]{2,1,0:T(8,128)(2,1)} %gate_ref.5) | copy-start | bytes 9437188
  0.6 1.1 %copy-start.5 = (bf16[8,3,4096]{2,0,1:T(8,128)(2,1)S(1)}, bf16[8,3,4096]{2,0,1:T(8,128)(2,1)}, u32[]{:S(2)}) copy-start(bf16[8,3,4096]{2,0,1:T(8,128)(2,1)} %param.18) | copy-start | bytes 589828
  1.7 0.7 copy-start.6
  2.4 0.7 copy-start.7
  3.3 10.8 %collective-permute-start = (bf16[24,2176]{1,0:T(8,128)(2,1)S(1)}, bf16[24,2176]{1,0:T(8,128)(2,1)S(1)}, u32[]{:S(2)}, u32[]{:S(2)}) collective-permute-start(bf16[24,2176]{1,0:T(8,128)(2,1)S(1)} %pack_tokens.1), channel_id=1, source_target_pairs={{0,16},{1,17},{2,18},{3,19},{4,20},{5,21},{6,22},{7,23},{8,24},{9,... | collective-permute-start | bytes 313352 | tf_op jit(solution)/shard_map/ppermute | solution.py:320
  7.4 6.7 %collective-permute-start.1 = (bf16[24,2176]{1,0:T(8,128)(2,1)S(1)}, bf16[24,2176]{1,0:T(8,128)(2,1)}, u32[]{:S(2)}, u32[]{:S(2)}) collective-permute-start(bf16[24,2176]{1,0:T(8,128)(2,1)S(1)} %pack_tokens.1), channel_id=1, source_target_pairs={{0,8},{1,9},{2,10},{3,11},{4,12},{5,13},{6,14},{7,15},{8,0},{9,1},... | collective-permute-start | bytes 313352 | tf_op jit(solution)/shard_map/ppermute | solution.py:320
  9.0 7.1 %collective-permute-start.2 = (bf16[24,2176]{1,0:T(8,128)(2,1)S(1)}, bf16[24,2176]{1,0:T(8,128)(2,1)}, u32[]{:S(2)}, u32[]{:S(2)}) collective-permute-start(bf16[24,2176]{1,0:T(8,128)(2,1)S(1)} %pack_tokens.1), channel_id=1, source_target_pairs={{0,24},{1,25},{2,26},{3,27},{4,28},{5,29},{6,30},{7,31},{8,16},{9,... | collective-permute-start | bytes 313352 | tf_op jit(solution)/shard_map/ppermute | solution.py:320
  10.0 0.7 copy-start.8
  17.8 14.5 %collective-permute-start.3 = (bf16[96,2176]{1,0:T(8,128)(2,1)}, bf16[96,2176]{1,0:T(8,128)(2,1)}, u32[]{:S(2)}, u32[]{:S(2)}) collective-permute-start(bf16[96,2176]{1,0:T(8,128)(2,1)} %pad_maximum_fusion.1), channel_id=1, source_target_pairs={{0,2},{1,5},{2,0},{3,7},{4,6},{5,1},{6,4},{7,3},{8,10},{9,13},{10,... | collective-permute-start | bytes 1253384 | tf_op jit(solution)/shard_map/ppermute | solution.py:320
  19.3 10.3 %collective-permute-start.4 = (bf16[8,2,2,16,128]{4,3,2,1,0:T(8,128)(2,1)}, bf16[8,2,2,16,128]{4,3,2,1,0:T(8,128)(2,1)S(1)}, u32[]{:S(2)}, u32[]{:S(2)}) collective-permute-start(bf16[8,2,2,16,128]{4,3,2,1,0:T(8,128)(2,1)} %get-tuple-element.52), channel_id=1, source_target_pairs={{0,2},{1,3},{2,0},{3,1},{4,6},{5,7},{6,4},{7,5},{8,10},{9,11},{10,... | collective-permute-start | bytes 393224 | tf_op jit(solution)/shard_map/ppermute | solution.py:320
  19.8 9.8 %collective-permute-start.5 = (bf16[8,2,2,16,128]{4,3,2,1,0:T(8,128)(2,1)}, bf16[8,2,2,16,128]{4,3,2,1,0:T(8,128)(2,1)}, u32[]{:S(2)}, u32[]{:S(2)}) collective-permute-start(bf16[8,2,2,16,128]{4,3,2,1,0:T(8,128)(2,1)} %get-tuple-element.53), channel_id=1, source_target_pairs={{0,4},{1,5},{2,6},{3,7},{4,0},{5,1},{6,2},{7,3},{8,12},{9,13},{10,... | collective-permute-start | bytes 393224 | tf_op jit(solution)/shard_map/ppermute | solution.py:320
  21.3 10.0 %collective-permute-start.6 = (bf16[8,2,2,16,128]{4,3,2,1,0:T(8,128)(2,1)}, bf16[8,2,2,16,128]{4,3,2,1,0:T(8,128)(2,1)}, u32[]{:S(2)}, u32[]{:S(2)}) collective-permute-start(bf16[8,2,2,16,128]{4,3,2,1,0:T(8,128)(2,1)} %get-tuple-element.54), channel_id=1, source_target_pairs={{0,6},{1,7},{2,4},{3,5},{4,2},{5,3},{6,0},{7,1},{8,14},{9,15},{10,... | collective-permute-start | bytes 393224 | tf_op jit(solution)/shard_map/ppermute | solution.py:320
  33.5 12.6 %collective-permute-start.11 = (bf16[192,2176]{1,0:T(8,128)(2,1)S(1)}, bf16[192,2176]{1,0:T(8,128)(2,1)S(1)}, u32[]{:S(2)}, u32[]{:S(2)}) collective-permute-start(bf16[192,2176]{1,0:T(8,128)(2,1)S(1)} %pad_maximum_fusion.x_ref.sr_ref), channel_id=1, source_target_pairs={{0,4},{1,3},{2,6},{3,1},{4,0},{5,7},{6,2},{7,5},{8,12},{9,11},{10,... | collective-permute-start | bytes 2506760 | tf_op jit(solution)/shard_map/ppermute | solution.py:320
  34.9 27.7 %collective-permute-start.10 = (bf16[192,2176]{1,0:T(8,128)(2,1)S(1)}, bf16[192,2176]{1,0:T(8,128)(2,1)S(1)}, u32[]{:S(2)}, u32[]{:S(2)}) collective-permute-start(bf16[192,2176]{1,0:T(8,128)(2,1)S(1)} %pad_maximum_fusion.x_ref.sr_ref), channel_id=1, source_target_pairs={{0,1},{1,0},{2,3},{3,2},{4,5},{5,4},{6,7},{7,6},{8,9},{9,8},{10,11... | collective-permute-start | bytes 2506760 | tf_op jit(solution)/shard_map/ppermute | solution.py:320
  34.9 1.9 %copy-start.1 = (bf16[1,4096,384]{2,1,0:T(8,128)(2,1)S(1)}, bf16[1,4096,384]{2,1,0:T(8,128)(2,1)}, u32[]{:S(2)}) copy-start(bf16[1,4096,384]{2,1,0:T(8,128)(2,1)} %up_ref.5) | copy-start | bytes 9437188
  46.1 16.5 %copy-start.2 = (bf16[1,4096,384]{2,1,0:T(8,128)(2,1)S(1)}, bf16[1,4096,384]{2,1,0:T(8,128)(2,1)}, u32[]{:S(2)}) copy-start(bf16[1,4096,384]{2,1,0:T(8,128)(2,1)} %up_ref.5) | copy-start | bytes 9437188
  46.1 16.5 %collective-permute-start.12 = (bf16[192,2176]{1,0:T(8,128)(2,1)S(1)}, bf16[192,2176]{1,0:T(8,128)(2,1)S(1)}, u32[]{:S(2)}, u32[]{:S(2)}) collective-permute-start(bf16[192,2176]{1,0:T(8,128)(2,1)S(1)} %collective-permute-done.11.x_ref.r2_ref), channel_id=1, source_target_pairs={{0,1},{1,0},{2,3},{3,2},{4,5},{5,4},{6,7},{7,6},{8,9},{9,8},{10,11... | collective-permute-start | bytes 2506760 | tf_op jit(solution)/shard_map/ppermute | solution.py:320
  46.1 9.3 %collective-permute-start.7 = (bf16[8,2,2,16,128]{4,3,2,1,0:T(8,128)(2,1)S(1)}, bf16[8,2,2,16,128]{4,3,2,1,0:T(8,128)(2,1)S(1)}, u32[]{:S(2)}, u32[]{:S(2)}) collective-permute-start(bf16[8,2,2,16,128]{4,3,2,1,0:T(8,128)(2,1)S(1)} %get-tuple-element.60), channel_id=1, source_target_pairs={{0,8},{1,9},{2,10},{3,11},{4,12},{5,13},{6,14},{7,15},{8,0},{9,1},... | collective-permute-start | bytes 393224 | tf_op jit(solution)/shard_map/ppermute | solution.py:320
  48.5 7.1 %collective-permute-start.8 = (bf16[8,2,2,16,128]{4,3,2,1,0:T(8,128)(2,1)S(1)}, bf16[8,2,2,16,128]{4,3,2,1,0:T(8,128)(2,1)S(1)}, u32[]{:S(2)}, u32[]{:S(2)}) collective-permute-start(bf16[8,2,2,16,128]{4,3,2,1,0:T(8,128)(2,1)S(1)} %get-tuple-element.61), channel_id=1, source_target_pairs={{0,16},{1,17},{2,18},{3,19},{4,20},{5,21},{6,22},{7,23},{8,24},{9,... | collective-permute-start | bytes 393224 | tf_op jit(solution)/shard_map/ppermute | solution.py:320
  50.6 11.0 %collective-permute-start.9 = (bf16[8,2,2,16,128]{4,3,2,1,0:T(8,128)(2,1)S(1)}, bf16[8,2,2,16,128]{4,3,2,1,0:T(8,128)(2,1)S(1)}, u32[]{:S(2)}, u32[]{:S(2)}) collective-permute-start(bf16[8,2,2,16,128]{4,3,2,1,0:T(8,128)(2,1)S(1)} %get-tuple-element.62), channel_id=1, source_target_pairs={{0,24},{1,25},{2,26},{3,27},{4,28},{5,29},{6,30},{7,31},{8,16},{9,... | collective-permute-start | bytes 393224 | tf_op jit(solution)/shard_map/ppermute | solution.py:320
  62.6 3.5 %copy-start.3 = (bf16[1,768,2048]{2,1,0:T(8,128)(2,1)S(1)}, bf16[1,768,2048]{2,1,0:T(8,128)(2,1)}, u32[]{:S(2)}) copy-start(bf16[1,768,2048]{2,1,0:T(8,128)(2,1)} %down_ref.3) | copy-start | bytes 9437188
  64.5 1.6 %collective-permute-start.13 = (bf16[384,384]{1,0:T(8,128)(2,1)S(1)}, bf16[384,384]{1,0:T(8,128)(2,1)S(1)}, u32[]{:S(2)}, u32[]{:S(2)}) collective-permute-start(bf16[384,384]{1,0:T(8,128)(2,1)S(1)} %expert_hidden.1.own_ref), channel_id=1, source_target_pairs={{0,1},{1,0},{2,3},{3,2},{4,5},{5,4},{6,7},{7,6},{8,9},{9,8},{10,11... | collective-permute-start | bytes 884744 | tf_op jit(solution)/shard_map/ppermute | solution.py:320
  67.7 7.9 %copy-start.4 = (bf16[8,3,32,128]{3,2,1,0:T(8,128)(2,1)S(1)}, bf16[8,3,32,128]{3,2,1,0:T(8,128)(2,1)}, u32[]{:S(2)}) copy-start(bf16[8,3,32,128]{3,2,1,0:T(8,128)(2,1)} %q_ref.1) | copy-start | bytes 589828
  67.7 9.8 %collective-permute-start.17 = (bf16[48,2048]{1,0:T(8,128)(2,1)S(1)}, bf16[48,2048]{1,0:T(8,128)(2,1)S(1)}, u32[]{:S(2)}, u32[]{:S(2)}) collective-permute-start(bf16[48,2048]{1,0:T(8,128)(2,1)S(1)} %get-tuple-element.80.after_ref), channel_id=1, source_target_pairs={{0,2},{1,5},{2,0},{3,7},{4,6},{5,1},{6,4},{7,3},{8,10},{9,13},{10,... | collective-permute-start | bytes 589832 | tf_op jit(solution)/shard_map/ppermute | solution.py:320
  69.2 9.0 %collective-permute-start.18 = (bf16[48,2048]{1,0:T(8,128)(2,1)S(1)}, bf16[48,2048]{1,0:T(8,128)(2,1)S(1)}, u32[]{:S(2)}, u32[]{:S(2)}) collective-permute-start(bf16[48,2048]{1,0:T(8,128)(2,1)S(1)} %get-tuple-element.87), channel_id=1, source_target_pairs={{0,4},{1,3},{2,6},{3,1},{4,0},{5,7},{6,2},{7,5},{8,12},{9,11},{10,... | collective-permute-start | bytes 589832 | tf_op jit(solution)/shard_map/ppermute | solution.py:320
  70.5 10.0 %collective-permute-start.19 = (bf16[48,2048]{1,0:T(8,128)(2,1)S(1)}, bf16[48,2048]{1,0:T(8,128)(2,1)S(1)}, u32[]{:S(2)}, u32[]{:S(2)}) collective-permute-start(bf16[48,2048]{1,0:T(8,128)(2,1)S(1)} %get-tuple-element.88), channel_id=1, source_target_pairs={{0,6},{1,7},{2,4},{3,5},{4,2},{5,3},{6,0},{7,1},{8,14},{9,15},{10,... | collective-permute-start | bytes 589832 | tf_op jit(solution)/shard_map/ppermute | solution.py:320
  72.8 12.3 %collective-permute-start.14 = (bf16[48,2048]{1,0:T(8,128)(2,1)S(1)}, bf16[48,2048]{1,0:T(8,128)(2,1)S(1)}, u32[]{:S(2)}, u32[]{:S(2)}) collective-permute-start(bf16[48,2048]{1,0:T(8,128)(2,1)S(1)} %get-tuple-element.73), channel_id=1, source_target_pairs={{0,2},{1,5},{2,0},{3,7},{4,6},{5,1},{6,4},{7,3},{8,10},{9,13},{10,... | collective-permute-start | bytes 589832 | tf_op jit(solution)/shard_map/ppermute | solution.py:320
  74.3 10.8 %collective-permute-start.15 = (bf16[48,2048]{1,0:T(8,128)(2,1)S(1)}, bf16[48,2048]{1,0:T(8,128)(2,1)S(1)}, u32[]{:S(2)}, u32[]{:S(2)}) collective-permute-start(bf16[48,2048]{1,0:T(8,128)(2,1)S(1)} %get-tuple-element.74), channel_id=1, source_target_pairs={{0,4},{1,3},{2,6},{3,1},{4,0},{5,7},{6,2},{7,5},{8,12},{9,11},{10,... | collective-permute-start | bytes 589832 | tf_op jit(solution)/shard_map/ppermute | solution.py:320
  77.5 11.1 %collective-permute-start.16 = (bf16[48,2048]{1,0:T(8,128)(2,1)S(1)}, bf16[48,2048]{1,0:T(8,128)(2,1)S(1)}, u32[]{:S(2)}, u32[]{:S(2)}) collective-permute-start(bf16[48,2048]{1,0:T(8,128)(2,1)S(1)} %get-tuple-element.75), channel_id=1, source_target_pairs={{0,6},{1,7},{2,4},{3,5},{4,2},{5,3},{6,0},{7,1},{8,14},{9,15},{10,... | collective-permute-start | bytes 589832 | tf_op jit(solution)/shard_map/ppermute | solution.py:320
  80.6 14.1 %collective-permute-start.20 = (bf16[24,2048]{1,0:T(8,128)(2,1)S(1)}, bf16[24,2048]{1,0:T(8,128)(2,1)S(1)}, u32[]{:S(2)}, u32[]{:S(2)}) collective-permute-start(bf16[24,2048]{1,0:T(8,128)(2,1)S(1)} %slice.33), channel_id=1, source_target_pairs={{0,16},{1,17},{2,18},{3,19},{4,20},{5,21},{6,22},{7,23},{8,24},{9,... | collective-permute-start | bytes 294920 | tf_op jit(solution)/shard_map/ppermute | solution.py:320
  88.7 6.0 %collective-permute-start.21 = (bf16[24,2048]{1,0:T(8,128)(2,1)S(1)}, bf16[24,2048]{1,0:T(8,128)(2,1)S(1)}, u32[]{:S(2)}, u32[]{:S(2)}) collective-permute-start(bf16[24,2048]{1,0:T(8,128)(2,1)S(1)} %get-tuple-element.90), channel_id=1, source_target_pairs={{0,8},{1,9},{2,10},{3,11},{4,12},{5,13},{6,14},{7,15},{8,0},{9,1},... | collective-permute-start | bytes 294920 | tf_op jit(solution)/shard_map/ppermute | solution.py:320
  91.3 7.9 %collective-permute-start.22 = (bf16[24,2048]{1,0:T(8,128)(2,1)S(1)}, bf16[24,2048]{1,0:T(8,128)(2,1)S(1)}, u32[]{:S(2)}, u32[]{:S(2)}) collective-permute-start(bf16[24,2048]{1,0:T(8,128)(2,1)S(1)} %get-tuple-element.91), channel_id=1, source_target_pairs={{0,24},{1,25},{2,26},{3,27},{4,28},{5,29},{6,30},{7,31},{8,16},{9,... | collective-permute-start | bytes 294920 | tf_op jit(solution)/shard_map/ppermute | solution.py:320

commit v10 on v3

--- a/solution.py
+++ b/solution.py
@@ -11,6 +11,7 @@
 CAP = 2
 LIMIT = 448.0
 MIB = 1024 * 1024
+LARGE = 49 * MIB
 
 
 def vmem():
@@ -30,19 +31,18 @@
     largest = jnp.max(jnp.abs(values), axis=(3, 4), keepdims=True)
     scale = jnp.full(largest.shape, 2.0 ** (-16), jnp.float32)
     inverse = jnp.full(largest.shape, 2.0**16, jnp.float32)
-    for exponent in range(-16, 4):
+    for exponent in range(-16, -6):
         exceeds = largest > LIMIT * 2.0**exponent
         scale = jnp.where(exceeds, scale * 2.0, scale)
         inverse = jnp.where(exceeds, inverse * 0.5, inverse)
     scaled = values * inverse
-    magnitude = jnp.abs(scaled)
+    rest = jnp.abs(scaled) * 2.0**6
     step = jnp.full(scaled.shape, 2.0 ** (-9), jnp.float32)
-    back = jnp.full(scaled.shape, 2.0**9, jnp.float32)
-    for exponent in range(-5, 9):
-        exceeds = magnitude >= 2.0**exponent
-        step = jnp.where(exceeds, step * 2.0, step)
-        back = jnp.where(exceeds, back * 0.5, back)
-    levels = jnp.minimum(jnp.floor(magnitude * back + 0.5) * step, LIMIT)
+    for bits in (8, 4, 2, 1):
+        exceeds = rest >= 2.0**bits
+        rest = jnp.where(exceeds, rest * 2.0**-bits, rest)
+        step = jnp.where(exceeds, step * 2.0**bits, step)
+    levels = jnp.minimum(jnp.floor(rest * 8.0 + 0.5) * step, LIMIT)
     cache = (jnp.where(scaled < 0.0, -levels, levels) * scale).astype(jnp.bfloat16)
 
     send_ref[...] = jnp.zeros(send_ref.shape, send_ref.dtype)
@@ -144,6 +144,10 @@
     out_ref[:, half:] = jnp.where(part < 3, chosen, 0.0).astype(out_ref.dtype)
 
 
+def room(*arrays):
+    return sum(math.prod(a.shape) * a.dtype.itemsize for a in arrays) * 9 // 8 + 4 * MIB
+
+
 def weight_copies(half, core, gate_ref, up_ref, held, sems):
     depth = half // sems.shape[1]
     pairs = []
@@ -208,7 +212,7 @@
         out_specs=vmem() if last else [vmem(), vmem()],
         scratch_shapes=scratch + ([pltpu.VMEM((2, tokens, f), jnp.float32)] if last else []),
         out_shape=jax.ShapeDtypeStruct((tokens, f), jnp.bfloat16) if last else [total, total],
-        compiler_params=pltpu.CompilerParams(vmem_limit_bytes=40 * MIB),
+        compiler_params=pltpu.CompilerParams(vmem_limit_bytes=LARGE),
         cost_estimate=pl.CostEstimate(
             flops=2 * tokens * d * f,
             bytes_accessed=tokens * d + 2 * d * f + 8 * tokens * f,
@@ -277,7 +281,7 @@
             pltpu.VMEM(w_down.shape[1:], jnp.bfloat16),
             pltpu.SemaphoreType.DMA((4,)),
         ],
-        compiler_params=pltpu.CompilerParams(vmem_limit_bytes=40 * MIB),
+        compiler_params=pltpu.CompilerParams(vmem_limit_bytes=LARGE),
         cost_estimate=pl.CostEstimate(
             flops=2 * tokens * f * width,
             bytes_accessed=2 * (2 * tokens * f + 2 * f * width + 2 * group2 * width),
@@ -349,29 +353,31 @@
         expert_routes.reshape(tokens, top),
         route_probs.transpose(1, 0, 2).reshape(tokens, top),
     )
+    line = [mine] + [moves.along_z(mine, -shift) for shift in range(1, moves.lines)]
+    line = jnp.concatenate(line, axis=0)
+    fresh = new_kv.transpose(2, 3, 0, 1, 4).reshape(2, heads, tokens, width)
+    fresh = jnp.pad(fresh, ((0, 0), (0, 0), (0, 128 - tokens), (0, 0)))
+    tables = [t.reshape(owners, pages) for t in (page_owner, page_slot, page_fill)]
+    sr = jnp.concatenate([line, moves.flip(line, 0)], axis=0)
+    sr, fresh, tables, prompt_kv = lax.optimization_barrier((sr, fresh, tables, prompt_kv))
+    r2 = moves.flip(sr, 1)
     send = pl.pallas_call(
         functools.partial(page_kernel, pages),
         out_shape=jax.ShapeDtypeStruct((slots, 2, heads, page_len, width), jnp.bfloat16),
         in_specs=[smem(), smem(), vmem()],
         out_specs=vmem(),
         scratch_shapes=[pltpu.SMEM((owners,), jnp.int32)],
-        compiler_params=pltpu.CompilerParams(vmem_limit_bytes=40 * MIB),
+        compiler_params=pltpu.CompilerParams(vmem_limit_bytes=room(prompt_kv) * 4),
         name="quantize_pages",
     )(me_ref, page_owner.reshape(-1), prompt_kv.transpose(0, 1, 3, 2, 4))
-    line = [mine] + [moves.along_z(mine, -shift) for shift in range(1, moves.lines)]
-    line = jnp.concatenate(line, axis=0)
-    fresh = new_kv.transpose(2, 3, 0, 1, 4).reshape(2, heads, tokens, width)
-    fresh = jnp.pad(fresh, ((0, 0), (0, 0), (0, 128 - tokens), (0, 0)))
-    tables = [t.reshape(owners, pages) for t in (page_owner, page_slot, page_fill)]
-    line, send, fresh, tables = lax.optimization_barrier((line, send, fresh, tables))
-    sr = jnp.concatenate([line, moves.flip(line, 0)], axis=0)
-    r2 = moves.flip(sr, 1)
+    r2, send = lax.optimization_barrier((r2, send))
     cache = lax.all_to_all(send, "ep", split_axis=0, concat_axis=0, tiled=True)
     other_sr, other_r2 = moves.cores(sr), moves.cores(r2)
 
     parts = expert_front(own_core, (sr, r2), w_gate, w_up, None)
     hidden = expert_front(own_core, (other_sr, other_r2), w_gate, w_up, parts)
     other_hidden = moves.cores(hidden)
+    at, cache = lax.optimization_barrier((at, cache))
     sent = expert_back(True, owners, at, hidden, other_hidden, w_down, sr, r2, lanes)
     kept = expert_back(False, owners, at, hidden, other_hidden, w_down, sr, r2, lanes)
     attn_out = pl.pallas_call(
@@ -379,7 +385,9 @@
         out_shape=jax.ShapeDtypeStruct(queries.shape, jnp.bfloat16),
         in_specs=[smem()] + [vmem()] * 6,
         out_specs=vmem(),
-        compiler_params=pltpu.CompilerParams(vmem_limit_bytes=48 * MIB),
+        compiler_params=pltpu.CompilerParams(
+            vmem_limit_bytes=8 * MIB + 16 * slots * page_len * tokens * q_heads
+        ),
         name="attention",
     )(
         me_ref,

time: 102 us -> 93.7 us (0.919)
  local copies, waits for them, and re-layouts: 13.5 us -> 4.01 us
  waiting for transfers between devices: 37.7 us -> 41 us
  Pallas kernels: 23.8 us -> 20.8 us
  starting transfers between devices: 21.6 us -> 23.3 us
    unnamed x31 -> x11, local copies, waits for them, and re-layouts: 10.4 us -> 1.5 us
    ppermute x13, waiting for transfers between devices: 30.4 us -> 34 us  [go(): return lax.ppermute(x, ('ep', 'pd'), perm)]
    all_to_all x1, starting transfers between devices: 4.42 us -> 7 us  [body(): cache = lax.all_to_all(send, 'ep', split_axis=0, concat_axis=0, tiled=True)]
    pallas_call x1, Pallas kernels: 4.13 us -> 2.66 us  [body(): pl.pallas_call(functools.partial(page_kernel, pages), out_shape=jax.Shape...]
    add x1, other arithmetic: 1.31 us -> 0.18 us  [body(): kept = kept + moves.flip(sent, 0).astype(jnp.float32)]
    pallas_call x1, Pallas kernels: 3.04 us -> 1.93 us  [body(): pl.pallas_call(functools.partial(attention_kernel, pages), out_shape=jax....]
  transfers between devices with their start and end apart: 14 -> 14, of which waited for: 7 -> 9; matrix products, arithmetic and copies ran while one was open for 6% -> 6% of each run, Pallas kernels for 18% -> 17%
where the time goes in v10:
time: 93.7 us; the launch traced here: 93.2 us
  waiting for transfers between devices  41 us (44%)
  starting transfers between devices  23.3 us (25%)
  Pallas kernels  20.8 us (22%)
  local copies, waits for them, and re-layouts  4.01 us (4%)
  other arithmetic  3.33 us (4%)
    ppermute x13, waiting for transfers between devices, go(): return lax.ppermute(x, ('ep', 'pd'), perm)  34 us
    ppermute x13, starting transfers between devices, go(): return lax.ppermute(x, ('ep', 'pd'), perm)  16.3 us
    pallas_call x2, Pallas kernels, expert_front(): pl.pallas_call(hidden_kernel if last else partial_kernel, in_specs=[smem(...  8.09 us
    all_to_all x1, starting transfers between devices, body(): cache = lax.all_to_all(send, 'ep', split_axis=0, concat_axis=0, tiled=True)  7 us
    all_to_all x1, waiting for transfers between devices, body(): cache = lax.all_to_all(send, 'ep', split_axis=0, concat_axis=0, tiled=True)  6.96 us
    pallas_call x2, Pallas kernels, expert_back(): pl.pallas_call(functools.partial(back_kernel, send, experts, lanes), out_...  6.39 us
    pallas_call x1, Pallas kernels, body(): pl.pallas_call(functools.partial(page_kernel, pages), out_shape=jax.Shape...  2.66 us
    pallas_call x1, Pallas kernels, body(): pl.pallas_call(functools.partial(attention_kernel, pages), out_shape=jax....  1.93 us
  transfers between devices with their start and end apart: 14, of which 9 were waited for; matrix products, arithmetic and copies ran while one was open for 6% of the time, Pallas kernels for 17%

profile of v10, /device:TPU:0, one launch (start us, length us, event | category | flops | bytes accessed | tf_op | source)
XLA Modules:
  0.0 93.2 jit_solution(182812517253046237)
XLA Ops:
  0.6 1.8 %pack_tokens.1 = bf16[24,2176]{1,0:T(8,128)(2,1)} custom-call(s32[1]{0:T(128)} %bitcast.1.core_ref, bf16[24,4096]{1,0:T(8,128)(2,1)} %bitcast.23, s32[24,8]{1,0:T(8,128)} %bitcast.25, f32[24,8]{1,0:T(8,128)} %bitcast.26), custom_call_target="tpu_custom_call" | custom-call | tf_op jit(solution)/shard_map/pack_tokens/pallas_call | solution.py:344
  2.4 3.0 %collective-permute-start.2 = (bf16[24,2176]{1,0:T(8,128)(2,1)}, bf16[24,2176]{1,0:T(8,128)(2,1)S(1)}, u32[]{:S(2)}, u32[]{:S(2)}) collective-permute-start(bf16[24,2176]{1,0:T(8,128)(2,1)} %pack_tokens.1), channel_id=1, source_target_pairs={{0,8},{1,9},{2,10},{3,11},{4,12},{5,13},{6,14},{7,15},{8,16},{9,17... | collective-permute-start | bytes 313352 | tf_op jit(solution)/shard_map/ppermute | solution.py:303
  5.4 2.6 %collective-permute-start.1 = (bf16[24,2176]{1,0:T(8,128)(2,1)}, bf16[24,2176]{1,0:T(8,128)(2,1)S(1)}, u32[]{:S(2)}, u32[]{:S(2)}) collective-permute-start(bf16[24,2176]{1,0:T(8,128)(2,1)} %pack_tokens.1), channel_id=1, source_target_pairs={{0,16},{1,17},{2,18},{3,19},{4,20},{5,21},{6,22},{7,23},{8,24},{9,... | collective-permute-start | bytes 313352 | tf_op jit(solution)/shard_map/ppermute | solution.py:303
  8.0 1.3 %collective-permute-start = (bf16[24,2176]{1,0:T(8,128)(2,1)}, bf16[24,2176]{1,0:T(8,128)(2,1)S(1)}, u32[]{:S(2)}, u32[]{:S(2)}) collective-permute-start(bf16[24,2176]{1,0:T(8,128)(2,1)} %pack_tokens.1), channel_id=1, source_target_pairs={{0,24},{1,25},{2,26},{3,27},{4,28},{5,29},{6,30},{7,31},{8,0},{9,1... | collective-permute-start | bytes 313352 | tf_op jit(solution)/shard_map/ppermute | solution.py:303
  9.4 0.9 %constant_dynamic-update-slice_fusion.4 = bf16[192,2176]{1,0:T(8,128)(2,1)S(1)} fusion(bf16[24,2176]{1,0:T(8,128)(2,1)} %pack_tokens.1), kind=kLoop, calls=%fused_computation.14 | loop fusion | bytes 208896
  10.8 1.3 %reduce.3 = s32[256]{0:T(256)S(1)} reduce(s32[256,1]{0,1:T(1,128)} %param.13, s32[]{:T(128)} %broadcast.5), dimensions={1}, to_apply=%param.13.reduce_sub_computation.3 | reduce | bytes 2052 | tf_op args[1]
  12.3 0.8 reshape.38.slot_ref
  13.0 0.8 reshape.39.fill_ref
  13.8 0.7 copy.17
  14.6 0.7 collective-permute-done.1
  15.2 0.9 pad_maximum_fusion
  16.1 1.6 %collective-permute-start.3 = (bf16[96,2176]{1,0:T(8,128)(2,1)S(1)}, bf16[96,2176]{1,0:T(8,128)(2,1)S(1)}, u32[]{:S(2)}, u32[]{:S(2)}) collective-permute-start(bf16[96,2176]{1,0:T(8,128)(2,1)S(1)} %pad_maximum_fusion), channel_id=1, source_target_pairs={{0,2},{1,5},{2,0},{3,7},{4,6},{5,1},{6,4},{7,3},{8,10},{9,13},{10,... | collective-permute-start | bytes 1253384 | tf_op jit(solution)/shard_map/ppermute | solution.py:303
  17.8 6.5 %collective-permute-done.3 = bf16[96,2176]{1,0:T(8,128)(2,1)S(1)} collective-permute-done((bf16[96,2176]{1,0:T(8,128)(2,1)S(1)}, bf16[96,2176]{1,0:T(8,128)(2,1)S(1)}, u32[]{:S(2)}, u32[]{:S(2)}) %collective-permute-start.3) | collective-permute-done | bytes 417824 | tf_op jit(solution)/shard_map/ppermute | solution.py:303
  24.3 1.6 %collective-permute-start.4 = (bf16[192,2176]{1,0:T(8,128)(2,1)S(1)}, bf16[192,2176]{1,0:T(8,128)(2,1)S(1)}, u32[]{:S(2)}, u32[]{:S(2)}) collective-permute-start(bf16[192,2176]{1,0:T(8,128)(2,1)S(1)} %constant_dynamic-update-slice_fusion.sr_ref), channel_id=1, source_target_pairs={{0,4},{1,3},{2,6},{3,1},{4,0},{5,7},{6,2},{7,5},{8,12},{9,11},{10,... | collective-permute-start | bytes 2506760 | tf_op jit(solution)/shard_map/ppermute | solution.py:303
  25.9 2.7 %quantize_pages.1 = bf16[32,2,2,16,128]{4,3,2,1,0:T(8,128)(2,1)} custom-call(s32[1]{0:T(128)} %bitcast.me_ref, s32[256]{0:T(256)S(1)} %bitcast.22, bf16[16,2,2,16,128]{4,3,2,1,0:T(8,128)(2,1)S(1)} %bitcast.21), custom_call_target="tpu_custom_call" | custom-call | tf_op jit(solution)/shard_map/quantize_pages/pallas_call | solution.py:364
  28.6 8.3 %collective-permute-done.4.r2_ref = bf16[192,2176]{1,0:T(8,128)(2,1)S(1)} collective-permute-done((bf16[192,2176]{1,0:T(8,128)(2,1)S(1)}, bf16[192,2176]{1,0:T(8,128)(2,1)S(1)}, u32[]{:S(2)}, u32[]{:S(2)}) %collective-permute-start.4) | collective-permute-done | bytes 835616 | tf_op jit(solution)/shard_map/ppermute | solution.py:303
  36.9 7.0 %all-to-all-start = ((bf16[32,2,2,16,128]{4,3,2,1,0:T(8,128)(2,1)}), bf16[32,2,2,16,128]{4,3,2,1,0:T(8,128)(2,1)S(1)}, u32[]{:S(2)}, u32[]{:S(2)}) async-start(bf16[32,2,2,16,128]{4,3,2,1,0:T(8,128)(2,1)} %quantize_pages.1), calls=%async_computation | async-start | bytes 1048576 | tf_op jit(solution)/shard_map/all_to_all | solution.py:374
  43.9 3.4 %expert_partial.1 = (f32[384,384]{1,0:T(8,128)S(1)}, f32[384,384]{1,0:T(8,128)S(1)}) custom-call(s32[1]{0:T(128)} %bitcast.1.core_ref, bf16[192,2176]{1,0:T(8,128)(2,1)S(1)} %constant_dynamic-update-slice_fusion.sr_ref, bf16[192,2176]{1,0:T(8,128)(2,1)S(1)} %collective-permute-done.4.r2_ref, bf16[1,4096,384]{2,1,0:T(8,128)(2,1)} %gate_ref.3, ...), custom_call_target="tpu_custom_call" | custom-call | flops 1207959552 | bytes 5898240 | tf_op jit(solution)/shard_map/expert_partial/pallas_call | solution.py:209
  47.3 4.7 %expert_hidden.1.own_ref = bf16[384,384]{1,0:T(8,128)(2,1)S(1)} custom-call(s32[1]{0:T(128)} %bitcast.1.core_ref, bf16[192,2176]{1,0:T(8,128)(2,1)S(1)} %collective-permute-done.5.sr_ref, bf16[192,2176]{1,0:T(8,128)(2,1)} %collective-permute-done.6.r2_ref, bf16[1,4096,384]{2,1,0:T(8,128)(2,1)} %gate_ref.3, bf16[1,4096,384]{2,1,0:T(8,128)(2,1)} %up_ref.3, ...), custom_call_target="tpu_custom_call" | custom-call | flops 1207959552 | bytes 5898240 | tf_op jit(solution)/shard_map/expert_hidden/pallas_call | solution.py:209
  52.4 7.0 %all-to-all-done.cache_ref = bf16[32,2,2,16,128]{4,3,2,1,0:T(8,128)(2,1)S(1)} async-done(((bf16[32,2,2,16,128]{4,3,2,1,0:T(8,128)(2,1)}), bf16[32,2,2,16,128]{4,3,2,1,0:T(8,128)(2,1)S(1)}, u32[]{:S(2)}, u32[]{:S(2)}) %all-to-all-start) | async-done | bytes 524320 | tf_op jit(solution)/shard_map/all_to_all | solution.py:374
  59.3 3.2 %expert_back_send.1 = bf16[192,2048]{1,0:T(8,128)(2,1)S(1)} custom-call(s32[2]{0:T(128)S(1)} %pad_add_fusion.at_ref, bf16[384,384]{1,0:T(8,128)(2,1)S(1)} %expert_hidden.1.own_ref, bf16[384,384]{1,0:T(8,128)(2,1)S(1)} %collective-permute-done.7.other_ref, bf16[192,2176]{1,0:T(8,128)(2,1)S(1)} %constant_dynamic-update-slice_fusion.sr_ref, ...), custom_call_target="tpu_custom_call" | custom-call | flops 603979776 | bytes 5308416 | tf_op jit(solution)/shard_map/expert_back_send/pallas_call | solution.py:275
  63.2 1.9 %attention.1 = bf16[8,3,32,128]{3,2,1,0:T(8,128)(2,1)} custom-call(s32[1]{0:T(128)} %bitcast.me_ref, s32[16,16]{1,0:T(8,128)S(1)} %reshape.37.owner_ref, s32[16,16]{1,0:T(8,128)S(1)} %reshape.38.slot_ref, s32[16,16]{1,0:T(8,128)S(1)} %reshape.39.fill_ref, bf16[8,3,32,128]{3,2,1,0:T(8,128)(2,1)S(1)} %copy-done, ...), custom_call_target="tpu_custom_call" | custom-call | tf_op jit(solution)/shard_map/attention/pallas_call | solution.py:383
  65.1 3.2 %expert_back_keep.1 = f32[192,2048]{1,0:T(8,128)S(1)} custom-call(s32[2]{0:T(128)S(1)} %pad_add_fusion.at_ref, bf16[384,384]{1,0:T(8,128)(2,1)S(1)} %expert_hidden.1.own_ref, bf16[384,384]{1,0:T(8,128)(2,1)S(1)} %collective-permute-done.7.other_ref, bf16[192,2176]{1,0:T(8,128)(2,1)S(1)} %constant_dynamic-update-slice_fusion.sr_ref, ...), custom_call_target="tpu_custom_call" | custom-call | flops 603979776 | bytes 5308416 | tf_op jit(solution)/shard_map/expert_back_keep/pallas_call | solution.py:275
  68.3 6.3 %collective-permute-done.8 = bf16[192,2048]{1,0:T(8,128)(2,1)S(1)} collective-permute-done((bf16[192,2048]{1,0:T(8,128)(2,1)S(1)}, bf16[192,2048]{1,0:T(8,128)(2,1)S(1)}, u32[]{:S(2)}, u32[]{:S(2)}) %collective-permute-start.8) | collective-permute-done | bytes 786464 | tf_op jit(solution)/shard_map/ppermute | solution.py:303
  74.8 1.3 %collective-permute-start.9 = (bf16[96,2048]{1,0:T(8,128)(2,1)S(1)}, bf16[96,2048]{1,0:T(8,128)(2,1)S(1)}, u32[]{:S(2)}, u32[]{:S(2)}) collective-permute-start(bf16[96,2048]{1,0:T(8,128)(2,1)S(1)} %slice.44), channel_id=1, source_target_pairs={{0,4},{1,3},{2,6},{3,1},{4,0},{5,7},{6,2},{7,5},{8,12},{9,11},{10,... | collective-permute-start | bytes 1179656 | tf_op jit(solution)/shard_map/ppermute | solution.py:303
  76.2 6.5 %collective-permute-done.9 = bf16[96,2048]{1,0:T(8,128)(2,1)S(1)} collective-permute-done((bf16[96,2048]{1,0:T(8,128)(2,1)S(1)}, bf16[96,2048]{1,0:T(8,128)(2,1)S(1)}, u32[]{:S(2)}, u32[]{:S(2)}) %collective-permute-start.9) | collective-permute-done | bytes 393248 | tf_op jit(solution)/shard_map/ppermute | solution.py:303
  82.8 1.7 %collective-permute-start.10 = (bf16[24,2048]{1,0:T(8,128)(2,1)S(1)}, bf16[24,2048]{1,0:T(8,128)(2,1)S(1)}, u32[]{:S(2)}, u32[]{:S(2)}) collective-permute-start(bf16[24,2048]{1,0:T(8,128)(2,1)S(1)} %get-tuple-element.32), channel_id=1, source_target_pairs={{0,8},{1,9},{2,10},{3,11},{4,12},{5,13},{6,14},{7,15},{8,16},{9,17... | collective-permute-start | bytes 294920 | tf_op jit(solution)/shard_map/ppermute | solution.py:303
  84.5 2.2 %collective-permute-start.12 = (bf16[24,2048]{1,0:T(8,128)(2,1)S(1)}, bf16[24,2048]{1,0:T(8,128)(2,1)S(1)}, u32[]{:S(2)}, u32[]{:S(2)}) collective-permute-start(bf16[24,2048]{1,0:T(8,128)(2,1)S(1)} %get-tuple-element.33), channel_id=1, source_target_pairs={{0,24},{1,25},{2,26},{3,27},{4,28},{5,29},{6,30},{7,31},{8,0},{9,1... | collective-permute-start | bytes 294920 | tf_op jit(solution)/shard_map/ppermute | solution.py:303
  86.7 2.7 %collective-permute-done.10 = bf16[24,2048]{1,0:T(8,128)(2,1)S(1)} collective-permute-done((bf16[24,2048]{1,0:T(8,128)(2,1)S(1)}, bf16[24,2048]{1,0:T(8,128)(2,1)S(1)}, u32[]{:S(2)}, u32[]{:S(2)}) %collective-permute-start.10) | collective-permute-done | bytes 98336 | tf_op jit(solution)/shard_map/ppermute | solution.py:303
  89.5 0.9 collective-permute-done.12
  90.3 2.2 %collective-permute-done.11 = bf16[24,2048]{1,0:T(8,128)(2,1)S(1)} collective-permute-done((bf16[24,2048]{1,0:T(8,128)(2,1)S(1)}, bf16[24,2048]{1,0:T(8,128)(2,1)S(1)}, u32[]{:S(2)}, u32[]{:S(2)}) %collective-permute-start.11) | collective-permute-done | bytes 98336 | tf_op jit(solution)/shard_map/ppermute | solution.py:303
  92.5 0.7 fusion.3
  (29 shorter events, 2.1 us)
Async XLA Ops:
  0.6 25.3 %copy-start.2 = (bf16[16,2,16,2,128]{4,3,2,1,0:T(2,128)(2,1)S(1)}, bf16[16,2,16,2,128]{4,3,2,1,0:T(2,128)(2,1)}, u32[]{:S(2)}) copy-start(bf16[16,2,16,2,128]{4,3,2,1,0:T(2,128)(2,1)} %param.12) | copy-start | bytes 786436
  2.4 12.1 %collective-permute-start.2 = (bf16[24,2176]{1,0:T(8,128)(2,1)}, bf16[24,2176]{1,0:T(8,128)(2,1)S(1)}, u32[]{:S(2)}, u32[]{:S(2)}) collective-permute-start(bf16[24,2176]{1,0:T(8,128)(2,1)} %pack_tokens.1), channel_id=1, source_target_pairs={{0,8},{1,9},{2,10},{3,11},{4,12},{5,13},{6,14},{7,15},{8,16},{9,17... | collective-permute-start | bytes 313352 | tf_op jit(solution)/shard_map/ppermute | solution.py:303
  5.4 9.8 %collective-permute-start.1 = (bf16[24,2176]{1,0:T(8,128)(2,1)}, bf16[24,2176]{1,0:T(8,128)(2,1)S(1)}, u32[]{:S(2)}, u32[]{:S(2)}) collective-permute-start(bf16[24,2176]{1,0:T(8,128)(2,1)} %pack_tokens.1), channel_id=1, source_target_pairs={{0,16},{1,17},{2,18},{3,19},{4,20},{5,21},{6,22},{7,23},{8,24},{9,... | collective-permute-start | bytes 313352 | tf_op jit(solution)/shard_map/ppermute | solution.py:303
  8.0 7.2 %collective-permute-start = (bf16[24,2176]{1,0:T(8,128)(2,1)}, bf16[24,2176]{1,0:T(8,128)(2,1)S(1)}, u32[]{:S(2)}, u32[]{:S(2)}) collective-permute-start(bf16[24,2176]{1,0:T(8,128)(2,1)} %pack_tokens.1), channel_id=1, source_target_pairs={{0,24},{1,25},{2,26},{3,27},{4,28},{5,29},{6,30},{7,31},{8,0},{9,1... | collective-permute-start | bytes 313352 | tf_op jit(solution)/shard_map/ppermute | solution.py:303
  10.3 15.6 %copy-start.1 = (s32[256,1]{0,1:T(1,128)S(1)}, s32[256,1]{0,1:T(1,128)}, u32[]{:S(2)}) copy-start(s32[256,1]{0,1:T(1,128)} %param.13) | copy-start | bytes 3076
  16.1 8.1 %collective-permute-start.3 = (bf16[96,2176]{1,0:T(8,128)(2,1)S(1)}, bf16[96,2176]{1,0:T(8,128)(2,1)S(1)}, u32[]{:S(2)}, u32[]{:S(2)}) collective-permute-start(bf16[96,2176]{1,0:T(8,128)(2,1)S(1)} %pad_maximum_fusion), channel_id=1, source_target_pairs={{0,2},{1,5},{2,0},{3,7},{4,6},{5,1},{6,4},{7,3},{8,10},{9,13},{10,... | collective-permute-start | bytes 1253384 | tf_op jit(solution)/shard_map/ppermute | solution.py:303
  24.3 12.6 %collective-permute-start.4 = (bf16[192,2176]{1,0:T(8,128)(2,1)S(1)}, bf16[192,2176]{1,0:T(8,128)(2,1)S(1)}, u32[]{:S(2)}, u32[]{:S(2)}) collective-permute-start(bf16[192,2176]{1,0:T(8,128)(2,1)S(1)} %constant_dynamic-update-slice_fusion.sr_ref), channel_id=1, source_target_pairs={{0,4},{1,3},{2,6},{3,1},{4,0},{5,7},{6,2},{7,5},{8,12},{9,11},{10,... | collective-permute-start | bytes 2506760 | tf_op jit(solution)/shard_map/ppermute | solution.py:303
  25.9 21.4 %collective-permute-start.5 = (bf16[192,2176]{1,0:T(8,128)(2,1)S(1)}, bf16[192,2176]{1,0:T(8,128)(2,1)S(1)}, u32[]{:S(2)}, u32[]{:S(2)}) collective-permute-start(bf16[192,2176]{1,0:T(8,128)(2,1)S(1)} %constant_dynamic-update-slice_fusion.sr_ref), channel_id=1, source_target_pairs={{0,1},{1,0},{2,3},{3,2},{4,5},{5,4},{6,7},{7,6},{8,9},{9,8},{10,11... | collective-permute-start | bytes 2506760 | tf_op jit(solution)/shard_map/ppermute | solution.py:303
  36.9 10.4 %collective-permute-start.6 = (bf16[192,2176]{1,0:T(8,128)(2,1)S(1)}, bf16[192,2176]{1,0:T(8,128)(2,1)}, u32[]{:S(2)}, u32[]{:S(2)}) collective-permute-start(bf16[192,2176]{1,0:T(8,128)(2,1)S(1)} %collective-permute-done.4.r2_ref), channel_id=1, source_target_pairs={{0,1},{1,0},{2,3},{3,2},{4,5},{5,4},{6,7},{7,6},{8,9},{9,8},{10,11... | collective-permute-start | bytes 2506760 | tf_op jit(solution)/shard_map/ppermute | solution.py:303
  36.9 22.5 %all-to-all-start = ((bf16[32,2,2,16,128]{4,3,2,1,0:T(8,128)(2,1)}), bf16[32,2,2,16,128]{4,3,2,1,0:T(8,128)(2,1)S(1)}, u32[]{:S(2)}, u32[]{:S(2)}) async-start(bf16[32,2,2,16,128]{4,3,2,1,0:T(8,128)(2,1)} %quantize_pages.1), calls=%async_computation | async-start | bytes 1048576 | tf_op jit(solution)/shard_map/all_to_all | solution.py:374
  52.0 7.3 %collective-permute-start.7 = (bf16[384,384]{1,0:T(8,128)(2,1)S(1)}, bf16[384,384]{1,0:T(8,128)(2,1)S(1)}, u32[]{:S(2)}, u32[]{:S(2)}) collective-permute-start(bf16[384,384]{1,0:T(8,128)(2,1)S(1)} %expert_hidden.1.own_ref), channel_id=1, source_target_pairs={{0,1},{1,0},{2,3},{3,2},{4,5},{5,4},{6,7},{7,6},{8,9},{9,8},{10,11... | collective-permute-start | bytes 884744 | tf_op jit(solution)/shard_map/ppermute | solution.py:303
  52.4 10.8 %copy-start = (bf16[8,3,32,128]{3,2,1,0:T(8,128)(2,1)S(1)}, bf16[8,3,32,128]{3,2,1,0:T(8,128)(2,1)}, u32[]{:S(2)}) copy-start(bf16[8,3,32,128]{3,2,1,0:T(8,128)(2,1)} %q_ref.1) | copy-start | bytes 589828
  62.5 12.1 %collective-permute-start.8 = (bf16[192,2048]{1,0:T(8,128)(2,1)S(1)}, bf16[192,2048]{1,0:T(8,128)(2,1)S(1)}, u32[]{:S(2)}, u32[]{:S(2)}) collective-permute-start(bf16[192,2048]{1,0:T(8,128)(2,1)S(1)} %expert_back_send.1), channel_id=1, source_target_pairs={{0,2},{1,5},{2,0},{3,7},{4,6},{5,1},{6,4},{7,3},{8,10},{9,13},{10,... | collective-permute-start | bytes 2359304 | tf_op jit(solution)/shard_map/ppermute | solution.py:303
  74.8 7.8 %collective-permute-start.9 = (bf16[96,2048]{1,0:T(8,128)(2,1)S(1)}, bf16[96,2048]{1,0:T(8,128)(2,1)S(1)}, u32[]{:S(2)}, u32[]{:S(2)}) collective-permute-start(bf16[96,2048]{1,0:T(8,128)(2,1)S(1)} %slice.44), channel_id=1, source_target_pairs={{0,4},{1,3},{2,6},{3,1},{4,0},{5,7},{6,2},{7,5},{8,12},{9,11},{10,... | collective-permute-start | bytes 1179656 | tf_op jit(solution)/shard_map/ppermute | solution.py:303
  82.8 6.6 %collective-permute-start.10 = (bf16[24,2048]{1,0:T(8,128)(2,1)S(1)}, bf16[24,2048]{1,0:T(8,128)(2,1)S(1)}, u32[]{:S(2)}, u32[]{:S(2)}) collective-permute-start(bf16[24,2048]{1,0:T(8,128)(2,1)S(1)} %get-tuple-element.32), channel_id=1, source_target_pairs={{0,8},{1,9},{2,10},{3,11},{4,12},{5,13},{6,14},{7,15},{8,16},{9,17... | collective-permute-start | bytes 294920 | tf_op jit(solution)/shard_map/ppermute | solution.py:303
  84.5 5.8 %collective-permute-start.12 = (bf16[24,2048]{1,0:T(8,128)(2,1)S(1)}, bf16[24,2048]{1,0:T(8,128)(2,1)S(1)}, u32[]{:S(2)}, u32[]{:S(2)}) collective-permute-start(bf16[24,2048]{1,0:T(8,128)(2,1)S(1)} %get-tuple-element.33), channel_id=1, source_target_pairs={{0,24},{1,25},{2,26},{3,27},{4,28},{5,29},{6,30},{7,31},{8,0},{9,1... | collective-permute-start | bytes 294920 | tf_op jit(solution)/shard_map/ppermute | solution.py:303
  86.7 5.8 %collective-permute-start.11 = (bf16[24,2048]{1,0:T(8,128)(2,1)S(1)}, bf16[24,2048]{1,0:T(8,128)(2,1)S(1)}, u32[]{:S(2)}, u32[]{:S(2)}) collective-permute-start(bf16[24,2048]{1,0:T(8,128)(2,1)S(1)} %get-tuple-element.34), channel_id=1, source_target_pairs={{0,16},{1,17},{2,18},{3,19},{4,20},{5,21},{6,22},{7,23},{8,24},{9,... | collective-permute-start | bytes 294920 | tf_op jit(solution)/shard_map/ppermute | solution.py:303

commit v11 on v4

--- a/solution.py
+++ b/solution.py
@@ -26,19 +26,18 @@
     largest = jnp.max(jnp.abs(values), axis=(3, 4), keepdims=True)
     scale = jnp.full(largest.shape, 2.0 ** (-16), jnp.float32)
     inverse = jnp.full(largest.shape, 2.0**16, jnp.float32)
-    for exponent in range(-16, 4):
+    for exponent in range(-16, -6):
         exceeds = largest > LIMIT * 2.0**exponent
         scale = jnp.where(exceeds, scale * 2.0, scale)
         inverse = jnp.where(exceeds, inverse * 0.5, inverse)
     scaled = values * inverse
-    magnitude = jnp.abs(scaled)
+    rest = jnp.abs(scaled) * 2.0**6
     step = jnp.full(scaled.shape, 2.0 ** (-9), jnp.float32)
-    back = jnp.full(scaled.shape, 2.0**9, jnp.float32)
-    for exponent in range(-5, 9):
-        exceeds = magnitude >= 2.0**exponent
-        step = jnp.where(exceeds, step * 2.0, step)
-        back = jnp.where(exceeds, back * 0.5, back)
-    levels = jnp.minimum(jnp.floor(magnitude * back + 0.5) * step, LIMIT)
+    for bits in (8, 4, 2, 1):
+        exceeds = rest >= 2.0**bits
+        rest = jnp.where(exceeds, rest * 2.0**-bits, rest)
+        step = jnp.where(exceeds, step * 2.0**bits, step)
+    levels = jnp.minimum(jnp.floor(rest * 8.0 + 0.5) * step, LIMIT)
     cache = (jnp.where(scaled < 0.0, -levels, levels) * scale).astype(jnp.bfloat16)
 
     send_ref[...] = jnp.zeros(send_ref.shape, send_ref.dtype)
@@ -140,20 +139,19 @@
     out_ref[:, half:] = jnp.where(part < 3, chosen, 0.0).astype(out_ref.dtype)
 
 
-def partial_kernel(chunks, core_ref, sr_ref, r2_ref, gate_ref, up_ref, gate_sum, up_sum):
+def partial_kernel(chunks, core_ref, x_ref, gate_ref, up_ref, gate_sum, up_sum):
     half = gate_ref.shape[1] // 2
     depth = half // chunks
     for c in range(chunks):
         at = slice(c * depth, (c + 1) * depth)
         rows = pl.ds(pl.multiple_of(core_ref[0] * half + c * depth, 128), depth)
-        x = jnp.concatenate([sr_ref[:, at], r2_ref[:, at]], axis=0)
         for weight, total in ((gate_ref, gate_sum), (up_ref, up_sum)):
-            part = jnp.dot(x, weight[0, rows], preferred_element_type=jnp.float32)
+            part = jnp.dot(x_ref[:, at], weight[0, rows], preferred_element_type=jnp.float32)
             total[...] = part if c == 0 else total[...] + part
 
 
 def hidden_kernel(
-    chunks, core_ref, sr_ref, r2_ref, gate_ref, up_ref, gate_part, up_part, out_ref, sums
+    chunks, core_ref, sr_ref, r2_ref, gate_ref, up_ref, g0_ref, u0_ref, g1_ref, u1_ref, out_ref, sums
 ):
     half = gate_ref.shape[1] // 2
     depth = half // chunks
@@ -165,9 +163,15 @@
             [sr_ref[:group, at], r2_ref[:group, at], sr_ref[group:, at], r2_ref[group:, at]],
             axis=0,
         )
-        for i, (weight, start) in enumerate(((gate_ref, gate_part), (up_ref, up_part))):
+        for i, (weight, early, late) in enumerate(
+            ((gate_ref, g0_ref, g1_ref), (up_ref, u0_ref, u1_ref))
+        ):
             part = jnp.dot(x, weight[0, rows], preferred_element_type=jnp.float32)
-            sums[i] = (start[...] if c == 0 else sums[i]) + part
+            if c == 0:
+                sums[i, : 2 * group] = early[...] + part[: 2 * group]
+                sums[i, 2 * group :] = late[...] + part[2 * group :]
+            else:
+                sums[i] += part
     gate = sums[0]
     out_ref[...] = (gate / (1.0 + jnp.exp(-gate)) * sums[1]).astype(out_ref.dtype)
 
@@ -176,28 +180,45 @@
     return sum(math.prod(a.shape) * a.dtype.itemsize for a in arrays) * 9 // 8 + 4 * MIB
 
 
-def expert_front(core, rows, w_gate, w_up, parts):
-    tokens = 2 * rows[0].shape[0]
+def expert_partial(core, x, w_gate, w_up):
+    tokens = x.shape[0]
     d, f = w_gate.shape[1:]
-    last = parts is not None
     total = jax.ShapeDtypeStruct((tokens, f), jnp.float32)
-    scratch = [pltpu.VMEM((2, tokens, f), jnp.float32)] if last else []
     return pl.pallas_call(
-        functools.partial(hidden_kernel if last else partial_kernel, 4),
-        in_specs=[smem()] + [vmem()] * (6 if last else 4),
-        out_specs=vmem() if last else [vmem(), vmem()],
-        scratch_shapes=scratch,
-        out_shape=jax.ShapeDtypeStruct((tokens, f), jnp.bfloat16) if last else [total, total],
-        compiler_params=pltpu.CompilerParams(
-            vmem_limit_bytes=room(*rows, w_gate, w_up, *[total] * (5 if last else 2))
-        ),
+        functools.partial(partial_kernel, 4),
+        in_specs=[smem()] + [vmem()] * 3,
+        out_specs=[vmem(), vmem()],
+        out_shape=[total, total],
+        compiler_params=pltpu.CompilerParams(vmem_limit_bytes=room(x, w_gate, w_up, total, total)),
         cost_estimate=pl.CostEstimate(
             flops=2 * tokens * d * f,
             bytes_accessed=tokens * d + 2 * d * f + 8 * tokens * f,
-            transcendentals=tokens * f if last else 0,
-        ),
-        name="expert_hidden" if last else "expert_partial",
-    )(core, *rows, w_gate, w_up, *(parts or ()))
+            transcendentals=0,
+        ),
+        name="expert_partial",
+    )(core, x, w_gate, w_up)
+
+
+def expert_hidden(core, sr, r2, w_gate, w_up, parts):
+    tokens = 2 * sr.shape[0]
+    d, f = w_gate.shape[1:]
+    total = jax.ShapeDtypeStruct((tokens, f), jnp.float32)
+    return pl.pallas_call(
+        functools.partial(hidden_kernel, 4),
+        in_specs=[smem()] + [vmem()] * 8,
+        out_specs=vmem(),
+        out_shape=jax.ShapeDtypeStruct((tokens, f), jnp.bfloat16),
+        scratch_shapes=[pltpu.VMEM((2, tokens, f), jnp.float32)],
+        compiler_params=pltpu.CompilerParams(
+            vmem_limit_bytes=room(sr, r2, w_gate, w_up, *[total] * 5)
+        ),
+        cost_estimate=pl.CostEstimate(
+            flops=2 * tokens * d * f,
+            bytes_accessed=tokens * d + 2 * d * f + 10 * tokens * f,
+            transcendentals=tokens * f,
+        ),
+        name="expert_hidden",
+    )(core, sr, r2, w_gate, w_up, *parts)
 
 
 def back_kernel(
@@ -339,11 +360,12 @@
     sr, fresh, tables = lax.optimization_barrier((sr, fresh, tables))
     r2 = moves.flip(sr, 1)
     cache = lax.all_to_all(send, "ep", split_axis=0, concat_axis=0, tiled=True)
-    r2, cache = lax.optimization_barrier((r2, cache))
+    core_then, cache = lax.optimization_barrier((own_core, cache))
+    early = expert_partial(core_then, sr, w_gate, w_up)
+    r2, early = lax.optimization_barrier((r2, early))
     other_sr, other_r2 = moves.cores(sr), moves.cores(r2)
-
-    parts = expert_front(own_core, (sr, r2), w_gate, w_up, None)
-    hidden = expert_front(own_core, (other_sr, other_r2), w_gate, w_up, parts)
+    parts = early + expert_partial(own_core, r2, w_gate, w_up)
+    hidden = expert_hidden(own_core, other_sr, other_r2, w_gate, w_up, parts)
     other_hidden = moves.cores(hidden)
     sent = expert_back(True, owners, at, hidden, other_hidden, w_down, sr, r2, lanes)
     kept = expert_back(False, owners, at, hidden, other_hidden, w_down, sr, r2, lanes)
@@ -352,7 +374,9 @@
         out_shape=jax.ShapeDtypeStruct(queries.shape, jnp.bfloat16),
         in_specs=[smem()] + [vmem()] * 6,
         out_specs=vmem(),
-        compiler_params=pltpu.CompilerParams(vmem_limit_bytes=8 * MIB + 16 * slots * page_len * tokens * q_heads),
+        compiler_params=pltpu.CompilerParams(
+            vmem_limit_bytes=8 * MIB + 16 * slots * page_len * tokens * q_heads
+        ),
         name="attention",
     )(
         me_ref,

time: 85.9 us -> 87.3 us (1.016)
  Pallas kernels: 15.3 us -> 18.9 us
  waiting for transfers between devices: 36.9 us -> 33.5 us
  other arithmetic: 2.73 us -> 5.7 us
  local copies, waits for them, and re-layouts: 6.38 us -> 5.22 us
    pallas_call x2 -> x3, Pallas kernels: 3.61 us -> 7.55 us  [the longest x2 4.42 us: expert_partial(): pl.pallas_call(functools.partial(partial_kernel, 4), in_specs=[smem()] +...]
    pallas_call x1, Pallas kernels: 4.93 us -> 1.86 us  [body(): pl.pallas_call(functools.partial(page_kernel, pages), out_shape=jax.Shape...]
    concatenate x1, other arithmetic: 0.06 us -> 2.11 us  [body(): sr = jnp.concatenate([line, moves.flip(line, 0)], axis=0)]
    all_to_all x1, waiting for transfers between devices: 12.1 us -> 10.3 us  [body(): cache = lax.all_to_all(send, 'ep', split_axis=0, concat_axis=0, tiled=True)]
    pallas_call x2, Pallas kernels: 3.07 us -> 4.8 us  [expert_back(): pl.pallas_call(functools.partial(back_kernel, send, experts, lanes, 4), o...]
    ppermute x13, starting transfers between devices: 18.1 us -> 16.5 us  [go(): return lax.ppermute(x, ('ep', 'pd'), perm)]
    ppermute x13, waiting for transfers between devices: 24.8 us -> 23.2 us  [go(): return lax.ppermute(x, ('ep', 'pd'), perm)]
    unnamed x22 -> x24, local copies, waits for them, and re-layouts: 6.05 us -> 4.88 us
  transfers between devices with their start and end apart: 14 -> 14, of which waited for: 7 -> 9; matrix products, arithmetic and copies ran while one was open for 3% -> 5% of each run, Pallas kernels for 12% -> 13%
where the time goes in v11:
time: 87.3 us; the launch traced here: 86.8 us
  waiting for transfers between devices  33.5 us (38%)
  starting transfers between devices  22.6 us (26%)
  Pallas kernels  18.9 us (22%)
  other arithmetic  5.7 us (7%)
  local copies, waits for them, and re-layouts  5.22 us (6%)
    ppermute x13, waiting for transfers between devices, go(): return lax.ppermute(x, ('ep', 'pd'), perm)  23.2 us
    ppermute x13, starting transfers between devices, go(): return lax.ppermute(x, ('ep', 'pd'), perm)  16.5 us
    all_to_all x1, waiting for transfers between devices, body(): cache = lax.all_to_all(send, 'ep', split_axis=0, concat_axis=0, tiled=True)  10.3 us
    all_to_all x1, starting transfers between devices, body(): cache = lax.all_to_all(send, 'ep', split_axis=0, concat_axis=0, tiled=True)  6.12 us
    unnamed x24, local copies, waits for them, and re-layouts  4.88 us
    pallas_call x2, Pallas kernels, expert_back(): pl.pallas_call(functools.partial(back_kernel, send, experts, lanes, 4), o...  4.8 us
    pallas_call x2, Pallas kernels, expert_partial(): pl.pallas_call(functools.partial(partial_kernel, 4), in_specs=[smem()] +...  4.42 us
    pallas_call x1, Pallas kernels, expert_hidden(): pl.pallas_call(functools.partial(hidden_kernel, 4), in_specs=[smem()] + [...  3.13 us
  transfers between devices with their start and end apart: 14, of which 9 were waited for; matrix products, arithmetic and copies ran while one was open for 5% of the time, Pallas kernels for 13%

profile of v11, /device:TPU:0, one launch (start us, length us, event | category | flops | bytes accessed | tf_op | source)
XLA Modules:
  0.0 86.8 jit_solution(10464931260423334391)
XLA Ops:
  0.7 1.7 %pack_tokens.1 = bf16[24,2176]{1,0:T(8,128)(2,1)} custom-call(s32[1]{0:T(128)} %bitcast.1.core_ref, bf16[24,4096]{1,0:T(8,128)(2,1)} %bitcast.23, s32[24,8]{1,0:T(8,128)} %bitcast.25, f32[24,8]{1,0:T(8,128)} %bitcast.26), custom_call_target="tpu_custom_call" | custom-call | tf_op jit(solution)/shard_map/pack_tokens/pallas_call | solution.py:332
  2.4 3.0 %collective-permute-start.2 = (bf16[24,2176]{1,0:T(8,128)(2,1)}, bf16[24,2176]{1,0:T(8,128)(2,1)S(1)}, u32[]{:S(2)}, u32[]{:S(2)}) collective-permute-start(bf16[24,2176]{1,0:T(8,128)(2,1)} %pack_tokens.1), channel_id=1, source_target_pairs={{0,8},{1,9},{2,10},{3,11},{4,12},{5,13},{6,14},{7,15},{8,16},{9,17... | collective-permute-start | bytes 313352 | tf_op jit(solution)/shard_map/ppermute | solution.py:291
  5.4 2.6 %collective-permute-start.1 = (bf16[24,2176]{1,0:T(8,128)(2,1)}, bf16[24,2176]{1,0:T(8,128)(2,1)S(1)}, u32[]{:S(2)}, u32[]{:S(2)}) collective-permute-start(bf16[24,2176]{1,0:T(8,128)(2,1)} %pack_tokens.1), channel_id=1, source_target_pairs={{0,16},{1,17},{2,18},{3,19},{4,20},{5,21},{6,22},{7,23},{8,24},{9,... | collective-permute-start | bytes 313352 | tf_op jit(solution)/shard_map/ppermute | solution.py:291
  8.0 1.3 %collective-permute-start = (bf16[24,2176]{1,0:T(8,128)(2,1)}, bf16[24,2176]{1,0:T(8,128)(2,1)S(1)}, u32[]{:S(2)}, u32[]{:S(2)}) collective-permute-start(bf16[24,2176]{1,0:T(8,128)(2,1)} %pack_tokens.1), channel_id=1, source_target_pairs={{0,24},{1,25},{2,26},{3,27},{4,28},{5,29},{6,30},{7,31},{8,0},{9,1... | collective-permute-start | bytes 313352 | tf_op jit(solution)/shard_map/ppermute | solution.py:291
  9.4 1.0 %copy.22 = bf16[16,2,16,2,128]{4,2,3,1,0:T(8,128)(2,1)S(1)} copy(bf16[16,2,16,2,128]{4,3,2,1,0:T(2,128)(2,1)} %param.12) | data formatting | bytes 524288 | tf_op args[0]
  10.4 0.7 copy-done.6
  11.1 1.9 %quantize_pages.1 = bf16[32,2,2,16,128]{4,3,2,1,0:T(8,128)(2,1)S(1)} custom-call(s32[1]{0:T(128)} %bitcast.me_ref, s32[256]{0:T(256)S(1)} %bitcast.22, bf16[16,2,2,16,128]{4,3,2,1,0:T(8,128)(2,1)S(1)} %bitcast.21), custom_call_target="tpu_custom_call" | custom-call | tf_op jit(solution)/shard_map/quantize_pages/pallas_call | solution.py:344
  12.9 0.8 copy-done.4
  13.7 1.5 %collective-permute-done.1 = bf16[24,2176]{1,0:T(8,128)(2,1)S(1)} collective-permute-done((bf16[24,2176]{1,0:T(8,128)(2,1)}, bf16[24,2176]{1,0:T(8,128)(2,1)S(1)}, u32[]{:S(2)}, u32[]{:S(2)}) %collective-permute-start.1) | collective-permute-done | bytes 104480 | tf_op jit(solution)/shard_map/ppermute | solution.py:291
  15.2 1.8 %pad_maximum_fusion.1 = bf16[96,2176]{1,0:T(8,128)(2,1)} fusion(bf16[24,2176]{1,0:T(8,128)(2,1)S(1)} %collective-permute-done.2, bf16[24,2176]{1,0:T(8,128)(2,1)S(1)} %collective-permute-done.1, bf16[24,2176]{1,0:T(8,128)(2,1)S(1)} %collective-permute-done, bf16[24,2176]{1,0:T(8,128)(2,1)} %pack_tokens.1), kind=kLoop, calls=%fused_computation.4 | loop fusion | flops 1671168 | bytes 835584 | tf_op jit(solution)/shard_map/concatenate | solution.py:354
  17.1 1.5 %collective-permute-start.3 = (bf16[96,2176]{1,0:T(8,128)(2,1)}, bf16[96,2176]{1,0:T(8,128)(2,1)}, u32[]{:S(2)}, u32[]{:S(2)}) collective-permute-start(bf16[96,2176]{1,0:T(8,128)(2,1)} %pad_maximum_fusion.1), channel_id=1, source_target_pairs={{0,2},{1,5},{2,0},{3,7},{4,6},{5,1},{6,4},{7,3},{8,10},{9,13},{10,... | collective-permute-start | bytes 1253384 | tf_op jit(solution)/shard_map/ppermute | solution.py:291
  19.1 0.7 reduce.3
  20.0 6.1 %all-to-all-start = ((bf16[32,2,2,16,128]{4,3,2,1,0:T(8,128)(2,1)}), bf16[32,2,2,16,128]{4,3,2,1,0:T(8,128)(2,1)}, u32[]{:S(2)}, u32[]{:S(2)}) async-start(bf16[32,2,2,16,128]{4,3,2,1,0:T(8,128)(2,1)} %copy-done.4), calls=%async_computation | async-start | bytes 1048576 | tf_op jit(solution)/shard_map/all_to_all | solution.py:362
  26.2 2.1 %pad_maximum_fusion.x_ref.sr_ref = bf16[192,2176]{1,0:T(8,128)(2,1)} fusion(bf16[96,2176]{1,0:T(8,128)(2,1)} %collective-permute-done.3, bf16[96,2176]{1,0:T(8,128)(2,1)} %pad_maximum_fusion.1), kind=kLoop, calls=%fused_computation.1 | loop fusion | flops 1671168 | bytes 1671168 | tf_op jit(solution)/shard_map/concatenate | solution.py:359
  28.3 1.9 %collective-permute-start.5 = (bf16[192,2176]{1,0:T(8,128)(2,1)}, bf16[192,2176]{1,0:T(8,128)(2,1)}, u32[]{:S(2)}, u32[]{:S(2)}) collective-permute-start(bf16[192,2176]{1,0:T(8,128)(2,1)} %pad_maximum_fusion.x_ref.sr_ref), channel_id=1, source_target_pairs={{0,4},{1,3},{2,6},{3,1},{4,0},{5,7},{6,2},{7,5},{8,12},{9,11},{10,... | collective-permute-start | bytes 2506760 | tf_op jit(solution)/shard_map/ppermute | solution.py:291
  30.2 10.3 %all-to-all-done.cache_ref = bf16[32,2,2,16,128]{4,3,2,1,0:T(8,128)(2,1)} async-done(((bf16[32,2,2,16,128]{4,3,2,1,0:T(8,128)(2,1)}), bf16[32,2,2,16,128]{4,3,2,1,0:T(8,128)(2,1)}, u32[]{:S(2)}, u32[]{:S(2)}) %all-to-all-start) | async-done | bytes 524320 | tf_op jit(solution)/shard_map/all_to_all | solution.py:362
  40.4 1.9 %copy-done.1 = bf16[1,4096,384]{2,1,0:T(8,128)(2,1)S(1)} copy-done((bf16[1,4096,384]{2,1,0:T(8,128)(2,1)S(1)}, bf16[1,4096,384]{2,1,0:T(8,128)(2,1)}, u32[]{:S(2)}) %copy-start.1) | copy-done | bytes 3145752
  42.3 2.1 %expert_partial.2 = (f32[192,384]{1,0:T(8,128)S(1)}, f32[192,384]{1,0:T(8,128)S(1)}) custom-call(s32[1]{0:T(128)} %bitcast.1.core_ref, bf16[192,2176]{1,0:T(8,128)(2,1)} %pad_maximum_fusion.x_ref.sr_ref, bf16[1,4096,384]{2,1,0:T(8,128)(2,1)S(1)} %copy-done, bf16[1,4096,384]{2,1,0:T(8,128)(2,1)S(1)} %copy-done.1), custom_call_target="tpu_custom_call" | custom-call | flops 603979776 | bytes 4521984 | tf_op jit(solution)/shard_map/expert_partial/pallas_call | solution.py:187
  44.5 2.3 %expert_partial.3 = (f32[192,384]{1,0:T(8,128)S(1)}, f32[192,384]{1,0:T(8,128)S(1)}) custom-call(s32[1]{0:T(128)} %bitcast.1.core_ref, bf16[192,2176]{1,0:T(8,128)(2,1)} %collective-permute-done.5.x_ref.r2_ref, bf16[1,4096,384]{2,1,0:T(8,128)(2,1)S(1)} %copy-done, bf16[1,4096,384]{2,1,0:T(8,128)(2,1)S(1)} %copy-done.1), custom_call_target="tpu_custom_call" | custom-call | flops 603979776 | bytes 4521984 | tf_op jit(solution)/shard_map/expert_partial/pallas_call | solution.py:187
  47.1 3.1 %expert_hidden.1.own_ref = bf16[384,384]{1,0:T(8,128)(2,1)S(1)} custom-call(s32[1]{0:T(128)} %bitcast.1.core_ref, bf16[192,2176]{1,0:T(8,128)(2,1)} %collective-permute-done.4.sr_ref, bf16[192,2176]{1,0:T(8,128)(2,1)S(1)} %collective-permute-done.6.r2_ref, bf16[1,4096,384]{2,1,0:T(8,128)(2,1)S(1)} %copy-done, bf16[1,4096,384]{2,1,0:T(8,128)(2,1)S(1)} %copy-done.2, ...), custom_call_target="tpu_custom_call" | custom-call | flops 1207959552 | bytes 6193152 | tf_op jit(solution)/shard_map/expert_hidden/pallas_call | solution.py:206
  50.6 1.2 %collective-permute-done.7.other_ref = bf16[384,384]{1,0:T(8,128)(2,1)S(1)} collective-permute-done((bf16[384,384]{1,0:T(8,128)(2,1)S(1)}, bf16[384,384]{1,0:T(8,128)(2,1)S(1)}, u32[]{:S(2)}, u32[]{:S(2)}) %collective-permute-start.7) | collective-permute-done | bytes 294944 | tf_op jit(solution)/shard_map/ppermute | solution.py:291
  51.9 2.4 %expert_back_send.1 = bf16[192,2048]{1,0:T(8,128)(2,1)S(1)} custom-call(s32[2]{0:T(128)S(1)} %pad_add_fusion.at_ref, bf16[384,384]{1,0:T(8,128)(2,1)S(1)} %expert_hidden.1.own_ref, bf16[384,384]{1,0:T(8,128)(2,1)S(1)} %collective-permute-done.7.other_ref, bf16[192,2176]{1,0:T(8,128)(2,1)} %pad_maximum_fusion.x_ref.sr_ref, ...), custom_call_target="tpu_custom_call" | custom-call | flops 603979776 | bytes 5308416 | tf_op jit(solution)/shard_map/expert_back_send/pallas_call | solution.py:265
  54.9 3.0 %attention.1 = bf16[8,3,32,128]{3,2,1,0:T(8,128)(2,1)} custom-call(s32[1]{0:T(128)} %bitcast.me_ref, s32[16,16]{1,0:T(8,128)S(1)} %reshape.38.owner_ref, s32[16,16]{1,0:T(8,128)S(1)} %reshape.39.slot_ref, s32[16,16]{1,0:T(8,128)S(1)} %reshape.40.fill_ref, bf16[8,3,32,128]{3,2,1,0:T(8,128)(2,1)S(1)} %copy-done.5, ...), custom_call_target="tpu_custom_call" | custom-call | tf_op jit(solution)/shard_map/attention/pallas_call | solution.py:372
  57.9 2.4 %expert_back_keep.1 = f32[192,2048]{1,0:T(8,128)S(1)} custom-call(s32[2]{0:T(128)S(1)} %pad_add_fusion.at_ref, bf16[384,384]{1,0:T(8,128)(2,1)S(1)} %expert_hidden.1.own_ref, bf16[384,384]{1,0:T(8,128)(2,1)S(1)} %collective-permute-done.7.other_ref, bf16[192,2176]{1,0:T(8,128)(2,1)} %pad_maximum_fusion.x_ref.sr_ref, ...), custom_call_target="tpu_custom_call" | custom-call | flops 603979776 | bytes 5308416 | tf_op jit(solution)/shard_map/expert_back_keep/pallas_call | solution.py:265
  60.3 6.0 %collective-permute-done.8 = bf16[192,2048]{1,0:T(8,128)(2,1)S(1)} collective-permute-done((bf16[192,2048]{1,0:T(8,128)(2,1)S(1)}, bf16[192,2048]{1,0:T(8,128)(2,1)S(1)}, u32[]{:S(2)}, u32[]{:S(2)}) %collective-permute-start.8) | collective-permute-done | bytes 786464 | tf_op jit(solution)/shard_map/ppermute | solution.py:291
  66.6 1.1 %collective-permute-start.9 = (bf16[96,2048]{1,0:T(8,128)(2,1)S(1)}, bf16[96,2048]{1,0:T(8,128)(2,1)S(1)}, u32[]{:S(2)}, u32[]{:S(2)}) collective-permute-start(bf16[96,2048]{1,0:T(8,128)(2,1)S(1)} %slice.44), channel_id=1, source_target_pairs={{0,4},{1,3},{2,6},{3,1},{4,0},{5,7},{6,2},{7,5},{8,12},{9,11},{10,... | collective-permute-start | bytes 1179656 | tf_op jit(solution)/shard_map/ppermute | solution.py:291
  67.7 6.8 %collective-permute-done.9 = bf16[96,2048]{1,0:T(8,128)(2,1)S(1)} collective-permute-done((bf16[96,2048]{1,0:T(8,128)(2,1)S(1)}, bf16[96,2048]{1,0:T(8,128)(2,1)S(1)}, u32[]{:S(2)}, u32[]{:S(2)}) %collective-permute-start.9) | collective-permute-done | bytes 393248 | tf_op jit(solution)/shard_map/ppermute | solution.py:291
  74.6 1.7 %collective-permute-start.10 = (bf16[24,2048]{1,0:T(8,128)(2,1)S(1)}, bf16[24,2048]{1,0:T(8,128)(2,1)S(1)}, u32[]{:S(2)}, u32[]{:S(2)}) collective-permute-start(bf16[24,2048]{1,0:T(8,128)(2,1)S(1)} %get-tuple-element.40), channel_id=1, source_target_pairs={{0,8},{1,9},{2,10},{3,11},{4,12},{5,13},{6,14},{7,15},{8,16},{9,17... | collective-permute-start | bytes 294920 | tf_op jit(solution)/shard_map/ppermute | solution.py:291
  76.3 2.2 %collective-permute-start.12 = (bf16[24,2048]{1,0:T(8,128)(2,1)S(1)}, bf16[24,2048]{1,0:T(8,128)(2,1)S(1)}, u32[]{:S(2)}, u32[]{:S(2)}) collective-permute-start(bf16[24,2048]{1,0:T(8,128)(2,1)S(1)} %get-tuple-element.41), channel_id=1, source_target_pairs={{0,24},{1,25},{2,26},{3,27},{4,28},{5,29},{6,30},{7,31},{8,0},{9,1... | collective-permute-start | bytes 294920 | tf_op jit(solution)/shard_map/ppermute | solution.py:291
  78.6 3.4 %collective-permute-done.10 = bf16[24,2048]{1,0:T(8,128)(2,1)S(1)} collective-permute-done((bf16[24,2048]{1,0:T(8,128)(2,1)S(1)}, bf16[24,2048]{1,0:T(8,128)(2,1)S(1)}, u32[]{:S(2)}, u32[]{:S(2)}) %collective-permute-start.10) | collective-permute-done | bytes 98336 | tf_op jit(solution)/shard_map/ppermute | solution.py:291
  82.1 4.0 %collective-permute-done.11 = bf16[24,2048]{1,0:T(8,128)(2,1)S(1)} collective-permute-done((bf16[24,2048]{1,0:T(8,128)(2,1)S(1)}, bf16[24,2048]{1,0:T(8,128)(2,1)S(1)}, u32[]{:S(2)}, u32[]{:S(2)}) %collective-permute-start.11) | collective-permute-done | bytes 98336 | tf_op jit(solution)/shard_map/ppermute | solution.py:291
  86.1 0.7 fusion.3
  (42 shorter events, 2.8 us)
Async XLA Ops:
  0.6 18.4 %copy-start.7 = (s32[256,1]{0,1:T(1,128)S(1)}, s32[256,1]{0,1:T(1,128)}, u32[]{:S(2)}) copy-start(s32[256,1]{0,1:T(1,128)} %param.13) | copy-start | bytes 3076
  0.6 19.2 %copy-start.9 = (s32[256]{0:T(256)S(1)}, s32[256]{0:T(256)}, u32[]{:S(2)}) copy-start(s32[256]{0:T(256)} %param.14) | copy-start | bytes 3076
  0.7 19.2 %copy-start.10 = (s32[256]{0:T(256)S(1)}, s32[256]{0:T(256)}, u32[]{:S(2)}) copy-start(s32[256]{0:T(256)} %param.15) | copy-start | bytes 3076
  0.7 19.3 %copy-start.8 = (bf16[8,3,2,2,128]{4,3,2,1,0:T(2,128)(2,1)S(1)}, bf16[8,3,2,2,128]{4,3,2,1,0:T(2,128)(2,1)}, u32[]{:S(2)}) copy-start(bf16[8,3,2,2,128]{4,3,2,1,0:T(2,128)(2,1)} %param.17) | copy-start | bytes 73732
  2.4 11.3 %collective-permute-start.2 = (bf16[24,2176]{1,0:T(8,128)(2,1)}, bf16[24,2176]{1,0:T(8,128)(2,1)S(1)}, u32[]{:S(2)}, u32[]{:S(2)}) collective-permute-start(bf16[24,2176]{1,0:T(8,128)(2,1)} %pack_tokens.1), channel_id=1, source_target_pairs={{0,8},{1,9},{2,10},{3,11},{4,12},{5,13},{6,14},{7,15},{8,16},{9,17... | collective-permute-start | bytes 313352 | tf_op jit(solution)/shard_map/ppermute | solution.py:291
  5.4 9.8 %collective-permute-start.1 = (bf16[24,2176]{1,0:T(8,128)(2,1)}, bf16[24,2176]{1,0:T(8,128)(2,1)S(1)}, u32[]{:S(2)}, u32[]{:S(2)}) collective-permute-start(bf16[24,2176]{1,0:T(8,128)(2,1)} %pack_tokens.1), channel_id=1, source_target_pairs={{0,16},{1,17},{2,18},{3,19},{4,20},{5,21},{6,22},{7,23},{8,24},{9,... | collective-permute-start | bytes 313352 | tf_op jit(solution)/shard_map/ppermute | solution.py:291
  8.0 7.2 %collective-permute-start = (bf16[24,2176]{1,0:T(8,128)(2,1)}, bf16[24,2176]{1,0:T(8,128)(2,1)S(1)}, u32[]{:S(2)}, u32[]{:S(2)}) collective-permute-start(bf16[24,2176]{1,0:T(8,128)(2,1)} %pack_tokens.1), channel_id=1, source_target_pairs={{0,24},{1,25},{2,26},{3,27},{4,28},{5,29},{6,30},{7,31},{8,0},{9,1... | collective-permute-start | bytes 313352 | tf_op jit(solution)/shard_map/ppermute | solution.py:291
  10.4 0.7 copy-start.6
  12.9 0.8 copy-start.4
  15.2 25.2 %copy-start = (bf16[1,4096,384]{2,1,0:T(8,128)(2,1)S(1)}, bf16[1,4096,384]{2,1,0:T(8,128)(2,1)}, u32[]{:S(2)}) copy-start(bf16[1,4096,384]{2,1,0:T(8,128)(2,1)} %gate_ref.5) | copy-start | bytes 9437188
  17.1 9.1 %collective-permute-start.3 = (bf16[96,2176]{1,0:T(8,128)(2,1)}, bf16[96,2176]{1,0:T(8,128)(2,1)}, u32[]{:S(2)}, u32[]{:S(2)}) collective-permute-start(bf16[96,2176]{1,0:T(8,128)(2,1)} %pad_maximum_fusion.1), channel_id=1, source_target_pairs={{0,2},{1,5},{2,0},{3,7},{4,6},{5,1},{6,4},{7,3},{8,10},{9,13},{10,... | collective-permute-start | bytes 1253384 | tf_op jit(solution)/shard_map/ppermute | solution.py:291
  20.0 20.4 %all-to-all-start = ((bf16[32,2,2,16,128]{4,3,2,1,0:T(8,128)(2,1)}), bf16[32,2,2,16,128]{4,3,2,1,0:T(8,128)(2,1)}, u32[]{:S(2)}, u32[]{:S(2)}) async-start(bf16[32,2,2,16,128]{4,3,2,1,0:T(8,128)(2,1)} %copy-done.4), calls=%async_computation | async-start | bytes 1048576 | tf_op jit(solution)/shard_map/all_to_all | solution.py:362
  28.3 16.2 %collective-permute-start.5 = (bf16[192,2176]{1,0:T(8,128)(2,1)}, bf16[192,2176]{1,0:T(8,128)(2,1)}, u32[]{:S(2)}, u32[]{:S(2)}) collective-permute-start(bf16[192,2176]{1,0:T(8,128)(2,1)} %pad_maximum_fusion.x_ref.sr_ref), channel_id=1, source_target_pairs={{0,4},{1,3},{2,6},{3,1},{4,0},{5,7},{6,2},{7,5},{8,12},{9,11},{10,... | collective-permute-start | bytes 2506760 | tf_op jit(solution)/shard_map/ppermute | solution.py:291
  30.2 16.7 %collective-permute-start.4 = (bf16[192,2176]{1,0:T(8,128)(2,1)}, bf16[192,2176]{1,0:T(8,128)(2,1)}, u32[]{:S(2)}, u32[]{:S(2)}) collective-permute-start(bf16[192,2176]{1,0:T(8,128)(2,1)} %pad_maximum_fusion.x_ref.sr_ref), channel_id=1, source_target_pairs={{0,1},{1,0},{2,3},{3,2},{4,5},{5,4},{6,7},{7,6},{8,9},{9,8},{10,11... | collective-permute-start | bytes 2506760 | tf_op jit(solution)/shard_map/ppermute | solution.py:291
  40.4 1.9 %copy-start.1 = (bf16[1,4096,384]{2,1,0:T(8,128)(2,1)S(1)}, bf16[1,4096,384]{2,1,0:T(8,128)(2,1)}, u32[]{:S(2)}) copy-start(bf16[1,4096,384]{2,1,0:T(8,128)(2,1)} %up_ref.5) | copy-start | bytes 9437188
  44.5 2.6 %collective-permute-start.6 = (bf16[192,2176]{1,0:T(8,128)(2,1)}, bf16[192,2176]{1,0:T(8,128)(2,1)S(1)}, u32[]{:S(2)}, u32[]{:S(2)}) collective-permute-start(bf16[192,2176]{1,0:T(8,128)(2,1)} %collective-permute-done.5.x_ref.r2_ref), channel_id=1, source_target_pairs={{0,1},{1,0},{2,3},{3,2},{4,5},{5,4},{6,7},{7,6},{8,9},{9,8},{10,11... | collective-permute-start | bytes 2506760 | tf_op jit(solution)/shard_map/ppermute | solution.py:291
  44.5 2.6 %copy-start.2 = (bf16[1,4096,384]{2,1,0:T(8,128)(2,1)S(1)}, bf16[1,4096,384]{2,1,0:T(8,128)(2,1)}, u32[]{:S(2)}) copy-start(bf16[1,4096,384]{2,1,0:T(8,128)(2,1)} %up_ref.5) | copy-start | bytes 9437188
  47.1 4.8 %copy-start.3 = (bf16[1,768,2048]{2,1,0:T(8,128)(2,1)S(1)}, bf16[1,768,2048]{2,1,0:T(8,128)(2,1)}, u32[]{:S(2)}) copy-start(bf16[1,768,2048]{2,1,0:T(8,128)(2,1)} %down_ref.3) | copy-start | bytes 9437188
  50.2 1.6 %collective-permute-start.7 = (bf16[384,384]{1,0:T(8,128)(2,1)S(1)}, bf16[384,384]{1,0:T(8,128)(2,1)S(1)}, u32[]{:S(2)}, u32[]{:S(2)}) collective-permute-start(bf16[384,384]{1,0:T(8,128)(2,1)S(1)} %expert_hidden.1.own_ref), channel_id=1, source_target_pairs={{0,1},{1,0},{2,3},{3,2},{4,5},{5,4},{6,7},{7,6},{8,9},{9,8},{10,11... | collective-permute-start | bytes 884744 | tf_op jit(solution)/shard_map/ppermute | solution.py:291
  50.6 4.3 %copy-start.5 = (bf16[8,3,32,128]{3,2,1,0:T(8,128)(2,1)S(1)}, bf16[8,3,32,128]{3,2,1,0:T(8,128)(2,1)}, u32[]{:S(2)}) copy-start(bf16[8,3,32,128]{3,2,1,0:T(8,128)(2,1)} %q_ref.1) | copy-start | bytes 589828
  54.3 12.1 %collective-permute-start.8 = (bf16[192,2048]{1,0:T(8,128)(2,1)S(1)}, bf16[192,2048]{1,0:T(8,128)(2,1)S(1)}, u32[]{:S(2)}, u32[]{:S(2)}) collective-permute-start(bf16[192,2048]{1,0:T(8,128)(2,1)S(1)} %expert_back_send.1), channel_id=1, source_target_pairs={{0,2},{1,5},{2,0},{3,7},{4,6},{5,1},{6,4},{7,3},{8,10},{9,13},{10,... | collective-permute-start | bytes 2359304 | tf_op jit(solution)/shard_map/ppermute | solution.py:291
  66.6 7.8 %collective-permute-start.9 = (bf16[96,2048]{1,0:T(8,128)(2,1)S(1)}, bf16[96,2048]{1,0:T(8,128)(2,1)S(1)}, u32[]{:S(2)}, u32[]{:S(2)}) collective-permute-start(bf16[96,2048]{1,0:T(8,128)(2,1)S(1)} %slice.44), channel_id=1, source_target_pairs={{0,4},{1,3},{2,6},{3,1},{4,0},{5,7},{6,2},{7,5},{8,12},{9,11},{10,... | collective-permute-start | bytes 1179656 | tf_op jit(solution)/shard_map/ppermute | solution.py:291
  74.6 7.4 %collective-permute-start.10 = (bf16[24,2048]{1,0:T(8,128)(2,1)S(1)}, bf16[24,2048]{1,0:T(8,128)(2,1)S(1)}, u32[]{:S(2)}, u32[]{:S(2)}) collective-permute-start(bf16[24,2048]{1,0:T(8,128)(2,1)S(1)} %get-tuple-element.40), channel_id=1, source_target_pairs={{0,8},{1,9},{2,10},{3,11},{4,12},{5,13},{6,14},{7,15},{8,16},{9,17... | collective-permute-start | bytes 294920 | tf_op jit(solution)/shard_map/ppermute | solution.py:291
  76.3 5.8 %collective-permute-start.12 = (bf16[24,2048]{1,0:T(8,128)(2,1)S(1)}, bf16[24,2048]{1,0:T(8,128)(2,1)S(1)}, u32[]{:S(2)}, u32[]{:S(2)}) collective-permute-start(bf16[24,2048]{1,0:T(8,128)(2,1)S(1)} %get-tuple-element.41), channel_id=1, source_target_pairs={{0,24},{1,25},{2,26},{3,27},{4,28},{5,29},{6,30},{7,31},{8,0},{9,1... | collective-permute-start | bytes 294920 | tf_op jit(solution)/shard_map/ppermute | solution.py:291
  78.5 7.6 %collective-permute-start.11 = (bf16[24,2048]{1,0:T(8,128)(2,1)S(1)}, bf16[24,2048]{1,0:T(8,128)(2,1)S(1)}, u32[]{:S(2)}, u32[]{:S(2)}) collective-permute-start(bf16[24,2048]{1,0:T(8,128)(2,1)S(1)} %get-tuple-element.42), channel_id=1, source_target_pairs={{0,16},{1,17},{2,18},{3,19},{4,20},{5,21},{6,22},{7,23},{8,24},{9,... | collective-permute-start | bytes 294920 | tf_op jit(solution)/shard_map/ppermute | solution.py:291

commit v12 on v4

--- a/solution.py
+++ b/solution.py
@@ -26,19 +26,18 @@
     largest = jnp.max(jnp.abs(values), axis=(3, 4), keepdims=True)
     scale = jnp.full(largest.shape, 2.0 ** (-16), jnp.float32)
     inverse = jnp.full(largest.shape, 2.0**16, jnp.float32)
-    for exponent in range(-16, 4):
+    for exponent in range(-16, -6):
         exceeds = largest > LIMIT * 2.0**exponent
         scale = jnp.where(exceeds, scale * 2.0, scale)
         inverse = jnp.where(exceeds, inverse * 0.5, inverse)
     scaled = values * inverse
-    magnitude = jnp.abs(scaled)
+    rest = jnp.abs(scaled) * 2.0**6
     step = jnp.full(scaled.shape, 2.0 ** (-9), jnp.float32)
-    back = jnp.full(scaled.shape, 2.0**9, jnp.float32)
-    for exponent in range(-5, 9):
-        exceeds = magnitude >= 2.0**exponent
-        step = jnp.where(exceeds, step * 2.0, step)
-        back = jnp.where(exceeds, back * 0.5, back)
-    levels = jnp.minimum(jnp.floor(magnitude * back + 0.5) * step, LIMIT)
+    for bits in (8, 4, 2, 1):
+        exceeds = rest >= 2.0**bits
+        rest = jnp.where(exceeds, rest * 2.0**-bits, rest)
+        step = jnp.where(exceeds, step * 2.0**bits, step)
+    levels = jnp.minimum(jnp.floor(rest * 8.0 + 0.5) * step, LIMIT)
     cache = (jnp.where(scaled < 0.0, -levels, levels) * scale).astype(jnp.bfloat16)
 
     send_ref[...] = jnp.zeros(send_ref.shape, send_ref.dtype)

time: 85.9 us -> 85.9 us (level)
  Pallas kernels: 15.3 us -> 13 us
  waiting for transfers between devices: 36.9 us -> 38.4 us
    pallas_call x1, Pallas kernels: 4.93 us -> 2.66 us  [body(): pl.pallas_call(functools.partial(page_kernel, pages), out_shape=jax.Shape...]
    ppermute x13, waiting for transfers between devices: 24.8 us -> 26.3 us  [go(): return lax.ppermute(x, ('ep', 'pd'), perm)]
  transfers between devices with their start and end apart: 14 -> 14, of which waited for: 7 -> 8; matrix products, arithmetic and copies ran while one was open for 3% -> 3% of each run, Pallas kernels for 12% -> 9%
where the time goes in v12:
time: 85.9 us; the launch traced here: 85.4 us
  waiting for transfers between devices  38.4 us (45%)
  starting transfers between devices  24.1 us (28%)
  Pallas kernels  13 us (15%)
  local copies, waits for them, and re-layouts  6.38 us (7%)
  other arithmetic  2.72 us (3%)
    ppermute x13, waiting for transfers between devices, go(): return lax.ppermute(x, ('ep', 'pd'), perm)  26.3 us
    ppermute x13, starting transfers between devices, go(): return lax.ppermute(x, ('ep', 'pd'), perm)  18.1 us
    all_to_all x1, waiting for transfers between devices, body(): cache = lax.all_to_all(send, 'ep', split_axis=0, concat_axis=0, tiled=True)  12.1 us
    all_to_all x1, starting transfers between devices, body(): cache = lax.all_to_all(send, 'ep', split_axis=0, concat_axis=0, tiled=True)  6.07 us
    unnamed x22, local copies, waits for them, and re-layouts  6.05 us
    pallas_call x2, Pallas kernels, expert_front(): pl.pallas_call(functools.partial(hidden_kernel if last else partial_kerne...  3.61 us
    pallas_call x2, Pallas kernels, expert_back(): pl.pallas_call(functools.partial(back_kernel, send, experts, lanes, 4), o...  3.07 us
    pallas_call x1, Pallas kernels, body(): pl.pallas_call(functools.partial(page_kernel, pages), out_shape=jax.Shape...  2.66 us
  transfers between devices with their start and end apart: 14, of which 8 were waited for; matrix products, arithmetic and copies ran while one was open for 3% of the time, Pallas kernels for 9%

profile of v12, /device:TPU:0, one launch (start us, length us, event | category | flops | bytes accessed | tf_op | source)
XLA Modules:
  0.0 85.4 jit_solution(14397446208451292305)
XLA Ops:
  0.7 1.7 %pack_tokens.1 = bf16[24,2176]{1,0:T(8,128)(2,1)} custom-call(s32[1]{0:T(128)} %bitcast.1.core_ref, bf16[24,4096]{1,0:T(8,128)(2,1)} %bitcast.23, s32[24,8]{1,0:T(8,128)} %bitcast.25, f32[24,8]{1,0:T(8,128)} %bitcast.26), custom_call_target="tpu_custom_call" | custom-call | tf_op jit(solution)/shard_map/pack_tokens/pallas_call | solution.py:310
  2.4 3.0 %collective-permute-start.2 = (bf16[24,2176]{1,0:T(8,128)(2,1)}, bf16[24,2176]{1,0:T(8,128)(2,1)S(1)}, u32[]{:S(2)}, u32[]{:S(2)}) collective-permute-start(bf16[24,2176]{1,0:T(8,128)(2,1)} %pack_tokens.1), channel_id=1, source_target_pairs={{0,8},{1,9},{2,10},{3,11},{4,12},{5,13},{6,14},{7,15},{8,16},{9,17... | collective-permute-start | bytes 313352 | tf_op jit(solution)/shard_map/ppermute | solution.py:269
  5.4 2.6 %collective-permute-start.1 = (bf16[24,2176]{1,0:T(8,128)(2,1)}, bf16[24,2176]{1,0:T(8,128)(2,1)S(1)}, u32[]{:S(2)}, u32[]{:S(2)}) collective-permute-start(bf16[24,2176]{1,0:T(8,128)(2,1)} %pack_tokens.1), channel_id=1, source_target_pairs={{0,16},{1,17},{2,18},{3,19},{4,20},{5,21},{6,22},{7,23},{8,24},{9,... | collective-permute-start | bytes 313352 | tf_op jit(solution)/shard_map/ppermute | solution.py:269
  8.0 1.3 %collective-permute-start = (bf16[24,2176]{1,0:T(8,128)(2,1)}, bf16[24,2176]{1,0:T(8,128)(2,1)S(1)}, u32[]{:S(2)}, u32[]{:S(2)}) collective-permute-start(bf16[24,2176]{1,0:T(8,128)(2,1)} %pack_tokens.1), channel_id=1, source_target_pairs={{0,24},{1,25},{2,26},{3,27},{4,28},{5,29},{6,30},{7,31},{8,0},{9,1... | collective-permute-start | bytes 313352 | tf_op jit(solution)/shard_map/ppermute | solution.py:269
  9.4 1.0 %copy.22 = bf16[16,2,16,2,128]{4,2,3,1,0:T(8,128)(2,1)S(1)} copy(bf16[16,2,16,2,128]{4,3,2,1,0:T(2,128)(2,1)} %param.12) | data formatting | bytes 524288 | tf_op args[0]
  10.4 0.7 copy-done.5
  11.1 2.7 %quantize_pages.1 = bf16[32,2,2,16,128]{4,3,2,1,0:T(8,128)(2,1)} custom-call(s32[1]{0:T(128)} %bitcast.me_ref, s32[256]{0:T(256)S(1)} %bitcast.22, bf16[16,2,2,16,128]{4,3,2,1,0:T(8,128)(2,1)S(1)} %bitcast.21), custom_call_target="tpu_custom_call" | custom-call | tf_op jit(solution)/shard_map/quantize_pages/pallas_call | solution.py:322
  13.7 1.5 %collective-permute-done.1 = bf16[24,2176]{1,0:T(8,128)(2,1)S(1)} collective-permute-done((bf16[24,2176]{1,0:T(8,128)(2,1)}, bf16[24,2176]{1,0:T(8,128)(2,1)S(1)}, u32[]{:S(2)}, u32[]{:S(2)}) %collective-permute-start.1) | collective-permute-done | bytes 104480 | tf_op jit(solution)/shard_map/ppermute | solution.py:269
  15.2 0.9 %pad_maximum_fusion.1 = bf16[96,2176]{1,0:T(8,128)(2,1)S(1)} fusion(bf16[24,2176]{1,0:T(8,128)(2,1)S(1)} %collective-permute-done.2, bf16[24,2176]{1,0:T(8,128)(2,1)S(1)} %collective-permute-done.1, bf16[24,2176]{1,0:T(8,128)(2,1)S(1)} %collective-permute-done, bf16[24,2176]{1,0:T(8,128)(2,1)} %pack_tokens.1), kind=kLoop, calls=%fused_computation.4 | loop fusion | flops 1671168 | bytes 835584 | tf_op jit(solution)/shard_map/concatenate | solution.py:332
  16.2 1.6 %collective-permute-start.3 = (bf16[96,2176]{1,0:T(8,128)(2,1)S(1)}, bf16[96,2176]{1,0:T(8,128)(2,1)S(1)}, u32[]{:S(2)}, u32[]{:S(2)}) collective-permute-start(bf16[96,2176]{1,0:T(8,128)(2,1)S(1)} %pad_maximum_fusion.1), channel_id=1, source_target_pairs={{0,2},{1,5},{2,0},{3,7},{4,6},{5,1},{6,4},{7,3},{8,10},{9,13},{10,... | collective-permute-start | bytes 1253384 | tf_op jit(solution)/shard_map/ppermute | solution.py:269
  19.2 6.1 %all-to-all-start = ((bf16[32,2,2,16,128]{4,3,2,1,0:T(8,128)(2,1)}), bf16[32,2,2,16,128]{4,3,2,1,0:T(8,128)(2,1)S(1)}, u32[]{:S(2)}, u32[]{:S(2)}) async-start(bf16[32,2,2,16,128]{4,3,2,1,0:T(8,128)(2,1)} %quantize_pages.1), calls=%async_computation | async-start | bytes 1048576 | tf_op jit(solution)/shard_map/all_to_all | solution.py:340
  25.4 2.0 %collective-permute-start.5 = (bf16[192,2176]{1,0:T(8,128)(2,1)S(1)}, bf16[192,2176]{1,0:T(8,128)(2,1)S(1)}, u32[]{:S(2)}, u32[]{:S(2)}) collective-permute-start(bf16[192,2176]{1,0:T(8,128)(2,1)S(1)} %pad_maximum_fusion.sr_ref), channel_id=1, source_target_pairs={{0,4},{1,3},{2,6},{3,1},{4,0},{5,7},{6,2},{7,5},{8,12},{9,11},{10,... | collective-permute-start | bytes 2506760 | tf_op jit(solution)/shard_map/ppermute | solution.py:269
  27.3 12.1 %all-to-all-done.cache_ref = bf16[32,2,2,16,128]{4,3,2,1,0:T(8,128)(2,1)S(1)} async-done(((bf16[32,2,2,16,128]{4,3,2,1,0:T(8,128)(2,1)}), bf16[32,2,2,16,128]{4,3,2,1,0:T(8,128)(2,1)S(1)}, u32[]{:S(2)}, u32[]{:S(2)}) %all-to-all-start) | async-done | bytes 524320 | tf_op jit(solution)/shard_map/all_to_all | solution.py:340
  39.5 2.6 %collective-permute-done.5.r2_ref = bf16[192,2176]{1,0:T(8,128)(2,1)S(1)} collective-permute-done((bf16[192,2176]{1,0:T(8,128)(2,1)S(1)}, bf16[192,2176]{1,0:T(8,128)(2,1)S(1)}, u32[]{:S(2)}, u32[]{:S(2)}) %collective-permute-start.5) | collective-permute-done | bytes 835616 | tf_op jit(solution)/shard_map/ppermute | solution.py:269
  42.1 1.9 %copy-done.1 = bf16[1,4096,384]{2,1,0:T(8,128)(2,1)S(1)} copy-done((bf16[1,4096,384]{2,1,0:T(8,128)(2,1)S(1)}, bf16[1,4096,384]{2,1,0:T(8,128)(2,1)}, u32[]{:S(2)}) %copy-start.1) | copy-done | bytes 3145752
  44.0 1.9 %copy-done.3 = bf16[1,4096,384]{2,1,0:T(8,128)(2,1)S(1)} copy-done((bf16[1,4096,384]{2,1,0:T(8,128)(2,1)S(1)}, bf16[1,4096,384]{2,1,0:T(8,128)(2,1)}, u32[]{:S(2)}) %copy-start.3) | copy-done | bytes 3145752
  45.9 1.8 %expert_partial.1 = (f32[384,384]{1,0:T(8,128)S(1)}, f32[384,384]{1,0:T(8,128)S(1)}) custom-call(s32[1]{0:T(128)} %bitcast.1.core_ref, bf16[192,2176]{1,0:T(8,128)(2,1)S(1)} %pad_maximum_fusion.sr_ref, bf16[192,2176]{1,0:T(8,128)(2,1)S(1)} %collective-permute-done.5.r2_ref, bf16[1,4096,384]{2,1,0:T(8,128)(2,1)S(1)} %copy-done.1, ...), custom_call_target="tpu_custom_call" | custom-call | flops 1207959552 | bytes 5898240 | tf_op jit(solution)/shard_map/expert_partial/pallas_call | solution.py:184
  47.8 1.8 %expert_hidden.1.own_ref = bf16[384,384]{1,0:T(8,128)(2,1)S(1)} custom-call(s32[1]{0:T(128)} %bitcast.1.core_ref, bf16[192,2176]{1,0:T(8,128)(2,1)S(1)} %collective-permute-done.4.sr_ref, bf16[192,2176]{1,0:T(8,128)(2,1)S(1)} %collective-permute-done.6.r2_ref, bf16[1,4096,384]{2,1,0:T(8,128)(2,1)S(1)} %copy-done.2, bf16[1,4096,384]{2,1,0:T(8,128)(2,1)S(1)} %copy-done.3, ...), custom_call_target="tpu_custom_call" | custom-call | flops 1207959552 | bytes 5898240 | tf_op jit(solution)/shard_map/expert_hidden/pallas_call | solution.py:184
  50.3 1.1 %collective-permute-done.7.other_ref = bf16[384,384]{1,0:T(8,128)(2,1)S(1)} collective-permute-done((bf16[384,384]{1,0:T(8,128)(2,1)S(1)}, bf16[384,384]{1,0:T(8,128)(2,1)S(1)}, u32[]{:S(2)}, u32[]{:S(2)}) %collective-permute-start.7) | collective-permute-done | bytes 294944 | tf_op jit(solution)/shard_map/ppermute | solution.py:269
  51.4 1.5 %expert_back_send.1 = bf16[192,2048]{1,0:T(8,128)(2,1)S(1)} custom-call(s32[2]{0:T(128)S(1)} %pad_add_fusion.at_ref, bf16[384,384]{1,0:T(8,128)(2,1)S(1)} %expert_hidden.1.own_ref, bf16[384,384]{1,0:T(8,128)(2,1)S(1)} %collective-permute-done.7.other_ref, bf16[192,2176]{1,0:T(8,128)(2,1)S(1)} %pad_maximum_fusion.sr_ref, ...), custom_call_target="tpu_custom_call" | custom-call | flops 603979776 | bytes 5308416 | tf_op jit(solution)/shard_map/expert_back_send/pallas_call | solution.py:243
  52.9 1.3 %collective-permute-start.8 = (bf16[192,2048]{1,0:T(8,128)(2,1)S(1)}, bf16[192,2048]{1,0:T(8,128)(2,1)S(1)}, u32[]{:S(2)}, u32[]{:S(2)}) collective-permute-start(bf16[192,2048]{1,0:T(8,128)(2,1)S(1)} %expert_back_send.1), channel_id=1, source_target_pairs={{0,2},{1,5},{2,0},{3,7},{4,6},{5,1},{6,4},{7,3},{8,10},{9,13},{10,... | collective-permute-start | bytes 2359304 | tf_op jit(solution)/shard_map/ppermute | solution.py:269
  54.3 1.9 %attention.1 = bf16[8,3,32,128]{3,2,1,0:T(8,128)(2,1)} custom-call(s32[1]{0:T(128)} %bitcast.me_ref, s32[16,16]{1,0:T(8,128)S(1)} %reshape.38.owner_ref, s32[16,16]{1,0:T(8,128)S(1)} %reshape.39.slot_ref, s32[16,16]{1,0:T(8,128)S(1)} %reshape.40.fill_ref, bf16[8,3,32,128]{3,2,1,0:T(8,128)(2,1)S(1)} %copy-done.4, ...), custom_call_target="tpu_custom_call" | custom-call | tf_op jit(solution)/shard_map/attention/pallas_call | solution.py:349
  56.2 1.5 %expert_back_keep.1 = f32[192,2048]{1,0:T(8,128)S(1)} custom-call(s32[2]{0:T(128)S(1)} %pad_add_fusion.at_ref, bf16[384,384]{1,0:T(8,128)(2,1)S(1)} %expert_hidden.1.own_ref, bf16[384,384]{1,0:T(8,128)(2,1)S(1)} %collective-permute-done.7.other_ref, bf16[192,2176]{1,0:T(8,128)(2,1)S(1)} %pad_maximum_fusion.sr_ref, ...), custom_call_target="tpu_custom_call" | custom-call | flops 603979776 | bytes 5308416 | tf_op jit(solution)/shard_map/expert_back_keep/pallas_call | solution.py:243
  57.7 7.3 %collective-permute-done.8 = bf16[192,2048]{1,0:T(8,128)(2,1)S(1)} collective-permute-done((bf16[192,2048]{1,0:T(8,128)(2,1)S(1)}, bf16[192,2048]{1,0:T(8,128)(2,1)S(1)}, u32[]{:S(2)}, u32[]{:S(2)}) %collective-permute-start.8) | collective-permute-done | bytes 786464 | tf_op jit(solution)/shard_map/ppermute | solution.py:269
  65.2 1.1 %collective-permute-start.9 = (bf16[96,2048]{1,0:T(8,128)(2,1)S(1)}, bf16[96,2048]{1,0:T(8,128)(2,1)S(1)}, u32[]{:S(2)}, u32[]{:S(2)}) collective-permute-start(bf16[96,2048]{1,0:T(8,128)(2,1)S(1)} %slice.44), channel_id=1, source_target_pairs={{0,4},{1,3},{2,6},{3,1},{4,0},{5,7},{6,2},{7,5},{8,12},{9,11},{10,... | collective-permute-start | bytes 1179656 | tf_op jit(solution)/shard_map/ppermute | solution.py:269
  66.3 6.8 %collective-permute-done.9 = bf16[96,2048]{1,0:T(8,128)(2,1)S(1)} collective-permute-done((bf16[96,2048]{1,0:T(8,128)(2,1)S(1)}, bf16[96,2048]{1,0:T(8,128)(2,1)S(1)}, u32[]{:S(2)}, u32[]{:S(2)}) %collective-permute-start.9) | collective-permute-done | bytes 393248 | tf_op jit(solution)/shard_map/ppermute | solution.py:269
  73.2 1.6 %collective-permute-start.10 = (bf16[24,2048]{1,0:T(8,128)(2,1)S(1)}, bf16[24,2048]{1,0:T(8,128)(2,1)S(1)}, u32[]{:S(2)}, u32[]{:S(2)}) collective-permute-start(bf16[24,2048]{1,0:T(8,128)(2,1)S(1)} %get-tuple-element.30), channel_id=1, source_target_pairs={{0,8},{1,9},{2,10},{3,11},{4,12},{5,13},{6,14},{7,15},{8,16},{9,17... | collective-permute-start | bytes 294920 | tf_op jit(solution)/shard_map/ppermute | solution.py:269
  74.9 2.2 %collective-permute-start.12 = (bf16[24,2048]{1,0:T(8,128)(2,1)S(1)}, bf16[24,2048]{1,0:T(8,128)(2,1)S(1)}, u32[]{:S(2)}, u32[]{:S(2)}) collective-permute-start(bf16[24,2048]{1,0:T(8,128)(2,1)S(1)} %get-tuple-element.31), channel_id=1, source_target_pairs={{0,24},{1,25},{2,26},{3,27},{4,28},{5,29},{6,30},{7,31},{8,0},{9,1... | collective-permute-start | bytes 294920 | tf_op jit(solution)/shard_map/ppermute | solution.py:269
  77.1 0.7 collective-permute-start.11
  77.8 2.8 %collective-permute-done.10 = bf16[24,2048]{1,0:T(8,128)(2,1)S(1)} collective-permute-done((bf16[24,2048]{1,0:T(8,128)(2,1)S(1)}, bf16[24,2048]{1,0:T(8,128)(2,1)S(1)}, u32[]{:S(2)}, u32[]{:S(2)}) %collective-permute-start.10) | collective-permute-done | bytes 98336 | tf_op jit(solution)/shard_map/ppermute | solution.py:269
  80.6 4.1 %collective-permute-done.11 = bf16[24,2048]{1,0:T(8,128)(2,1)S(1)} collective-permute-done((bf16[24,2048]{1,0:T(8,128)(2,1)S(1)}, bf16[24,2048]{1,0:T(8,128)(2,1)S(1)}, u32[]{:S(2)}, u32[]{:S(2)}) %collective-permute-start.11) | collective-permute-done | bytes 98336 | tf_op jit(solution)/shard_map/ppermute | solution.py:269
  84.8 0.7 fusion.3
  (39 shorter events, 2.6 us)
Async XLA Ops:
  0.6 17.6 %copy-start.6 = (s32[256,1]{0,1:T(1,128)S(1)}, s32[256,1]{0,1:T(1,128)}, u32[]{:S(2)}) copy-start(s32[256,1]{0,1:T(1,128)} %param.13) | copy-start | bytes 3076
  0.6 18.3 %copy-start.8 = (s32[256]{0:T(256)S(1)}, s32[256]{0:T(256)}, u32[]{:S(2)}) copy-start(s32[256]{0:T(256)} %param.14) | copy-start | bytes 3076
  0.7 18.4 %copy-start.9 = (s32[256]{0:T(256)S(1)}, s32[256]{0:T(256)}, u32[]{:S(2)}) copy-start(s32[256]{0:T(256)} %param.15) | copy-start | bytes 3076
  0.7 18.5 %copy-start.7 = (bf16[8,3,2,2,128]{4,3,2,1,0:T(2,128)(2,1)S(1)}, bf16[8,3,2,2,128]{4,3,2,1,0:T(2,128)(2,1)}, u32[]{:S(2)}) copy-start(bf16[8,3,2,2,128]{4,3,2,1,0:T(2,128)(2,1)} %param.17) | copy-start | bytes 73732
  2.4 11.3 %collective-permute-start.2 = (bf16[24,2176]{1,0:T(8,128)(2,1)}, bf16[24,2176]{1,0:T(8,128)(2,1)S(1)}, u32[]{:S(2)}, u32[]{:S(2)}) collective-permute-start(bf16[24,2176]{1,0:T(8,128)(2,1)} %pack_tokens.1), channel_id=1, source_target_pairs={{0,8},{1,9},{2,10},{3,11},{4,12},{5,13},{6,14},{7,15},{8,16},{9,17... | collective-permute-start | bytes 313352 | tf_op jit(solution)/shard_map/ppermute | solution.py:269
  5.4 9.8 %collective-permute-start.1 = (bf16[24,2176]{1,0:T(8,128)(2,1)}, bf16[24,2176]{1,0:T(8,128)(2,1)S(1)}, u32[]{:S(2)}, u32[]{:S(2)}) collective-permute-start(bf16[24,2176]{1,0:T(8,128)(2,1)} %pack_tokens.1), channel_id=1, source_target_pairs={{0,16},{1,17},{2,18},{3,19},{4,20},{5,21},{6,22},{7,23},{8,24},{9,... | collective-permute-start | bytes 313352 | tf_op jit(solution)/shard_map/ppermute | solution.py:269
  8.0 7.2 %collective-permute-start = (bf16[24,2176]{1,0:T(8,128)(2,1)}, bf16[24,2176]{1,0:T(8,128)(2,1)S(1)}, u32[]{:S(2)}, u32[]{:S(2)}) collective-permute-start(bf16[24,2176]{1,0:T(8,128)(2,1)} %pack_tokens.1), channel_id=1, source_target_pairs={{0,24},{1,25},{2,26},{3,27},{4,28},{5,29},{6,30},{7,31},{8,0},{9,1... | collective-permute-start | bytes 313352 | tf_op jit(solution)/shard_map/ppermute | solution.py:269
  10.4 0.7 copy-start.5
  16.2 9.1 %collective-permute-start.3 = (bf16[96,2176]{1,0:T(8,128)(2,1)S(1)}, bf16[96,2176]{1,0:T(8,128)(2,1)S(1)}, u32[]{:S(2)}, u32[]{:S(2)}) collective-permute-start(bf16[96,2176]{1,0:T(8,128)(2,1)S(1)} %pad_maximum_fusion.1), channel_id=1, source_target_pairs={{0,2},{1,5},{2,0},{3,7},{4,6},{5,1},{6,4},{7,3},{8,10},{9,13},{10,... | collective-permute-start | bytes 1253384 | tf_op jit(solution)/shard_map/ppermute | solution.py:269
  19.2 20.3 %all-to-all-start = ((bf16[32,2,2,16,128]{4,3,2,1,0:T(8,128)(2,1)}), bf16[32,2,2,16,128]{4,3,2,1,0:T(8,128)(2,1)S(1)}, u32[]{:S(2)}, u32[]{:S(2)}) async-start(bf16[32,2,2,16,128]{4,3,2,1,0:T(8,128)(2,1)} %quantize_pages.1), calls=%async_computation | async-start | bytes 1048576 | tf_op jit(solution)/shard_map/all_to_all | solution.py:340
  25.4 16.7 %collective-permute-start.5 = (bf16[192,2176]{1,0:T(8,128)(2,1)S(1)}, bf16[192,2176]{1,0:T(8,128)(2,1)S(1)}, u32[]{:S(2)}, u32[]{:S(2)}) collective-permute-start(bf16[192,2176]{1,0:T(8,128)(2,1)S(1)} %pad_maximum_fusion.sr_ref), channel_id=1, source_target_pairs={{0,4},{1,3},{2,6},{3,1},{4,0},{5,7},{6,2},{7,5},{8,12},{9,11},{10,... | collective-permute-start | bytes 2506760 | tf_op jit(solution)/shard_map/ppermute | solution.py:269
  27.3 20.3 %collective-permute-start.4 = (bf16[192,2176]{1,0:T(8,128)(2,1)S(1)}, bf16[192,2176]{1,0:T(8,128)(2,1)S(1)}, u32[]{:S(2)}, u32[]{:S(2)}) collective-permute-start(bf16[192,2176]{1,0:T(8,128)(2,1)S(1)} %pad_maximum_fusion.sr_ref), channel_id=1, source_target_pairs={{0,1},{1,0},{2,3},{3,2},{4,5},{5,4},{6,7},{7,6},{8,9},{9,8},{10,11... | collective-permute-start | bytes 2506760 | tf_op jit(solution)/shard_map/ppermute | solution.py:269
  42.1 5.6 %collective-permute-start.6 = (bf16[192,2176]{1,0:T(8,128)(2,1)S(1)}, bf16[192,2176]{1,0:T(8,128)(2,1)S(1)}, u32[]{:S(2)}, u32[]{:S(2)}) collective-permute-start(bf16[192,2176]{1,0:T(8,128)(2,1)S(1)} %collective-permute-done.5.r2_ref), channel_id=1, source_target_pairs={{0,1},{1,0},{2,3},{3,2},{4,5},{5,4},{6,7},{7,6},{8,9},{9,8},{10,11... | collective-permute-start | bytes 2506760 | tf_op jit(solution)/shard_map/ppermute | solution.py:269
  42.1 1.9 %copy-start.1 = (bf16[1,4096,384]{2,1,0:T(8,128)(2,1)S(1)}, bf16[1,4096,384]{2,1,0:T(8,128)(2,1)}, u32[]{:S(2)}) copy-start(bf16[1,4096,384]{2,1,0:T(8,128)(2,1)} %gate_ref.3) | copy-start | bytes 9437188
  44.0 1.9 %copy-start.3 = (bf16[1,4096,384]{2,1,0:T(8,128)(2,1)S(1)}, bf16[1,4096,384]{2,1,0:T(8,128)(2,1)}, u32[]{:S(2)}) copy-start(bf16[1,4096,384]{2,1,0:T(8,128)(2,1)} %up_ref.3) | copy-start | bytes 9437188
  45.9 1.9 %copy-start.2 = (bf16[1,4096,384]{2,1,0:T(8,128)(2,1)S(1)}, bf16[1,4096,384]{2,1,0:T(8,128)(2,1)}, u32[]{:S(2)}) copy-start(bf16[1,4096,384]{2,1,0:T(8,128)(2,1)} %gate_ref.3) | copy-start | bytes 9437188
  47.8 3.6 %copy-start = (bf16[1,768,2048]{2,1,0:T(8,128)(2,1)S(1)}, bf16[1,768,2048]{2,1,0:T(8,128)(2,1)}, u32[]{:S(2)}) copy-start(bf16[1,768,2048]{2,1,0:T(8,128)(2,1)} %down_ref.3) | copy-start | bytes 9437188
  49.6 1.8 %collective-permute-start.7 = (bf16[384,384]{1,0:T(8,128)(2,1)S(1)}, bf16[384,384]{1,0:T(8,128)(2,1)S(1)}, u32[]{:S(2)}, u32[]{:S(2)}) collective-permute-start(bf16[384,384]{1,0:T(8,128)(2,1)S(1)} %expert_hidden.1.own_ref), channel_id=1, source_target_pairs={{0,1},{1,0},{2,3},{3,2},{4,5},{5,4},{6,7},{7,6},{8,9},{9,8},{10,11... | collective-permute-start | bytes 884744 | tf_op jit(solution)/shard_map/ppermute | solution.py:269
  50.3 4.0 %copy-start.4 = (bf16[8,3,32,128]{3,2,1,0:T(8,128)(2,1)S(1)}, bf16[8,3,32,128]{3,2,1,0:T(8,128)(2,1)}, u32[]{:S(2)}) copy-start(bf16[8,3,32,128]{3,2,1,0:T(8,128)(2,1)} %q_ref.1) | copy-start | bytes 589828
  52.9 12.1 %collective-permute-start.8 = (bf16[192,2048]{1,0:T(8,128)(2,1)S(1)}, bf16[192,2048]{1,0:T(8,128)(2,1)S(1)}, u32[]{:S(2)}, u32[]{:S(2)}) collective-permute-start(bf16[192,2048]{1,0:T(8,128)(2,1)S(1)} %expert_back_send.1), channel_id=1, source_target_pairs={{0,2},{1,5},{2,0},{3,7},{4,6},{5,1},{6,4},{7,3},{8,10},{9,13},{10,... | collective-permute-start | bytes 2359304 | tf_op jit(solution)/shard_map/ppermute | solution.py:269
  65.2 7.8 %collective-permute-start.9 = (bf16[96,2048]{1,0:T(8,128)(2,1)S(1)}, bf16[96,2048]{1,0:T(8,128)(2,1)S(1)}, u32[]{:S(2)}, u32[]{:S(2)}) collective-permute-start(bf16[96,2048]{1,0:T(8,128)(2,1)S(1)} %slice.44), channel_id=1, source_target_pairs={{0,4},{1,3},{2,6},{3,1},{4,0},{5,7},{6,2},{7,5},{8,12},{9,11},{10,... | collective-permute-start | bytes 1179656 | tf_op jit(solution)/shard_map/ppermute | solution.py:269
  73.2 7.4 %collective-permute-start.10 = (bf16[24,2048]{1,0:T(8,128)(2,1)S(1)}, bf16[24,2048]{1,0:T(8,128)(2,1)S(1)}, u32[]{:S(2)}, u32[]{:S(2)}) collective-permute-start(bf16[24,2048]{1,0:T(8,128)(2,1)S(1)} %get-tuple-element.30), channel_id=1, source_target_pairs={{0,8},{1,9},{2,10},{3,11},{4,12},{5,13},{6,14},{7,15},{8,16},{9,17... | collective-permute-start | bytes 294920 | tf_op jit(solution)/shard_map/ppermute | solution.py:269
  74.9 5.8 %collective-permute-start.12 = (bf16[24,2048]{1,0:T(8,128)(2,1)S(1)}, bf16[24,2048]{1,0:T(8,128)(2,1)S(1)}, u32[]{:S(2)}, u32[]{:S(2)}) collective-permute-start(bf16[24,2048]{1,0:T(8,128)(2,1)S(1)} %get-tuple-element.31), channel_id=1, source_target_pairs={{0,24},{1,25},{2,26},{3,27},{4,28},{5,29},{6,30},{7,31},{8,0},{9,1... | collective-permute-start | bytes 294920 | tf_op jit(solution)/shard_map/ppermute | solution.py:269
  77.1 7.6 %collective-permute-start.11 = (bf16[24,2048]{1,0:T(8,128)(2,1)S(1)}, bf16[24,2048]{1,0:T(8,128)(2,1)S(1)}, u32[]{:S(2)}, u32[]{:S(2)}) collective-permute-start(bf16[24,2048]{1,0:T(8,128)(2,1)S(1)} %get-tuple-element.32), channel_id=1, source_target_pairs={{0,16},{1,17},{2,18},{3,19},{4,20},{5,21},{6,22},{7,23},{8,24},{9,... | collective-permute-start | bytes 294920 | tf_op jit(solution)/shard_map/ppermute | solution.py:269

commit v13 on v12

--- a/solution.py
+++ b/solution.py
@@ -139,33 +139,31 @@
     out_ref[:, half:] = jnp.where(part < 3, chosen, 0.0).astype(out_ref.dtype)
 
 
-def partial_kernel(chunks, core_ref, sr_ref, r2_ref, gate_ref, up_ref, gate_sum, up_sum):
-    half = gate_ref.shape[1] // 2
+def partial_kernel(chunks, sr_ref, r2_ref, gate_ref, up_ref, gate_sum, up_sum):
+    half = gate_ref.shape[0]
     depth = half // chunks
     for c in range(chunks):
         at = slice(c * depth, (c + 1) * depth)
-        rows = pl.ds(pl.multiple_of(core_ref[0] * half + c * depth, 128), depth)
         x = jnp.concatenate([sr_ref[:, at], r2_ref[:, at]], axis=0)
         for weight, total in ((gate_ref, gate_sum), (up_ref, up_sum)):
-            part = jnp.dot(x, weight[0, rows], preferred_element_type=jnp.float32)
+            part = jnp.dot(x, weight[at], preferred_element_type=jnp.float32)
             total[...] = part if c == 0 else total[...] + part
 
 
 def hidden_kernel(
-    chunks, core_ref, sr_ref, r2_ref, gate_ref, up_ref, gate_part, up_part, out_ref, sums
+    chunks, sr_ref, r2_ref, gate_ref, up_ref, gate_part, up_part, out_ref, sums
 ):
-    half = gate_ref.shape[1] // 2
+    half = gate_ref.shape[0]
     depth = half // chunks
     group = sr_ref.shape[0] // 2
     for c in range(chunks):
         at = slice(c * depth, (c + 1) * depth)
-        rows = pl.ds(pl.multiple_of((1 - core_ref[0]) * half + c * depth, 128), depth)
         x = jnp.concatenate(
             [sr_ref[:group, at], r2_ref[:group, at], sr_ref[group:, at], r2_ref[group:, at]],
             axis=0,
         )
         for i, (weight, start) in enumerate(((gate_ref, gate_part), (up_ref, up_part))):
-            part = jnp.dot(x, weight[0, rows], preferred_element_type=jnp.float32)
+            part = jnp.dot(x, weight[at], preferred_element_type=jnp.float32)
             sums[i] = (start[...] if c == 0 else sums[i]) + part
     gate = sums[0]
     out_ref[...] = (gate / (1.0 + jnp.exp(-gate)) * sums[1]).astype(out_ref.dtype)
@@ -175,15 +173,15 @@
     return sum(math.prod(a.shape) * a.dtype.itemsize for a in arrays) * 9 // 8 + 4 * MIB
 
 
-def expert_front(core, rows, w_gate, w_up, parts):
+def expert_front(rows, w_gate, w_up, parts):
     tokens = 2 * rows[0].shape[0]
-    d, f = w_gate.shape[1:]
+    half, f = w_gate.shape
     last = parts is not None
     total = jax.ShapeDtypeStruct((tokens, f), jnp.float32)
     scratch = [pltpu.VMEM((2, tokens, f), jnp.float32)] if last else []
     return pl.pallas_call(
         functools.partial(hidden_kernel if last else partial_kernel, 4),
-        in_specs=[smem()] + [vmem()] * (6 if last else 4),
+        in_specs=[vmem()] * (6 if last else 4),
         out_specs=vmem() if last else [vmem(), vmem()],
         scratch_shapes=scratch,
         out_shape=jax.ShapeDtypeStruct((tokens, f), jnp.bfloat16) if last else [total, total],
@@ -191,12 +189,12 @@
             vmem_limit_bytes=room(*rows, w_gate, w_up, *[total] * (5 if last else 2))
         ),
         cost_estimate=pl.CostEstimate(
-            flops=2 * tokens * d * f,
-            bytes_accessed=tokens * d + 2 * d * f + 8 * tokens * f,
+            flops=4 * tokens * half * f,
+            bytes_accessed=2 * tokens * half + 4 * half * f + 8 * tokens * f,
             transcendentals=tokens * f if last else 0,
         ),
         name="expert_hidden" if last else "expert_partial",
-    )(core, *rows, w_gate, w_up, *(parts or ()))
+    )(*rows, w_gate, w_up, *(parts or ()))
 
 
 def back_kernel(
@@ -338,11 +336,19 @@
     sr, fresh, tables = lax.optimization_barrier((sr, fresh, tables))
     r2 = moves.flip(sr, 1)
     cache = lax.all_to_all(send, "ep", split_axis=0, concat_axis=0, tiled=True)
-    r2, cache = lax.optimization_barrier((r2, cache))
+    core_then, cache = lax.optimization_barrier((core, cache))
+
+    def weights_of(half):
+        return [
+            lax.dynamic_slice_in_dim(w[0], half * (d // 2), d // 2, axis=0) for w in (w_gate, w_up)
+        ]
+
+    near_weights = weights_of(core_then)
+    r2, near_weights = lax.optimization_barrier((r2, near_weights))
     other_sr, other_r2 = moves.cores(sr), moves.cores(r2)
 
-    parts = expert_front(own_core, (sr, r2), w_gate, w_up, None)
-    hidden = expert_front(own_core, (other_sr, other_r2), w_gate, w_up, parts)
+    parts = expert_front((sr, r2), *near_weights, None)
+    hidden = expert_front((other_sr, other_r2), *weights_of(1 - core_then), parts)
     other_hidden = moves.cores(hidden)
     sent = expert_back(True, owners, at, hidden, other_hidden, w_down, sr, r2, lanes)
     kept = expert_back(False, owners, at, hidden, other_hidden, w_down, sr, r2, lanes)

time: 85.9 us -> 80.6 us (0.938)
  starting transfers between devices: 24.1 us -> 21.1 us
  waiting for transfers between devices: 38.4 us -> 36.6 us
    unnamed x22 -> x16, local copies, waits for them, and re-layouts: 6.05 us -> 2.25 us
    dynamic_slice x0 -> x1, local copies, waits for them, and re-layouts: none -> 3.46 us  [weights_of(): lax.dynamic_slice_in_dim(w[0], half * (d // 2), d // 2, axis=0)]
    all_to_all x1, waiting for transfers between devices: 12.1 us -> 10.4 us  [body(): cache = lax.all_to_all(send, 'ep', split_axis=0, concat_axis=0, tiled=True)]
    ppermute x13, starting transfers between devices: 18.1 us -> 16.4 us  [go(): return lax.ppermute(x, ('ep', 'pd'), perm)]
    all_to_all x1, starting transfers between devices: 6.07 us -> 4.68 us  [body(): cache = lax.all_to_all(send, 'ep', split_axis=0, concat_axis=0, tiled=True)]
  transfers between devices with their start and end apart: 14 -> 14, of which waited for: 8 -> 9; matrix products, arithmetic and copies ran while one was open for 3% -> 8% of each run, Pallas kernels for 9% -> 10%
where the time goes in v13:
time: 80.6 us; the launch traced here: 80.2 us
  waiting for transfers between devices  36.6 us (45%)
  starting transfers between devices  21.1 us (26%)
  Pallas kernels  13 us (16%)
  local copies, waits for them, and re-layouts  6.05 us (8%)
  other arithmetic  2.71 us (3%)
    ppermute x13, waiting for transfers between devices, go(): return lax.ppermute(x, ('ep', 'pd'), perm)  26.2 us
    ppermute x13, starting transfers between devices, go(): return lax.ppermute(x, ('ep', 'pd'), perm)  16.4 us
    all_to_all x1, waiting for transfers between devices, body(): cache = lax.all_to_all(send, 'ep', split_axis=0, concat_axis=0, tiled=True)  10.4 us
    all_to_all x1, starting transfers between devices, body(): cache = lax.all_to_all(send, 'ep', split_axis=0, concat_axis=0, tiled=True)  4.68 us
    pallas_call x2, Pallas kernels, expert_front(): pl.pallas_call(functools.partial(hidden_kernel if last else partial_kerne...  3.62 us
    dynamic_slice x1, local copies, waits for them, and re-layouts, weights_of(): lax.dynamic_slice_in_dim(w[0], half * (d // 2), d // 2, axis=0)  3.46 us
    pallas_call x2, Pallas kernels, expert_back(): pl.pallas_call(functools.partial(back_kernel, send, experts, lanes, 4), o...  3.05 us
    pallas_call x1, Pallas kernels, body(): pl.pallas_call(functools.partial(page_kernel, pages), out_shape=jax.Shape...  2.66 us
  transfers between devices with their start and end apart: 14, of which 9 were waited for; matrix products, arithmetic and copies ran while one was open for 8% of the time, Pallas kernels for 10%

profile of v13, /device:TPU:0, one launch (start us, length us, event | category | flops | bytes accessed | tf_op | source)
XLA Modules:
  0.0 80.2 jit_solution(13517603038958265231)
XLA Ops:
  0.6 1.7 %pack_tokens.1 = bf16[24,2176]{1,0:T(8,128)(2,1)} custom-call(s32[1]{0:T(128)} %bitcast.1.core_ref, bf16[24,4096]{1,0:T(8,128)(2,1)} %bitcast.31, s32[24,8]{1,0:T(8,128)} %bitcast.33, f32[24,8]{1,0:T(8,128)} %bitcast.34), custom_call_target="tpu_custom_call" | custom-call | tf_op jit(solution)/shard_map/pack_tokens/pallas_call | solution.py:308
  2.4 5.0 %collective-permute-start = (bf16[24,2176]{1,0:T(8,128)(2,1)}, bf16[24,2176]{1,0:T(8,128)(2,1)S(1)}, u32[]{:S(2)}, u32[]{:S(2)}) collective-permute-start(bf16[24,2176]{1,0:T(8,128)(2,1)} %pack_tokens.1), channel_id=1, source_target_pairs={{0,24},{1,25},{2,26},{3,27},{4,28},{5,29},{6,30},{7,31},{8,0},{9,1... | collective-permute-start | bytes 313352 | tf_op jit(solution)/shard_map/ppermute | solution.py:267
  7.4 1.0 %collective-permute-start.2 = (bf16[24,2176]{1,0:T(8,128)(2,1)}, bf16[24,2176]{1,0:T(8,128)(2,1)S(1)}, u32[]{:S(2)}, u32[]{:S(2)}) collective-permute-start(bf16[24,2176]{1,0:T(8,128)(2,1)} %pack_tokens.1), channel_id=1, source_target_pairs={{0,8},{1,9},{2,10},{3,11},{4,12},{5,13},{6,14},{7,15},{8,16},{9,17... | collective-permute-start | bytes 313352 | tf_op jit(solution)/shard_map/ppermute | solution.py:267
  8.4 1.0 %copy.22 = bf16[16,2,16,2,128]{4,2,3,1,0:T(8,128)(2,1)S(1)} copy(bf16[16,2,16,2,128]{4,3,2,1,0:T(2,128)(2,1)} %param.12) | data formatting | bytes 524288 | tf_op args[0]
  9.5 0.7 copy-done.2
  10.2 2.7 %quantize_pages.1 = bf16[32,2,2,16,128]{4,3,2,1,0:T(8,128)(2,1)} custom-call(s32[1]{0:T(128)} %bitcast.me_ref, s32[256]{0:T(256)S(1)} %bitcast.30, bf16[16,2,2,16,128]{4,3,2,1,0:T(8,128)(2,1)S(1)} %bitcast.29), custom_call_target="tpu_custom_call" | custom-call | tf_op jit(solution)/shard_map/quantize_pages/pallas_call | solution.py:320
  12.8 4.0 %collective-permute-done.1 = bf16[24,2176]{1,0:T(8,128)(2,1)S(1)} collective-permute-done((bf16[24,2176]{1,0:T(8,128)(2,1)}, bf16[24,2176]{1,0:T(8,128)(2,1)S(1)}, u32[]{:S(2)}, u32[]{:S(2)}) %collective-permute-start.1) | collective-permute-done | bytes 104480 | tf_op jit(solution)/shard_map/ppermute | solution.py:267
  16.8 0.9 %pad_maximum_fusion.1 = bf16[96,2176]{1,0:T(8,128)(2,1)S(1)} fusion(bf16[24,2176]{1,0:T(8,128)(2,1)S(1)} %collective-permute-done.2, bf16[24,2176]{1,0:T(8,128)(2,1)S(1)} %collective-permute-done.1, bf16[24,2176]{1,0:T(8,128)(2,1)S(1)} %collective-permute-done, bf16[24,2176]{1,0:T(8,128)(2,1)} %pack_tokens.1), kind=kLoop, calls=%fused_computation.8 | loop fusion | flops 1671168 | bytes 835584 | tf_op jit(solution)/shard_map/concatenate | solution.py:330
  17.8 1.6 %collective-permute-start.3 = (bf16[96,2176]{1,0:T(8,128)(2,1)S(1)}, bf16[96,2176]{1,0:T(8,128)(2,1)S(1)}, u32[]{:S(2)}, u32[]{:S(2)}) collective-permute-start(bf16[96,2176]{1,0:T(8,128)(2,1)S(1)} %pad_maximum_fusion.1), channel_id=1, source_target_pairs={{0,2},{1,5},{2,0},{3,7},{4,6},{5,1},{6,4},{7,3},{8,10},{9,13},{10,... | collective-permute-start | bytes 1253384 | tf_op jit(solution)/shard_map/ppermute | solution.py:267
  19.3 4.7 %all-to-all-start = ((bf16[32,2,2,16,128]{4,3,2,1,0:T(8,128)(2,1)}), bf16[32,2,2,16,128]{4,3,2,1,0:T(8,128)(2,1)S(1)}, u32[]{:S(2)}, u32[]{:S(2)}) async-start(bf16[32,2,2,16,128]{4,3,2,1,0:T(8,128)(2,1)} %quantize_pages.1), calls=%async_computation | async-start | bytes 1048576 | tf_op jit(solution)/shard_map/all_to_all | solution.py:338
  24.5 0.7 reduce.3
  25.5 0.8 %collective-permute-done.3 = bf16[96,2176]{1,0:T(8,128)(2,1)S(1)} collective-permute-done((bf16[96,2176]{1,0:T(8,128)(2,1)S(1)}, bf16[96,2176]{1,0:T(8,128)(2,1)S(1)}, u32[]{:S(2)}, u32[]{:S(2)}) %collective-permute-start.3) | collective-permute-done | bytes 417824 | tf_op jit(solution)/shard_map/ppermute | solution.py:267
  26.4 1.6 %collective-permute-start.5 = (bf16[192,2176]{1,0:T(8,128)(2,1)S(1)}, bf16[192,2176]{1,0:T(8,128)(2,1)S(1)}, u32[]{:S(2)}, u32[]{:S(2)}) collective-permute-start(bf16[192,2176]{1,0:T(8,128)(2,1)S(1)} %pad_maximum_fusion.sr_ref), channel_id=1, source_target_pairs={{0,4},{1,3},{2,6},{3,1},{4,0},{5,7},{6,2},{7,5},{8,12},{9,11},{10,... | collective-permute-start | bytes 2506760 | tf_op jit(solution)/shard_map/ppermute | solution.py:267
  28.0 10.4 %all-to-all-done.cache_ref = bf16[32,2,2,16,128]{4,3,2,1,0:T(8,128)(2,1)S(1)} async-done(((bf16[32,2,2,16,128]{4,3,2,1,0:T(8,128)(2,1)}), bf16[32,2,2,16,128]{4,3,2,1,0:T(8,128)(2,1)S(1)}, u32[]{:S(2)}, u32[]{:S(2)}) %all-to-all-start) | async-done | bytes 524320 | tf_op jit(solution)/shard_map/all_to_all | solution.py:338
  38.4 3.5 %dynamic-slice_bitcast_fusion = (bf16[2048,384]{1,0:T(8,128)(2,1)S(1)}, bf16[2048,384]{1,0:T(8,128)(2,1)S(1)}, bf16[2048,384]{1,0:T(8,128)(2,1)S(1)}, bf16[2048,384]{1,0:T(8,128)(2,1)S(1)}) fusion(bf16[1,4096,384]{2,1,0:T(8,128)(2,1)} %param.22, s32[]{:T(128)S(6)} %select_n.9, s32[]{:T(128)S(6)} %select_n.8, bf16[1,4096,384]{2,1,0:T(8,128)(2,1)} %param.21), kind=kLoop, calls=%fused_computation.1 | loop fusion | bytes 12582920 | tf_op jit(solution)/shard_map/dynamic_slice | solution.py:343
  42.0 1.8 %expert_partial.1 = (f32[384,384]{1,0:T(8,128)S(1)}, f32[384,384]{1,0:T(8,128)S(1)}) custom-call(bf16[192,2176]{1,0:T(8,128)(2,1)S(1)} %pad_maximum_fusion.sr_ref, bf16[192,2176]{1,0:T(8,128)(2,1)S(1)} %collective-permute-done.5.r2_ref, bf16[2048,384]{1,0:T(8,128)(2,1)S(1)} %get-tuple-element.23.gate_ref, bf16[2048,384]{1,0:T(8,128)(2,1)S(1)} %get-tuple-element.24.up_ref), custom_call_target="tpu_custom_call" | custom-call | flops 1207959552 | bytes 5898240 | tf_op jit(solution)/shard_map/expert_partial/pallas_call | solution.py:182
  43.8 0.5 collective-permute-done.6.r2_ref
  44.3 1.8 %expert_hidden.1.own_ref = bf16[384,384]{1,0:T(8,128)(2,1)S(1)} custom-call(bf16[192,2176]{1,0:T(8,128)(2,1)S(1)} %collective-permute-done.4.sr_ref, bf16[192,2176]{1,0:T(8,128)(2,1)S(1)} %collective-permute-done.6.r2_ref, bf16[2048,384]{1,0:T(8,128)(2,1)S(1)} %get-tuple-element.44.gate_ref, bf16[2048,384]{1,0:T(8,128)(2,1)S(1)} %get-tuple-element.36.up_ref, ...), custom_call_target="tpu_custom_call" | custom-call | flops 1207959552 | bytes 5898240 | tf_op jit(solution)/shard_map/expert_hidden/pallas_call | solution.py:182
  46.4 1.4 %collective-permute-done.7.other_ref = bf16[384,384]{1,0:T(8,128)(2,1)S(1)} collective-permute-done((bf16[384,384]{1,0:T(8,128)(2,1)S(1)}, bf16[384,384]{1,0:T(8,128)(2,1)S(1)}, u32[]{:S(2)}, u32[]{:S(2)}) %collective-permute-start.7) | collective-permute-done | bytes 294944 | tf_op jit(solution)/shard_map/ppermute | solution.py:267
  47.8 1.5 %expert_back_send.1 = bf16[192,2048]{1,0:T(8,128)(2,1)S(1)} custom-call(s32[2]{0:T(128)S(1)} %pad_add_fusion.at_ref, bf16[384,384]{1,0:T(8,128)(2,1)S(1)} %expert_hidden.1.own_ref, bf16[384,384]{1,0:T(8,128)(2,1)S(1)} %collective-permute-done.7.other_ref, bf16[192,2176]{1,0:T(8,128)(2,1)S(1)} %pad_maximum_fusion.sr_ref, ...), custom_call_target="tpu_custom_call" | custom-call | flops 603979776 | bytes 5308416 | tf_op jit(solution)/shard_map/expert_back_send/pallas_call | solution.py:241
  49.3 0.9 %collective-permute-start.8 = (bf16[192,2048]{1,0:T(8,128)(2,1)S(1)}, bf16[192,2048]{1,0:T(8,128)(2,1)S(1)}, u32[]{:S(2)}, u32[]{:S(2)}) collective-permute-start(bf16[192,2048]{1,0:T(8,128)(2,1)S(1)} %expert_back_send.1), channel_id=1, source_target_pairs={{0,2},{1,5},{2,0},{3,7},{4,6},{5,1},{6,4},{7,3},{8,10},{9,13},{10,... | collective-permute-start | bytes 2359304 | tf_op jit(solution)/shard_map/ppermute | solution.py:267
  50.3 1.9 %attention.1 = bf16[8,3,32,128]{3,2,1,0:T(8,128)(2,1)} custom-call(s32[1]{0:T(128)} %bitcast.me_ref, s32[16,16]{1,0:T(8,128)S(1)} %reshape.42.owner_ref, s32[16,16]{1,0:T(8,128)S(1)} %reshape.43.slot_ref, s32[16,16]{1,0:T(8,128)S(1)} %reshape.44.fill_ref, bf16[8,3,32,128]{3,2,1,0:T(8,128)(2,1)S(1)} %copy-done.1, ...), custom_call_target="tpu_custom_call" | custom-call | tf_op jit(solution)/shard_map/attention/pallas_call | solution.py:355
  52.2 1.5 %expert_back_keep.1 = f32[192,2048]{1,0:T(8,128)S(1)} custom-call(s32[2]{0:T(128)S(1)} %pad_add_fusion.at_ref, bf16[384,384]{1,0:T(8,128)(2,1)S(1)} %expert_hidden.1.own_ref, bf16[384,384]{1,0:T(8,128)(2,1)S(1)} %collective-permute-done.7.other_ref, bf16[192,2176]{1,0:T(8,128)(2,1)S(1)} %pad_maximum_fusion.sr_ref, ...), custom_call_target="tpu_custom_call" | custom-call | flops 603979776 | bytes 5308416 | tf_op jit(solution)/shard_map/expert_back_keep/pallas_call | solution.py:241
  53.7 7.7 %collective-permute-done.8 = bf16[192,2048]{1,0:T(8,128)(2,1)S(1)} collective-permute-done((bf16[192,2048]{1,0:T(8,128)(2,1)S(1)}, bf16[192,2048]{1,0:T(8,128)(2,1)S(1)}, u32[]{:S(2)}, u32[]{:S(2)}) %collective-permute-start.8) | collective-permute-done | bytes 786464 | tf_op jit(solution)/shard_map/ppermute | solution.py:267
  61.6 1.1 %collective-permute-start.9 = (bf16[96,2048]{1,0:T(8,128)(2,1)S(1)}, bf16[96,2048]{1,0:T(8,128)(2,1)S(1)}, u32[]{:S(2)}, u32[]{:S(2)}) collective-permute-start(bf16[96,2048]{1,0:T(8,128)(2,1)S(1)} %slice.44), channel_id=1, source_target_pairs={{0,4},{1,3},{2,6},{3,1},{4,0},{5,7},{6,2},{7,5},{8,12},{9,11},{10,... | collective-permute-start | bytes 1179656 | tf_op jit(solution)/shard_map/ppermute | solution.py:267
  62.7 6.8 %collective-permute-done.9 = bf16[96,2048]{1,0:T(8,128)(2,1)S(1)} collective-permute-done((bf16[96,2048]{1,0:T(8,128)(2,1)S(1)}, bf16[96,2048]{1,0:T(8,128)(2,1)S(1)}, u32[]{:S(2)}, u32[]{:S(2)}) %collective-permute-start.9) | collective-permute-done | bytes 393248 | tf_op jit(solution)/shard_map/ppermute | solution.py:267
  69.6 1.3 %collective-permute-start.10 = (bf16[24,2048]{1,0:T(8,128)(2,1)S(1)}, bf16[24,2048]{1,0:T(8,128)(2,1)S(1)}, u32[]{:S(2)}, u32[]{:S(2)}) collective-permute-start(bf16[24,2048]{1,0:T(8,128)(2,1)S(1)} %get-tuple-element.40), channel_id=1, source_target_pairs={{0,8},{1,9},{2,10},{3,11},{4,12},{5,13},{6,14},{7,15},{8,16},{9,17... | collective-permute-start | bytes 294920 | tf_op jit(solution)/shard_map/ppermute | solution.py:267
  71.0 1.6 %collective-permute-start.11 = (bf16[24,2048]{1,0:T(8,128)(2,1)S(1)}, bf16[24,2048]{1,0:T(8,128)(2,1)S(1)}, u32[]{:S(2)}, u32[]{:S(2)}) collective-permute-start(bf16[24,2048]{1,0:T(8,128)(2,1)S(1)} %get-tuple-element.42), channel_id=1, source_target_pairs={{0,16},{1,17},{2,18},{3,19},{4,20},{5,21},{6,22},{7,23},{8,24},{9,... | collective-permute-start | bytes 294920 | tf_op jit(solution)/shard_map/ppermute | solution.py:267
  72.5 2.0 %collective-permute-start.12 = (bf16[24,2048]{1,0:T(8,128)(2,1)S(1)}, bf16[24,2048]{1,0:T(8,128)(2,1)S(1)}, u32[]{:S(2)}, u32[]{:S(2)}) collective-permute-start(bf16[24,2048]{1,0:T(8,128)(2,1)S(1)} %get-tuple-element.41), channel_id=1, source_target_pairs={{0,24},{1,25},{2,26},{3,27},{4,28},{5,29},{6,30},{7,31},{8,0},{9,1... | collective-permute-start | bytes 294920 | tf_op jit(solution)/shard_map/ppermute | solution.py:267
  74.6 2.3 %collective-permute-done.10 = bf16[24,2048]{1,0:T(8,128)(2,1)S(1)} collective-permute-done((bf16[24,2048]{1,0:T(8,128)(2,1)S(1)}, bf16[24,2048]{1,0:T(8,128)(2,1)S(1)}, u32[]{:S(2)}, u32[]{:S(2)}) %collective-permute-start.10) | collective-permute-done | bytes 98336 | tf_op jit(solution)/shard_map/ppermute | solution.py:267
  76.8 2.7 %collective-permute-done.11 = bf16[24,2048]{1,0:T(8,128)(2,1)S(1)} collective-permute-done((bf16[24,2048]{1,0:T(8,128)(2,1)S(1)}, bf16[24,2048]{1,0:T(8,128)(2,1)S(1)}, u32[]{:S(2)}, u32[]{:S(2)}) %collective-permute-start.11) | collective-permute-done | bytes 98336 | tf_op jit(solution)/shard_map/ppermute | solution.py:267
  79.5 0.7 fusion.3
  (34 shorter events, 1.6 us)
Async XLA Ops:
  2.4 10.5 %collective-permute-start = (bf16[24,2176]{1,0:T(8,128)(2,1)}, bf16[24,2176]{1,0:T(8,128)(2,1)S(1)}, u32[]{:S(2)}, u32[]{:S(2)}) collective-permute-start(bf16[24,2176]{1,0:T(8,128)(2,1)} %pack_tokens.1), channel_id=1, source_target_pairs={{0,24},{1,25},{2,26},{3,27},{4,28},{5,29},{6,30},{7,31},{8,0},{9,1... | collective-permute-start | bytes 313352 | tf_op jit(solution)/shard_map/ppermute | solution.py:267
  7.4 9.4 %collective-permute-start.1 = (bf16[24,2176]{1,0:T(8,128)(2,1)}, bf16[24,2176]{1,0:T(8,128)(2,1)S(1)}, u32[]{:S(2)}, u32[]{:S(2)}) collective-permute-start(bf16[24,2176]{1,0:T(8,128)(2,1)} %pack_tokens.1), channel_id=1, source_target_pairs={{0,16},{1,17},{2,18},{3,19},{4,20},{5,21},{6,22},{7,23},{8,24},{9,... | collective-permute-start | bytes 313352 | tf_op jit(solution)/shard_map/ppermute | solution.py:267
  7.4 9.4 %collective-permute-start.2 = (bf16[24,2176]{1,0:T(8,128)(2,1)}, bf16[24,2176]{1,0:T(8,128)(2,1)S(1)}, u32[]{:S(2)}, u32[]{:S(2)}) collective-permute-start(bf16[24,2176]{1,0:T(8,128)(2,1)} %pack_tokens.1), channel_id=1, source_target_pairs={{0,8},{1,9},{2,10},{3,11},{4,12},{5,13},{6,14},{7,15},{8,16},{9,17... | collective-permute-start | bytes 313352 | tf_op jit(solution)/shard_map/ppermute | solution.py:267
  8.4 15.6 %copy-start.4 = (bf16[8,3,2,2,128]{4,3,2,1,0:T(2,128)(2,1)S(1)}, bf16[8,3,2,2,128]{4,3,2,1,0:T(2,128)(2,1)}, u32[]{:S(2)}) copy-start(bf16[8,3,2,2,128]{4,3,2,1,0:T(2,128)(2,1)} %param.17) | copy-start | bytes 73732
  8.4 16.1 %copy-start.3 = (s32[256,1]{0,1:T(1,128)S(1)}, s32[256,1]{0,1:T(1,128)}, u32[]{:S(2)}) copy-start(s32[256,1]{0,1:T(1,128)} %param.13) | copy-start | bytes 3076
  8.4 16.9 %copy-start.5 = (s32[256]{0:T(256)S(1)}, s32[256]{0:T(256)}, u32[]{:S(2)}) copy-start(s32[256]{0:T(256)} %param.14) | copy-start | bytes 3076
  8.4 16.9 %copy-start.6 = (s32[256]{0:T(256)S(1)}, s32[256]{0:T(256)}, u32[]{:S(2)}) copy-start(s32[256]{0:T(256)} %param.15) | copy-start | bytes 3076
  9.5 0.7 copy-start.2
  17.8 8.5 %collective-permute-start.3 = (bf16[96,2176]{1,0:T(8,128)(2,1)S(1)}, bf16[96,2176]{1,0:T(8,128)(2,1)S(1)}, u32[]{:S(2)}, u32[]{:S(2)}) collective-permute-start(bf16[96,2176]{1,0:T(8,128)(2,1)S(1)} %pad_maximum_fusion.1), channel_id=1, source_target_pairs={{0,2},{1,5},{2,0},{3,7},{4,6},{5,1},{6,4},{7,3},{8,10},{9,13},{10,... | collective-permute-start | bytes 1253384 | tf_op jit(solution)/shard_map/ppermute | solution.py:267
  19.3 19.1 %all-to-all-start = ((bf16[32,2,2,16,128]{4,3,2,1,0:T(8,128)(2,1)}), bf16[32,2,2,16,128]{4,3,2,1,0:T(8,128)(2,1)S(1)}, u32[]{:S(2)}, u32[]{:S(2)}) async-start(bf16[32,2,2,16,128]{4,3,2,1,0:T(8,128)(2,1)} %quantize_pages.1), calls=%async_computation | async-start | bytes 1048576 | tf_op jit(solution)/shard_map/all_to_all | solution.py:338
  26.4 15.5 %collective-permute-start.5 = (bf16[192,2176]{1,0:T(8,128)(2,1)S(1)}, bf16[192,2176]{1,0:T(8,128)(2,1)S(1)}, u32[]{:S(2)}, u32[]{:S(2)}) collective-permute-start(bf16[192,2176]{1,0:T(8,128)(2,1)S(1)} %pad_maximum_fusion.sr_ref), channel_id=1, source_target_pairs={{0,4},{1,3},{2,6},{3,1},{4,0},{5,7},{6,2},{7,5},{8,12},{9,11},{10,... | collective-permute-start | bytes 2506760 | tf_op jit(solution)/shard_map/ppermute | solution.py:267
  28.0 15.8 %collective-permute-start.4 = (bf16[192,2176]{1,0:T(8,128)(2,1)S(1)}, bf16[192,2176]{1,0:T(8,128)(2,1)S(1)}, u32[]{:S(2)}, u32[]{:S(2)}) collective-permute-start(bf16[192,2176]{1,0:T(8,128)(2,1)S(1)} %pad_maximum_fusion.sr_ref), channel_id=1, source_target_pairs={{0,1},{1,0},{2,3},{3,2},{4,5},{5,4},{6,7},{7,6},{8,9},{9,8},{10,11... | collective-permute-start | bytes 2506760 | tf_op jit(solution)/shard_map/ppermute | solution.py:267
  41.9 2.4 %collective-permute-start.6 = (bf16[192,2176]{1,0:T(8,128)(2,1)S(1)}, bf16[192,2176]{1,0:T(8,128)(2,1)S(1)}, u32[]{:S(2)}, u32[]{:S(2)}) collective-permute-start(bf16[192,2176]{1,0:T(8,128)(2,1)S(1)} %collective-permute-done.5.r2_ref), channel_id=1, source_target_pairs={{0,1},{1,0},{2,3},{3,2},{4,5},{5,4},{6,7},{7,6},{8,9},{9,8},{10,11... | collective-permute-start | bytes 2506760 | tf_op jit(solution)/shard_map/ppermute | solution.py:267
  44.3 3.5 %copy-start = (bf16[1,768,2048]{2,1,0:T(8,128)(2,1)S(1)}, bf16[1,768,2048]{2,1,0:T(8,128)(2,1)}, u32[]{:S(2)}) copy-start(bf16[1,768,2048]{2,1,0:T(8,128)(2,1)} %down_ref.3) | copy-start | bytes 9437188
  46.2 1.6 %collective-permute-start.7 = (bf16[384,384]{1,0:T(8,128)(2,1)S(1)}, bf16[384,384]{1,0:T(8,128)(2,1)S(1)}, u32[]{:S(2)}, u32[]{:S(2)}) collective-permute-start(bf16[384,384]{1,0:T(8,128)(2,1)S(1)} %expert_hidden.1.own_ref), channel_id=1, source_target_pairs={{0,1},{1,0},{2,3},{3,2},{4,5},{5,4},{6,7},{7,6},{8,9},{9,8},{10,11... | collective-permute-start | bytes 884744 | tf_op jit(solution)/shard_map/ppermute | solution.py:267
  46.4 3.8 %copy-start.1 = (bf16[8,3,32,128]{3,2,1,0:T(8,128)(2,1)S(1)}, bf16[8,3,32,128]{3,2,1,0:T(8,128)(2,1)}, u32[]{:S(2)}) copy-start(bf16[8,3,32,128]{3,2,1,0:T(8,128)(2,1)} %q_ref.1) | copy-start | bytes 589828
  49.3 12.1 %collective-permute-start.8 = (bf16[192,2048]{1,0:T(8,128)(2,1)S(1)}, bf16[192,2048]{1,0:T(8,128)(2,1)S(1)}, u32[]{:S(2)}, u32[]{:S(2)}) collective-permute-start(bf16[192,2048]{1,0:T(8,128)(2,1)S(1)} %expert_back_send.1), channel_id=1, source_target_pairs={{0,2},{1,5},{2,0},{3,7},{4,6},{5,1},{6,4},{7,3},{8,10},{9,13},{10,... | collective-permute-start | bytes 2359304 | tf_op jit(solution)/shard_map/ppermute | solution.py:267
  61.6 7.8 %collective-permute-start.9 = (bf16[96,2048]{1,0:T(8,128)(2,1)S(1)}, bf16[96,2048]{1,0:T(8,128)(2,1)S(1)}, u32[]{:S(2)}, u32[]{:S(2)}) collective-permute-start(bf16[96,2048]{1,0:T(8,128)(2,1)S(1)} %slice.44), channel_id=1, source_target_pairs={{0,4},{1,3},{2,6},{3,1},{4,0},{5,7},{6,2},{7,5},{8,12},{9,11},{10,... | collective-permute-start | bytes 1179656 | tf_op jit(solution)/shard_map/ppermute | solution.py:267
  69.6 7.2 %collective-permute-start.10 = (bf16[24,2048]{1,0:T(8,128)(2,1)S(1)}, bf16[24,2048]{1,0:T(8,128)(2,1)S(1)}, u32[]{:S(2)}, u32[]{:S(2)}) collective-permute-start(bf16[24,2048]{1,0:T(8,128)(2,1)S(1)} %get-tuple-element.40), channel_id=1, source_target_pairs={{0,8},{1,9},{2,10},{3,11},{4,12},{5,13},{6,14},{7,15},{8,16},{9,17... | collective-permute-start | bytes 294920 | tf_op jit(solution)/shard_map/ppermute | solution.py:267
  71.0 8.6 %collective-permute-start.11 = (bf16[24,2048]{1,0:T(8,128)(2,1)S(1)}, bf16[24,2048]{1,0:T(8,128)(2,1)S(1)}, u32[]{:S(2)}, u32[]{:S(2)}) collective-permute-start(bf16[24,2048]{1,0:T(8,128)(2,1)S(1)} %get-tuple-element.42), channel_id=1, source_target_pairs={{0,16},{1,17},{2,18},{3,19},{4,20},{5,21},{6,22},{7,23},{8,24},{9,... | collective-permute-start | bytes 294920 | tf_op jit(solution)/shard_map/ppermute | solution.py:267
  72.5 7.0 %collective-permute-start.12 = (bf16[24,2048]{1,0:T(8,128)(2,1)S(1)}, bf16[24,2048]{1,0:T(8,128)(2,1)S(1)}, u32[]{:S(2)}, u32[]{:S(2)}) collective-permute-start(bf16[24,2048]{1,0:T(8,128)(2,1)S(1)} %get-tuple-element.41), channel_id=1, source_target_pairs={{0,24},{1,25},{2,26},{3,27},{4,28},{5,29},{6,30},{7,31},{8,0},{9,1... | collective-permute-start | bytes 294920 | tf_op jit(solution)/shard_map/ppermute | solution.py:267

commit v14 on v13

--- a/solution.py
+++ b/solution.py
@@ -266,8 +266,8 @@
         ]
         return lax.ppermute(x, ("ep", "pd"), perm)
 
-    def along_z(self, x, shift):
-        return self.go(x, lambda ep, core: (ep + 4 * shift) % self.owners * 2 + core)
+    def along_z(self, x, turn):
+        return self.go(x, lambda ep, core: (ep ^ (4 * turn)) * 2 + core)
 
     def flip(self, x, turn):
         return self.go(x, lambda ep, core: (ep ^ (1 << ((core + turn) % 2))) * 2 + core)
@@ -326,7 +326,7 @@
         compiler_params=pltpu.CompilerParams(vmem_limit_bytes=room(prompt_kv) * 4),
         name="quantize_pages",
     )(me_ref, page_owner.reshape(-1), prompt_kv.transpose(0, 1, 3, 2, 4))
-    line = [mine] + [moves.along_z(mine, -shift) for shift in range(1, moves.lines)]
+    line = [mine] + [moves.along_z(mine, shift) for shift in range(1, moves.lines)]
     line = jnp.concatenate(line, axis=0)
     fresh = new_kv.transpose(2, 3, 0, 1, 4).reshape(2, heads, tokens, width)
     fresh = jnp.pad(fresh, ((0, 0), (0, 0), (0, 128 - tokens), (0, 0)))

time: 80.6 us -> 81.3 us (level)
    ppermute x13, waiting for transfers between devices: 26.2 us -> 27.5 us  [go(): return lax.ppermute(x, ('ep', 'pd'), perm)]
  transfers between devices with their start and end apart: 14 -> 14, of which waited for: 9 -> 10; matrix products, arithmetic and copies ran while one was open for 8% -> 7% of each run, Pallas kernels for 10% -> 10%
where the time goes in v14:
time: 81.3 us; the launch traced here: 81 us
  waiting for transfers between devices  37.4 us (46%)
  starting transfers between devices  21 us (26%)
  Pallas kernels  13 us (16%)
  local copies, waits for them, and re-layouts  6.04 us (7%)
  other arithmetic  2.71 us (3%)
    ppermute x13, waiting for transfers between devices, go(): return lax.ppermute(x, ('ep', 'pd'), perm)  27.5 us
    ppermute x13, starting transfers between devices, go(): return lax.ppermute(x, ('ep', 'pd'), perm)  16 us
    all_to_all x1, waiting for transfers between devices, body(): cache = lax.all_to_all(send, 'ep', split_axis=0, concat_axis=0, tiled=True)  9.97 us
    all_to_all x1, starting transfers between devices, body(): cache = lax.all_to_all(send, 'ep', split_axis=0, concat_axis=0, tiled=True)  5.01 us
    pallas_call x2, Pallas kernels, expert_front(): pl.pallas_call(functools.partial(hidden_kernel if last else partial_kerne...  3.62 us
    dynamic_slice x1, local copies, waits for them, and re-layouts, weights_of(): lax.dynamic_slice_in_dim(w[0], half * (d // 2), d // 2, axis=0)  3.46 us
    pallas_call x2, Pallas kernels, expert_back(): pl.pallas_call(functools.partial(back_kernel, send, experts, lanes, 4), o...  3.06 us
    pallas_call x1, Pallas kernels, body(): pl.pallas_call(functools.partial(page_kernel, pages), out_shape=jax.Shape...  2.66 us
  transfers between devices with their start and end apart: 14, of which 10 were waited for; matrix products, arithmetic and copies ran while one was open for 7% of the time, Pallas kernels for 10%

profile of v14, /device:TPU:0, one launch (start us, length us, event | category | flops | bytes accessed | tf_op | source)
XLA Modules:
  0.0 81.0 jit_solution(12537871068947350677)
XLA Ops:
  0.6 1.7 %pack_tokens.1 = bf16[24,2176]{1,0:T(8,128)(2,1)} custom-call(s32[1]{0:T(128)} %bitcast.1.core_ref, bf16[24,4096]{1,0:T(8,128)(2,1)} %bitcast.31, s32[24,8]{1,0:T(8,128)} %bitcast.33, f32[24,8]{1,0:T(8,128)} %bitcast.34), custom_call_target="tpu_custom_call" | custom-call | tf_op jit(solution)/shard_map/pack_tokens/pallas_call | solution.py:308
  2.4 3.0 %collective-permute-start = (bf16[24,2176]{1,0:T(8,128)(2,1)}, bf16[24,2176]{1,0:T(8,128)(2,1)S(1)}, u32[]{:S(2)}, u32[]{:S(2)}) collective-permute-start(bf16[24,2176]{1,0:T(8,128)(2,1)} %pack_tokens.1), channel_id=1, source_target_pairs={{0,8},{1,9},{2,10},{3,11},{4,12},{5,13},{6,14},{7,15},{8,0},{9,1},... | collective-permute-start | bytes 313352 | tf_op jit(solution)/shard_map/ppermute | solution.py:267
  5.4 2.6 %collective-permute-start.1 = (bf16[24,2176]{1,0:T(8,128)(2,1)}, bf16[24,2176]{1,0:T(8,128)(2,1)S(1)}, u32[]{:S(2)}, u32[]{:S(2)}) collective-permute-start(bf16[24,2176]{1,0:T(8,128)(2,1)} %pack_tokens.1), channel_id=1, source_target_pairs={{0,16},{1,17},{2,18},{3,19},{4,20},{5,21},{6,22},{7,23},{8,24},{9,... | collective-permute-start | bytes 313352 | tf_op jit(solution)/shard_map/ppermute | solution.py:267
  8.0 1.0 %copy.22 = bf16[16,2,16,2,128]{4,2,3,1,0:T(8,128)(2,1)S(1)} copy(bf16[16,2,16,2,128]{4,3,2,1,0:T(2,128)(2,1)} %param.12) | data formatting | bytes 524288 | tf_op args[0]
  9.1 0.7 copy-done.2
  9.7 2.7 %quantize_pages.1 = bf16[32,2,2,16,128]{4,3,2,1,0:T(8,128)(2,1)} custom-call(s32[1]{0:T(128)} %bitcast.me_ref, s32[256]{0:T(256)S(1)} %bitcast.30, bf16[16,2,2,16,128]{4,3,2,1,0:T(8,128)(2,1)S(1)} %bitcast.29), custom_call_target="tpu_custom_call" | custom-call | tf_op jit(solution)/shard_map/quantize_pages/pallas_call | solution.py:320
  12.4 4.1 %collective-permute-done.1 = bf16[24,2176]{1,0:T(8,128)(2,1)S(1)} collective-permute-done((bf16[24,2176]{1,0:T(8,128)(2,1)}, bf16[24,2176]{1,0:T(8,128)(2,1)S(1)}, u32[]{:S(2)}, u32[]{:S(2)}) %collective-permute-start.1) | collective-permute-done | bytes 104480 | tf_op jit(solution)/shard_map/ppermute | solution.py:267
  16.5 0.9 %pad_maximum_fusion.1 = bf16[96,2176]{1,0:T(8,128)(2,1)S(1)} fusion(bf16[24,2176]{1,0:T(8,128)(2,1)S(1)} %collective-permute-done.2, bf16[24,2176]{1,0:T(8,128)(2,1)S(1)} %collective-permute-done.1, bf16[24,2176]{1,0:T(8,128)(2,1)S(1)} %collective-permute-done, bf16[24,2176]{1,0:T(8,128)(2,1)} %pack_tokens.1), kind=kLoop, calls=%fused_computation.8 | loop fusion | flops 1671168 | bytes 835584 | tf_op jit(solution)/shard_map/concatenate | solution.py:330
  17.4 1.6 %collective-permute-start.3 = (bf16[96,2176]{1,0:T(8,128)(2,1)S(1)}, bf16[96,2176]{1,0:T(8,128)(2,1)S(1)}, u32[]{:S(2)}, u32[]{:S(2)}) collective-permute-start(bf16[96,2176]{1,0:T(8,128)(2,1)S(1)} %pad_maximum_fusion.1), channel_id=1, source_target_pairs={{0,2},{1,5},{2,0},{3,7},{4,6},{5,1},{6,4},{7,3},{8,10},{9,13},{10,... | collective-permute-start | bytes 1253384 | tf_op jit(solution)/shard_map/ppermute | solution.py:267
  19.0 5.0 %all-to-all-start = ((bf16[32,2,2,16,128]{4,3,2,1,0:T(8,128)(2,1)}), bf16[32,2,2,16,128]{4,3,2,1,0:T(8,128)(2,1)S(1)}, u32[]{:S(2)}, u32[]{:S(2)}) async-start(bf16[32,2,2,16,128]{4,3,2,1,0:T(8,128)(2,1)} %quantize_pages.1), calls=%async_computation | async-start | bytes 1048576 | tf_op jit(solution)/shard_map/all_to_all | solution.py:338
  24.5 0.7 reduce.3
  25.5 0.7 collective-permute-done.3
  26.3 1.6 %collective-permute-start.5 = (bf16[192,2176]{1,0:T(8,128)(2,1)S(1)}, bf16[192,2176]{1,0:T(8,128)(2,1)S(1)}, u32[]{:S(2)}, u32[]{:S(2)}) collective-permute-start(bf16[192,2176]{1,0:T(8,128)(2,1)S(1)} %pad_maximum_fusion.sr_ref), channel_id=1, source_target_pairs={{0,4},{1,3},{2,6},{3,1},{4,0},{5,7},{6,2},{7,5},{8,12},{9,11},{10,... | collective-permute-start | bytes 2506760 | tf_op jit(solution)/shard_map/ppermute | solution.py:267
  27.9 10.0 %all-to-all-done.cache_ref = bf16[32,2,2,16,128]{4,3,2,1,0:T(8,128)(2,1)S(1)} async-done(((bf16[32,2,2,16,128]{4,3,2,1,0:T(8,128)(2,1)}), bf16[32,2,2,16,128]{4,3,2,1,0:T(8,128)(2,1)S(1)}, u32[]{:S(2)}, u32[]{:S(2)}) %all-to-all-start) | async-done | bytes 524320 | tf_op jit(solution)/shard_map/all_to_all | solution.py:338
  37.9 3.5 %dynamic-slice_bitcast_fusion = (bf16[2048,384]{1,0:T(8,128)(2,1)S(1)}, bf16[2048,384]{1,0:T(8,128)(2,1)S(1)}, bf16[2048,384]{1,0:T(8,128)(2,1)S(1)}, bf16[2048,384]{1,0:T(8,128)(2,1)S(1)}) fusion(bf16[1,4096,384]{2,1,0:T(8,128)(2,1)} %param.22, s32[]{:T(128)S(6)} %select_n.9, s32[]{:T(128)S(6)} %select_n.8, bf16[1,4096,384]{2,1,0:T(8,128)(2,1)} %param.21), kind=kLoop, calls=%fused_computation.1 | loop fusion | bytes 12582920 | tf_op jit(solution)/shard_map/dynamic_slice | solution.py:343
  41.7 1.8 %expert_partial.1 = (f32[384,384]{1,0:T(8,128)S(1)}, f32[384,384]{1,0:T(8,128)S(1)}) custom-call(bf16[192,2176]{1,0:T(8,128)(2,1)S(1)} %pad_maximum_fusion.sr_ref, bf16[192,2176]{1,0:T(8,128)(2,1)S(1)} %collective-permute-done.5.r2_ref, bf16[2048,384]{1,0:T(8,128)(2,1)S(1)} %get-tuple-element.23.gate_ref, bf16[2048,384]{1,0:T(8,128)(2,1)S(1)} %get-tuple-element.24.up_ref), custom_call_target="tpu_custom_call" | custom-call | flops 1207959552 | bytes 5898240 | tf_op jit(solution)/shard_map/expert_partial/pallas_call | solution.py:182
  43.5 0.5 collective-permute-done.6.r2_ref
  44.0 1.8 %expert_hidden.1.own_ref = bf16[384,384]{1,0:T(8,128)(2,1)S(1)} custom-call(bf16[192,2176]{1,0:T(8,128)(2,1)S(1)} %collective-permute-done.4.sr_ref, bf16[192,2176]{1,0:T(8,128)(2,1)S(1)} %collective-permute-done.6.r2_ref, bf16[2048,384]{1,0:T(8,128)(2,1)S(1)} %get-tuple-element.44.gate_ref, bf16[2048,384]{1,0:T(8,128)(2,1)S(1)} %get-tuple-element.36.up_ref, ...), custom_call_target="tpu_custom_call" | custom-call | flops 1207959552 | bytes 5898240 | tf_op jit(solution)/shard_map/expert_hidden/pallas_call | solution.py:182
  46.1 1.4 %collective-permute-done.7.other_ref = bf16[384,384]{1,0:T(8,128)(2,1)S(1)} collective-permute-done((bf16[384,384]{1,0:T(8,128)(2,1)S(1)}, bf16[384,384]{1,0:T(8,128)(2,1)S(1)}, u32[]{:S(2)}, u32[]{:S(2)}) %collective-permute-start.7) | collective-permute-done | bytes 294944 | tf_op jit(solution)/shard_map/ppermute | solution.py:267
  47.5 1.5 %expert_back_send.1 = bf16[192,2048]{1,0:T(8,128)(2,1)S(1)} custom-call(s32[2]{0:T(128)S(1)} %pad_add_fusion.at_ref, bf16[384,384]{1,0:T(8,128)(2,1)S(1)} %expert_hidden.1.own_ref, bf16[384,384]{1,0:T(8,128)(2,1)S(1)} %collective-permute-done.7.other_ref, bf16[192,2176]{1,0:T(8,128)(2,1)S(1)} %pad_maximum_fusion.sr_ref, ...), custom_call_target="tpu_custom_call" | custom-call | flops 603979776 | bytes 5308416 | tf_op jit(solution)/shard_map/expert_back_send/pallas_call | solution.py:241
  49.0 1.3 %collective-permute-start.8 = (bf16[192,2048]{1,0:T(8,128)(2,1)S(1)}, bf16[192,2048]{1,0:T(8,128)(2,1)S(1)}, u32[]{:S(2)}, u32[]{:S(2)}) collective-permute-start(bf16[192,2048]{1,0:T(8,128)(2,1)S(1)} %expert_back_send.1), channel_id=1, source_target_pairs={{0,2},{1,5},{2,0},{3,7},{4,6},{5,1},{6,4},{7,3},{8,10},{9,13},{10,... | collective-permute-start | bytes 2359304 | tf_op jit(solution)/shard_map/ppermute | solution.py:267
  50.3 1.9 %attention.1 = bf16[8,3,32,128]{3,2,1,0:T(8,128)(2,1)} custom-call(s32[1]{0:T(128)} %bitcast.me_ref, s32[16,16]{1,0:T(8,128)S(1)} %reshape.42.owner_ref, s32[16,16]{1,0:T(8,128)S(1)} %reshape.43.slot_ref, s32[16,16]{1,0:T(8,128)S(1)} %reshape.44.fill_ref, bf16[8,3,32,128]{3,2,1,0:T(8,128)(2,1)S(1)} %copy-done.1, ...), custom_call_target="tpu_custom_call" | custom-call | tf_op jit(solution)/shard_map/attention/pallas_call | solution.py:355
  52.3 1.5 %expert_back_keep.1 = f32[192,2048]{1,0:T(8,128)S(1)} custom-call(s32[2]{0:T(128)S(1)} %pad_add_fusion.at_ref, bf16[384,384]{1,0:T(8,128)(2,1)S(1)} %expert_hidden.1.own_ref, bf16[384,384]{1,0:T(8,128)(2,1)S(1)} %collective-permute-done.7.other_ref, bf16[192,2176]{1,0:T(8,128)(2,1)S(1)} %pad_maximum_fusion.sr_ref, ...), custom_call_target="tpu_custom_call" | custom-call | flops 603979776 | bytes 5308416 | tf_op jit(solution)/shard_map/expert_back_keep/pallas_call | solution.py:241
  53.8 7.3 %collective-permute-done.8 = bf16[192,2048]{1,0:T(8,128)(2,1)S(1)} collective-permute-done((bf16[192,2048]{1,0:T(8,128)(2,1)S(1)}, bf16[192,2048]{1,0:T(8,128)(2,1)S(1)}, u32[]{:S(2)}, u32[]{:S(2)}) %collective-permute-start.8) | collective-permute-done | bytes 786464 | tf_op jit(solution)/shard_map/ppermute | solution.py:267
  61.3 1.3 %collective-permute-start.9 = (bf16[96,2048]{1,0:T(8,128)(2,1)S(1)}, bf16[96,2048]{1,0:T(8,128)(2,1)S(1)}, u32[]{:S(2)}, u32[]{:S(2)}) collective-permute-start(bf16[96,2048]{1,0:T(8,128)(2,1)S(1)} %slice.44), channel_id=1, source_target_pairs={{0,4},{1,3},{2,6},{3,1},{4,0},{5,7},{6,2},{7,5},{8,12},{9,11},{10,... | collective-permute-start | bytes 1179656 | tf_op jit(solution)/shard_map/ppermute | solution.py:267
  62.6 6.6 %collective-permute-done.9 = bf16[96,2048]{1,0:T(8,128)(2,1)S(1)} collective-permute-done((bf16[96,2048]{1,0:T(8,128)(2,1)S(1)}, bf16[96,2048]{1,0:T(8,128)(2,1)S(1)}, u32[]{:S(2)}, u32[]{:S(2)}) %collective-permute-start.9) | collective-permute-done | bytes 393248 | tf_op jit(solution)/shard_map/ppermute | solution.py:267
  69.3 1.9 %collective-permute-start.10 = (bf16[24,2048]{1,0:T(8,128)(2,1)S(1)}, bf16[24,2048]{1,0:T(8,128)(2,1)S(1)}, u32[]{:S(2)}, u32[]{:S(2)}) collective-permute-start(bf16[24,2048]{1,0:T(8,128)(2,1)S(1)} %get-tuple-element.40), channel_id=1, source_target_pairs={{0,8},{1,9},{2,10},{3,11},{4,12},{5,13},{6,14},{7,15},{8,0},{9,1},... | collective-permute-start | bytes 294920 | tf_op jit(solution)/shard_map/ppermute | solution.py:267
  71.3 1.2 %collective-permute-start.11 = (bf16[24,2048]{1,0:T(8,128)(2,1)S(1)}, bf16[24,2048]{1,0:T(8,128)(2,1)S(1)}, u32[]{:S(2)}, u32[]{:S(2)}) collective-permute-start(bf16[24,2048]{1,0:T(8,128)(2,1)S(1)} %get-tuple-element.42), channel_id=1, source_target_pairs={{0,16},{1,17},{2,18},{3,19},{4,20},{5,21},{6,22},{7,23},{8,24},{9,... | collective-permute-start | bytes 294920 | tf_op jit(solution)/shard_map/ppermute | solution.py:267
  72.5 1.3 %collective-permute-start.12 = (bf16[24,2048]{1,0:T(8,128)(2,1)S(1)}, bf16[24,2048]{1,0:T(8,128)(2,1)S(1)}, u32[]{:S(2)}, u32[]{:S(2)}) collective-permute-start(bf16[24,2048]{1,0:T(8,128)(2,1)S(1)} %get-tuple-element.41), channel_id=1, source_target_pairs={{0,24},{1,25},{2,26},{3,27},{4,28},{5,29},{6,30},{7,31},{8,16},{9,... | collective-permute-start | bytes 294920 | tf_op jit(solution)/shard_map/ppermute | solution.py:267
  73.8 0.7 collective-permute-done.10
  74.5 5.8 %collective-permute-done.11 = bf16[24,2048]{1,0:T(8,128)(2,1)S(1)} collective-permute-done((bf16[24,2048]{1,0:T(8,128)(2,1)S(1)}, bf16[24,2048]{1,0:T(8,128)(2,1)S(1)}, u32[]{:S(2)}, u32[]{:S(2)}) %collective-permute-start.11) | collective-permute-done | bytes 98336 | tf_op jit(solution)/shard_map/ppermute | solution.py:267
  80.3 0.7 fusion.3
  (34 shorter events, 1.9 us)
Async XLA Ops:
  2.4 10.0 %collective-permute-start = (bf16[24,2176]{1,0:T(8,128)(2,1)}, bf16[24,2176]{1,0:T(8,128)(2,1)S(1)}, u32[]{:S(2)}, u32[]{:S(2)}) collective-permute-start(bf16[24,2176]{1,0:T(8,128)(2,1)} %pack_tokens.1), channel_id=1, source_target_pairs={{0,8},{1,9},{2,10},{3,11},{4,12},{5,13},{6,14},{7,15},{8,0},{9,1},... | collective-permute-start | bytes 313352 | tf_op jit(solution)/shard_map/ppermute | solution.py:267
  5.4 11.1 %collective-permute-start.1 = (bf16[24,2176]{1,0:T(8,128)(2,1)}, bf16[24,2176]{1,0:T(8,128)(2,1)S(1)}, u32[]{:S(2)}, u32[]{:S(2)}) collective-permute-start(bf16[24,2176]{1,0:T(8,128)(2,1)} %pack_tokens.1), channel_id=1, source_target_pairs={{0,16},{1,17},{2,18},{3,19},{4,20},{5,21},{6,22},{7,23},{8,24},{9,... | collective-permute-start | bytes 313352 | tf_op jit(solution)/shard_map/ppermute | solution.py:267
  8.0 8.5 %collective-permute-start.2 = (bf16[24,2176]{1,0:T(8,128)(2,1)}, bf16[24,2176]{1,0:T(8,128)(2,1)S(1)}, u32[]{:S(2)}, u32[]{:S(2)}) collective-permute-start(bf16[24,2176]{1,0:T(8,128)(2,1)} %pack_tokens.1), channel_id=1, source_target_pairs={{0,24},{1,25},{2,26},{3,27},{4,28},{5,29},{6,30},{7,31},{8,16},{9,... | collective-permute-start | bytes 313352 | tf_op jit(solution)/shard_map/ppermute | solution.py:267
  8.0 16.0 %copy-start.4 = (bf16[8,3,2,2,128]{4,3,2,1,0:T(2,128)(2,1)S(1)}, bf16[8,3,2,2,128]{4,3,2,1,0:T(2,128)(2,1)}, u32[]{:S(2)}) copy-start(bf16[8,3,2,2,128]{4,3,2,1,0:T(2,128)(2,1)} %param.17) | copy-start | bytes 73732
  8.0 16.6 %copy-start.3 = (s32[256,1]{0,1:T(1,128)S(1)}, s32[256,1]{0,1:T(1,128)}, u32[]{:S(2)}) copy-start(s32[256,1]{0,1:T(1,128)} %param.13) | copy-start | bytes 3076
  8.0 17.3 %copy-start.5 = (s32[256]{0:T(256)S(1)}, s32[256]{0:T(256)}, u32[]{:S(2)}) copy-start(s32[256]{0:T(256)} %param.14) | copy-start | bytes 3076
  8.0 17.4 %copy-start.6 = (s32[256]{0:T(256)S(1)}, s32[256]{0:T(256)}, u32[]{:S(2)}) copy-start(s32[256]{0:T(256)} %param.15) | copy-start | bytes 3076
  9.0 0.7 copy-start.2
  17.4 8.8 %collective-permute-start.3 = (bf16[96,2176]{1,0:T(8,128)(2,1)S(1)}, bf16[96,2176]{1,0:T(8,128)(2,1)S(1)}, u32[]{:S(2)}, u32[]{:S(2)}) collective-permute-start(bf16[96,2176]{1,0:T(8,128)(2,1)S(1)} %pad_maximum_fusion.1), channel_id=1, source_target_pairs={{0,2},{1,5},{2,0},{3,7},{4,6},{5,1},{6,4},{7,3},{8,10},{9,13},{10,... | collective-permute-start | bytes 1253384 | tf_op jit(solution)/shard_map/ppermute | solution.py:267
  19.0 18.9 %all-to-all-start = ((bf16[32,2,2,16,128]{4,3,2,1,0:T(8,128)(2,1)}), bf16[32,2,2,16,128]{4,3,2,1,0:T(8,128)(2,1)S(1)}, u32[]{:S(2)}, u32[]{:S(2)}) async-start(bf16[32,2,2,16,128]{4,3,2,1,0:T(8,128)(2,1)} %quantize_pages.1), calls=%async_computation | async-start | bytes 1048576 | tf_op jit(solution)/shard_map/all_to_all | solution.py:338
  26.3 15.4 %collective-permute-start.5 = (bf16[192,2176]{1,0:T(8,128)(2,1)S(1)}, bf16[192,2176]{1,0:T(8,128)(2,1)S(1)}, u32[]{:S(2)}, u32[]{:S(2)}) collective-permute-start(bf16[192,2176]{1,0:T(8,128)(2,1)S(1)} %pad_maximum_fusion.sr_ref), channel_id=1, source_target_pairs={{0,4},{1,3},{2,6},{3,1},{4,0},{5,7},{6,2},{7,5},{8,12},{9,11},{10,... | collective-permute-start | bytes 2506760 | tf_op jit(solution)/shard_map/ppermute | solution.py:267
  27.9 15.6 %collective-permute-start.4 = (bf16[192,2176]{1,0:T(8,128)(2,1)S(1)}, bf16[192,2176]{1,0:T(8,128)(2,1)S(1)}, u32[]{:S(2)}, u32[]{:S(2)}) collective-permute-start(bf16[192,2176]{1,0:T(8,128)(2,1)S(1)} %pad_maximum_fusion.sr_ref), channel_id=1, source_target_pairs={{0,1},{1,0},{2,3},{3,2},{4,5},{5,4},{6,7},{7,6},{8,9},{9,8},{10,11... | collective-permute-start | bytes 2506760 | tf_op jit(solution)/shard_map/ppermute | solution.py:267
  41.7 2.4 %collective-permute-start.6 = (bf16[192,2176]{1,0:T(8,128)(2,1)S(1)}, bf16[192,2176]{1,0:T(8,128)(2,1)S(1)}, u32[]{:S(2)}, u32[]{:S(2)}) collective-permute-start(bf16[192,2176]{1,0:T(8,128)(2,1)S(1)} %collective-permute-done.5.r2_ref), channel_id=1, source_target_pairs={{0,1},{1,0},{2,3},{3,2},{4,5},{5,4},{6,7},{7,6},{8,9},{9,8},{10,11... | collective-permute-start | bytes 2506760 | tf_op jit(solution)/shard_map/ppermute | solution.py:267
  44.0 3.5 %copy-start = (bf16[1,768,2048]{2,1,0:T(8,128)(2,1)S(1)}, bf16[1,768,2048]{2,1,0:T(8,128)(2,1)}, u32[]{:S(2)}) copy-start(bf16[1,768,2048]{2,1,0:T(8,128)(2,1)} %down_ref.3) | copy-start | bytes 9437188
  45.9 1.6 %collective-permute-start.7 = (bf16[384,384]{1,0:T(8,128)(2,1)S(1)}, bf16[384,384]{1,0:T(8,128)(2,1)S(1)}, u32[]{:S(2)}, u32[]{:S(2)}) collective-permute-start(bf16[384,384]{1,0:T(8,128)(2,1)S(1)} %expert_hidden.1.own_ref), channel_id=1, source_target_pairs={{0,1},{1,0},{2,3},{3,2},{4,5},{5,4},{6,7},{7,6},{8,9},{9,8},{10,11... | collective-permute-start | bytes 884744 | tf_op jit(solution)/shard_map/ppermute | solution.py:267
  46.1 4.2 %copy-start.1 = (bf16[8,3,32,128]{3,2,1,0:T(8,128)(2,1)S(1)}, bf16[8,3,32,128]{3,2,1,0:T(8,128)(2,1)}, u32[]{:S(2)}) copy-start(bf16[8,3,32,128]{3,2,1,0:T(8,128)(2,1)} %q_ref.1) | copy-start | bytes 589828
  49.0 12.1 %collective-permute-start.8 = (bf16[192,2048]{1,0:T(8,128)(2,1)S(1)}, bf16[192,2048]{1,0:T(8,128)(2,1)S(1)}, u32[]{:S(2)}, u32[]{:S(2)}) collective-permute-start(bf16[192,2048]{1,0:T(8,128)(2,1)S(1)} %expert_back_send.1), channel_id=1, source_target_pairs={{0,2},{1,5},{2,0},{3,7},{4,6},{5,1},{6,4},{7,3},{8,10},{9,13},{10,... | collective-permute-start | bytes 2359304 | tf_op jit(solution)/shard_map/ppermute | solution.py:267
  61.3 7.8 %collective-permute-start.9 = (bf16[96,2048]{1,0:T(8,128)(2,1)S(1)}, bf16[96,2048]{1,0:T(8,128)(2,1)S(1)}, u32[]{:S(2)}, u32[]{:S(2)}) collective-permute-start(bf16[96,2048]{1,0:T(8,128)(2,1)S(1)} %slice.44), channel_id=1, source_target_pairs={{0,4},{1,3},{2,6},{3,1},{4,0},{5,7},{6,2},{7,5},{8,12},{9,11},{10,... | collective-permute-start | bytes 1179656 | tf_op jit(solution)/shard_map/ppermute | solution.py:267
  69.3 5.2 %collective-permute-start.10 = (bf16[24,2048]{1,0:T(8,128)(2,1)S(1)}, bf16[24,2048]{1,0:T(8,128)(2,1)S(1)}, u32[]{:S(2)}, u32[]{:S(2)}) collective-permute-start(bf16[24,2048]{1,0:T(8,128)(2,1)S(1)} %get-tuple-element.40), channel_id=1, source_target_pairs={{0,8},{1,9},{2,10},{3,11},{4,12},{5,13},{6,14},{7,15},{8,0},{9,1},... | collective-permute-start | bytes 294920 | tf_op jit(solution)/shard_map/ppermute | solution.py:267
  71.3 9.0 %collective-permute-start.11 = (bf16[24,2048]{1,0:T(8,128)(2,1)S(1)}, bf16[24,2048]{1,0:T(8,128)(2,1)S(1)}, u32[]{:S(2)}, u32[]{:S(2)}) collective-permute-start(bf16[24,2048]{1,0:T(8,128)(2,1)S(1)} %get-tuple-element.42), channel_id=1, source_target_pairs={{0,16},{1,17},{2,18},{3,19},{4,20},{5,21},{6,22},{7,23},{8,24},{9,... | collective-permute-start | bytes 294920 | tf_op jit(solution)/shard_map/ppermute | solution.py:267
  72.5 7.8 %collective-permute-start.12 = (bf16[24,2048]{1,0:T(8,128)(2,1)S(1)}, bf16[24,2048]{1,0:T(8,128)(2,1)S(1)}, u32[]{:S(2)}, u32[]{:S(2)}) collective-permute-start(bf16[24,2048]{1,0:T(8,128)(2,1)S(1)} %get-tuple-element.41), channel_id=1, source_target_pairs={{0,24},{1,25},{2,26},{3,27},{4,28},{5,29},{6,30},{7,31},{8,16},{9,... | collective-permute-start | bytes 294920 | tf_op jit(solution)/shard_map/ppermute | solution.py:267

commit v15 on v13

--- a/solution.py
+++ b/solution.py
@@ -122,9 +122,8 @@
 
 
 def pack_kernel(experts, core_ref, x_ref, route_ref, prob_ref, out_ref):
-    half = x_ref.shape[1] // 2
-    begin = pl.multiple_of(core_ref[0] * half, 128)
-    out_ref[:, :half] = x_ref[:, pl.ds(begin, half)]
+    half = x_ref.shape[1]
+    out_ref[:, :half] = x_ref[...]
     shape = (x_ref.shape[0], out_ref.shape[1] - half)
     lane = lax.broadcasted_iota(jnp.int32, shape, 1)
     expert = lane % experts
@@ -308,8 +307,16 @@
     mine = pl.pallas_call(
         functools.partial(pack_kernel, owners),
         out_shape=jax.ShapeDtypeStruct((tokens, d // 2 + lanes), jnp.bfloat16),
-        in_specs=[smem()] + [vmem()] * 3,
-        out_specs=vmem(),
+        grid_spec=pltpu.PrefetchScalarGridSpec(
+            num_scalar_prefetch=1,
+            grid=(1,),
+            in_specs=[
+                pl.BlockSpec((tokens, d // 2), lambda i, core: (0, core[0])),
+                pl.BlockSpec((tokens, top), lambda i, core: (0, 0)),
+                pl.BlockSpec((tokens, top), lambda i, core: (0, 0)),
+            ],
+            out_specs=pl.BlockSpec((tokens, d // 2 + lanes), lambda i, core: (0, 0)),
+        ),
         name="pack_tokens",
     )(
         own_core,

time: 80.6 us -> 80.5 us (level)
  no operation moved by 1% of the time
where the time goes in v15:
time: 80.5 us; the launch traced here: 80.2 us
  waiting for transfers between devices  36.6 us (45%)
  starting transfers between devices  21.1 us (26%)
  Pallas kernels  12.9 us (16%)
  local copies, waits for them, and re-layouts  6.05 us (8%)
  other arithmetic  2.71 us (3%)
    ppermute x13, waiting for transfers between devices, go(): return lax.ppermute(x, ('ep', 'pd'), perm)  26.2 us
    ppermute x13, starting transfers between devices, go(): return lax.ppermute(x, ('ep', 'pd'), perm)  16.4 us
    all_to_all x1, waiting for transfers between devices, body(): cache = lax.all_to_all(send, 'ep', split_axis=0, concat_axis=0, tiled=True)  10.4 us
    all_to_all x1, starting transfers between devices, body(): cache = lax.all_to_all(send, 'ep', split_axis=0, concat_axis=0, tiled=True)  4.68 us
    pallas_call x2, Pallas kernels, expert_front(): pl.pallas_call(functools.partial(hidden_kernel if last else partial_kerne...  3.62 us
    dynamic_slice x1, local copies, waits for them, and re-layouts, weights_of(): lax.dynamic_slice_in_dim(w[0], half * (d // 2), d // 2, axis=0)  3.46 us
    pallas_call x2, Pallas kernels, expert_back(): pl.pallas_call(functools.partial(back_kernel, send, experts, lanes, 4), o...  3.05 us
    pallas_call x1, Pallas kernels, body(): pl.pallas_call(functools.partial(page_kernel, pages), out_shape=jax.Shape...  2.66 us
  transfers between devices with their start and end apart: 14, of which 9 were waited for; matrix products, arithmetic and copies ran while one was open for 8% of the time, Pallas kernels for 10%

profile of v15, /device:TPU:0, one launch (start us, length us, event | category | flops | bytes accessed | tf_op | source)
XLA Modules:
  0.0 80.2 jit_solution(18298293533236694698)
XLA Ops:
  0.6 1.7 %pack_tokens.1 = bf16[24,2176]{1,0:T(8,128)(2,1)} custom-call(s32[1]{0:T(128)} %bitcast.1.core_ref, bf16[24,4096]{1,0:T(8,128)(2,1)} %bitcast.31, s32[24,8]{1,0:T(8,128)} %bitcast.33, f32[24,8]{1,0:T(8,128)} %bitcast.34), custom_call_target="tpu_custom_call" | custom-call | tf_op jit(solution)/shard_map/pack_tokens/pallas_call | solution.py:307
  2.3 5.0 %collective-permute-start = (bf16[24,2176]{1,0:T(8,128)(2,1)}, bf16[24,2176]{1,0:T(8,128)(2,1)S(1)}, u32[]{:S(2)}, u32[]{:S(2)}) collective-permute-start(bf16[24,2176]{1,0:T(8,128)(2,1)} %pack_tokens.1), channel_id=1, source_target_pairs={{0,24},{1,25},{2,26},{3,27},{4,28},{5,29},{6,30},{7,31},{8,0},{9,1... | collective-permute-start | bytes 313352 | tf_op jit(solution)/shard_map/ppermute | solution.py:266
  7.4 1.0 %collective-permute-start.2 = (bf16[24,2176]{1,0:T(8,128)(2,1)}, bf16[24,2176]{1,0:T(8,128)(2,1)S(1)}, u32[]{:S(2)}, u32[]{:S(2)}) collective-permute-start(bf16[24,2176]{1,0:T(8,128)(2,1)} %pack_tokens.1), channel_id=1, source_target_pairs={{0,8},{1,9},{2,10},{3,11},{4,12},{5,13},{6,14},{7,15},{8,16},{9,17... | collective-permute-start | bytes 313352 | tf_op jit(solution)/shard_map/ppermute | solution.py:266
  8.4 1.0 %copy.22 = bf16[16,2,16,2,128]{4,2,3,1,0:T(8,128)(2,1)S(1)} copy(bf16[16,2,16,2,128]{4,3,2,1,0:T(2,128)(2,1)} %param.12) | data formatting | bytes 524288 | tf_op args[0]
  9.5 0.7 copy-done.2
  10.1 2.7 %quantize_pages.1 = bf16[32,2,2,16,128]{4,3,2,1,0:T(8,128)(2,1)} custom-call(s32[1]{0:T(128)} %bitcast.me_ref, s32[256]{0:T(256)S(1)} %bitcast.30, bf16[16,2,2,16,128]{4,3,2,1,0:T(8,128)(2,1)S(1)} %bitcast.29), custom_call_target="tpu_custom_call" | custom-call | tf_op jit(solution)/shard_map/quantize_pages/pallas_call | solution.py:327
  12.8 4.0 %collective-permute-done.1 = bf16[24,2176]{1,0:T(8,128)(2,1)S(1)} collective-permute-done((bf16[24,2176]{1,0:T(8,128)(2,1)}, bf16[24,2176]{1,0:T(8,128)(2,1)S(1)}, u32[]{:S(2)}, u32[]{:S(2)}) %collective-permute-start.1) | collective-permute-done | bytes 104480 | tf_op jit(solution)/shard_map/ppermute | solution.py:266
  16.8 0.9 %pad_maximum_fusion.1 = bf16[96,2176]{1,0:T(8,128)(2,1)S(1)} fusion(bf16[24,2176]{1,0:T(8,128)(2,1)S(1)} %collective-permute-done.2, bf16[24,2176]{1,0:T(8,128)(2,1)S(1)} %collective-permute-done.1, bf16[24,2176]{1,0:T(8,128)(2,1)S(1)} %collective-permute-done, bf16[24,2176]{1,0:T(8,128)(2,1)} %pack_tokens.1), kind=kLoop, calls=%fused_computation.8 | loop fusion | flops 1671168 | bytes 835584 | tf_op jit(solution)/shard_map/concatenate | solution.py:337
  17.7 1.6 %collective-permute-start.3 = (bf16[96,2176]{1,0:T(8,128)(2,1)S(1)}, bf16[96,2176]{1,0:T(8,128)(2,1)S(1)}, u32[]{:S(2)}, u32[]{:S(2)}) collective-permute-start(bf16[96,2176]{1,0:T(8,128)(2,1)S(1)} %pad_maximum_fusion.1), channel_id=1, source_target_pairs={{0,2},{1,5},{2,0},{3,7},{4,6},{5,1},{6,4},{7,3},{8,10},{9,13},{10,... | collective-permute-start | bytes 1253384 | tf_op jit(solution)/shard_map/ppermute | solution.py:266
  19.3 4.7 %all-to-all-start = ((bf16[32,2,2,16,128]{4,3,2,1,0:T(8,128)(2,1)}), bf16[32,2,2,16,128]{4,3,2,1,0:T(8,128)(2,1)S(1)}, u32[]{:S(2)}, u32[]{:S(2)}) async-start(bf16[32,2,2,16,128]{4,3,2,1,0:T(8,128)(2,1)} %quantize_pages.1), calls=%async_computation | async-start | bytes 1048576 | tf_op jit(solution)/shard_map/all_to_all | solution.py:345
  24.5 0.7 reduce.3
  25.5 0.8 %collective-permute-done.3 = bf16[96,2176]{1,0:T(8,128)(2,1)S(1)} collective-permute-done((bf16[96,2176]{1,0:T(8,128)(2,1)S(1)}, bf16[96,2176]{1,0:T(8,128)(2,1)S(1)}, u32[]{:S(2)}, u32[]{:S(2)}) %collective-permute-start.3) | collective-permute-done | bytes 417824 | tf_op jit(solution)/shard_map/ppermute | solution.py:266
  26.3 1.6 %collective-permute-start.5 = (bf16[192,2176]{1,0:T(8,128)(2,1)S(1)}, bf16[192,2176]{1,0:T(8,128)(2,1)S(1)}, u32[]{:S(2)}, u32[]{:S(2)}) collective-permute-start(bf16[192,2176]{1,0:T(8,128)(2,1)S(1)} %pad_maximum_fusion.sr_ref), channel_id=1, source_target_pairs={{0,4},{1,3},{2,6},{3,1},{4,0},{5,7},{6,2},{7,5},{8,12},{9,11},{10,... | collective-permute-start | bytes 2506760 | tf_op jit(solution)/shard_map/ppermute | solution.py:266
  28.0 10.4 %all-to-all-done.cache_ref = bf16[32,2,2,16,128]{4,3,2,1,0:T(8,128)(2,1)S(1)} async-done(((bf16[32,2,2,16,128]{4,3,2,1,0:T(8,128)(2,1)}), bf16[32,2,2,16,128]{4,3,2,1,0:T(8,128)(2,1)S(1)}, u32[]{:S(2)}, u32[]{:S(2)}) %all-to-all-start) | async-done | bytes 524320 | tf_op jit(solution)/shard_map/all_to_all | solution.py:345
  38.4 3.5 %dynamic-slice_bitcast_fusion = (bf16[2048,384]{1,0:T(8,128)(2,1)S(1)}, bf16[2048,384]{1,0:T(8,128)(2,1)S(1)}, bf16[2048,384]{1,0:T(8,128)(2,1)S(1)}, bf16[2048,384]{1,0:T(8,128)(2,1)S(1)}) fusion(bf16[1,4096,384]{2,1,0:T(8,128)(2,1)} %param.22, s32[]{:T(128)S(6)} %select_n.9, s32[]{:T(128)S(6)} %select_n.8, bf16[1,4096,384]{2,1,0:T(8,128)(2,1)} %param.21), kind=kLoop, calls=%fused_computation.1 | loop fusion | bytes 12582920 | tf_op jit(solution)/shard_map/dynamic_slice | solution.py:350
  42.0 1.8 %expert_partial.1 = (f32[384,384]{1,0:T(8,128)S(1)}, f32[384,384]{1,0:T(8,128)S(1)}) custom-call(bf16[192,2176]{1,0:T(8,128)(2,1)S(1)} %pad_maximum_fusion.sr_ref, bf16[192,2176]{1,0:T(8,128)(2,1)S(1)} %collective-permute-done.5.r2_ref, bf16[2048,384]{1,0:T(8,128)(2,1)S(1)} %get-tuple-element.23.gate_ref, bf16[2048,384]{1,0:T(8,128)(2,1)S(1)} %get-tuple-element.24.up_ref), custom_call_target="tpu_custom_call" | custom-call | flops 1207959552 | bytes 5898240 | tf_op jit(solution)/shard_map/expert_partial/pallas_call | solution.py:181
  43.8 0.5 collective-permute-done.6.r2_ref
  44.3 1.8 %expert_hidden.1.own_ref = bf16[384,384]{1,0:T(8,128)(2,1)S(1)} custom-call(bf16[192,2176]{1,0:T(8,128)(2,1)S(1)} %collective-permute-done.4.sr_ref, bf16[192,2176]{1,0:T(8,128)(2,1)S(1)} %collective-permute-done.6.r2_ref, bf16[2048,384]{1,0:T(8,128)(2,1)S(1)} %get-tuple-element.44.gate_ref, bf16[2048,384]{1,0:T(8,128)(2,1)S(1)} %get-tuple-element.36.up_ref, ...), custom_call_target="tpu_custom_call" | custom-call | flops 1207959552 | bytes 5898240 | tf_op jit(solution)/shard_map/expert_hidden/pallas_call | solution.py:181
  46.4 1.4 %collective-permute-done.7.other_ref = bf16[384,384]{1,0:T(8,128)(2,1)S(1)} collective-permute-done((bf16[384,384]{1,0:T(8,128)(2,1)S(1)}, bf16[384,384]{1,0:T(8,128)(2,1)S(1)}, u32[]{:S(2)}, u32[]{:S(2)}) %collective-permute-start.7) | collective-permute-done | bytes 294944 | tf_op jit(solution)/shard_map/ppermute | solution.py:266
  47.8 1.5 %expert_back_send.1 = bf16[192,2048]{1,0:T(8,128)(2,1)S(1)} custom-call(s32[2]{0:T(128)S(1)} %pad_add_fusion.at_ref, bf16[384,384]{1,0:T(8,128)(2,1)S(1)} %expert_hidden.1.own_ref, bf16[384,384]{1,0:T(8,128)(2,1)S(1)} %collective-permute-done.7.other_ref, bf16[192,2176]{1,0:T(8,128)(2,1)S(1)} %pad_maximum_fusion.sr_ref, ...), custom_call_target="tpu_custom_call" | custom-call | flops 603979776 | bytes 5308416 | tf_op jit(solution)/shard_map/expert_back_send/pallas_call | solution.py:240
  49.3 0.9 %collective-permute-start.8 = (bf16[192,2048]{1,0:T(8,128)(2,1)S(1)}, bf16[192,2048]{1,0:T(8,128)(2,1)S(1)}, u32[]{:S(2)}, u32[]{:S(2)}) collective-permute-start(bf16[192,2048]{1,0:T(8,128)(2,1)S(1)} %expert_back_send.1), channel_id=1, source_target_pairs={{0,2},{1,5},{2,0},{3,7},{4,6},{5,1},{6,4},{7,3},{8,10},{9,13},{10,... | collective-permute-start | bytes 2359304 | tf_op jit(solution)/shard_map/ppermute | solution.py:266
  50.2 1.9 %attention.1 = bf16[8,3,32,128]{3,2,1,0:T(8,128)(2,1)} custom-call(s32[1]{0:T(128)} %bitcast.me_ref, s32[16,16]{1,0:T(8,128)S(1)} %reshape.42.owner_ref, s32[16,16]{1,0:T(8,128)S(1)} %reshape.43.slot_ref, s32[16,16]{1,0:T(8,128)S(1)} %reshape.44.fill_ref, bf16[8,3,32,128]{3,2,1,0:T(8,128)(2,1)S(1)} %copy-done.1, ...), custom_call_target="tpu_custom_call" | custom-call | tf_op jit(solution)/shard_map/attention/pallas_call | solution.py:362
  52.2 1.5 %expert_back_keep.1 = f32[192,2048]{1,0:T(8,128)S(1)} custom-call(s32[2]{0:T(128)S(1)} %pad_add_fusion.at_ref, bf16[384,384]{1,0:T(8,128)(2,1)S(1)} %expert_hidden.1.own_ref, bf16[384,384]{1,0:T(8,128)(2,1)S(1)} %collective-permute-done.7.other_ref, bf16[192,2176]{1,0:T(8,128)(2,1)S(1)} %pad_maximum_fusion.sr_ref, ...), custom_call_target="tpu_custom_call" | custom-call | flops 603979776 | bytes 5308416 | tf_op jit(solution)/shard_map/expert_back_keep/pallas_call | solution.py:240
  53.7 7.7 %collective-permute-done.8 = bf16[192,2048]{1,0:T(8,128)(2,1)S(1)} collective-permute-done((bf16[192,2048]{1,0:T(8,128)(2,1)S(1)}, bf16[192,2048]{1,0:T(8,128)(2,1)S(1)}, u32[]{:S(2)}, u32[]{:S(2)}) %collective-permute-start.8) | collective-permute-done | bytes 786464 | tf_op jit(solution)/shard_map/ppermute | solution.py:266
  61.6 1.1 %collective-permute-start.9 = (bf16[96,2048]{1,0:T(8,128)(2,1)S(1)}, bf16[96,2048]{1,0:T(8,128)(2,1)S(1)}, u32[]{:S(2)}, u32[]{:S(2)}) collective-permute-start(bf16[96,2048]{1,0:T(8,128)(2,1)S(1)} %slice.44), channel_id=1, source_target_pairs={{0,4},{1,3},{2,6},{3,1},{4,0},{5,7},{6,2},{7,5},{8,12},{9,11},{10,... | collective-permute-start | bytes 1179656 | tf_op jit(solution)/shard_map/ppermute | solution.py:266
  62.7 6.8 %collective-permute-done.9 = bf16[96,2048]{1,0:T(8,128)(2,1)S(1)} collective-permute-done((bf16[96,2048]{1,0:T(8,128)(2,1)S(1)}, bf16[96,2048]{1,0:T(8,128)(2,1)S(1)}, u32[]{:S(2)}, u32[]{:S(2)}) %collective-permute-start.9) | collective-permute-done | bytes 393248 | tf_op jit(solution)/shard_map/ppermute | solution.py:266
  69.6 1.3 %collective-permute-start.10 = (bf16[24,2048]{1,0:T(8,128)(2,1)S(1)}, bf16[24,2048]{1,0:T(8,128)(2,1)S(1)}, u32[]{:S(2)}, u32[]{:S(2)}) collective-permute-start(bf16[24,2048]{1,0:T(8,128)(2,1)S(1)} %get-tuple-element.40), channel_id=1, source_target_pairs={{0,8},{1,9},{2,10},{3,11},{4,12},{5,13},{6,14},{7,15},{8,16},{9,17... | collective-permute-start | bytes 294920 | tf_op jit(solution)/shard_map/ppermute | solution.py:266
  70.9 1.6 %collective-permute-start.11 = (bf16[24,2048]{1,0:T(8,128)(2,1)S(1)}, bf16[24,2048]{1,0:T(8,128)(2,1)S(1)}, u32[]{:S(2)}, u32[]{:S(2)}) collective-permute-start(bf16[24,2048]{1,0:T(8,128)(2,1)S(1)} %get-tuple-element.42), channel_id=1, source_target_pairs={{0,16},{1,17},{2,18},{3,19},{4,20},{5,21},{6,22},{7,23},{8,24},{9,... | collective-permute-start | bytes 294920 | tf_op jit(solution)/shard_map/ppermute | solution.py:266
  72.5 2.0 %collective-permute-start.12 = (bf16[24,2048]{1,0:T(8,128)(2,1)S(1)}, bf16[24,2048]{1,0:T(8,128)(2,1)S(1)}, u32[]{:S(2)}, u32[]{:S(2)}) collective-permute-start(bf16[24,2048]{1,0:T(8,128)(2,1)S(1)} %get-tuple-element.41), channel_id=1, source_target_pairs={{0,24},{1,25},{2,26},{3,27},{4,28},{5,29},{6,30},{7,31},{8,0},{9,1... | collective-permute-start | bytes 294920 | tf_op jit(solution)/shard_map/ppermute | solution.py:266
  74.5 2.3 %collective-permute-done.10 = bf16[24,2048]{1,0:T(8,128)(2,1)S(1)} collective-permute-done((bf16[24,2048]{1,0:T(8,128)(2,1)S(1)}, bf16[24,2048]{1,0:T(8,128)(2,1)S(1)}, u32[]{:S(2)}, u32[]{:S(2)}) %collective-permute-start.10) | collective-permute-done | bytes 98336 | tf_op jit(solution)/shard_map/ppermute | solution.py:266
  76.8 2.7 %collective-permute-done.11 = bf16[24,2048]{1,0:T(8,128)(2,1)S(1)} collective-permute-done((bf16[24,2048]{1,0:T(8,128)(2,1)S(1)}, bf16[24,2048]{1,0:T(8,128)(2,1)S(1)}, u32[]{:S(2)}, u32[]{:S(2)}) %collective-permute-start.11) | collective-permute-done | bytes 98336 | tf_op jit(solution)/shard_map/ppermute | solution.py:266
  79.5 0.7 fusion.3
  (34 shorter events, 1.6 us)
Async XLA Ops:
  2.3 10.5 %collective-permute-start = (bf16[24,2176]{1,0:T(8,128)(2,1)}, bf16[24,2176]{1,0:T(8,128)(2,1)S(1)}, u32[]{:S(2)}, u32[]{:S(2)}) collective-permute-start(bf16[24,2176]{1,0:T(8,128)(2,1)} %pack_tokens.1), channel_id=1, source_target_pairs={{0,24},{1,25},{2,26},{3,27},{4,28},{5,29},{6,30},{7,31},{8,0},{9,1... | collective-permute-start | bytes 313352 | tf_op jit(solution)/shard_map/ppermute | solution.py:266
  7.4 9.4 %collective-permute-start.1 = (bf16[24,2176]{1,0:T(8,128)(2,1)}, bf16[24,2176]{1,0:T(8,128)(2,1)S(1)}, u32[]{:S(2)}, u32[]{:S(2)}) collective-permute-start(bf16[24,2176]{1,0:T(8,128)(2,1)} %pack_tokens.1), channel_id=1, source_target_pairs={{0,16},{1,17},{2,18},{3,19},{4,20},{5,21},{6,22},{7,23},{8,24},{9,... | collective-permute-start | bytes 313352 | tf_op jit(solution)/shard_map/ppermute | solution.py:266
  7.4 9.4 %collective-permute-start.2 = (bf16[24,2176]{1,0:T(8,128)(2,1)}, bf16[24,2176]{1,0:T(8,128)(2,1)S(1)}, u32[]{:S(2)}, u32[]{:S(2)}) collective-permute-start(bf16[24,2176]{1,0:T(8,128)(2,1)} %pack_tokens.1), channel_id=1, source_target_pairs={{0,8},{1,9},{2,10},{3,11},{4,12},{5,13},{6,14},{7,15},{8,16},{9,17... | collective-permute-start | bytes 313352 | tf_op jit(solution)/shard_map/ppermute | solution.py:266
  8.4 15.6 %copy-start.4 = (bf16[8,3,2,2,128]{4,3,2,1,0:T(2,128)(2,1)S(1)}, bf16[8,3,2,2,128]{4,3,2,1,0:T(2,128)(2,1)}, u32[]{:S(2)}) copy-start(bf16[8,3,2,2,128]{4,3,2,1,0:T(2,128)(2,1)} %param.17) | copy-start | bytes 73732
  8.4 16.1 %copy-start.3 = (s32[256,1]{0,1:T(1,128)S(1)}, s32[256,1]{0,1:T(1,128)}, u32[]{:S(2)}) copy-start(s32[256,1]{0,1:T(1,128)} %param.13) | copy-start | bytes 3076
  8.4 16.9 %copy-start.5 = (s32[256]{0:T(256)S(1)}, s32[256]{0:T(256)}, u32[]{:S(2)}) copy-start(s32[256]{0:T(256)} %param.14) | copy-start | bytes 3076
  8.4 16.9 %copy-start.6 = (s32[256]{0:T(256)S(1)}, s32[256]{0:T(256)}, u32[]{:S(2)}) copy-start(s32[256]{0:T(256)} %param.15) | copy-start | bytes 3076
  9.5 0.7 copy-start.2
  17.7 8.5 %collective-permute-start.3 = (bf16[96,2176]{1,0:T(8,128)(2,1)S(1)}, bf16[96,2176]{1,0:T(8,128)(2,1)S(1)}, u32[]{:S(2)}, u32[]{:S(2)}) collective-permute-start(bf16[96,2176]{1,0:T(8,128)(2,1)S(1)} %pad_maximum_fusion.1), channel_id=1, source_target_pairs={{0,2},{1,5},{2,0},{3,7},{4,6},{5,1},{6,4},{7,3},{8,10},{9,13},{10,... | collective-permute-start | bytes 1253384 | tf_op jit(solution)/shard_map/ppermute | solution.py:266
  19.3 19.1 %all-to-all-start = ((bf16[32,2,2,16,128]{4,3,2,1,0:T(8,128)(2,1)}), bf16[32,2,2,16,128]{4,3,2,1,0:T(8,128)(2,1)S(1)}, u32[]{:S(2)}, u32[]{:S(2)}) async-start(bf16[32,2,2,16,128]{4,3,2,1,0:T(8,128)(2,1)} %quantize_pages.1), calls=%async_computation | async-start | bytes 1048576 | tf_op jit(solution)/shard_map/all_to_all | solution.py:345
  26.3 15.5 %collective-permute-start.5 = (bf16[192,2176]{1,0:T(8,128)(2,1)S(1)}, bf16[192,2176]{1,0:T(8,128)(2,1)S(1)}, u32[]{:S(2)}, u32[]{:S(2)}) collective-permute-start(bf16[192,2176]{1,0:T(8,128)(2,1)S(1)} %pad_maximum_fusion.sr_ref), channel_id=1, source_target_pairs={{0,4},{1,3},{2,6},{3,1},{4,0},{5,7},{6,2},{7,5},{8,12},{9,11},{10,... | collective-permute-start | bytes 2506760 | tf_op jit(solution)/shard_map/ppermute | solution.py:266
  28.0 15.8 %collective-permute-start.4 = (bf16[192,2176]{1,0:T(8,128)(2,1)S(1)}, bf16[192,2176]{1,0:T(8,128)(2,1)S(1)}, u32[]{:S(2)}, u32[]{:S(2)}) collective-permute-start(bf16[192,2176]{1,0:T(8,128)(2,1)S(1)} %pad_maximum_fusion.sr_ref), channel_id=1, source_target_pairs={{0,1},{1,0},{2,3},{3,2},{4,5},{5,4},{6,7},{7,6},{8,9},{9,8},{10,11... | collective-permute-start | bytes 2506760 | tf_op jit(solution)/shard_map/ppermute | solution.py:266
  41.9 2.4 %collective-permute-start.6 = (bf16[192,2176]{1,0:T(8,128)(2,1)S(1)}, bf16[192,2176]{1,0:T(8,128)(2,1)S(1)}, u32[]{:S(2)}, u32[]{:S(2)}) collective-permute-start(bf16[192,2176]{1,0:T(8,128)(2,1)S(1)} %collective-permute-done.5.r2_ref), channel_id=1, source_target_pairs={{0,1},{1,0},{2,3},{3,2},{4,5},{5,4},{6,7},{7,6},{8,9},{9,8},{10,11... | collective-permute-start | bytes 2506760 | tf_op jit(solution)/shard_map/ppermute | solution.py:266
  44.3 3.5 %copy-start = (bf16[1,768,2048]{2,1,0:T(8,128)(2,1)S(1)}, bf16[1,768,2048]{2,1,0:T(8,128)(2,1)}, u32[]{:S(2)}) copy-start(bf16[1,768,2048]{2,1,0:T(8,128)(2,1)} %down_ref.3) | copy-start | bytes 9437188
  46.1 1.6 %collective-permute-start.7 = (bf16[384,384]{1,0:T(8,128)(2,1)S(1)}, bf16[384,384]{1,0:T(8,128)(2,1)S(1)}, u32[]{:S(2)}, u32[]{:S(2)}) collective-permute-start(bf16[384,384]{1,0:T(8,128)(2,1)S(1)} %expert_hidden.1.own_ref), channel_id=1, source_target_pairs={{0,1},{1,0},{2,3},{3,2},{4,5},{5,4},{6,7},{7,6},{8,9},{9,8},{10,11... | collective-permute-start | bytes 884744 | tf_op jit(solution)/shard_map/ppermute | solution.py:266
  46.4 3.8 %copy-start.1 = (bf16[8,3,32,128]{3,2,1,0:T(8,128)(2,1)S(1)}, bf16[8,3,32,128]{3,2,1,0:T(8,128)(2,1)}, u32[]{:S(2)}) copy-start(bf16[8,3,32,128]{3,2,1,0:T(8,128)(2,1)} %q_ref.1) | copy-start | bytes 589828
  49.3 12.1 %collective-permute-start.8 = (bf16[192,2048]{1,0:T(8,128)(2,1)S(1)}, bf16[192,2048]{1,0:T(8,128)(2,1)S(1)}, u32[]{:S(2)}, u32[]{:S(2)}) collective-permute-start(bf16[192,2048]{1,0:T(8,128)(2,1)S(1)} %expert_back_send.1), channel_id=1, source_target_pairs={{0,2},{1,5},{2,0},{3,7},{4,6},{5,1},{6,4},{7,3},{8,10},{9,13},{10,... | collective-permute-start | bytes 2359304 | tf_op jit(solution)/shard_map/ppermute | solution.py:266
  61.6 7.8 %collective-permute-start.9 = (bf16[96,2048]{1,0:T(8,128)(2,1)S(1)}, bf16[96,2048]{1,0:T(8,128)(2,1)S(1)}, u32[]{:S(2)}, u32[]{:S(2)}) collective-permute-start(bf16[96,2048]{1,0:T(8,128)(2,1)S(1)} %slice.44), channel_id=1, source_target_pairs={{0,4},{1,3},{2,6},{3,1},{4,0},{5,7},{6,2},{7,5},{8,12},{9,11},{10,... | collective-permute-start | bytes 1179656 | tf_op jit(solution)/shard_map/ppermute | solution.py:266
  69.6 7.2 %collective-permute-start.10 = (bf16[24,2048]{1,0:T(8,128)(2,1)S(1)}, bf16[24,2048]{1,0:T(8,128)(2,1)S(1)}, u32[]{:S(2)}, u32[]{:S(2)}) collective-permute-start(bf16[24,2048]{1,0:T(8,128)(2,1)S(1)} %get-tuple-element.40), channel_id=1, source_target_pairs={{0,8},{1,9},{2,10},{3,11},{4,12},{5,13},{6,14},{7,15},{8,16},{9,17... | collective-permute-start | bytes 294920 | tf_op jit(solution)/shard_map/ppermute | solution.py:266
  70.9 8.6 %collective-permute-start.11 = (bf16[24,2048]{1,0:T(8,128)(2,1)S(1)}, bf16[24,2048]{1,0:T(8,128)(2,1)S(1)}, u32[]{:S(2)}, u32[]{:S(2)}) collective-permute-start(bf16[24,2048]{1,0:T(8,128)(2,1)S(1)} %get-tuple-element.42), channel_id=1, source_target_pairs={{0,16},{1,17},{2,18},{3,19},{4,20},{5,21},{6,22},{7,23},{8,24},{9,... | collective-permute-start | bytes 294920 | tf_op jit(solution)/shard_map/ppermute | solution.py:266
  72.5 7.0 %collective-permute-start.12 = (bf16[24,2048]{1,0:T(8,128)(2,1)S(1)}, bf16[24,2048]{1,0:T(8,128)(2,1)S(1)}, u32[]{:S(2)}, u32[]{:S(2)}) collective-permute-start(bf16[24,2048]{1,0:T(8,128)(2,1)S(1)} %get-tuple-element.41), channel_id=1, source_target_pairs={{0,24},{1,25},{2,26},{3,27},{4,28},{5,29},{6,30},{7,31},{8,0},{9,1... | collective-permute-start | bytes 294920 | tf_op jit(solution)/shard_map/ppermute | solution.py:266

commit v16 on v13

--- a/solution.py
+++ b/solution.py
@@ -345,10 +345,11 @@
 
     near_weights = weights_of(core_then)
     r2, near_weights = lax.optimization_barrier((r2, near_weights))
+    core_last, r2 = lax.optimization_barrier((core_then, r2))
     other_sr, other_r2 = moves.cores(sr), moves.cores(r2)
 
     parts = expert_front((sr, r2), *near_weights, None)
-    hidden = expert_front((other_sr, other_r2), *weights_of(1 - core_then), parts)
+    hidden = expert_front((other_sr, other_r2), *weights_of(1 - core_last), parts)
     other_hidden = moves.cores(hidden)
     sent = expert_back(True, owners, at, hidden, other_hidden, w_down, sr, r2, lanes)
     kept = expert_back(False, owners, at, hidden, other_hidden, w_down, sr, r2, lanes)

time: 80.6 us -> 86.9 us (1.078)
  local copies, waits for them, and re-layouts: 6.05 us -> 10.3 us
  starting transfers between devices: 21.1 us -> 22.7 us
  Pallas kernels: 13 us -> 14.5 us
  waiting for transfers between devices: 36.6 us -> 35.4 us
    unnamed x16 -> x26, local copies, waits for them, and re-layouts: 2.25 us -> 6.28 us
    pallas_call x2, Pallas kernels: 3.62 us -> 5.16 us  [expert_front(): pl.pallas_call(functools.partial(hidden_kernel if last else partial_kerne...]
    ppermute x13, waiting for transfers between devices: 26.2 us -> 24.8 us  [go(): return lax.ppermute(x, ('ep', 'pd'), perm)]
    all_to_all x1, starting transfers between devices: 4.68 us -> 6.06 us  [body(): cache = lax.all_to_all(send, 'ep', split_axis=0, concat_axis=0, tiled=True)]
    dynamic_slice x1 -> x3, local copies, waits for them, and re-layouts: 3.46 us -> 3.69 us  [weights_of(): lax.dynamic_slice_in_dim(w[0], half * (d // 2), d // 2, axis=0)]
  transfers between devices with their start and end apart: 14 -> 14, of which waited for: 9 -> 7; matrix products, arithmetic and copies ran while one was open for 8% -> 7% of each run, Pallas kernels for 10% -> 9%
where the time goes in v16:
time: 86.9 us; the launch traced here: 86.5 us
  waiting for transfers between devices  35.4 us (41%)
  starting transfers between devices  22.7 us (26%)
  Pallas kernels  14.5 us (17%)
  local copies, waits for them, and re-layouts  10.3 us (12%)
  other arithmetic  2.72 us (3%)
    ppermute x13, waiting for transfers between devices, go(): return lax.ppermute(x, ('ep', 'pd'), perm)  24.8 us
    ppermute x13, starting transfers between devices, go(): return lax.ppermute(x, ('ep', 'pd'), perm)  16.7 us
    all_to_all x1, waiting for transfers between devices, body(): cache = lax.all_to_all(send, 'ep', split_axis=0, concat_axis=0, tiled=True)  10.6 us
    unnamed x26, local copies, waits for them, and re-layouts  6.28 us
    all_to_all x1, starting transfers between devices, body(): cache = lax.all_to_all(send, 'ep', split_axis=0, concat_axis=0, tiled=True)  6.06 us
    pallas_call x2, Pallas kernels, expert_front(): pl.pallas_call(functools.partial(hidden_kernel if last else partial_kerne...  5.16 us
    dynamic_slice x3, local copies, waits for them, and re-layouts, weights_of(): lax.dynamic_slice_in_dim(w[0], half * (d // 2), d // 2, axis=0)  3.69 us
    pallas_call x2, Pallas kernels, expert_back(): pl.pallas_call(functools.partial(back_kernel, send, experts, lanes, 4), o...  3.05 us
  transfers between devices with their start and end apart: 14, of which 7 were waited for; matrix products, arithmetic and copies ran while one was open for 7% of the time, Pallas kernels for 9%

profile of v16, /device:TPU:0, one launch (start us, length us, event | category | flops | bytes accessed | tf_op | source)
XLA Modules:
  0.0 86.5 jit_solution(6874404563415768621)
XLA Ops:
  0.6 1.7 %pack_tokens.1 = bf16[24,2176]{1,0:T(8,128)(2,1)} custom-call(s32[1]{0:T(128)} %bitcast.1.core_ref, bf16[24,4096]{1,0:T(8,128)(2,1)} %bitcast.31, s32[24,8]{1,0:T(8,128)} %bitcast.33, f32[24,8]{1,0:T(8,128)} %bitcast.34), custom_call_target="tpu_custom_call" | custom-call | tf_op jit(solution)/shard_map/pack_tokens/pallas_call | solution.py:308
  2.4 3.0 %collective-permute-start.2 = (bf16[24,2176]{1,0:T(8,128)(2,1)}, bf16[24,2176]{1,0:T(8,128)(2,1)S(1)}, u32[]{:S(2)}, u32[]{:S(2)}) collective-permute-start(bf16[24,2176]{1,0:T(8,128)(2,1)} %pack_tokens.1), channel_id=1, source_target_pairs={{0,8},{1,9},{2,10},{3,11},{4,12},{5,13},{6,14},{7,15},{8,16},{9,17... | collective-permute-start | bytes 313352 | tf_op jit(solution)/shard_map/ppermute | solution.py:267
  5.4 2.6 %collective-permute-start.1 = (bf16[24,2176]{1,0:T(8,128)(2,1)}, bf16[24,2176]{1,0:T(8,128)(2,1)S(1)}, u32[]{:S(2)}, u32[]{:S(2)}) collective-permute-start(bf16[24,2176]{1,0:T(8,128)(2,1)} %pack_tokens.1), channel_id=1, source_target_pairs={{0,16},{1,17},{2,18},{3,19},{4,20},{5,21},{6,22},{7,23},{8,24},{9,... | collective-permute-start | bytes 313352 | tf_op jit(solution)/shard_map/ppermute | solution.py:267
  8.0 1.3 %collective-permute-start = (bf16[24,2176]{1,0:T(8,128)(2,1)}, bf16[24,2176]{1,0:T(8,128)(2,1)S(1)}, u32[]{:S(2)}, u32[]{:S(2)}) collective-permute-start(bf16[24,2176]{1,0:T(8,128)(2,1)} %pack_tokens.1), channel_id=1, source_target_pairs={{0,24},{1,25},{2,26},{3,27},{4,28},{5,29},{6,30},{7,31},{8,0},{9,1... | collective-permute-start | bytes 313352 | tf_op jit(solution)/shard_map/ppermute | solution.py:267
  9.3 1.0 %copy.22 = bf16[16,2,16,2,128]{4,2,3,1,0:T(8,128)(2,1)S(1)} copy(bf16[16,2,16,2,128]{4,3,2,1,0:T(2,128)(2,1)} %param.12) | data formatting | bytes 524288 | tf_op args[0]
  10.4 0.7 copy-done.5
  11.1 2.7 %quantize_pages.1 = bf16[32,2,2,16,128]{4,3,2,1,0:T(8,128)(2,1)} custom-call(s32[1]{0:T(128)} %bitcast.me_ref, s32[256]{0:T(256)S(1)} %bitcast.30, bf16[16,2,2,16,128]{4,3,2,1,0:T(8,128)(2,1)S(1)} %bitcast.29), custom_call_target="tpu_custom_call" | custom-call | tf_op jit(solution)/shard_map/quantize_pages/pallas_call | solution.py:320
  13.7 1.4 %collective-permute-done.1 = bf16[24,2176]{1,0:T(8,128)(2,1)S(1)} collective-permute-done((bf16[24,2176]{1,0:T(8,128)(2,1)}, bf16[24,2176]{1,0:T(8,128)(2,1)S(1)}, u32[]{:S(2)}, u32[]{:S(2)}) %collective-permute-start.1) | collective-permute-done | bytes 104480 | tf_op jit(solution)/shard_map/ppermute | solution.py:267
  15.2 0.9 %pad_maximum_fusion.1 = bf16[96,2176]{1,0:T(8,128)(2,1)S(1)} fusion(bf16[24,2176]{1,0:T(8,128)(2,1)S(1)} %collective-permute-done.2, bf16[24,2176]{1,0:T(8,128)(2,1)S(1)} %collective-permute-done.1, bf16[24,2176]{1,0:T(8,128)(2,1)S(1)} %collective-permute-done, bf16[24,2176]{1,0:T(8,128)(2,1)} %pack_tokens.1), kind=kLoop, calls=%fused_computation.8 | loop fusion | flops 1671168 | bytes 835584 | tf_op jit(solution)/shard_map/concatenate | solution.py:330
  16.1 1.6 %collective-permute-start.3 = (bf16[96,2176]{1,0:T(8,128)(2,1)S(1)}, bf16[96,2176]{1,0:T(8,128)(2,1)S(1)}, u32[]{:S(2)}, u32[]{:S(2)}) collective-permute-start(bf16[96,2176]{1,0:T(8,128)(2,1)S(1)} %pad_maximum_fusion.1), channel_id=1, source_target_pairs={{0,2},{1,5},{2,0},{3,7},{4,6},{5,1},{6,4},{7,3},{8,10},{9,13},{10,... | collective-permute-start | bytes 1253384 | tf_op jit(solution)/shard_map/ppermute | solution.py:267
  17.7 6.1 %all-to-all-start = ((bf16[32,2,2,16,128]{4,3,2,1,0:T(8,128)(2,1)}), bf16[32,2,2,16,128]{4,3,2,1,0:T(8,128)(2,1)S(1)}, u32[]{:S(2)}, u32[]{:S(2)}) async-start(bf16[32,2,2,16,128]{4,3,2,1,0:T(8,128)(2,1)} %quantize_pages.1), calls=%async_computation | async-start | bytes 1048576 | tf_op jit(solution)/shard_map/all_to_all | solution.py:338
  24.2 0.7 reduce.3
  25.3 2.0 %collective-permute-start.5 = (bf16[192,2176]{1,0:T(8,128)(2,1)S(1)}, bf16[192,2176]{1,0:T(8,128)(2,1)S(1)}, u32[]{:S(2)}, u32[]{:S(2)}) collective-permute-start(bf16[192,2176]{1,0:T(8,128)(2,1)S(1)} %pad_maximum_fusion.sr_ref), channel_id=1, source_target_pairs={{0,4},{1,3},{2,6},{3,1},{4,0},{5,7},{6,2},{7,5},{8,12},{9,11},{10,... | collective-permute-start | bytes 2506760 | tf_op jit(solution)/shard_map/ppermute | solution.py:267
  27.3 10.6 %all-to-all-done.cache_ref = bf16[32,2,2,16,128]{4,3,2,1,0:T(8,128)(2,1)S(1)} async-done(((bf16[32,2,2,16,128]{4,3,2,1,0:T(8,128)(2,1)}), bf16[32,2,2,16,128]{4,3,2,1,0:T(8,128)(2,1)S(1)}, u32[]{:S(2)}, u32[]{:S(2)}) %all-to-all-start) | async-done | bytes 524320 | tf_op jit(solution)/shard_map/all_to_all | solution.py:338
  37.9 0.8 copy-done.2
  38.7 3.4 %dynamic-slice_bitcast_fusion.2 = (bf16[2048,384]{1,0:T(8,128)(2,1)S(1)}, bf16[2048,384]{1,0:T(8,128)(2,1)}) fusion(bf16[1,4096,384]{2,1,0:T(8,128)(2,1)} %param.22, s32[]{:T(128)S(6)} %select_n.8, bf16[1,4096,384]{2,1,0:T(8,128)(2,1)} %param.21), kind=kLoop, calls=%fused_computation.3 | loop fusion | bytes 6291460 | tf_op jit(solution)/shard_map/dynamic_slice | solution.py:343
  42.1 1.4 %copy-done.1 = bf16[2048,384]{1,0:T(8,128)(2,1)S(1)} copy-done((bf16[2048,384]{1,0:T(8,128)(2,1)S(1)}, bf16[2048,384]{1,0:T(8,128)(2,1)}, u32[]{:S(2)}) %copy-start.1) | copy-done | bytes 1572888
  43.5 1.8 %expert_partial.1 = (f32[384,384]{1,0:T(8,128)S(1)}, f32[384,384]{1,0:T(8,128)S(1)}) custom-call(bf16[192,2176]{1,0:T(8,128)(2,1)S(1)} %pad_maximum_fusion.sr_ref, bf16[192,2176]{1,0:T(8,128)(2,1)S(1)} %collective-permute-done.5.r2_ref, bf16[2048,384]{1,0:T(8,128)(2,1)S(1)} %copy-done.1, bf16[2048,384]{1,0:T(8,128)(2,1)S(1)} %get-tuple-element.28.up_ref), custom_call_target="tpu_custom_call" | custom-call | flops 1207959552 | bytes 5898240 | tf_op jit(solution)/shard_map/expert_partial/pallas_call | solution.py:182
  45.6 1.7 %copy-done.8 = bf16[1,4096,384]{2,1,0:T(8,128)(2,1)S(1)} copy-done((bf16[1,4096,384]{2,1,0:T(8,128)(2,1)S(1)}, bf16[1,4096,384]{2,1,0:T(8,128)(2,1)}, u32[]{:S(2)}) %copy-start.8) | copy-done | bytes 3145752
  47.5 3.4 %expert_hidden.1.own_ref = bf16[384,384]{1,0:T(8,128)(2,1)S(1)} custom-call(bf16[192,2176]{1,0:T(8,128)(2,1)} %collective-permute-done.4.sr_ref, bf16[192,2176]{1,0:T(8,128)(2,1)} %collective-permute-done.6.r2_ref, bf16[2048,384]{1,0:T(8,128)(2,1)S(1)} %dynamic-slice_bitcast_fusion.1.gate_ref, bf16[2048,384]{1,0:T(8,128)(2,1)S(1)} %dynamic-slice_bitcast_fusion.up_ref, ...), custom_call_target="tpu_custom_call" | custom-call | flops 1207959552 | bytes 5898240 | tf_op jit(solution)/shard_map/expert_hidden/pallas_call | solution.py:182
  51.5 1.1 %collective-permute-done.7.other_ref = bf16[384,384]{1,0:T(8,128)(2,1)S(1)} collective-permute-done((bf16[384,384]{1,0:T(8,128)(2,1)S(1)}, bf16[384,384]{1,0:T(8,128)(2,1)S(1)}, u32[]{:S(2)}, u32[]{:S(2)}) %collective-permute-start.7) | collective-permute-done | bytes 294944 | tf_op jit(solution)/shard_map/ppermute | solution.py:267
  52.6 1.5 %expert_back_send.1 = bf16[192,2048]{1,0:T(8,128)(2,1)S(1)} custom-call(s32[2]{0:T(128)S(1)} %pad_add_fusion.at_ref, bf16[384,384]{1,0:T(8,128)(2,1)S(1)} %expert_hidden.1.own_ref, bf16[384,384]{1,0:T(8,128)(2,1)S(1)} %collective-permute-done.7.other_ref, bf16[192,2176]{1,0:T(8,128)(2,1)S(1)} %pad_maximum_fusion.sr_ref, ...), custom_call_target="tpu_custom_call" | custom-call | flops 603979776 | bytes 5308416 | tf_op jit(solution)/shard_map/expert_back_send/pallas_call | solution.py:241
  54.8 1.9 %attention.1 = bf16[8,3,32,128]{3,2,1,0:T(8,128)(2,1)} custom-call(s32[1]{0:T(128)} %bitcast.me_ref, s32[16,16]{1,0:T(8,128)S(1)} %reshape.42.owner_ref, s32[16,16]{1,0:T(8,128)S(1)} %reshape.43.slot_ref, s32[16,16]{1,0:T(8,128)S(1)} %reshape.44.fill_ref, bf16[8,3,32,128]{3,2,1,0:T(8,128)(2,1)S(1)} %copy-done.4, bf16[32,2,2,16,128]{4,3,2,1,0:T(8,128)(2,1)S(1)} %copy-done.3, ...), custom_call_target="tpu_custom_call" | custom-call | tf_op jit(solution)/shard_map/attention/pallas_call | solution.py:356
  56.7 1.5 %expert_back_keep.1 = f32[192,2048]{1,0:T(8,128)S(1)} custom-call(s32[2]{0:T(128)S(1)} %pad_add_fusion.at_ref, bf16[384,384]{1,0:T(8,128)(2,1)S(1)} %expert_hidden.1.own_ref, bf16[384,384]{1,0:T(8,128)(2,1)S(1)} %collective-permute-done.7.other_ref, bf16[192,2176]{1,0:T(8,128)(2,1)S(1)} %pad_maximum_fusion.sr_ref, ...), custom_call_target="tpu_custom_call" | custom-call | flops 603979776 | bytes 5308416 | tf_op jit(solution)/shard_map/expert_back_keep/pallas_call | solution.py:241
  58.3 7.9 %collective-permute-done.8 = bf16[192,2048]{1,0:T(8,128)(2,1)S(1)} collective-permute-done((bf16[192,2048]{1,0:T(8,128)(2,1)S(1)}, bf16[192,2048]{1,0:T(8,128)(2,1)S(1)}, u32[]{:S(2)}, u32[]{:S(2)}) %collective-permute-start.8) | collective-permute-done | bytes 786464 | tf_op jit(solution)/shard_map/ppermute | solution.py:267
  66.5 1.1 %collective-permute-start.9 = (bf16[96,2048]{1,0:T(8,128)(2,1)S(1)}, bf16[96,2048]{1,0:T(8,128)(2,1)S(1)}, u32[]{:S(2)}, u32[]{:S(2)}) collective-permute-start(bf16[96,2048]{1,0:T(8,128)(2,1)S(1)} %slice.44), channel_id=1, source_target_pairs={{0,4},{1,3},{2,6},{3,1},{4,0},{5,7},{6,2},{7,5},{8,12},{9,11},{10,... | collective-permute-start | bytes 1179656 | tf_op jit(solution)/shard_map/ppermute | solution.py:267
  67.5 6.8 %collective-permute-done.9 = bf16[96,2048]{1,0:T(8,128)(2,1)S(1)} collective-permute-done((bf16[96,2048]{1,0:T(8,128)(2,1)S(1)}, bf16[96,2048]{1,0:T(8,128)(2,1)S(1)}, u32[]{:S(2)}, u32[]{:S(2)}) %collective-permute-start.9) | collective-permute-done | bytes 393248 | tf_op jit(solution)/shard_map/ppermute | solution.py:267
  74.5 1.3 %collective-permute-start.10 = (bf16[24,2048]{1,0:T(8,128)(2,1)S(1)}, bf16[24,2048]{1,0:T(8,128)(2,1)S(1)}, u32[]{:S(2)}, u32[]{:S(2)}) collective-permute-start(bf16[24,2048]{1,0:T(8,128)(2,1)S(1)} %get-tuple-element.40), channel_id=1, source_target_pairs={{0,8},{1,9},{2,10},{3,11},{4,12},{5,13},{6,14},{7,15},{8,16},{9,17... | collective-permute-start | bytes 294920 | tf_op jit(solution)/shard_map/ppermute | solution.py:267
  75.8 2.5 %collective-permute-start.12 = (bf16[24,2048]{1,0:T(8,128)(2,1)S(1)}, bf16[24,2048]{1,0:T(8,128)(2,1)S(1)}, u32[]{:S(2)}, u32[]{:S(2)}) collective-permute-start(bf16[24,2048]{1,0:T(8,128)(2,1)S(1)} %get-tuple-element.41), channel_id=1, source_target_pairs={{0,24},{1,25},{2,26},{3,27},{4,28},{5,29},{6,30},{7,31},{8,0},{9,1... | collective-permute-start | bytes 294920 | tf_op jit(solution)/shard_map/ppermute | solution.py:267
  78.3 3.6 %collective-permute-done.10 = bf16[24,2048]{1,0:T(8,128)(2,1)S(1)} collective-permute-done((bf16[24,2048]{1,0:T(8,128)(2,1)S(1)}, bf16[24,2048]{1,0:T(8,128)(2,1)S(1)}, u32[]{:S(2)}, u32[]{:S(2)}) %collective-permute-start.10) | collective-permute-done | bytes 98336 | tf_op jit(solution)/shard_map/ppermute | solution.py:267
  81.9 3.9 %collective-permute-done.11 = bf16[24,2048]{1,0:T(8,128)(2,1)S(1)} collective-permute-done((bf16[24,2048]{1,0:T(8,128)(2,1)S(1)}, bf16[24,2048]{1,0:T(8,128)(2,1)S(1)}, u32[]{:S(2)}, u32[]{:S(2)}) %collective-permute-start.11) | collective-permute-done | bytes 98336 | tf_op jit(solution)/shard_map/ppermute | solution.py:267
  85.8 0.7 fusion.3
  (46 shorter events, 3.0 us)
Async XLA Ops:
  2.4 11.4 %collective-permute-start.2 = (bf16[24,2176]{1,0:T(8,128)(2,1)}, bf16[24,2176]{1,0:T(8,128)(2,1)S(1)}, u32[]{:S(2)}, u32[]{:S(2)}) collective-permute-start(bf16[24,2176]{1,0:T(8,128)(2,1)} %pack_tokens.1), channel_id=1, source_target_pairs={{0,8},{1,9},{2,10},{3,11},{4,12},{5,13},{6,14},{7,15},{8,16},{9,17... | collective-permute-start | bytes 313352 | tf_op jit(solution)/shard_map/ppermute | solution.py:267
  5.4 9.8 %collective-permute-start.1 = (bf16[24,2176]{1,0:T(8,128)(2,1)}, bf16[24,2176]{1,0:T(8,128)(2,1)S(1)}, u32[]{:S(2)}, u32[]{:S(2)}) collective-permute-start(bf16[24,2176]{1,0:T(8,128)(2,1)} %pack_tokens.1), channel_id=1, source_target_pairs={{0,16},{1,17},{2,18},{3,19},{4,20},{5,21},{6,22},{7,23},{8,24},{9,... | collective-permute-start | bytes 313352 | tf_op jit(solution)/shard_map/ppermute | solution.py:267
  8.0 7.2 %collective-permute-start = (bf16[24,2176]{1,0:T(8,128)(2,1)}, bf16[24,2176]{1,0:T(8,128)(2,1)S(1)}, u32[]{:S(2)}, u32[]{:S(2)}) collective-permute-start(bf16[24,2176]{1,0:T(8,128)(2,1)} %pack_tokens.1), channel_id=1, source_target_pairs={{0,24},{1,25},{2,26},{3,27},{4,28},{5,29},{6,30},{7,31},{8,0},{9,1... | collective-permute-start | bytes 313352 | tf_op jit(solution)/shard_map/ppermute | solution.py:267
  9.3 14.9 %copy-start.6 = (s32[256,1]{0,1:T(1,128)S(1)}, s32[256,1]{0,1:T(1,128)}, u32[]{:S(2)}) copy-start(s32[256,1]{0,1:T(1,128)} %param.13) | copy-start | bytes 3076
  9.3 15.7 %copy-start.10 = (s32[256]{0:T(256)S(1)}, s32[256]{0:T(256)}, u32[]{:S(2)}) copy-start(s32[256]{0:T(256)} %param.14) | copy-start | bytes 3076
  9.3 15.7 %copy-start.11 = (s32[256]{0:T(256)S(1)}, s32[256]{0:T(256)}, u32[]{:S(2)}) copy-start(s32[256]{0:T(256)} %param.15) | copy-start | bytes 3076
  9.3 15.8 %copy-start.9 = (bf16[8,3,2,2,128]{4,3,2,1,0:T(2,128)(2,1)S(1)}, bf16[8,3,2,2,128]{4,3,2,1,0:T(2,128)(2,1)}, u32[]{:S(2)}) copy-start(bf16[8,3,2,2,128]{4,3,2,1,0:T(2,128)(2,1)} %param.17) | copy-start | bytes 73732
  10.4 0.7 copy-start.5
  16.1 9.1 %collective-permute-start.3 = (bf16[96,2176]{1,0:T(8,128)(2,1)S(1)}, bf16[96,2176]{1,0:T(8,128)(2,1)S(1)}, u32[]{:S(2)}, u32[]{:S(2)}) collective-permute-start(bf16[96,2176]{1,0:T(8,128)(2,1)S(1)} %pad_maximum_fusion.1), channel_id=1, source_target_pairs={{0,2},{1,5},{2,0},{3,7},{4,6},{5,1},{6,4},{7,3},{8,10},{9,13},{10,... | collective-permute-start | bytes 1253384 | tf_op jit(solution)/shard_map/ppermute | solution.py:267
  17.7 20.3 %all-to-all-start = ((bf16[32,2,2,16,128]{4,3,2,1,0:T(8,128)(2,1)}), bf16[32,2,2,16,128]{4,3,2,1,0:T(8,128)(2,1)S(1)}, u32[]{:S(2)}, u32[]{:S(2)}) async-start(bf16[32,2,2,16,128]{4,3,2,1,0:T(8,128)(2,1)} %quantize_pages.1), calls=%async_computation | async-start | bytes 1048576 | tf_op jit(solution)/shard_map/all_to_all | solution.py:338
  25.3 16.8 %collective-permute-start.5 = (bf16[192,2176]{1,0:T(8,128)(2,1)S(1)}, bf16[192,2176]{1,0:T(8,128)(2,1)S(1)}, u32[]{:S(2)}, u32[]{:S(2)}) collective-permute-start(bf16[192,2176]{1,0:T(8,128)(2,1)S(1)} %pad_maximum_fusion.sr_ref), channel_id=1, source_target_pairs={{0,4},{1,3},{2,6},{3,1},{4,0},{5,7},{6,2},{7,5},{8,12},{9,11},{10,... | collective-permute-start | bytes 2506760 | tf_op jit(solution)/shard_map/ppermute | solution.py:267
  27.3 20.2 %collective-permute-start.4 = (bf16[192,2176]{1,0:T(8,128)(2,1)S(1)}, bf16[192,2176]{1,0:T(8,128)(2,1)}, u32[]{:S(2)}, u32[]{:S(2)}) collective-permute-start(bf16[192,2176]{1,0:T(8,128)(2,1)S(1)} %pad_maximum_fusion.sr_ref), channel_id=1, source_target_pairs={{0,1},{1,0},{2,3},{3,2},{4,5},{5,4},{6,7},{7,6},{8,9},{9,8},{10,11... | collective-permute-start | bytes 2506760 | tf_op jit(solution)/shard_map/ppermute | solution.py:267
  37.9 0.8 copy-start.2
  42.1 5.4 %collective-permute-start.6 = (bf16[192,2176]{1,0:T(8,128)(2,1)S(1)}, bf16[192,2176]{1,0:T(8,128)(2,1)}, u32[]{:S(2)}, u32[]{:S(2)}) collective-permute-start(bf16[192,2176]{1,0:T(8,128)(2,1)S(1)} %collective-permute-done.5.r2_ref), channel_id=1, source_target_pairs={{0,1},{1,0},{2,3},{3,2},{4,5},{5,4},{6,7},{7,6},{8,9},{9,8},{10,11... | collective-permute-start | bytes 2506760 | tf_op jit(solution)/shard_map/ppermute | solution.py:267
  42.1 1.4 %copy-start.1 = (bf16[2048,384]{1,0:T(8,128)(2,1)S(1)}, bf16[2048,384]{1,0:T(8,128)(2,1)}, u32[]{:S(2)}) copy-start(bf16[2048,384]{1,0:T(8,128)(2,1)} %get-tuple-element.27.gate_ref) | copy-start | bytes 4718596
  43.5 1.9 %copy-start.7 = (bf16[1,4096,384]{2,1,0:T(8,128)(2,1)S(1)}, bf16[1,4096,384]{2,1,0:T(8,128)(2,1)}, u32[]{:S(2)}) copy-start(bf16[1,4096,384]{2,1,0:T(8,128)(2,1)} %param.22) | copy-start | bytes 9437188
  45.4 1.9 %copy-start.8 = (bf16[1,4096,384]{2,1,0:T(8,128)(2,1)S(1)}, bf16[1,4096,384]{2,1,0:T(8,128)(2,1)}, u32[]{:S(2)}) copy-start(bf16[1,4096,384]{2,1,0:T(8,128)(2,1)} %param.21) | copy-start | bytes 9437188
  47.5 5.2 %copy-start = (bf16[1,768,2048]{2,1,0:T(8,128)(2,1)S(1)}, bf16[1,768,2048]{2,1,0:T(8,128)(2,1)}, u32[]{:S(2)}) copy-start(bf16[1,768,2048]{2,1,0:T(8,128)(2,1)} %down_ref.3) | copy-start | bytes 9437188
  50.9 1.8 %collective-permute-start.7 = (bf16[384,384]{1,0:T(8,128)(2,1)S(1)}, bf16[384,384]{1,0:T(8,128)(2,1)S(1)}, u32[]{:S(2)}, u32[]{:S(2)}) collective-permute-start(bf16[384,384]{1,0:T(8,128)(2,1)S(1)} %expert_hidden.1.own_ref), channel_id=1, source_target_pairs={{0,1},{1,0},{2,3},{3,2},{4,5},{5,4},{6,7},{7,6},{8,9},{9,8},{10,11... | collective-permute-start | bytes 884744 | tf_op jit(solution)/shard_map/ppermute | solution.py:267
  51.5 3.3 %copy-start.3 = (bf16[32,2,2,16,128]{4,3,2,1,0:T(8,128)(2,1)S(1)}, bf16[32,2,2,16,128]{4,3,2,1,0:T(8,128)(2,1)}, u32[]{:S(2)}) copy-start(bf16[32,2,2,16,128]{4,3,2,1,0:T(8,128)(2,1)} %copy-done.2) | copy-start | bytes 1572868
  51.5 3.3 %copy-start.4 = (bf16[8,3,32,128]{3,2,1,0:T(8,128)(2,1)S(1)}, bf16[8,3,32,128]{3,2,1,0:T(8,128)(2,1)}, u32[]{:S(2)}) copy-start(bf16[8,3,32,128]{3,2,1,0:T(8,128)(2,1)} %q_ref.1) | copy-start | bytes 589828
  54.2 12.1 %collective-permute-start.8 = (bf16[192,2048]{1,0:T(8,128)(2,1)S(1)}, bf16[192,2048]{1,0:T(8,128)(2,1)S(1)}, u32[]{:S(2)}, u32[]{:S(2)}) collective-permute-start(bf16[192,2048]{1,0:T(8,128)(2,1)S(1)} %expert_back_send.1), channel_id=1, source_target_pairs={{0,2},{1,5},{2,0},{3,7},{4,6},{5,1},{6,4},{7,3},{8,10},{9,13},{10,... | collective-permute-start | bytes 2359304 | tf_op jit(solution)/shard_map/ppermute | solution.py:267
  66.5 7.8 %collective-permute-start.9 = (bf16[96,2048]{1,0:T(8,128)(2,1)S(1)}, bf16[96,2048]{1,0:T(8,128)(2,1)S(1)}, u32[]{:S(2)}, u32[]{:S(2)}) collective-permute-start(bf16[96,2048]{1,0:T(8,128)(2,1)S(1)} %slice.44), channel_id=1, source_target_pairs={{0,4},{1,3},{2,6},{3,1},{4,0},{5,7},{6,2},{7,5},{8,12},{9,11},{10,... | collective-permute-start | bytes 1179656 | tf_op jit(solution)/shard_map/ppermute | solution.py:267
  74.5 7.5 %collective-permute-start.10 = (bf16[24,2048]{1,0:T(8,128)(2,1)S(1)}, bf16[24,2048]{1,0:T(8,128)(2,1)S(1)}, u32[]{:S(2)}, u32[]{:S(2)}) collective-permute-start(bf16[24,2048]{1,0:T(8,128)(2,1)S(1)} %get-tuple-element.40), channel_id=1, source_target_pairs={{0,8},{1,9},{2,10},{3,11},{4,12},{5,13},{6,14},{7,15},{8,16},{9,17... | collective-permute-start | bytes 294920 | tf_op jit(solution)/shard_map/ppermute | solution.py:267
  75.8 6.1 %collective-permute-start.12 = (bf16[24,2048]{1,0:T(8,128)(2,1)S(1)}, bf16[24,2048]{1,0:T(8,128)(2,1)S(1)}, u32[]{:S(2)}, u32[]{:S(2)}) collective-permute-start(bf16[24,2048]{1,0:T(8,128)(2,1)S(1)} %get-tuple-element.41), channel_id=1, source_target_pairs={{0,24},{1,25},{2,26},{3,27},{4,28},{5,29},{6,30},{7,31},{8,0},{9,1... | collective-permute-start | bytes 294920 | tf_op jit(solution)/shard_map/ppermute | solution.py:267
  78.3 7.5 %collective-permute-start.11 = (bf16[24,2048]{1,0:T(8,128)(2,1)S(1)}, bf16[24,2048]{1,0:T(8,128)(2,1)S(1)}, u32[]{:S(2)}, u32[]{:S(2)}) collective-permute-start(bf16[24,2048]{1,0:T(8,128)(2,1)S(1)} %get-tuple-element.42), channel_id=1, source_target_pairs={{0,16},{1,17},{2,18},{3,19},{4,20},{5,21},{6,22},{7,23},{8,24},{9,... | collective-permute-start | bytes 294920 | tf_op jit(solution)/shard_map/ppermute | solution.py:267
